TPU v7x, 32 devices: a whole 2x2x4 slice. The times are simulated.
32 devices in a mesh: items: 8 (over z, x), frames: 4 (over y, core).
Axes of the slice: x: 2, y: 2, z: 4, core: 2. Of those that a mesh axis runs over, the one named last changes fastest.
Arguments:
- frames_in: bfloat16 [64, 1024, 768], P('items', 'frames'), may hold values from -6 to 6
- cond: bfloat16 [64, 768], P('items'), may hold values from -6 to 6
- text: bfloat16 [64, 256, 768], P('items', 'frames'), may hold values from -6 to 6
- item_lengths: int32 [64], P('items'), may hold values from 256 to 1024, as said below
- text_lengths: int32 [64], P('items'), may hold values from 64 to 256, as said below
- ada_weight: bfloat16 [768, 6912], replicated, may hold values from -0.21875 to 0.21875
- qkv_weight: bfloat16 [768, 2304], replicated, may hold values from -0.21875 to 0.21875
- out_weight: bfloat16 [768, 768], replicated, may hold values from -0.875 to 0.875
- cross_q_weight: bfloat16 [768, 768], replicated, may hold values from -0.21875 to 0.21875
- cross_kv_weight: bfloat16 [768, 1536], replicated, may hold values from -0.21875 to 0.21875
- cross_out_weight: bfloat16 [768, 768], replicated, may hold values from -0.625 to 0.625
- up_weight: bfloat16 [768, 3072], replicated, may hold values from -0.21875 to 0.21875
- down_weight: bfloat16 [3072, 768], replicated, may hold values from -0.109375 to 0.109375
- cotangent: bfloat16 [64, 1024, 768], P('items', 'frames'), may hold values from -6 to 6
Outputs:
- layer_out: bfloat16 [64, 1024, 768], P('items', 'frames')
- input_grad: float32 [64, 1024, 768], P('items', 'frames')
- text_grad: float32 [64, 256, 768], P('items', 'frames')
- cond_grad: float32 [64, 768], P('items', 'frames')
- grad_ada: float32 [768, 6912], P('items', 'frames')
- grad_qkv: float32 [768, 2304], P('items', 'frames')
- grad_out: float32 [768, 768], P('items', 'frames')
- grad_cross_q: float32 [768, 768], P('items', 'frames')
- grad_cross_kv: float32 [768, 1536], P('items', 'frames')
- grad_cross_out: float32 [768, 768], P('items', 'frames')
- grad_up: float32 [768, 3072], P('items', 'frames')
- grad_down: float32 [3072, 768], P('items', 'frames')
Inputs may be any that keep to these rules, and one draw needn't show every extreme that they name: `item_lengths`: each item has 1024, 512 or 256 frames; of every 8 consecutive items one has all 1024. `text_lengths`: of every 8 consecutive items one has all 256 text tokens.
All inputs are finite; a program needn't handle non-finite values.
Results may differ from a plain program's by a relative error of at most 0.025.
Values may be sent and summed in bfloat16 or wider, within the bound.
No kernel may reach another device: no remote copies, remote signals or barrier semaphores. Data moves between devices by JAX's collectives and lax.ppermute only.
A program may use at most 640 MiB of HBM per device.

v0:
```python
from functools import partial

import jax
import jax.numpy as jnp
from jax import lax
from jax.sharding import PartitionSpec as P

H = 12


def norm_parts(tensor):
    centered = tensor - jnp.mean(tensor, -1, keepdims=True)
    inverse = lax.rsqrt(jnp.mean(centered * centered, -1, keepdims=True) + 1e-06)
    return (centered * inverse, inverse)


def norm_back(normed, inverse, incoming):
    return inverse * (
        incoming
        - jnp.mean(incoming, -1, keepdims=True)
        - normed * jnp.mean(incoming * normed, -1, keepdims=True)
    )


def split_heads(tensor):
    return tensor.reshape(tensor.shape[0], tensor.shape[1], H, -1)


def attend(queries, keys_in, values_in, key_valid, score_scale):
    scores = (
        jnp.einsum(
            "ifhd,ijhd->ihfj",
            split_heads(queries),
            split_heads(keys_in),
            preferred_element_type=jnp.float32,
        )
        * score_scale
    )
    scores = jnp.where(key_valid[:, None, None, :], scores, -1e30)
    attn_prob = jax.nn.softmax(scores, axis=-1)
    log_total = jax.nn.logsumexp(scores, axis=-1)
    low_prob = attn_prob.astype(jnp.bfloat16)
    mixed = jnp.einsum(
        "ihfj,ijhd->ifhd", low_prob, split_heads(values_in), preferred_element_type=jnp.float32
    )
    return (attn_prob, low_prob, mixed.astype(jnp.bfloat16).reshape(queries.shape), log_total)


def attend_back(grad_mixed, queries, keys_in, values_in, attn_prob, low_prob, score_scale):
    grad_heads = split_heads(grad_mixed)
    grad_prob = jnp.einsum(
        "ifhd,ijhd->ihfj", grad_heads, split_heads(values_in), preferred_element_type=jnp.float32
    )
    grad_values = jnp.einsum(
        "ihfj,ifhd->ijhd", low_prob, grad_heads, preferred_element_type=jnp.float32
    )
    grad_scores = (
        attn_prob * (grad_prob - jnp.sum(attn_prob * grad_prob, -1, keepdims=True))
    ).astype(jnp.bfloat16)
    grad_queries = (
        jnp.einsum(
            "ihfj,ijhd->ifhd", grad_scores, split_heads(keys_in), preferred_element_type=jnp.float32
        )
        * score_scale
    )
    grad_keys = (
        jnp.einsum(
            "ihfj,ifhd->ijhd", grad_scores, split_heads(queries), preferred_element_type=jnp.float32
        )
        * score_scale
    )
    return (
        grad_queries.reshape(queries.shape),
        grad_keys.reshape(keys_in.shape),
        grad_values.reshape(values_in.shape),
    )


def project(tensor, weight):
    return jnp.einsum("ifd,de->ife", tensor, weight, preferred_element_type=jnp.float32)


def project_back(tensor, weight):
    return jnp.einsum("ife,de->ifd", tensor, weight, preferred_element_type=jnp.float32)


def weight_grad(left, right):
    return jnp.einsum("ifd,ife->de", left, right, preferred_element_type=jnp.float32)


def on_device(
    frames_in,
    cond,
    text,
    item_lengths,
    text_lengths,
    ada_weight,
    qkv_weight,
    out_weight,
    cross_q_weight,
    cross_kv_weight,
    cross_out_weight,
    up_weight,
    down_weight,
    cotangent,
):
    model_width = frames_in.shape[-1]
    score_scale = (model_width // H) ** (-0.5)
    cond_f = cond.astype(jnp.float32)
    low_cond = jax.nn.silu(cond_f).astype(jnp.bfloat16)
    modulation = jnp.dot(low_cond, ada_weight, preferred_element_type=jnp.float32)
    pieces = [
        modulation[:, None, position * model_width : (position + 1) * model_width]
        for position in range(9)
    ]
    shift_a, scale_a, gate_a, shift_b, scale_b, gate_b, shift_c, scale_c, gate_c = pieces
    residual_in = frames_in.astype(jnp.float32)
    normed_a, inverse_a = norm_parts(residual_in)
    hidden_a = (normed_a * (1.0 + scale_a) + shift_a).astype(jnp.bfloat16)
    qkv = project(hidden_a, qkv_weight).astype(jnp.bfloat16)
    queries = qkv[..., :model_width]
    keys_own = qkv[..., model_width : 2 * model_width]
    values_own = qkv[..., 2 * model_width :]
    keys_all, values_all = (
        lax.all_gather(keys_own, "frames", axis=1, tiled=True),
        lax.all_gather(values_own, "frames", axis=1, tiled=True),
    )
    key_valid = jnp.arange(keys_all.shape[1], dtype=jnp.int32)[None, :] < item_lengths[:, None]
    attn_prob, low_prob, attended, self_total = attend(
        queries, keys_all, values_all, key_valid, score_scale
    )
    branch_a = project(attended, out_weight)
    first = residual_in + gate_a * branch_a
    normed_b, inverse_b = norm_parts(first)
    hidden_b = (normed_b * (1.0 + scale_b) + shift_b).astype(jnp.bfloat16)
    cross_q = project(hidden_b, cross_q_weight).astype(jnp.bfloat16)
    text_own = project(text, cross_kv_weight).astype(jnp.bfloat16)
    text_kv = lax.all_gather(text_own, "frames", axis=1, tiled=True)
    text_keys = text_kv[..., :model_width]
    text_values = text_kv[..., model_width:]
    text_valid = jnp.arange(text_kv.shape[1], dtype=jnp.int32)[None, :] < text_lengths[:, None]
    cross_prob, cross_low, crossed, cross_total = attend(
        cross_q, text_keys, text_values, text_valid, score_scale
    )
    branch_b = project(crossed, cross_out_weight)
    second = first + gate_b * branch_b
    normed_c, inverse_c = norm_parts(second)
    hidden_c = (normed_c * (1.0 + scale_c) + shift_c).astype(jnp.bfloat16)
    up_proj = project(hidden_c, up_weight)
    activated, gelu_back = jax.vjp(partial(jax.nn.gelu, approximate=False), up_proj)
    low_act = activated.astype(jnp.bfloat16)
    branch_c = project(low_act, down_weight)
    layer_out = (second + gate_c * branch_c).astype(jnp.bfloat16)
    upstream = cotangent.astype(jnp.float32)
    d_gate_c = jnp.sum(upstream * branch_c, 1)
    d_branch_c = (upstream * gate_c).astype(jnp.bfloat16)
    grad_down = weight_grad(low_act, d_branch_c)
    d_up = gelu_back(project_back(d_branch_c, down_weight))[0].astype(jnp.bfloat16)
    grad_up = weight_grad(hidden_c, d_up)
    d_hidden_c = project_back(d_up, up_weight)
    d_shift_c = jnp.sum(d_hidden_c, 1)
    d_scale_c = jnp.sum(d_hidden_c * normed_c, 1)
    upstream = upstream + norm_back(normed_c, inverse_c, d_hidden_c * (1.0 + scale_c))
    d_gate_b = jnp.sum(upstream * branch_b, 1)
    d_branch_b = (upstream * gate_b).astype(jnp.bfloat16)
    grad_cross_out = weight_grad(crossed, d_branch_b)
    d_crossed = project_back(d_branch_b, cross_out_weight).astype(jnp.bfloat16)
    d_cross_q, d_text_keys, d_text_values = attend_back(
        d_crossed, cross_q, text_keys, text_values, cross_prob, cross_low, score_scale
    )
    d_cross_q = d_cross_q.astype(jnp.bfloat16)
    grad_cross_q = weight_grad(hidden_b, d_cross_q)
    d_hidden_b = project_back(d_cross_q, cross_q_weight)
    d_text_local = jnp.concatenate([d_text_keys, d_text_values], -1)
    d_shift_b = jnp.sum(d_hidden_b, 1)
    d_scale_b = jnp.sum(d_hidden_b * normed_b, 1)
    upstream = upstream + norm_back(normed_b, inverse_b, d_hidden_b * (1.0 + scale_b))
    d_gate_a = jnp.sum(upstream * branch_a, 1)
    d_branch_a = (upstream * gate_a).astype(jnp.bfloat16)
    grad_out = weight_grad(attended, d_branch_a)
    d_attended = project_back(d_branch_a, out_weight).astype(jnp.bfloat16)
    keys_back, values_back = (
        lax.all_gather(keys_own, "frames", axis=1, tiled=True),
        lax.all_gather(values_own, "frames", axis=1, tiled=True),
    )
    d_queries, d_keys_all, d_values_all = attend_back(
        d_attended, queries, keys_back, values_back, attn_prob, low_prob, score_scale
    )
    d_keys, d_values = (
        lax.psum_scatter(
            d_keys_all.astype(jnp.bfloat16), "frames", scatter_dimension=1, tiled=True
        ).astype(jnp.float32),
        lax.psum_scatter(
            d_values_all.astype(jnp.bfloat16), "frames", scatter_dimension=1, tiled=True
        ).astype(jnp.float32),
    )
    d_qkv = jnp.concatenate(
        [
            d_queries.astype(jnp.bfloat16),
            d_keys.astype(jnp.bfloat16),
            d_values.astype(jnp.bfloat16),
        ],
        -1,
    )
    grad_qkv = weight_grad(hidden_a, d_qkv)
    d_hidden_a = project_back(d_qkv, qkv_weight)
    d_shift_a = jnp.sum(d_hidden_a, 1)
    d_scale_a = jnp.sum(d_hidden_a * normed_a, 1)
    input_grad = upstream + norm_back(normed_a, inverse_a, d_hidden_a * (1.0 + scale_a))
    d_modulation = jnp.concatenate(
        [
            d_shift_a,
            d_scale_a,
            d_gate_a,
            d_shift_b,
            d_scale_b,
            d_gate_b,
            d_shift_c,
            d_scale_c,
            d_gate_c,
        ],
        -1,
    )
    grad_ada = jnp.dot(
        low_cond.astype(jnp.float32).T,
        d_modulation,
        precision=lax.Precision.HIGHEST,
        preferred_element_type=jnp.float32,
    )
    sigmoid_c = jax.nn.sigmoid(cond_f)
    cond_part = jnp.dot(
        d_modulation,
        ada_weight.T,
        precision=lax.Precision.HIGHEST,
        preferred_element_type=jnp.float32,
    ) * (sigmoid_c * (1.0 + cond_f * (1.0 - sigmoid_c)))
    d_text_kv, cond_grad = (
        lax.psum_scatter(d_text_local, "frames", scatter_dimension=1, tiled=True),
        lax.psum_scatter(cond_part, "frames", scatter_dimension=1, tiled=True),
    )
    low_text_kv = d_text_kv.astype(jnp.bfloat16)
    grad_cross_kv = weight_grad(text, low_text_kv)
    text_grad = project_back(low_text_kv, cross_kv_weight)
    grads = (
        grad_ada,
        grad_qkv,
        grad_out,
        grad_cross_q,
        grad_cross_kv,
        grad_cross_out,
        grad_up,
        grad_down,
    )
    partial_sums = (
        lax.psum_scatter(
            grads[0].astype(jnp.bfloat16), "frames", scatter_dimension=1, tiled=True
        ).astype(jnp.float32),
        lax.psum_scatter(
            grads[1].astype(jnp.bfloat16), "frames", scatter_dimension=1, tiled=True
        ).astype(jnp.float32),
        lax.psum_scatter(
            grads[2].astype(jnp.bfloat16), "frames", scatter_dimension=1, tiled=True
        ).astype(jnp.float32),
        lax.psum_scatter(
            grads[3].astype(jnp.bfloat16), "frames", scatter_dimension=1, tiled=True
        ).astype(jnp.float32),
        lax.psum_scatter(
            grads[4].astype(jnp.bfloat16), "frames", scatter_dimension=1, tiled=True
        ).astype(jnp.float32),
        lax.psum_scatter(
            grads[5].astype(jnp.bfloat16), "frames", scatter_dimension=1, tiled=True
        ).astype(jnp.float32),
        lax.psum_scatter(
            grads[6].astype(jnp.bfloat16), "frames", scatter_dimension=1, tiled=True
        ).astype(jnp.float32),
        lax.psum_scatter(
            grads[7].astype(jnp.bfloat16), "frames", scatter_dimension=1, tiled=True
        ).astype(jnp.float32),
    )
    totals = (
        lax.psum_scatter(
            partial_sums[0].astype(jnp.bfloat16), "items", scatter_dimension=0, tiled=True
        ).astype(jnp.float32),
        lax.psum_scatter(
            partial_sums[1].astype(jnp.bfloat16), "items", scatter_dimension=0, tiled=True
        ).astype(jnp.float32),
        lax.psum_scatter(
            partial_sums[2].astype(jnp.bfloat16), "items", scatter_dimension=0, tiled=True
        ).astype(jnp.float32),
        lax.psum_scatter(
            partial_sums[3].astype(jnp.bfloat16), "items", scatter_dimension=0, tiled=True
        ).astype(jnp.float32),
        lax.psum_scatter(
            partial_sums[4].astype(jnp.bfloat16), "items", scatter_dimension=0, tiled=True
        ).astype(jnp.float32),
        lax.psum_scatter(
            partial_sums[5].astype(jnp.bfloat16), "items", scatter_dimension=0, tiled=True
        ).astype(jnp.float32),
        lax.psum_scatter(
            partial_sums[6].astype(jnp.bfloat16), "items", scatter_dimension=0, tiled=True
        ).astype(jnp.float32),
        lax.psum_scatter(
            partial_sums[7].astype(jnp.bfloat16), "items", scatter_dimension=0, tiled=True
        ).astype(jnp.float32),
    )
    return (
        layer_out,
        input_grad,
        text_grad,
        cond_grad,
        totals[0],
        totals[1],
        totals[2],
        totals[3],
        totals[4],
        totals[5],
        totals[6],
        totals[7],
    )


def solution(mesh):
    in_specs = (
        P("items", "frames", None),
        P("items", None),
        P("items", "frames", None),
        P("items"),
        P("items"),
        P(),
        P(),
        P(),
        P(),
        P(),
        P(),
        P(),
        P(),
        P("items", "frames", None),
    )
    out_specs = (
        P("items", "frames", None),
        P("items", "frames", None),
        P("items", "frames", None),
        P("items", "frames"),
        P("items", "frames"),
        P("items", "frames"),
        P("items", "frames"),
        P("items", "frames"),
        P("items", "frames"),
        P("items", "frames"),
        P("items", "frames"),
        P("items", "frames"),
    )
    return jax.shard_map(
        on_device, mesh=mesh, in_specs=in_specs, out_specs=out_specs, check_vma=False
    )
```

profile of v0, /device:TPU:0, one launch (start us, length us, event | category | flops | bytes accessed | tf_op | source)
XLA Modules:
  0.0 1916.4 jit_solution(2597478630928197644)
XLA Ops:
  43.4 17.7 all-gather.8.cloned.1.call-done
  76.9 68.5 %all-gather.6.cloned.1.call-done = bf16[8,1024,768]{2,1,0:T(8,128)(2,1)} async-done(((bf16[8,256,768]{2,1,0:T(8,128)(2,1)}), bf16[8,1024,768]{2,1,0:T(8,128)(2,1)}) %all-gather.6.cloned.1.call-update) | async-done | bytes 12582928 | tf_op jit(solution)/shard_map/all_gather | solution.py:125
  145.4 17.2 copy.102
  162.6 44.2 %fusion.105 = (f32[8,12,256]{2,1,0:T(8,128)}, f32[8,12,256,1024]{3,2,1,0:T(8,128)}) fusion(pred[8,1024]{1,0:T(8,128)(4,1)S(1)} %iota_compare_fusion, bf16[8,256,12,64]{1,3,2,0:T(8,128)(2,1)} %bitcast.160, bf16[8,1024,12,64]{1,3,2,0:T(8,128)(2,1)} %bitcast.152), kind=kOutput, calls=%fused_computation.190 | convolution fusion | flops 3321889792 | bytes 116498432 | tf_op jit(solution)/shard_map/sub | solution.py:40
  206.8 22.3 %all-gather.4.cloned.1.call-done = bf16[8,1024,768]{2,1,0:T(8,128)(2,1)} async-done(((bf16[8,256,768]{2,1,0:T(8,128)(2,1)}), bf16[8,1024,768]{2,1,0:T(8,128)(2,1)}) %all-gather.4.cloned.1.call-update) | async-done | bytes 12582928 | tf_op jit(solution)/shard_map/all_gather | solution.py:126
  229.1 16.7 copy.100
  245.7 38.3 %fusion.68 = bf16[8,12,64,256]{3,2,1,0:T(8,128)(2,1)} fusion(bf16[8,1024,12,64]{1,3,2,0:T(8,128)(2,1)} %bitcast.163, f32[8,12,256,1024]{3,2,1,0:T(8,128)} %get-tuple-element.91, f32[8,12,256]{2,1,0:T(8,128)} %get-tuple-element.90), kind=kOutput, calls=%fused_computation.127 | convolution fusion | flops 3273129984 | bytes 116490240 | tf_op jit(solution)/shard_map/ihfj,ijhd->ifhd/dot_general | solution.py:43
  304.9 16.7 fusion.106
  321.6 13.0 fusion.65
  348.0 26.2 %fusion.46 = (u8[256,3072]{1,0:T(8,128)(4,1)}, u8[256,3072]{1,0:T(8,128)(4,1)}, f32[8,256,3072]{2,1,0:T(8,128)}) fusion(bf16[768,3072]{1,0:T(8,128)(2,1)} %param.25, f32[8,256,768]{2,1,0:T(8,128)} %copy-done.5, f32[8,768]{1,0:T(8,128)} %get-tuple-element.82, f32[8,768]{1,0:T(8,128)} %get-tuple-element.83, f32[8,256]{1,0:T(8,128)S(1)} %add_rsqrt_fusion, ...), kind=kOutput, calls=%fused_computation.99 | convolution fusion | flops 9751756800 | bytes 37814272 | tf_op jit(solution)/shard_map/ifd,de->ife/dot_general | solution.py:80
  374.2 59.4 %multiply_convert_fusion.3 = (bf16[8,256,3072]{2,1,0:T(8,128)(2,1)}, f32[8,256,3072]{2,1,0:T(8,128)}) fusion(f32[8,256,3072]{2,1,0:T(8,128)} %get-tuple-element.96, u8[256,3072]{1,0:T(8,128)(4,1)} %get-tuple-element.49, u8[256,3072]{1,0:T(8,128)(4,1)} %get-tuple-element.48), kind=kLoop, calls=%fused_computation.22 | loop fusion | flops 440401920 | bytes 64487424 | tf_op jit(solution)/shard_map/convert_element_type | solution.py:151
  433.6 26.7 %add_convert_fusion = bf16[8,256,3072]{2,1,0:T(8,128)(2,1)} fusion(f32[8,256,3072]{2,1,0:T(8,128)} %get-tuple-element.67, f32[8,256,3072]{2,1,0:T(8,128)} %get-tuple-element.96, bf16[3072,768]{1,0:T(8,128)(2,1)} %param.26, bf16[8,256,768]{2,1,0:T(8,128)(2,1)S(1)} %copy-done.46, f32[8,768]{1,0:T(8,128)S(1)} %copy-done.33), kind=kOutput, calls=%fused_computation.21 | convolution fusion | flops 9756475392 | bytes 70803456 | tf_op jit(solution)/shard_map/ife,de->ifd/dot_general | solution.py:84
  460.3 18.6 multiply_reduce_fusion.2
  479.5 22.1 %fusion.40 = (f32[8,768]{1,0:T(8,128)}, bf16[8,256,768]{2,1,0:T(8,128)(2,1)}, f32[8,768]{1,0:T(8,128)}, f32[8,256,768]{2,1,0:T(8,128)}) fusion(bf16[8,256,768]{2,1,0:T(8,128)(2,1)} %param.27, f32[8,256,768]{2,1,0:T(8,128)} %copy-done.5, f32[8,768]{1,0:T(8,128)} %get-tuple-element.81, f32[8,256,768]{2,1,0:T(8,128)} %get-tuple-element.95, ...), kind=kOutput, calls=%fused_computation.76 | convolution fusion | flops 9688829952 | bytes 48889856 | tf_op jit(solution)/shard_map/ifd,de->ife/dot_general | solution.py:80
  513.8 14.0 fusion.41
  527.8 21.6 %multiply_reduce_fusion.1 = (f32[8,12,256]{2,1,0:T(8,128)}, f32[8,12,256,256]{2,3,1,0:T(8,128)}) fusion(f32[8,12,256,256]{2,3,1,0:T(8,128)} %get-tuple-element.94, f32[8,12,256]{2,1,0:T(8,128)S(1)} %copy-done.10, bf16[8,256,12,64]{1,3,2,0:T(8,128)(2,1)} %bitcast.178, bf16[8,256,12,64]{1,3,2,0:T(8,128)(2,1)} %bitcast.174), kind=kOutput, calls=%fused_computation.20 | convolution fusion | flops 824156160 | bytes 56819712 | tf_op jit(solution)/shard_map/ifhd,ijhd->ihfj/dot_general | solution.py:51
  555.9 21.7 %multiply_convert_fusion.2 = bf16[8,12,256,256]{2,3,1,0:T(8,128)(2,1)} fusion(f32[8,12,256,256]{2,3,1,0:T(8,128)} %get-tuple-element.99, f32[8,12,256]{2,1,0:T(8,128)} %get-tuple-element.98, f32[8,12,256,256]{2,3,1,0:T(8,128)} %get-tuple-element.94, f32[8,12,256]{2,1,0:T(8,128)} %get-tuple-element.93), kind=kLoop, calls=%fused_computation.19 | loop fusion | flops 25165824 | bytes 63111168 | tf_op jit(solution)/shard_map/convert_element_type | solution.py:59
  577.6 12.1 broadcast_multiply_fusion
  596.2 10.6 pad_maximum_fusion
  615.3 12.4 multiply_reduce_fusion.4
  647.8 39.6 %fusion.28 = bf16[8,12,64,1024]{3,2,1,0:T(8,128)(2,1)} fusion(bf16[8,256,12,64]{1,3,2,0:T(8,128)(2,1)} %bitcast.175, f32[8,12,256,1024]{3,2,1,0:T(8,128)} %get-tuple-element.91, f32[8,12,256]{2,1,0:T(8,128)} %get-tuple-element.90), kind=kOutput, calls=%fused_computation.66 | convolution fusion | flops 3277848576 | bytes 116490240 | tf_op jit(solution)/shard_map/ihfj,ifhd->ijhd/dot_general | solution.py:54
  687.4 16.7 copy.114
  704.1 74.0 %multiply_reduce_fusion = (f32[8,12,256]{2,1,0:T(8,128)}, f32[8,12,256,1024]{3,2,1,0:T(8,128)}) fusion(f32[8,12,256,1024]{3,2,1,0:T(8,128)} %get-tuple-element.91, f32[8,12,256]{2,1,0:T(8,128)} %get-tuple-element.90, bf16[8,256,12,64]{1,3,2,0:T(8,128)(2,1)} %bitcast.176, bf16[8,1024,12,64]{1,3,2,0:T(8,128)(2,1)} %bitcast.164), kind=kOutput, calls=%fused_computation.3 | convolution fusion | flops 3296698368 | bytes 217251840 | tf_op jit(solution)/shard_map/ifhd,ijhd->ihfj/dot_general | solution.py:51
  778.2 78.6 %multiply_convert_fusion = bf16[8,12,256,1024]{3,2,1,0:T(8,128)(2,1)} fusion(f32[8,12,256,1024]{3,2,1,0:T(8,128)} %get-tuple-element.102, f32[8,12,256]{2,1,0:T(8,128)} %get-tuple-element.101, f32[8,12,256,1024]{3,2,1,0:T(8,128)} %get-tuple-element.91, f32[8,12,256]{2,1,0:T(8,128)} %get-tuple-element.90), kind=kLoop, calls=%fused_computation.2 | loop fusion | flops 100663296 | bytes 251854848 | tf_op jit(solution)/shard_map/convert_element_type | solution.py:59
  856.8 23.0 %multiply_convert_fusion.1 = bf16[8,12,64,1024]{3,2,1,0:T(8,128)(2,1)} fusion(bf16[8,256,12,64]{1,3,2,0:T(8,128)(2,1)} %bitcast.161, bf16[8,12,256,1024]{3,2,1,0:T(8,128)(2,1)} %multiply_convert_fusion), kind=kOutput, calls=%fused_computation.18 | convolution fusion | flops 3233808384 | bytes 66060288 | tf_op jit(solution)/shard_map/ihfj,ifhd->ijhd/dot_general | solution.py:67
  879.8 16.6 copy.113
  922.5 16.5 bitcast_convert_fusion
  939.2 17.9 bitcast_convert_fusion.1
  962.2 25.3 %multiply_convert_fusion.4 = bf16[8,12,64,256]{3,2,1,0:T(8,128)(2,1)} fusion(bf16[8,1024,12,64]{1,3,2,0:T(8,128)(2,1)} %bitcast.153, bf16[8,12,256,1024]{3,2,1,0:T(8,128)(2,1)} %multiply_convert_fusion), kind=kOutput, calls=%fused_computation.81 | convolution fusion | flops 3224371200 | bytes 66060288 | tf_op jit(solution)/shard_map/ihfj,ijhd->ifhd/dot_general | solution.py:61
  996.0 15.0 bitcast_convert_fusion.2
  1011.2 14.0 fusion.37
  1026.1 10.8 convolution_convert_fusion
  1038.9 13.9 reduce-scatter.49.cloned.1.call-done
  1054.8 26.9 %reduce-scatter.47.cloned.1.call-done = bf16[768,192]{0,1:T(8,128)(2,1)} async-done(((bf16[768,768]{0,1:T(8,128)(2,1)}), bf16[768,192]{0,1:T(8,128)(2,1)}) %reduce-scatter.47.cloned.1.call-update) | async-done | bytes 294928 | tf_op jit(solution)/shard_map/reduce_scatter | solution.py:261
  1083.7 48.5 %reduce-scatter.59.cloned.1.call-done = bf16[3072,192]{0,1:T(8,128)(2,1)} async-done(((bf16[3072,768]{0,1:T(8,128)(2,1)}), bf16[3072,192]{0,1:T(8,128)(2,1)}) %reduce-scatter.59.cloned.1.call-update) | async-done | bytes 1179664 | tf_op jit(solution)/shard_map/reduce_scatter | solution.py:276
  1134.7 47.8 %reduce-scatter.55.cloned.1.call-done = bf16[768,768]{1,0:T(8,128)(2,1)} async-done(((bf16[768,3072]{1,0:T(8,128)(2,1)}), bf16[768,768]{1,0:T(8,128)(2,1)}) %reduce-scatter.55.cloned.1.call-update) | async-done | bytes 1179664 | tf_op jit(solution)/shard_map/reduce_scatter | solution.py:273
  1182.6 13.1 convolution_multiply_fusion
  1197.5 20.7 %reduce-scatter.51.cloned.1.call-done = bf16[768,384]{0,1:T(8,128)(2,1)} async-done(((bf16[768,1536]{0,1:T(8,128)(2,1)}), bf16[768,384]{0,1:T(8,128)(2,1)}) %reduce-scatter.51.cloned.1.call-update) | async-done | bytes 589840 | tf_op jit(solution)/shard_map/reduce_scatter | solution.py:267
  1220.4 40.8 %reduce-scatter.45.cloned.1.call-done = bf16[768,576]{0,1:T(8,128)(2,1)} async-done(((bf16[768,2304]{0,1:T(8,128)(2,1)}), bf16[768,576]{0,1:T(8,128)(2,1)}) %reduce-scatter.45.cloned.1.call-update) | async-done | bytes 884752 | tf_op jit(solution)/shard_map/reduce_scatter | solution.py:258
  1263.5 86.5 %reduce-scatter.43.cloned.1.call-done = bf16[768,1728]{0,1:T(8,128)(2,1)} async-done(((bf16[768,6912]{0,1:T(8,128)(2,1)}), bf16[768,1728]{0,1:T(8,128)(2,1)}) %reduce-scatter.43.cloned.1.call-update) | async-done | bytes 2654224 | tf_op jit(solution)/shard_map/reduce_scatter | solution.py:255
  1355.0 59.9 %reduce-scatter.73.cloned.1.call-done = bf16[96,192]{1,0:T(8,128)(2,1)} async-done(((bf16[768,192]{1,0:T(8,128)(2,1)}), bf16[96,192]{1,0:T(8,128)(2,1)}) %reduce-scatter.73.cloned.1.call-update) | async-done | bytes 36880
  1417.9 60.8 %reduce-scatter.69.cloned.1.call-done = bf16[96,192]{1,0:T(8,128)(2,1)} async-done(((bf16[768,192]{1,0:T(8,128)(2,1)}), bf16[96,192]{1,0:T(8,128)(2,1)}) %reduce-scatter.69.cloned.1.call-update) | async-done | bytes 36880
  1481.8 60.8 %reduce-scatter.67.cloned.1.call-done = bf16[96,192]{1,0:T(8,128)(2,1)} async-done(((bf16[768,192]{1,0:T(8,128)(2,1)}), bf16[96,192]{1,0:T(8,128)(2,1)}) %reduce-scatter.67.cloned.1.call-update) | async-done | bytes 36880
  1545.6 65.1 %reduce-scatter.75.cloned.1.call-done = bf16[384,192]{1,0:T(8,128)(2,1)} async-done(((bf16[3072,192]{1,0:T(8,128)(2,1)}), bf16[384,192]{1,0:T(8,128)(2,1)}) %reduce-scatter.75.cloned.1.call-update) | async-done | bytes 147472
  1614.1 62.9 %reduce-scatter.57.cloned.1.call-done = bf16[96,768]{1,0:T(8,128)(2,1)} async-done(((bf16[768,768]{1,0:T(8,128)(2,1)}), bf16[96,768]{1,0:T(8,128)(2,1)}) %reduce-scatter.57.cloned.1.call-update) | async-done | bytes 147472 | tf_op jit(solution)/shard_map/reduce_scatter | solution.py:299
  1700.8 64.4 %reduce-scatter.71.cloned.1.call-done = bf16[96,384]{1,0:T(8,128)(2,1)} async-done(((bf16[768,384]{1,0:T(8,128)(2,1)}), bf16[96,384]{1,0:T(8,128)(2,1)}) %reduce-scatter.71.cloned.1.call-update) | async-done | bytes 73744
  1768.5 62.9 %reduce-scatter.65.cloned.1.call-done = bf16[96,576]{1,0:T(8,128)(2,1)} async-done(((bf16[768,576]{1,0:T(8,128)(2,1)}), bf16[96,576]{1,0:T(8,128)(2,1)}) %reduce-scatter.65.cloned.1.call-update) | async-done | bytes 110608
  1834.8 70.6 %reduce-scatter.63.cloned.1.call-done = bf16[96,1728]{1,0:T(8,128)(2,1)} async-done(((bf16[768,1728]{1,0:T(8,128)(2,1)}), bf16[96,1728]{1,0:T(8,128)(2,1)}) %reduce-scatter.63.cloned.1.call-update) | async-done | bytes 331792
  (237 shorter events, 247.3 us)
Async XLA Ops:
  7.2 16.8 copy-start
  7.2 53.9 %all-gather.8.cloned.1.call-start = ((), (), s32[]{:S(2)}) async-start(), calls=%async_computation.22 | async-start | bytes 7864320 | tf_op jit(solution)/shard_map/all_gather | solution.py:138
  11.9 133.5 %all-gather.6.cloned.1.call-start = ((), (), s32[]{:S(2)}) async-start(), calls=%async_computation.21 | async-start | bytes 15728640 | tf_op jit(solution)/shard_map/all_gather | solution.py:125
  37.0 192.1 %all-gather.4.cloned.1.call-start = ((), (), s32[]{:S(2)}) async-start(), calls=%async_computation.20 | async-start | bytes 15728640 | tf_op jit(solution)/shard_map/all_gather | solution.py:126
  37.7 919.5 %reduce-scatter.41.cloned.1.call-start = ((), (), s32[]{:S(2)}) async-start(), calls=%async_computation.25 | async-start | bytes 15728640 | tf_op jit(solution)/shard_map/reduce_scatter | solution.py:238
  344.5 135.0 %copy-start.26 = (f32[8,256]{1,0:T(8,128)}, f32[8,256]{1,0:T(8,128)S(1)}, u32[]{:S(2)}) copy-start(f32[8,256]{1,0:T(8,128)S(1)} %broadcast_multiply_fusion.7) | copy-start | bytes 24580
  348.0 131.6 %copy-start.41 = (f32[8,256]{1,0:T(8,128)}, f32[8,256]{1,0:T(8,128)S(1)}, u32[]{:S(2)}) copy-start(f32[8,256]{1,0:T(8,128)S(1)} %add_rsqrt_fusion) | copy-start | bytes 24580
  374.2 59.4 %copy-start.33 = (f32[8,768]{1,0:T(8,128)S(1)}, f32[8,768]{1,0:T(8,128)}, u32[]{:S(2)}) copy-start(f32[8,768]{1,0:T(8,128)} %get-tuple-element.81) | copy-start | bytes 73732
  374.2 59.4 %copy-start.46 = (bf16[8,256,768]{2,1,0:T(8,128)(2,1)S(1)}, bf16[8,256,768]{2,1,0:T(8,128)(2,1)}, u32[]{:S(2)}) copy-start(bf16[8,256,768]{2,1,0:T(8,128)(2,1)} %param.27) | copy-start | bytes 9437188
  433.6 26.7 %copy-start.32 = (f32[8,768]{1,0:T(8,128)S(1)}, f32[8,768]{1,0:T(8,128)}, u32[]{:S(2)}) copy-start(f32[8,768]{1,0:T(8,128)} %get-tuple-element.83) | copy-start | bytes 73732
  513.8 14.0 copy-start.10
  606.9 385.6 %reduce-scatter.39.cloned.1.call-start = ((), (), s32[]{:S(2)}) async-start(), calls=%async_computation.24 | async-start | bytes 15728640 | tf_op jit(solution)/shard_map/reduce_scatter | solution.py:193
  607.0 20.7 %slice-start = ((s8[6291456]{0:T(1024)(128)(4,1)}), s8[4194304]{0:T(1024)(128)(4,1)S(1)}, s32[]{:S(2)}) async-start(s8[6291456]{0:T(1024)(128)(4,1)} %bitcast.150), calls=%async_computation.43 | async-start | bytes 8388608
  607.0 20.7 %slice-start.2 = ((s8[6291456]{0:T(1024)(128)(4,1)}), s8[4194304]{0:T(1024)(128)(4,1)S(1)}, s32[]{:S(2)}) async-start(s8[6291456]{0:T(1024)(128)(4,1)} %bitcast.155), calls=%async_computation.45 | async-start | bytes 8388608
  615.2 12.5 copy-start.6
  615.3 12.4 slice-start.1
  615.3 12.4 slice-start.3
  627.8 10.0 copy-start.13
  704.1 291.9 %reduce-scatter.37.cloned.1.call-start = ((), (), s32[]{:S(2)}) async-start(), calls=%async_computation.23 | async-start | bytes 15728640 | tf_op jit(solution)/shard_map/reduce_scatter | solution.py:190
  896.5 140.4 %reduce-scatter.53.cloned.1.call-start = ((), (), s32[]{:S(2)}) async-start(), calls=%async_computation.31 | async-start | bytes 1474560 | tf_op jit(solution)/shard_map/reduce_scatter | solution.py:270
  904.0 148.8 %reduce-scatter.49.cloned.1.call-start = ((), (), s32[]{:S(2)}) async-start(), calls=%async_computation.29 | async-start | bytes 1474560 | tf_op jit(solution)/shard_map/reduce_scatter | solution.py:264
  914.0 167.7 %reduce-scatter.47.cloned.1.call-start = ((), (), s32[]{:S(2)}) async-start(), calls=%async_computation.28 | async-start | bytes 1474560 | tf_op jit(solution)/shard_map/reduce_scatter | solution.py:261
  922.4 16.8 copy-start.27
  922.4 16.8 copy-start.42
  922.4 209.7 %reduce-scatter.59.cloned.1.call-start = ((), (), s32[]{:S(2)}) async-start(), calls=%async_computation.34 | async-start | bytes 5898240 | tf_op jit(solution)/shard_map/reduce_scatter | solution.py:276
  939.0 243.6 %reduce-scatter.55.cloned.1.call-start = ((), (), s32[]{:S(2)}) async-start(), calls=%async_computation.32 | async-start | bytes 5898240 | tf_op jit(solution)/shard_map/reduce_scatter | solution.py:273
  957.1 261.1 %reduce-scatter.51.cloned.1.call-start = ((), (), s32[]{:S(2)}) async-start(), calls=%async_computation.30 | async-start | bytes 2949120 | tf_op jit(solution)/shard_map/reduce_scatter | solution.py:267
  962.2 299.0 %reduce-scatter.45.cloned.1.call-start = ((), (), s32[]{:S(2)}) async-start(), calls=%async_computation.27 | async-start | bytes 4423680 | tf_op jit(solution)/shard_map/reduce_scatter | solution.py:258
  1011.1 15.0 copy-start.9
  1011.1 339.0 %reduce-scatter.43.cloned.1.call-start = ((), (), s32[]{:S(2)}) async-start(), calls=%async_computation.26 | async-start | bytes 13271040 | tf_op jit(solution)/shard_map/reduce_scatter | solution.py:255
  1011.1 14.1 copy-start.16
  1011.2 14.1 copy-start.40
  1011.2 14.1 copy-start.39
  1011.2 14.1 copy-start.38
  1011.2 14.1 copy-start.36
  1011.2 14.1 copy-start.35
  1011.2 14.2 copy-start.37
  1036.9 378.0 %reduce-scatter.73.cloned.1.call-start = ((), (), s32[]{:S(2)}) async-start(), calls=%async_computation.41 | async-start | bytes 442368
  1038.9 439.9 %reduce-scatter.69.cloned.1.call-start = ((), (), s32[]{:S(2)}) async-start(), calls=%async_computation.39 | async-start | bytes 442368
  1054.7 487.8 %reduce-scatter.67.cloned.1.call-start = ((), (), s32[]{:S(2)}) async-start(), calls=%async_computation.38 | async-start | bytes 442368
  1083.6 527.1 %reduce-scatter.75.cloned.1.call-start = ((), (), s32[]{:S(2)}) async-start(), calls=%async_computation.42 | async-start | bytes 1769472
  1134.7 542.4 %reduce-scatter.57.cloned.1.call-start = ((), (), s32[]{:S(2)}) async-start(), calls=%async_computation.33 | async-start | bytes 1327104 | tf_op jit(solution)/shard_map/reduce_scatter | solution.py:299
  1182.6 516.7 %reduce-scatter.61.cloned.1.call-start = ((), (), s32[]{:S(2)}) async-start(), calls=%async_computation.35 | async-start | bytes 491520
  1197.4 567.8 %reduce-scatter.71.cloned.1.call-start = ((), (), s32[]{:S(2)}) async-start(), calls=%async_computation.40 | async-start | bytes 663552
  1220.3 611.1 %reduce-scatter.65.cloned.1.call-start = ((), (), s32[]{:S(2)}) async-start(), calls=%async_computation.37 | async-start | bytes 1105920
  1263.5 641.9 %reduce-scatter.63.cloned.1.call-start = ((), (), s32[]{:S(2)}) async-start(), calls=%async_computation.36 | async-start | bytes 3096576
  1354.9 330.5 %copy-start.19 = (f32[8,256]{1,0:T(8,128)S(1)}, f32[8,256]{1,0:T(8,128)}, u32[]{:S(2)}) copy-start(f32[8,256]{1,0:T(8,128)} %copy-done.17) | copy-start | bytes 24580
  1354.9 330.5 %copy-start.25 = (f32[8,256]{1,0:T(8,128)S(1)}, f32[8,256]{1,0:T(8,128)}, u32[]{:S(2)}) copy-start(f32[8,256]{1,0:T(8,128)} %copy-done.23) | copy-start | bytes 24580
  (28 other events, 166.4 us)
Sparse Core Ops, SparseCore 0:
  12.0 49.0 all-gather.7
  63.2 82.0 all-gather.5
  146.9 82.0 all-gather.3
  607.0 99.0 reduce-scatter.40
  708.6 99.0 reduce-scatter.38
  896.6 99.3 reduce-scatter.36
  998.6 25.7 reduce-scatter.52
  1027.1 25.7 reduce-scatter.48
  1056.0 25.7 reduce-scatter.46
  1084.2 47.8 reduce-scatter.58
  1134.7 47.8 reduce-scatter.54
  1185.1 33.0 reduce-scatter.50
  1220.7 40.4 reduce-scatter.44
  1263.8 86.1 reduce-scatter.42
  1353.5 61.3 reduce-scatter.72
  1418.3 60.3 reduce-scatter.68
  1482.2 60.3 reduce-scatter.66
  1546.8 63.8 reduce-scatter.74
  1614.1 62.8 reduce-scatter.56
  1679.4 19.8 reduce-scatter.60
  1703.1 62.0 reduce-scatter.70
  1768.9 62.4 reduce-scatter.64
  1835.0 70.3 reduce-scatter.62
where the time goes:
time: 1920 us
  waiting for transfers between devices  912 us (48%)
  matrix products  615 us (32%)
  other arithmetic  199 us (10%)
  local copies, waits for them, and re-layouts  174 us (9%)
    unnamed x31, waiting for transfers between devices  452 us
    convert_element_type x2, other arithmetic, attend_back(): grad_scores = (attn_prob * (grad_prob - jnp.sum(attn_prob * grad_prob, -1...  100 us
    dot_general x2, matrix products, attend_back(): jnp.einsum('ifhd,ijhd->ihfj', grad_heads, split_heads(values_in), preferr...  95.6 us
    dot_general x7, matrix products, project_back(): jnp.einsum('ife,de->ifd', tensor, weight, preferred_element_type=jnp.floa...  89.8 us
    reduce_scatter x1, waiting for transfers between devices, on_device(): lax.psum_scatter(grads[0].astype(jnp.bfloat16), 'frames', scatter_dimensi...  86.5 us
    dot_general x7, matrix products, project(): jnp.einsum('ifd,de->ife', tensor, weight, preferred_element_type=jnp.floa...  85.4 us
    dot_general x7, matrix products, weight_grad(): jnp.einsum('ifd,ife->de', left, right, preferred_element_type=jnp.float32)  79.6 us
    all_gather x1, waiting for transfers between devices, on_device(): lax.all_gather(keys_own, 'frames', axis=1, tiled=True)  68.5 us
  transfers between devices with their start and end apart: 23, of which 20 were waited for; matrix products, arithmetic and copies ran while one was open for 31% of the time, Pallas kernels for 0%

commit v1 on v0

--- a/solution.py
+++ b/solution.py
@@ -1,8 +1,11 @@
+import functools
 from functools import partial
 
 import jax
 import jax.numpy as jnp
 from jax import lax
+from jax.experimental import pallas as pl
+from jax.experimental.pallas import tpu as pltpu
 from jax.sharding import PartitionSpec as P
 
 H = 12
@@ -88,7 +91,7 @@
     return jnp.einsum("ifd,ife->de", left, right, preferred_element_type=jnp.float32)
 
 
-def on_device(
+def frames_split(
     frames_in,
     cond,
     text,
@@ -319,6 +322,753 @@
     )
 
 
+LOG2E = 1.4426950408889634
+BF = jnp.bfloat16
+F32 = jnp.float32
+PACK = 384
+LIMIT = 60 * 2**20
+
+
+def nn(left, right):
+    return jnp.dot(left, right, preferred_element_type=F32)
+
+
+def nt(left, right):
+    return lax.dot_general(left, right, (((1,), (1,)), ((), ())), preferred_element_type=F32)
+
+
+def tn(left, right):
+    return lax.dot_general(left, right, (((0,), (0,)), ((), ())), preferred_element_type=F32)
+
+
+def ln_parts(rows):
+    share = 1.0 / rows.shape[-1]
+    centered = rows - jnp.sum(rows, -1, keepdims=True) * share
+    inverse = lax.rsqrt(jnp.sum(centered * centered, -1, keepdims=True) * share + 1e-06)
+    return centered * inverse, inverse
+
+
+def ln_back(normed, inverse, incoming):
+    share = 1.0 / normed.shape[-1]
+    mean_in = jnp.sum(incoming, -1, keepdims=True) * share
+    mean_dot = jnp.sum(incoming * normed, -1, keepdims=True) * share
+    return inverse * (incoming - mean_in - normed * mean_dot)
+
+
+def gelu_parts(value):
+    size = jnp.abs(value)
+    inner = 1.0 / (1.0 + (0.3275911 * 0.7071067811865476) * size)
+    series = inner * (
+        0.5 * 0.254829592
+        + inner
+        * (
+            0.5 * -0.284496736
+            + inner * (0.5 * 1.421413741 + inner * (0.5 * -1.453152027 + inner * (0.5 * 1.061405429)))
+        )
+    )
+    bell = jnp.exp2(value * value * (-0.5 * LOG2E))
+    tail = series * bell
+    below = jnp.where(value >= 0.0, 1.0 - tail, tail)
+    return below, below + value * bell * 0.3989422804014327
+
+
+def lane_half(half):
+    lane = lax.broadcasted_iota(jnp.int32, (1, 128), 1)
+    return lane < 64 if half == 0 else lane >= 64
+
+
+def keep_half(rows, half):
+    return jnp.where(lane_half(half), rows, jnp.zeros_like(rows))
+
+
+def pack_square(acc, item, ra, cb, col):
+    first = acc[pl.ds(pl.multiple_of(item * ra, 16), ra // 2), col : col + cb]
+    second = acc[pl.ds(pl.multiple_of(item * ra + ra // 2, 16), ra // 2), col : col + cb]
+    return jnp.concatenate([first, second], 1).astype(BF)
+
+
+def qkv_kernel(x_ref, mod_ref, w_ref, o_ref, *, score_scale):
+    width = x_ref.shape[-1]
+    normed, _ = ln_parts(x_ref[0].astype(F32))
+    hidden = (normed * (1.0 + mod_ref[0, 1:2]) + mod_ref[0, 0:1]).astype(BF)
+    o_ref[0, :, :width] = (nn(hidden, w_ref[:, :width]) * (score_scale * LOG2E)).astype(BF)
+    o_ref[0, :, width:] = nn(hidden, w_ref[:, width:]).astype(BF)
+
+
+def self_fwd_kernel(lens, q_ref, k_ref, v_ref, o_ref, lse_ref, *, qb):
+    count = q_ref.shape[1]
+    used = lens[pl.program_id(0)]
+    for klen in (count // 4, count // 2, count):
+
+        @pl.when(used == klen)
+        def _(klen=klen):
+            keys = k_ref[0, :klen]
+            values = jnp.concatenate([v_ref[0, :klen], jnp.ones((klen, 128), BF)], 1)
+
+            def step(position, carry):
+                rows = pl.ds(pl.multiple_of(position * qb, qb), qb)
+                queries = q_ref[0, rows]
+                outs = []
+                for half in (0, 1):
+                    scores = nt(keep_half(queries, half), keys)
+                    top = jnp.max(scores, 1, keepdims=True)
+                    prob = jnp.exp2(scores - top).astype(BF)
+                    mixed = nn(prob, values)
+                    total = mixed[:, 128:]
+                    lse_ref[0, 0, half : half + 1, rows] = (top + jnp.log2(total[:, :1])).T
+                    outs.append(mixed[:, :128] / total)
+                o_ref[0, rows] = jnp.where(lane_half(0), outs[0], outs[1]).astype(BF)
+                return carry
+
+            lax.fori_loop(0, count // qb, step, 0)
+
+
+def self_bwd_kernel(
+    lens, q_ref, k_ref, v_ref, o_ref, do_ref, lse_ref, dq_ref, dk_ref, dv_ref, dk_acc, dv_acc, *, qb, score_scale
+):
+    count = q_ref.shape[1]
+    used = lens[pl.program_id(0)]
+    for klen in (count // 4, count // 2, count):
+
+        @pl.when(used == klen)
+        def _(klen=klen):
+            keys = k_ref[0, :klen]
+            values = v_ref[0, :klen]
+            dk_acc[:klen] = jnp.zeros((klen, 128), F32)
+            dv_acc[:klen] = jnp.zeros((klen, 128), F32)
+
+            def step(position, carry):
+                rows = pl.ds(pl.multiple_of(position * qb, qb), qb)
+                queries = q_ref[0, rows]
+                grad = do_ref[0, rows]
+                dots = (grad.astype(F32) * o_ref[0, rows].astype(F32)).T
+                d_queries = []
+                for half in (0, 1):
+                    q_half = keep_half(queries, half)
+                    grad_half = keep_half(grad, half)
+                    delta = jnp.sum(dots[64 * half : 64 * half + 64], 0, keepdims=True)
+                    prob = jnp.exp2(nt(keys, q_half) - lse_ref[0, 0, half : half + 1, rows])
+                    d_scores = (prob * (nt(values, grad_half) - delta)).astype(BF)
+                    dv_acc[:klen] += nn(prob.astype(BF), grad_half)
+                    dk_acc[:klen] += nn(d_scores, q_half)
+                    d_queries.append(tn(d_scores, keys))
+                dq_ref[0, rows] = (
+                    jnp.where(lane_half(0), d_queries[0], d_queries[1]) * score_scale
+                ).astype(BF)
+                return carry
+
+            lax.fori_loop(0, count // qb, step, 0)
+            dk_ref[0, :klen] = (dk_acc[:klen] * (1.0 / LOG2E)).astype(BF)
+            dv_ref[0, :klen] = dv_acc[:klen].astype(BF)
+            if klen < count:
+                dk_ref[0, klen:] = jnp.zeros((count - klen, 128), BF)
+                dv_ref[0, klen:] = jnp.zeros((count - klen, 128), BF)
+
+
+def cross_kernel(
+    tlens, att_ref, x_ref, mod_ref, kv_ref, wo_ref, wq_ref, wco_ref,
+    first_ref, second_ref, ba_ref, bb_ref, cq_ref, cr_ref, lse_ref, *, score_scale,
+):
+    width = x_ref.shape[-1]
+    slots = kv_ref.shape[1]
+    used = tlens[pl.program_id(0)]
+    branch_a = nn(att_ref[0], wo_ref[...])
+    ba_ref[0] = branch_a.astype(BF)
+    first = x_ref[0].astype(F32) + mod_ref[0, 2:3] * branch_a
+    first_ref[0] = first
+    normed, _ = ln_parts(first)
+    hidden = (normed * (1.0 + mod_ref[0, 4:5]) + mod_ref[0, 3:4]).astype(BF)
+    cq_ref[0] = (nn(hidden, wq_ref[...]) * (score_scale * LOG2E)).astype(BF)
+    valid = lax.broadcasted_iota(jnp.int32, (1, slots), 1) < used
+    ones = jnp.ones((slots, 128), BF)
+    for pair in range(H // 2):
+        cols = slice(pair * 128, pair * 128 + 128)
+        queries = cq_ref[0, :, cols]
+        keys = kv_ref[0, :, cols]
+        values = jnp.concatenate([kv_ref[0, :, width + pair * 128 : width + pair * 128 + 128], ones], 1)
+        outs = []
+        for half in (0, 1):
+            scores = jnp.where(valid, nt(keep_half(queries, half), keys), -1e30)
+            top = jnp.max(scores, 1, keepdims=True)
+            prob = jnp.exp2(scores - top).astype(BF)
+            mixed = nn(prob, values)
+            total = mixed[:, 128:]
+            lse_ref[0, pair, half : half + 1] = (top + jnp.log2(total[:, :1])).T
+            outs.append(mixed[:, :128] / total)
+        cr_ref[0, :, cols] = jnp.where(lane_half(0), outs[0], outs[1]).astype(BF)
+    branch_b = nn(cr_ref[0], wco_ref[...])
+    bb_ref[0] = branch_b.astype(BF)
+    second_ref[0] = first + mod_ref[0, 5:6] * branch_b
+
+
+def mlp_kernel(
+    second_ref, cot_ref, mod_ref, wup_ref, wdn_ref,
+    out_ref, g2_ref, dmod_ref, gup_ref, gdn_ref, up_acc, dn_acc, *, blocks, total, chunk, nf, ni,
+):
+    step = pl.program_id(0)
+    width = second_ref.shape[-1]
+    ff = wup_ref.shape[-1]
+
+    @pl.when(step == 0)
+    def _():
+        up_acc[...] = jnp.zeros_like(up_acc)
+        dn_acc[...] = jnp.zeros_like(dn_acc)
+
+    @pl.when(step < total)
+    def _():
+        shift, scale, gate = mod_ref[0, 6:7], mod_ref[0, 7:8], mod_ref[0, 8:9]
+        second = second_ref[0]
+        normed, inverse = ln_parts(second)
+        hidden = (normed * (1.0 + scale) + shift).astype(BF)
+        upstream = cot_ref[0].astype(F32)
+        d_branch = (upstream * gate).astype(BF)
+        branch = jnp.zeros(second.shape, F32)
+        d_hidden = jnp.zeros(second.shape, F32)
+        for at in range(0, ff, chunk):
+            cols = slice(at, at + chunk)
+            up_proj = nn(hidden, wup_ref[:, cols])
+            below, slope = gelu_parts(up_proj)
+            act = (up_proj * below).astype(BF)
+            branch += nn(act, wdn_ref[cols])
+            d_up = (nt(d_branch, wdn_ref[cols]) * slope).astype(BF)
+            d_hidden += nt(d_up, wup_ref[:, cols])
+            dn_acc[cols] += tn(act, d_branch)
+            up_acc[:, cols] += tn(hidden, d_up)
+        out_ref[0] = (second + gate * branch).astype(BF)
+        g2_ref[0] = upstream + ln_back(normed, inverse, d_hidden * (1.0 + scale))
+
+        @pl.when(step % blocks == 0)
+        def _():
+            dmod_ref[...] = jnp.zeros_like(dmod_ref)
+
+        dmod_ref[0, 0:1] += jnp.sum(d_hidden, 0, keepdims=True)
+        dmod_ref[0, 1:2] += jnp.sum(d_hidden * normed, 0, keepdims=True)
+        dmod_ref[0, 2:3] += jnp.sum(upstream * branch, 0, keepdims=True)
+
+    @pl.when(step >= total)
+    def _():
+        item = step - total
+        ra, cb = width // ni, ff // nf
+        for frame in range(nf):
+            part = up_acc[pl.ds(pl.multiple_of(item * ra, 16), ra), frame * cb : (frame + 1) * cb].astype(BF)
+            gup_ref[0, frame] = jnp.concatenate([part[:, :PACK], part[:, PACK:]], 0)
+            gdn_ref[0, frame] = pack_square(dn_acc, item, ff // ni, width // nf, frame * (width // nf))
+
+
+def cross_back_kernel(
+    tlens, g2_ref, ba_ref, bb_ref, cr_ref, att_ref, cq_ref, first_ref, mod_ref, kv_ref, lse_ref,
+    wo_ref, wq_ref, wco_ref,
+    g1_ref, datt_ref, dtext_ref, dmod_ref, gw_ref,
+    o_acc, q_acc, co_acc, dcq_ref, *, blocks, total, score_scale, nf, ni,
+):
+    step = pl.program_id(0)
+    width = g2_ref.shape[-1]
+    slots = kv_ref.shape[1]
+
+    @pl.when(step == 0)
+    def _():
+        o_acc[...] = jnp.zeros_like(o_acc)
+        q_acc[...] = jnp.zeros_like(q_acc)
+        co_acc[...] = jnp.zeros_like(co_acc)
+
+    @pl.when(step < total)
+    def _():
+        @pl.when(step % blocks == 0)
+        def _():
+            dmod_ref[...] = jnp.zeros_like(dmod_ref)
+            dtext_ref[...] = jnp.zeros_like(dtext_ref)
+
+        used = tlens[step // blocks]
+        upstream = g2_ref[0]
+        dmod_ref[0, 3:4] += jnp.sum(upstream * bb_ref[0].astype(F32), 0, keepdims=True)
+        d_branch_b = (upstream * mod_ref[0, 5:6]).astype(BF)
+        co_acc[...] += tn(cr_ref[0], d_branch_b)
+        d_crossed = nt(d_branch_b, wco_ref[...])
+        valid = lax.broadcasted_iota(jnp.int32, (slots, 1), 0) < used
+        for pair in range(H // 2):
+            cols = slice(pair * 128, pair * 128 + 128)
+            vcols = slice(width + pair * 128, width + pair * 128 + 128)
+            queries = cq_ref[0, :, cols]
+            keys = kv_ref[0, :, cols]
+            values = kv_ref[0, :, vcols]
+            grad = d_crossed[:, cols].astype(BF)
+            dots = (grad.astype(F32) * cr_ref[0, :, cols].astype(F32)).T
+            d_queries = []
+            d_keys = 0.0
+            d_values = 0.0
+            for half in (0, 1):
+                q_half = keep_half(queries, half)
+                grad_half = keep_half(grad, half)
+                delta = jnp.sum(dots[64 * half : 64 * half + 64], 0, keepdims=True)
+                scores = jnp.where(valid, nt(keys, q_half), -1e30)
+                prob = jnp.exp2(scores - lse_ref[0, pair, half : half + 1])
+                d_scores = (prob * (nt(values, grad_half) - delta)).astype(BF)
+                d_values += nn(prob.astype(BF), grad_half)
+                d_keys += nn(d_scores, q_half)
+                d_queries.append(tn(d_scores, keys))
+            dtext_ref[0, :, cols] += d_keys * (1.0 / LOG2E)
+            dtext_ref[0, :, vcols] += d_values
+            dcq_ref[:, cols] = (
+                jnp.where(lane_half(0), d_queries[0], d_queries[1]) * score_scale
+            ).astype(BF)
+        d_cq = dcq_ref[...]
+        normed, inverse = ln_parts(first_ref[0])
+        shift, scale = mod_ref[0, 3:4], mod_ref[0, 4:5]
+        hidden = (normed * (1.0 + scale) + shift).astype(BF)
+        q_acc[...] += tn(hidden, d_cq)
+        d_hidden = nt(d_cq, wq_ref[...])
+        dmod_ref[0, 1:2] += jnp.sum(d_hidden, 0, keepdims=True)
+        dmod_ref[0, 2:3] += jnp.sum(d_hidden * normed, 0, keepdims=True)
+        upstream = upstream + ln_back(normed, inverse, d_hidden * (1.0 + scale))
+        g1_ref[0] = upstream
+        dmod_ref[0, 0:1] += jnp.sum(upstream * ba_ref[0].astype(F32), 0, keepdims=True)
+        d_branch_a = (upstream * mod_ref[0, 2:3]).astype(BF)
+        o_acc[...] += tn(att_ref[0], d_branch_a)
+        datt_ref[0] = nt(d_branch_a, wo_ref[...]).astype(BF)
+
+    @pl.when(step >= total)
+    def _():
+        item = step - total
+        ra, cb = width // ni, width // nf
+        for frame in range(nf):
+            for place, acc in enumerate((o_acc, q_acc, co_acc)):
+                gw_ref[0, frame, place * (ra // 2) : (place + 1) * (ra // 2)] = pack_square(
+                    acc, item, ra, cb, frame * cb
+                )
+
+
+def qkv_back_kernel(
+    dq_ref, dk_ref, dv_ref, x_ref, g1_ref, mod_ref, w_ref, dx_ref, dmod_ref, gw_ref, acc, *, blocks, total, nf, ni
+):
+    step = pl.program_id(0)
+    width = x_ref.shape[-1]
+
+    @pl.when(step == 0)
+    def _():
+        acc[...] = jnp.zeros_like(acc)
+
+    @pl.when(step < total)
+    def _():
+        @pl.when(step % blocks == 0)
+        def _():
+            dmod_ref[...] = jnp.zeros_like(dmod_ref)
+
+        normed, inverse = ln_parts(x_ref[0].astype(F32))
+        shift, scale = mod_ref[0, 0:1], mod_ref[0, 1:2]
+        hidden = (normed * (1.0 + scale) + shift).astype(BF)
+        d_hidden = jnp.zeros(normed.shape, F32)
+        for place, ref in enumerate((dq_ref, dk_ref, dv_ref)):
+            cols = slice(place * width, (place + 1) * width)
+            acc[:, cols] += tn(hidden, ref[0])
+            d_hidden += nt(ref[0], w_ref[:, cols])
+        dmod_ref[0, 0:1] += jnp.sum(d_hidden, 0, keepdims=True)
+        dmod_ref[0, 1:2] += jnp.sum(d_hidden * normed, 0, keepdims=True)
+        dx_ref[0] = (g1_ref[0] + ln_back(normed, inverse, d_hidden * (1.0 + scale))).astype(BF)
+
+    @pl.when(step >= total)
+    def _():
+        item = step - total
+        ra, cb = width // ni, 3 * width // nf
+        for frame in range(nf):
+            part = acc[pl.ds(pl.multiple_of(item * ra, 16), ra), frame * cb : (frame + 1) * cb].astype(BF)
+            gw_ref[0, frame, :ra] = part[:, :PACK]
+            gw_ref[0, frame, ra:] = jnp.concatenate([part[: ra // 2, PACK:], part[ra // 2 :, PACK:]], 1)
+
+
+def cost(flops, moved, exps=0):
+    return pl.CostEstimate(flops=int(flops), bytes_accessed=int(moved), transcendentals=int(exps))
+
+
+def params():
+    return pltpu.CompilerParams(vmem_limit_bytes=LIMIT)
+
+
+def whole(shape):
+    return pl.BlockSpec(shape, lambda *_: (0,) * len(shape), pipeline_mode=pl.Buffered(1))
+
+
+def struct(shape, dtype):
+    return jax.ShapeDtypeStruct(shape, dtype)
+
+
+def qkv_call(rows, mod, weight, score_scale, block):
+    items, count, width = rows.shape
+    return pl.pallas_call(
+        partial(qkv_kernel, score_scale=score_scale),
+        grid=(items, count // block),
+        in_specs=[
+            pl.BlockSpec((1, block, width), lambda i, j: (i, j, 0)),
+            pl.BlockSpec((1, 9, width), lambda i, j: (i, 0, 0)),
+            whole(weight.shape),
+        ],
+        out_specs=pl.BlockSpec((1, block, 3 * width), lambda i, j: (i, j, 0)),
+        out_shape=struct((items, count, 3 * width), BF),
+        compiler_params=params(),
+        cost_estimate=cost(2 * items * count * width * 3 * width, items * count * width * 8),
+        name="qkv_fwd",
+    )(rows, mod, weight)
+
+
+def self_fwd_call(lens, qkv, qb):
+    items, count, width = qkv.shape
+    width //= 3
+    pairs = H // 2
+    spec = pltpu.PrefetchScalarGridSpec(
+        num_scalar_prefetch=1,
+        grid=(items, pairs),
+        in_specs=[
+            pl.BlockSpec((1, count, 128), lambda i, h, s, part=part: (i, 0, part * pairs + h)) for part in range(3)
+        ],
+        out_specs=[
+            pl.BlockSpec((1, count, 128), lambda i, h, s: (i, 0, h)),
+            pl.BlockSpec((1, 1, 2, count), lambda i, h, s: (i, h, 0, 0)),
+        ],
+    )
+    return pl.pallas_call(
+        partial(self_fwd_kernel, qb=qb),
+        grid_spec=spec,
+        out_shape=[struct((items, count, width), BF), struct((items, pairs, 2, count), F32)],
+        compiler_params=params(),
+        cost_estimate=cost(16 * items * count * count * width, items * count * width * 8, items * H * count * count),
+        name="self_fwd",
+    )(lens, qkv, qkv, qkv)
+
+
+def self_bwd_call(lens, qkv, att, d_att, lse, qb, score_scale):
+    items, count, width = att.shape
+    pairs = H // 2
+    block = pl.BlockSpec((1, count, 128), lambda i, h, s: (i, 0, h))
+    spec = pltpu.PrefetchScalarGridSpec(
+        num_scalar_prefetch=1,
+        grid=(items, pairs),
+        in_specs=[
+            pl.BlockSpec((1, count, 128), lambda i, h, s, part=part: (i, 0, part * pairs + h)) for part in range(3)
+        ]
+        + [block, block, pl.BlockSpec((1, 1, 2, count), lambda i, h, s: (i, h, 0, 0))],
+        out_specs=[block] * 3,
+        scratch_shapes=[pltpu.VMEM((count, 128), F32)] * 2,
+    )
+    return pl.pallas_call(
+        partial(self_bwd_kernel, qb=qb, score_scale=score_scale),
+        grid_spec=spec,
+        out_shape=[struct((items, count, width), BF)] * 3,
+        compiler_params=params(),
+        cost_estimate=cost(40 * items * count * count * width, items * count * width * 16, items * H * count * count),
+        name="self_bwd",
+    )(lens, qkv, qkv, qkv, att, d_att, lse)
+
+
+def cross_call(tlens, att, rows, mod, kv, wo, wq, wco, score_scale, block):
+    items, count, width = rows.shape
+    slots = kv.shape[1]
+    row = pl.BlockSpec((1, block, width), lambda i, j, s: (i, j, 0))
+    spec = pltpu.PrefetchScalarGridSpec(
+        num_scalar_prefetch=1,
+        grid=(items, count // block),
+        in_specs=[
+            row,
+            row,
+            pl.BlockSpec((1, 9, width), lambda i, j, s: (i, 0, 0)),
+            pl.BlockSpec((1, slots, 2 * width), lambda i, j, s: (i, 0, 0)),
+            whole(wo.shape),
+            whole(wq.shape),
+            whole(wco.shape),
+        ],
+        out_specs=[row] * 6 + [pl.BlockSpec((1, H // 2, 2, block), lambda i, j, s: (i, 0, 0, j))],
+    )
+    return pl.pallas_call(
+        partial(cross_kernel, score_scale=score_scale),
+        grid_spec=spec,
+        out_shape=[struct(rows.shape, F32)] * 2
+        + [struct(rows.shape, BF)] * 4
+        + [struct((items, H // 2, 2, count), F32)],
+        compiler_params=params(),
+        cost_estimate=cost(
+            items * count * (6 * width * width + 16 * slots * width), items * count * width * 20, items * H * count * slots
+        ),
+        name="cross_fwd",
+    )(tlens, att, rows, mod, kv, wo, wq, wco)
+
+
+def mlp_call(second, cot, mod, wup, wdn, block, chunk, nf, ni):
+    items, count, width = second.shape
+    ff = wup.shape[1]
+    blocks = count // block
+    total = items * blocks
+
+    def at(t):
+        return jnp.minimum(t, total - 1)
+
+    row = pl.BlockSpec((1, block, width), lambda t: (at(t) // blocks, at(t) % blocks, 0))
+    grad = pl.BlockSpec((1, nf, width * ff // (nf * ni * PACK), PACK), lambda t: (jnp.maximum(t - total, 0), 0, 0, 0))
+    grad_shape = struct((ni, nf, width * ff // (nf * ni * PACK), PACK), BF)
+    return pl.pallas_call(
+        partial(mlp_kernel, blocks=blocks, total=total, chunk=chunk, nf=nf, ni=ni),
+        grid=(total + ni,),
+        in_specs=[
+            row,
+            row,
+            pl.BlockSpec((1, 9, width), lambda t: (at(t) // blocks, 0, 0)),
+            whole(wup.shape),
+            whole(wdn.shape),
+        ],
+        out_specs=[row, row, pl.BlockSpec((1, 3, width), lambda t: (at(t) // blocks, 0, 0)), grad, grad],
+        out_shape=[
+            struct(second.shape, BF),
+            struct(second.shape, F32),
+            struct((items, 3, width), F32),
+            grad_shape,
+            grad_shape,
+        ],
+        scratch_shapes=[pltpu.VMEM((width, ff), F32), pltpu.VMEM((ff, width), F32)],
+        compiler_params=params(),
+        cost_estimate=cost(12 * items * count * width * ff, items * count * width * 12, items * count * ff * 2),
+        name="mlp",
+    )(second, cot, mod, wup, wdn)
+
+
+def cross_back_call(tlens, g2, ba, bb, cr, att, cq, first, mod, kv, lse, wo, wq, wco, score_scale, block, nf, ni):
+    items, count, width = g2.shape
+    slots = kv.shape[1]
+    blocks = count // block
+    total = items * blocks
+
+    def at(t):
+        return jnp.minimum(t, total - 1)
+
+    def by_item(t, s):
+        return (at(t) // blocks, 0, 0)
+
+    row = pl.BlockSpec((1, block, width), lambda t, s: (at(t) // blocks, at(t) % blocks, 0))
+    depth = 3 * width * width // (nf * ni * PACK)
+    spec = pltpu.PrefetchScalarGridSpec(
+        num_scalar_prefetch=1,
+        grid=(total + ni,),
+        in_specs=[row] * 7
+        + [
+            pl.BlockSpec((1, 9, width), by_item),
+            pl.BlockSpec((1, slots, 2 * width), by_item),
+            pl.BlockSpec((1, H // 2, 2, block), lambda t, s: (at(t) // blocks, 0, 0, at(t) % blocks)),
+            whole(wo.shape),
+            whole(wq.shape),
+            whole(wco.shape),
+        ],
+        out_specs=[
+            row,
+            row,
+            pl.BlockSpec((1, slots, 2 * width), by_item),
+            pl.BlockSpec((1, 4, width), by_item),
+            pl.BlockSpec((1, nf, depth, PACK), lambda t, s: (jnp.maximum(t - total, 0), 0, 0, 0)),
+        ],
+        scratch_shapes=[pltpu.VMEM((width, width), F32)] * 3 + [pltpu.VMEM((block, width), BF)],
+    )
+    return pl.pallas_call(
+        partial(cross_back_kernel, blocks=blocks, total=total, score_scale=score_scale, nf=nf, ni=ni),
+        grid_spec=spec,
+        out_shape=[
+            struct(g2.shape, F32),
+            struct(g2.shape, BF),
+            struct(kv.shape, F32),
+            struct((items, 4, width), F32),
+            struct((ni, nf, depth, PACK), BF),
+        ],
+        compiler_params=params(),
+        cost_estimate=cost(
+            items * count * (12 * width * width + 40 * slots * width), items * count * width * 24, items * H * count * slots
+        ),
+        name="cross_bwd",
+    )(tlens, g2, ba, bb, cr, att, cq, first, mod, kv, lse, wo, wq, wco)
+
+
+def qkv_back_call(dq, dk, dv, rows, g1, mod, weight, block, nf, ni):
+    items, count, width = rows.shape
+    blocks = count // block
+    total = items * blocks
+
+    def at(t):
+        return jnp.minimum(t, total - 1)
+
+    row = pl.BlockSpec((1, block, width), lambda t: (at(t) // blocks, at(t) % blocks, 0))
+    depth = 3 * width * width // (nf * ni * PACK)
+    return pl.pallas_call(
+        partial(qkv_back_kernel, blocks=blocks, total=total, nf=nf, ni=ni),
+        grid=(total + ni,),
+        in_specs=[row] * 5 + [pl.BlockSpec((1, 9, width), lambda t: (at(t) // blocks, 0, 0)), whole(weight.shape)],
+        out_specs=[
+            row,
+            pl.BlockSpec((1, 2, width), lambda t: (at(t) // blocks, 0, 0)),
+            pl.BlockSpec((1, nf, depth, PACK), lambda t: (jnp.maximum(t - total, 0), 0, 0, 0)),
+        ],
+        out_shape=[
+            struct(rows.shape, BF),
+            struct((items, 2, width), F32),
+            struct((ni, nf, depth, PACK), BF),
+        ],
+        scratch_shapes=[pltpu.VMEM((width, 3 * width), F32)],
+        compiler_params=params(),
+        cost_estimate=cost(12 * items * count * width * width * 2, items * count * width * 20),
+        name="qkv_bwd",
+    )(dq, dk, dv, rows, g1, mod, weight)
+
+
+def place_items(lengths, nf):
+    count = lengths.shape[0]
+    index = jnp.arange(count, dtype=jnp.int32)
+    ahead = (lengths[None, :] > lengths[:, None]) | (
+        (lengths[None, :] == lengths[:, None]) & (index[None, :] < index[:, None])
+    )
+    rank = jnp.sum(ahead.astype(jnp.int32), 1)
+    turn, seat = rank // nf, rank % nf
+    device = jnp.where(turn % 2 == 0, seat, nf - 1 - seat)
+    place = device * (count // nf) + turn
+    held = jnp.sum(jnp.where(place[None, :] == index[:, None], index[None, :], 0), 1)
+    return place, held
+
+
+def swap(block, offset, nf):
+    if offset == 0:
+        return block
+    return lax.ppermute(block, "frames", [(i, i ^ offset) for i in range(nf)])
+
+
+def to_items(shard, held, me, nf):
+    count, rows, width = shard.shape
+    per = count // nf
+    out = jnp.zeros((per, nf, rows, width), shard.dtype)
+    for offset in range(nf):
+        partner = me ^ offset
+        block = jnp.concatenate(
+            [lax.dynamic_slice_in_dim(shard, held[partner * per + slot], 1, 0) for slot in range(per)], 0
+        )
+        block = swap(block, offset, nf)
+        out = lax.dynamic_update_slice(out, block[:, None], (0, partner, 0, 0))
+    return out.reshape(per, nf * rows, width)
+
+
+def to_frames(items, place, me, nf):
+    per, count, width = items.shape
+    rows = count // nf
+    got = []
+    for offset in range(nf):
+        block = lax.dynamic_slice_in_dim(items, (me ^ offset) * rows, rows, 1)
+        got.append(swap(block, offset, nf))
+    stacked = jnp.concatenate(got, 0)
+    return jnp.concatenate(
+        [
+            lax.dynamic_slice_in_dim(stacked, ((place[i] // per) ^ me) * per + place[i] % per, 1, 0)
+            for i in range(per * nf)
+        ],
+        0,
+    )
+
+
+def reduce_blocks(blocks):
+    ni, nf, depth, pack = blocks.shape
+    flat = blocks.reshape(ni * nf, depth, pack)
+    return lax.psum_scatter(flat, ("items", "frames"), scatter_dimension=0, tiled=True)[0].astype(F32)
+
+
+def wide(block, parts):
+    rows = block.shape[0] // parts
+    return jnp.concatenate([block[p * rows : (p + 1) * rows] for p in range(parts)], 1)
+
+
+def tall(block):
+    half = block.shape[1] // 2
+    return jnp.concatenate([block[:, :half], block[:, half:]], 0)
+
+
+def items_whole(
+    ni, nf, frames_in, cond, text, item_lengths, text_lengths, ada_weight, qkv_weight, out_weight,
+    cross_q_weight, cross_kv_weight, cross_out_weight, up_weight, down_weight, cotangent,
+):
+    width = frames_in.shape[-1]
+    items = frames_in.shape[0]
+    per = items // nf
+    score_scale = (width // H) ** (-0.5)
+    me = lax.axis_index("frames")
+    row_item = lax.axis_index("items")
+    place, held = place_items(item_lengths, nf)
+    mine = lax.dynamic_slice_in_dim(held, me * per, per, 0)
+    pick = (mine[:, None] == jnp.arange(items, dtype=jnp.int32)[None, :]).astype(F32)
+
+    rows = to_items(frames_in, held, me, nf)
+    text_rows = to_items(text, held, me, nf)
+    cot = to_items(cotangent, held, me, nf)
+    lens = jnp.take(item_lengths, mine)
+    tlens = jnp.take(text_lengths, mine)
+
+    cond_f = cond.astype(F32)
+    low_cond = jax.nn.silu(cond_f).astype(BF)
+    modulation = nn(low_cond, ada_weight)
+    mod = jnp.sum(pick[:, :, None] * modulation[None], 1).reshape(per, 9, width)
+    cond_mine = jnp.sum(pick[:, :, None] * low_cond.astype(F32)[None], 1)
+
+    text_kv = jnp.einsum("itd,de->ite", text_rows, cross_kv_weight, preferred_element_type=F32).astype(BF)
+    qkv = qkv_call(rows, mod, qkv_weight, score_scale, 256)
+    attended, self_lse = self_fwd_call(lens, qkv, 512)
+    first, second, branch_a, branch_b, cross_q, crossed, cross_lse = cross_call(
+        tlens, attended, rows, mod, text_kv, out_weight, cross_q_weight, cross_out_weight, score_scale, 256
+    )
+    layer_rows, g2, dmod_c, g_up, g_down = mlp_call(second, cot, mod, up_weight, down_weight, 256, 768, nf, ni)
+    layer_out = to_frames(layer_rows, place, me, nf)
+    sum_up, sum_down = reduce_blocks(g_up), reduce_blocks(g_down)
+    g1, d_att, d_text, dmod_b, g_sq = cross_back_call(
+        tlens, g2, branch_a, branch_b, crossed, attended, cross_q, first, mod, text_kv, cross_lse,
+        out_weight, cross_q_weight, cross_out_weight, score_scale, 256, nf, ni,
+    )
+    low_text = d_text.astype(BF)
+    g_kv = weight_grad(text_rows, low_text).astype(BF)
+    g_kv = g_kv.reshape(ni, width // ni, nf, 2 * width // nf).transpose(0, 2, 1, 3)
+    text_grad = to_frames(project_back(low_text, cross_kv_weight).astype(BF), place, me, nf).astype(F32)
+    sum_sq = reduce_blocks(jnp.concatenate([g_sq, g_kv], 2))
+    dq, dk, dv = self_bwd_call(lens, qkv, attended, d_att, self_lse, 512, score_scale)
+    d_rows, dmod_a, g_qkv = qkv_back_call(dq, dk, dv, rows, g1, mod, qkv_weight, 256, nf, ni)
+    sum_qkv = reduce_blocks(g_qkv)
+    input_grad = to_frames(d_rows, place, me, nf).astype(F32)
+
+    d_mod = jnp.concatenate([dmod_a, dmod_b, dmod_c], 1).reshape(per, 9 * width)
+    every = lax.all_gather(jnp.concatenate([cond_mine, d_mod], 1), ("items", "frames"), axis=0, tiled=True)
+    ada_rows, ada_cols = width // ni, 9 * width // nf
+    grad_ada = lax.dot_general(
+        lax.dynamic_slice_in_dim(every[:, :width], row_item * ada_rows, ada_rows, 1),
+        lax.dynamic_slice_in_dim(every[:, width:], me * ada_cols, ada_cols, 1),
+        (((0,), (0,)), ((), ())),
+        precision=lax.Precision.HIGHEST,
+        preferred_element_type=F32,
+    )
+    cond_part = lax.dot_general(
+        d_mod, ada_weight, (((1,), (1,)), ((), ())), precision=lax.Precision.HIGHEST, preferred_element_type=F32
+    )
+    cond_all = jnp.take(lax.all_gather(cond_part, "frames", axis=0, tiled=True), place, axis=0)
+    sigmoid_c = jax.nn.sigmoid(cond_f)
+    slope = sigmoid_c * (1.0 + cond_f * (1.0 - sigmoid_c))
+    cond_grad = lax.dynamic_slice_in_dim(cond_all * slope, me * (width // nf), width // nf, 1)
+
+    half = width // ni // 2
+    return (
+        layer_out,
+        input_grad,
+        text_grad,
+        cond_grad,
+        grad_ada,
+        jnp.concatenate([sum_qkv[: 2 * half], tall(sum_qkv[2 * half :])], 1),
+        tall(sum_sq[:half]),
+        tall(sum_sq[half : 2 * half]),
+        sum_sq[3 * half :],
+        tall(sum_sq[2 * half : 3 * half]),
+        wide(sum_up, 2),
+        tall(sum_down),
+    )
+
+
+def on_device(mesh, *args):
+    ni, nf = mesh.shape["items"], mesh.shape["frames"]
+    if nf == 4 and args[0].shape[0] % nf == 0 and args[0].shape[-1] == 768 and 768 % (32 * ni) == 0:
+        return items_whole(ni, nf, *args)
+    return frames_split(*args)
+
+
 def solution(mesh):
     in_specs = (
         P("items", "frames", None),
@@ -351,5 +1101,5 @@
         P("items", "frames"),
     )
     return jax.shard_map(
-        on_device, mesh=mesh, in_specs=in_specs, out_specs=out_specs, check_vma=False
-    )
+        partial(on_device, mesh), mesh=mesh, in_specs=in_specs, out_specs=out_specs, check_vma=False
+    )

time: 1920 us -> 990 us (0.52)
  matrix products: 615 us -> 29.1 us
  waiting for transfers between devices: 912 us -> 465 us
  Pallas kernels: 0 us -> 304 us
  other arithmetic: 199 us -> 40.1 us
  local copies, waits for them, and re-layouts: 174 us -> 59.2 us
  between operations: 15.3 us -> 51.2 us
    unnamed x31 -> x5, waiting for transfers between devices: 452 us -> 1.43 us
    dot_general x20 -> x4, matrix products: 384 us -> 20.7 us  [the longest x1 11 us: items_whole(): lax.dot_general(d_mod, ada_weight, (((1,), (1,)), ((), ())), precision=la...]
    pallas_call x0 -> x7, Pallas kernels: none -> 304 us  [the longest x1 89 us: mlp_call(): pl.pallas_call(partial(mlp_kernel, blocks=blocks, total=total, chunk=chun...]
    convert_element_type x5 -> x9, other arithmetic: 163 us -> 9.76 us  [the longest x4 3.78 us: reduce_blocks(): lax.psum_scatter(flat, ('items', 'frames'), scatter_dimension=0, tiled=True)]
    all_gather x3 -> x1, waiting for transfers between devices: 109 us -> 0.01 us  [items_whole(): lax.all_gather(jnp.concatenate([cond_mine, d_mod], 1), ('items', 'frames'...]
    ppermute x0 -> x18, waiting for transfers between devices: none -> 90.8 us  [swap(): return lax.ppermute(block, 'frames', [(i, i ^ offset) for i in range(nf)])]
    dot_general x7 -> x1, matrix products: 89.8 us -> 3.64 us  [project_back(): jnp.einsum('ife,de->ifd', tensor, weight, preferred_element_type=jnp.floa...]
    dot_general x7 -> x1, matrix products: 79.6 us -> 4.71 us  [weight_grad(): jnp.einsum('ifd,ife->de', left, right, preferred_element_type=jnp.float32)]
  transfers between devices with their start and end apart: 23 -> 23, of which waited for: 20 -> 12; matrix products, arithmetic and copies ran while one was open for 31% -> 11% of each run, Pallas kernels for 0% -> 7%
where the time goes in v1:
time: 990 us; the launch traced here: 982 us
  waiting for transfers between devices  465 us (47%)
  Pallas kernels  304 us (31%)
  local copies, waits for them, and re-layouts  59.2 us (6%)
  between operations  51.2 us (5%)
  other arithmetic  40.1 us (4%)
  matrix products  29.1 us (3%)
  blocking collectives  18.9 us (2%)
  starting transfers between devices  14.5 us (1%)
    reduce_scatter x4, waiting for transfers between devices, reduce_blocks(): lax.psum_scatter(flat, ('items', 'frames'), scatter_dimension=0, tiled=True)  373 us
    ppermute x18, waiting for transfers between devices, swap(): return lax.ppermute(block, 'frames', [(i, i ^ offset) for i in range(nf)])  90.8 us
    pallas_call x1, Pallas kernels, mlp_call(): pl.pallas_call(partial(mlp_kernel, blocks=blocks, total=total, chunk=chun...  89 us
    pallas_call x1, Pallas kernels, cross_back_call(): pl.pallas_call(partial(cross_back_kernel, blocks=blocks, total=total, sco...  60.7 us
    pallas_call x1, Pallas kernels, self_bwd_call(): pl.pallas_call(partial(self_bwd_kernel, qb=qb, score_scale=score_scale),...  52.2 us
    pallas_call x1, Pallas kernels, self_fwd_call(): pl.pallas_call(partial(self_fwd_kernel, qb=qb), grid_spec=spec, out_shape...  34.3 us
    pallas_call x1, Pallas kernels, qkv_back_call(): pl.pallas_call(partial(qkv_back_kernel, blocks=blocks, total=total, nf=nf...  28.9 us
    pallas_call x1, Pallas kernels, cross_call(): pl.pallas_call(partial(cross_kernel, score_scale=score_scale), grid_spec=...  25.1 us
  transfers between devices with their start and end apart: 23, of which 12 were waited for; matrix products, arithmetic and copies ran while one was open for 11% of the time, Pallas kernels for 7%

profile of v1, /device:TPU:0, one launch (start us, length us, event | category | flops | bytes accessed | tf_op | source)
XLA Modules:
  0.0 982.1 jit_solution(15355765058474494845)
XLA Ops:
  25.7 4.2 constant_dynamic-slice_fusion.16
  32.3 2.5 collective-permute-start.7
  41.3 5.5 fusion.26
  47.7 1.5 reshape.269.mod_ref
  51.7 1.4 multiply_reduce_fusion.1
  53.1 2.1 pad_maximum_fusion.8
  58.8 1.9 broadcast.355.clone
  62.3 2.0 collective-permute-start.4
  65.3 9.0 collective-permute-done.4
  75.4 5.8 collective-permute-done.5
  81.2 1.6 collective-permute-start.2
  82.9 2.5 convolution_convert_fusion.kv_ref
  85.6 2.1 bitcast_dynamic-update-slice_fusion.5
  87.7 2.1 bitcast_dynamic-update-slice_fusion.4
  89.8 11.0 %collective-permute-done.2 = bf16[2,256,768]{2,1,0:T(8,128)(2,1)S(1)} collective-permute-done((bf16[2,256,768]{2,1,0:T(8,128)(2,1)S(1)}, bf16[2,256,768]{2,1,0:T(8,128)(2,1)S(1)}, u32[]{:S(2)}, u32[]{:S(2)}) %collective-permute-start.2) | collective-permute-done | bytes 786464 | tf_op jit(solution)/shard_map/ppermute | solution.py:931
  101.7 14.0 %qkv_fwd.1.q_ref.k_ref.v_ref = bf16[2,1024,2304]{2,1,0:T(8,128)(2,1)} custom-call(bf16[2,1024,768]{2,1,0:T(8,128)(2,1)} %bitcast.16.x_ref, f32[2,9,768]{2,1,0:T(8,128)} %reshape.269.mod_ref, bf16[768,2304]{1,0:T(8,128)(2,1)} %w_ref.3), custom_call_target="tpu_custom_call" | custom-call | flops 7247757312 | bytes 12582912 | tf_op jit(solution)/shard_map/qkv_fwd/pallas_call | solution.py:696
  115.7 34.3 %self_fwd.1 = (bf16[2,1024,768]{2,1,0:T(8,128)(2,1)}, f32[2,6,2,1024]{3,2,1,0:T(2,128)}) custom-call(s32[2]{0:T(128)} %get-tuple-element.137.lens, bf16[2,1024,2304]{2,1,0:T(8,128)(2,1)} %qkv_fwd.1.q_ref.k_ref.v_ref, bf16[2,1024,2304]{2,1,0:T(8,128)(2,1)} %qkv_fwd.1.q_ref.k_ref.v_ref, bf16[2,1024,2304]{2,1,0:T(8,128)(2,1)} %qkv_fwd.1.q_ref.k_ref.v_ref), custom_call_target="tpu_custom_call" | custom-call | flops 25769803776 | bytes 12582912 | tf_op jit(solution)/shard_map/self_fwd/pallas_call | solution.py:727
  150.0 2.1 bitcast_dynamic-update-slice_fusion.2
  152.1 2.0 bitcast_dynamic-update-slice_fusion.1
  154.2 25.1 %cross_fwd.1 = (f32[2,1024,768]{2,1,0:T(8,128)}, f32[2,1024,768]{2,1,0:T(8,128)}, bf16[2,1024,768]{2,1,0:T(8,128)(2,1)}, bf16[2,1024,768]{2,1,0:T(8,128)(2,1)}, ...) custom-call(s32[2]{0:T(128)} %get-tuple-element.138.tlens, ...), custom_call_target="tpu_custom_call" | custom-call | flops 13690208256 | bytes 31457280 | tf_op jit(solution)/shard_map/cross_fwd/pallas_call | solution.py:779
  180.3 89.0 %mlp.1 = (bf16[2,1024,768]{2,1,0:T(8,128)(2,1)}, f32[2,1024,768]{2,1,0:T(8,128)}, f32[2,3,768]{2,1,0:T(4,128)}, bf16[8,4,192,384]{3,2,1,0:T(8,128)(2,1)}, bf16[8,4,192,384]{3,2,1,0:T(8,128)(2,1)}) custom-call(f32[2,1024,768]{2,1,0:T(8,128)} %get-tuple-element.39.second_ref, bf16[2,1024,768]{2,1,0:T(8,128)(2,1)} %bitcast.128, f32[2,9,768]{2,1,0:T(8,128)} %reshape.269.mod_ref, ...), custom_call_target="tpu_custom_call" | custom-call | flops 57982058496 | bytes 18874368 | tf_op jit(solution)/shard_map/mlp/pallas_call | solution.py:805
  269.3 60.7 %cross_bwd.1 = (f32[2,1024,768]{2,1,0:T(8,128)}, bf16[2,1024,768]{2,1,0:T(8,128)(2,1)}, f32[2,256,1536]{2,1,0:T(8,128)}, f32[2,4,768]{2,1,0:T(4,128)}, bf16[8,4,144,384]{3,2,1,0:T(8,128)(2,1)}) custom-call(s32[2]{0:T(128)} %get-tuple-element.138.tlens, f32[2,1024,768]{2,1,0:T(8,128)} %get-tuple-element.41.g2_ref, ...), custom_call_target="tpu_custom_call" | custom-call | flops 30601641984 | bytes 37748736 | tf_op jit(solution)/shard_map/cross_bwd/pallas_call | solution.py:865
  330.0 52.2 %self_bwd.1 = (bf16[2,1024,768]{2,1,0:T(8,128)(2,1)}, bf16[2,1024,768]{2,1,0:T(8,128)(2,1)}, bf16[2,1024,768]{2,1,0:T(8,128)(2,1)}) custom-call(s32[2]{0:T(128)} %get-tuple-element.137.lens, bf16[2,1024,2304]{2,1,0:T(8,128)(2,1)} %qkv_fwd.1.q_ref.k_ref.v_ref, bf16[2,1024,2304]{2,1,0:T(8,128)(2,1)} %qkv_fwd.1.q_ref.k_ref.v_ref, ...), custom_call_target="tpu_custom_call" | custom-call | flops 64424509440 | bytes 25165824 | tf_op jit(solution)/shard_map/self_bwd/pallas_call | solution.py:751
  382.2 28.9 %qkv_bwd.1 = (bf16[2,1024,768]{2,1,0:T(8,128)(2,1)}, f32[2,2,768]{2,1,0:T(2,128)}, bf16[8,4,144,384]{3,2,1,0:T(8,128)(2,1)}) custom-call(bf16[2,1024,768]{2,1,0:T(8,128)(2,1)} %get-tuple-element.50.dq_ref, bf16[2,1024,768]{2,1,0:T(8,128)(2,1)} %get-tuple-element.51.dk_ref, bf16[2,1024,768]{2,1,0:T(8,128)(2,1)} %get-tuple-element.52.dv_ref, ...), custom_call_target="tpu_custom_call" | custom-call | flops 28991029248 | bytes 31457280 | tf_op jit(solution)/shard_map/qkv_bwd/pallas_call | solution.py:893
  414.1 7.9 copy.71
  423.1 4.7 bitcast_convert_fusion
  427.9 5.2 reshape.274
  433.0 2.2 copy.75
  435.8 3.1 pad_maximum_fusion
  461.2 11.0 %convolution_bitcast_fusion = f32[1,2,768]{2,1,0:T(2,128)S(1)} fusion(f32[2,6912]{1,0:T(2,128)S(1)} %bitcast.132, bf16[768,6912]{1,0:T(8,128)(2,1)} %param.21), kind=kOutput, calls=%fused_computation.13 | convolution fusion | flops 127401984 | bytes 10678272 | tf_op jit(solution)/shard_map/dot_general | solution.py:1040
  472.2 18.9 %all-gather = f32[4,2,768]{2,1,0:T(2,128)S(1)} all-gather(f32[1,2,768]{2,1,0:T(2,128)S(1)} %convolution_bitcast_fusion), channel_id=1, replica_groups=mesh['items'=8,'frames'=4] {'frames'}, dimensions={0}, use_global_device_ids=true | all-gather | bytes 30720 | tf_op jit(solution)/shard_map/all_gather | solution.py:1043
  491.1 3.6 fusion.3
  497.4 1.4 constant_dynamic-slice_fusion.10
  500.5 1.4 fusion.16
  501.9 2.2 constant_dynamic-slice_fusion.14
  510.7 14.3 %collective-permute-done.13 = bf16[2,256,768]{2,1,0:T(8,128)(2,1)} collective-permute-done((bf16[2,256,768]{2,1,0:T(8,128)(2,1)}, bf16[2,256,768]{2,1,0:T(8,128)(2,1)}, u32[]{:S(2)}, u32[]{:S(2)}) %collective-permute-start.13) | collective-permute-done | bytes 786464 | tf_op jit(solution)/shard_map/ppermute | solution.py:931
  525.0 15.3 %collective-permute-done.14 = bf16[2,256,768]{2,1,0:T(8,128)(2,1)S(1)} collective-permute-done((bf16[2,256,768]{2,1,0:T(8,128)(2,1)S(1)}, bf16[2,256,768]{2,1,0:T(8,128)(2,1)S(1)}, u32[]{:S(2)}, u32[]{:S(2)}) %collective-permute-start.14) | collective-permute-done | bytes 786464 | tf_op jit(solution)/shard_map/ppermute | solution.py:931
  540.3 1.8 pad_maximum_fusion.2
  542.5 3.3 convert_element_type.64
  545.7 12.9 %collective-permute-done.10 = bf16[2,256,768]{2,1,0:T(8,128)(2,1)S(1)} collective-permute-done((bf16[2,256,768]{2,1,0:T(8,128)(2,1)S(1)}, bf16[2,256,768]{2,1,0:T(8,128)(2,1)S(1)}, u32[]{:S(2)}, u32[]{:S(2)}) %collective-permute-start.10) | collective-permute-done | bytes 786464 | tf_op jit(solution)/shard_map/ppermute | solution.py:931
  558.6 21.7 %collective-permute-done.11 = bf16[2,256,768]{2,1,0:T(8,128)(2,1)S(1)} collective-permute-done((bf16[2,256,768]{2,1,0:T(8,128)(2,1)S(1)}, bf16[2,256,768]{2,1,0:T(8,128)(2,1)S(1)}, u32[]{:S(2)}, u32[]{:S(2)}) %collective-permute-start.11) | collective-permute-done | bytes 786464 | tf_op jit(solution)/shard_map/ppermute | solution.py:931
  586.9 3.6 reshape.308
  590.5 1.5 slice-done
  591.9 1.7 fusion.10
  593.6 28.9 %reduce-scatter.5.cloned.1.call-done = bf16[1,144,384]{2,1,0:T(8,128)(2,1)} async-done(((bf16[32,144,384]{2,1,0:T(8,128)(2,1)}), bf16[1,144,384]{2,1,0:T(8,128)(2,1)}) %reduce-scatter.5.cloned.1.call-update) | async-done | bytes 110608 | tf_op jit(solution)/shard_map/reduce_scatter | solution.py:968
  624.2 109.7 %reduce-scatter.9.cloned.1.call-done = bf16[1,192,384]{2,1,0:T(8,128)(2,1)} async-done(((bf16[32,192,384]{2,1,0:T(8,128)(2,1)}), bf16[1,192,384]{2,1,0:T(8,128)(2,1)}) %reduce-scatter.9.cloned.1.call-update) | async-done | bytes 147472 | tf_op jit(solution)/shard_map/reduce_scatter | solution.py:968
  734.9 119.2 %reduce-scatter.11.cloned.1.call-done = bf16[1,192,384]{1,2,0:T(8,128)(2,1)} async-done(((bf16[32,192,384]{1,2,0:T(8,128)(2,1)}), bf16[1,192,384]{1,2,0:T(8,128)(2,1)}) %reduce-scatter.11.cloned.1.call-update) | async-done | bytes 147472 | tf_op jit(solution)/shard_map/reduce_scatter | solution.py:968
  856.7 114.9 %reduce-scatter.7.cloned.1.call-done = bf16[1,240,384]{2,1,0:T(8,128)(2,1)} async-done(((bf16[32,240,384]{2,1,0:T(8,128)(2,1)}), bf16[1,240,384]{2,1,0:T(8,128)(2,1)}) %reduce-scatter.7.cloned.1.call-update) | async-done | bytes 184336 | tf_op jit(solution)/shard_map/reduce_scatter | solution.py:968
  (176 shorter events, 57.0 us)
Async XLA Ops:
  7.2 75.7 %copy-start = (bf16[768,1536]{1,0:T(8,128)(2,1)S(1)}, bf16[768,1536]{1,0:T(8,128)(2,1)}, u32[]{:S(2)}) copy-start(bf16[768,1536]{1,0:T(8,128)(2,1)} %param.25) | copy-start | bytes 7077892
  7.2 579.7 %all-gather.4.cloned.1.call-start = ((), (), s32[]{:S(2)}) async-start(), calls=%async_computation.8 | async-start | bytes 2027520 | tf_op jit(solution)/shard_map/all_gather | solution.py:1031
  30.0 7.0 copy-start.7
  30.9 119.1 %collective-permute-start.6 = (bf16[2,256,768]{2,1,0:T(8,128)(2,1)}, bf16[2,256,768]{2,1,0:T(8,128)(2,1)}, u32[]{:S(2)}, u32[]{:S(2)}) collective-permute-start(bf16[2,256,768]{2,1,0:T(8,128)(2,1)} %pad_maximum_fusion.6), channel_id=1, source_target_pairs={{0,1},{1,0},{2,3},{3,2},{4,5},{5,4},{6,7},{7,6},{8,9},{9,8},{10,11... | collective-permute-start | bytes 2359304 | tf_op jit(solution)/shard_map/ppermute | solution.py:931
  32.3 119.8 %collective-permute-start.7 = (bf16[2,256,768]{2,1,0:T(8,128)(2,1)}, bf16[2,256,768]{2,1,0:T(8,128)(2,1)}, u32[]{:S(2)}, u32[]{:S(2)}) collective-permute-start(bf16[2,256,768]{2,1,0:T(8,128)(2,1)} %pad_maximum_fusion.7), channel_id=1, source_target_pairs={{0,2},{1,3},{2,0},{3,1},{4,6},{5,7},{6,4},{7,5},{8,10},{9,11},{10,... | collective-permute-start | bytes 2359304 | tf_op jit(solution)/shard_map/ppermute | solution.py:931
  35.8 51.9 %collective-permute-start.1 = (bf16[2,256,768]{2,1,0:T(8,128)(2,1)}, bf16[2,256,768]{2,1,0:T(8,128)(2,1)}, u32[]{:S(2)}, u32[]{:S(2)}) collective-permute-start(bf16[2,256,768]{2,1,0:T(8,128)(2,1)} %pad_maximum_fusion.4), channel_id=1, source_target_pairs={{0,2},{1,3},{2,0},{3,1},{4,6},{5,7},{6,4},{7,5},{8,10},{9,11},{10,... | collective-permute-start | bytes 2359304 | tf_op jit(solution)/shard_map/ppermute | solution.py:931
  36.8 48.6 %collective-permute-start = (bf16[2,256,768]{2,1,0:T(8,128)(2,1)}, bf16[2,256,768]{2,1,0:T(8,128)(2,1)}, u32[]{:S(2)}, u32[]{:S(2)}) collective-permute-start(bf16[2,256,768]{2,1,0:T(8,128)(2,1)} %pad_maximum_fusion.3), channel_id=1, source_target_pairs={{0,1},{1,0},{2,3},{3,2},{4,5},{5,4},{6,7},{7,6},{8,9},{9,8},{10,11... | collective-permute-start | bytes 2359304 | tf_op jit(solution)/shard_map/ppermute | solution.py:931
  38.5 23.8 %collective-permute-start.3 = (bf16[2,64,768]{2,1,0:T(8,128)(2,1)}, bf16[2,64,768]{2,1,0:T(8,128)(2,1)}, u32[]{:S(2)}, u32[]{:S(2)}) collective-permute-start(bf16[2,64,768]{2,1,0:T(8,128)(2,1)} %pad_maximum_fusion.12), channel_id=1, source_target_pairs={{0,1},{1,0},{2,3},{3,2},{4,5},{5,4},{6,7},{7,6},{8,9},{9,8},{10,11... | collective-permute-start | bytes 589832 | tf_op jit(solution)/shard_map/ppermute | solution.py:931
  41.3 8.6 copy-start.1
  41.3 9.8 copy-start.2
  55.3 3.4 copy-start.6
  58.7 6.6 copy-start.5
  58.7 3.0 copy-start.12
  58.7 3.0 copy-start.13
  58.8 3.0 copy-start.21
  58.8 3.0 copy-start.22
  62.3 12.0 %collective-permute-start.4 = (bf16[2,64,768]{2,1,0:T(8,128)(2,1)S(1)}, bf16[2,64,768]{2,1,0:T(8,128)(2,1)S(1)}, u32[]{:S(2)}, u32[]{:S(2)}) collective-permute-start(bf16[2,64,768]{2,1,0:T(8,128)(2,1)S(1)} %pad_maximum_fusion.13), channel_id=1, source_target_pairs={{0,2},{1,3},{2,0},{3,1},{4,6},{5,7},{6,4},{7,5},{8,10},{9,11},{10,... | collective-permute-start | bytes 589832 | tf_op jit(solution)/shard_map/ppermute | solution.py:931
  74.3 6.9 collective-permute-start.5
  81.2 19.5 %collective-permute-start.2 = (bf16[2,256,768]{2,1,0:T(8,128)(2,1)S(1)}, bf16[2,256,768]{2,1,0:T(8,128)(2,1)S(1)}, u32[]{:S(2)}, u32[]{:S(2)}) collective-permute-start(bf16[2,256,768]{2,1,0:T(8,128)(2,1)S(1)} %pad_maximum_fusion.5), channel_id=1, source_target_pairs={{0,3},{1,2},{2,1},{3,0},{4,7},{5,6},{6,5},{7,4},{8,11},{9,10},{10,... | collective-permute-start | bytes 2359304 | tf_op jit(solution)/shard_map/ppermute | solution.py:931
  82.8 2.6 copy-start.9
  82.8 2.5 copy-start.8
  85.4 93.9 %collective-permute-start.8 = (bf16[2,256,768]{2,1,0:T(8,128)(2,1)S(1)}, bf16[2,256,768]{2,1,0:T(8,128)(2,1)S(1)}, u32[]{:S(2)}, u32[]{:S(2)}) collective-permute-start(bf16[2,256,768]{2,1,0:T(8,128)(2,1)S(1)} %copy-done.8), channel_id=1, source_target_pairs={{0,3},{1,2},{2,1},{3,0},{4,7},{5,6},{6,5},{7,4},{8,11},{9,10},{10,... | collective-permute-start | bytes 2359304 | tf_op jit(solution)/shard_map/ppermute | solution.py:931
  382.2 28.9 %copy-start.17 = (f32[2,3,768]{2,1,0:T(4,128)S(1)}, f32[2,3,768]{2,1,0:T(4,128)}, u32[]{:S(2)}) copy-start(f32[2,3,768]{2,1,0:T(4,128)} %get-tuple-element.58) | copy-start | bytes 55300
  382.2 28.9 %copy-start.18 = (f32[2,4,768]{2,1,0:T(4,128)S(1)}, f32[2,4,768]{2,1,0:T(4,128)}, u32[]{:S(2)}) copy-start(f32[2,4,768]{2,1,0:T(4,128)} %get-tuple-element.57) | copy-start | bytes 73732
  382.2 29.7 %copy-start.19 = (f32[2,768]{1,0:T(2,128)S(1)}, f32[2,768]{1,0:T(2,128)}, u32[]{:S(2)}) copy-start(f32[2,768]{1,0:T(2,128)} %multiply_reduce_fusion.1) | copy-start | bytes 18436
  412.5 209.9 %reduce-scatter.5.cloned.1.call-start = ((), (), s32[]{:S(2)}) async-start(), calls=%async_computation.4 | async-start | bytes 3649536 | tf_op jit(solution)/shard_map/reduce_scatter | solution.py:968
  413.3 320.6 %reduce-scatter.9.cloned.1.call-start = ((), (), s32[]{:S(2)}) async-start(), calls=%async_computation.6 | async-start | bytes 4866048 | tf_op jit(solution)/shard_map/reduce_scatter | solution.py:968
  414.0 440.0 %reduce-scatter.11.cloned.1.call-start = ((), (), s32[]{:S(2)}) async-start(), calls=%async_computation.7 | async-start | bytes 6488064 | tf_op jit(solution)/shard_map/reduce_scatter | solution.py:968
  422.0 1.1 copy-start.10
  422.0 549.5 %reduce-scatter.7.cloned.1.call-start = ((), (), s32[]{:S(2)}) async-start(), calls=%async_computation.5 | async-start | bytes 6082560 | tf_op jit(solution)/shard_map/reduce_scatter | solution.py:968
  433.0 2.7 copy-start.3
  438.9 0.7 copy-start.14
  438.9 0.7 copy-start.16
  438.9 22.3 %copy-start.25 = (s32[8]{0:T(128)S(1)}, s32[8]{0:T(128)}, u32[]{:S(2)}) copy-start(s32[8]{0:T(128)} %copy-done.24) | copy-start | bytes 100
  491.1 6.4 copy-start.4
  495.6 8.5 collective-permute-start.15
  495.9 9.2 collective-permute-start.16
  496.3 10.4 %collective-permute-start.17 = (bf16[2,64,768]{2,1,0:T(8,128)(2,1)}, bf16[2,64,768]{2,1,0:T(8,128)(2,1)}, u32[]{:S(2)}, u32[]{:S(2)}) collective-permute-start(bf16[2,64,768]{2,1,0:T(8,128)(2,1)} %get-tuple-element.92), channel_id=1, source_target_pairs={{0,3},{1,2},{2,1},{3,0},{4,7},{5,6},{6,5},{7,4},{8,11},{9,10},{10,... | collective-permute-start | bytes 589832 | tf_op jit(solution)/shard_map/ppermute | solution.py:931
  497.4 3.0 copy-start.23
  498.9 11.8 %collective-permute-start.12 = (bf16[2,256,768]{2,1,0:T(8,128)(2,1)}, bf16[2,256,768]{2,1,0:T(8,128)(2,1)}, u32[]{:S(2)}, u32[]{:S(2)}) collective-permute-start(bf16[2,256,768]{2,1,0:T(8,128)(2,1)} %get-tuple-element.70), channel_id=1, source_target_pairs={{0,1},{1,0},{2,3},{3,2},{4,5},{5,4},{6,7},{7,6},{8,9},{9,8},{10,11... | collective-permute-start | bytes 2359304 | tf_op jit(solution)/shard_map/ppermute | solution.py:931
  499.5 25.5 %collective-permute-start.13 = (bf16[2,256,768]{2,1,0:T(8,128)(2,1)}, bf16[2,256,768]{2,1,0:T(8,128)(2,1)}, u32[]{:S(2)}, u32[]{:S(2)}) collective-permute-start(bf16[2,256,768]{2,1,0:T(8,128)(2,1)} %get-tuple-element.69), channel_id=1, source_target_pairs={{0,2},{1,3},{2,0},{3,1},{4,6},{5,7},{6,4},{7,5},{8,10},{9,11},{10,... | collective-permute-start | bytes 2359304 | tf_op jit(solution)/shard_map/ppermute | solution.py:931
  501.8 2.2 copy-start.11
  504.0 36.2 %collective-permute-start.14 = (bf16[2,256,768]{2,1,0:T(8,128)(2,1)S(1)}, bf16[2,256,768]{2,1,0:T(8,128)(2,1)S(1)}, u32[]{:S(2)}, u32[]{:S(2)}) collective-permute-start(bf16[2,256,768]{2,1,0:T(8,128)(2,1)S(1)} %copy-done.11), channel_id=1, source_target_pairs={{0,3},{1,2},{2,1},{3,0},{4,7},{5,6},{6,5},{7,4},{8,11},{9,10},{10,... | collective-permute-start | bytes 2359304 | tf_op jit(solution)/shard_map/ppermute | solution.py:931
  505.0 53.6 %collective-permute-start.10 = (bf16[2,256,768]{2,1,0:T(8,128)(2,1)S(1)}, bf16[2,256,768]{2,1,0:T(8,128)(2,1)S(1)}, u32[]{:S(2)}, u32[]{:S(2)}) collective-permute-start(bf16[2,256,768]{2,1,0:T(8,128)(2,1)S(1)} %get-tuple-element.73), channel_id=1, source_target_pairs={{0,2},{1,3},{2,0},{3,1},{4,6},{5,7},{6,4},{7,5},{8,10},{9,11},{10,... | collective-permute-start | bytes 2359304 | tf_op jit(solution)/shard_map/ppermute | solution.py:931
  506.7 73.6 %collective-permute-start.11 = (bf16[2,256,768]{2,1,0:T(8,128)(2,1)S(1)}, bf16[2,256,768]{2,1,0:T(8,128)(2,1)S(1)}, u32[]{:S(2)}, u32[]{:S(2)}) collective-permute-start(bf16[2,256,768]{2,1,0:T(8,128)(2,1)S(1)} %get-tuple-element.72), channel_id=1, source_target_pairs={{0,3},{1,2},{2,1},{3,0},{4,7},{5,6},{6,5},{7,4},{8,11},{9,10},{10,... | collective-permute-start | bytes 2359304 | tf_op jit(solution)/shard_map/ppermute | solution.py:931
  510.7 69.6 %collective-permute-start.9 = (bf16[2,256,768]{2,1,0:T(8,128)(2,1)S(1)}, bf16[2,256,768]{2,1,0:T(8,128)(2,1)S(1)}, u32[]{:S(2)}, u32[]{:S(2)}) collective-permute-start(bf16[2,256,768]{2,1,0:T(8,128)(2,1)S(1)} %get-tuple-element.74), channel_id=1, source_target_pairs={{0,1},{1,0},{2,3},{3,2},{4,5},{5,4},{6,7},{7,6},{8,9},{9,8},{10,11... | collective-permute-start | bytes 2359304 | tf_op jit(solution)/shard_map/ppermute | solution.py:931
  590.5 1.5 slice-start
  590.5 1.5 slice-start.1
  (3 other events, 1.7 us)
Sparse Core Ops, SparseCore 0:
  412.7 96.3 all-gather.3
  514.5 107.9 reduce-scatter.4
  628.0 105.9 reduce-scatter.8
  740.4 113.6 reduce-scatter.10
  859.6 111.9 reduce-scatter.6

commit v2 on v0

--- a/solution.py
+++ b/solution.py
@@ -1,8 +1,11 @@
+import functools
 from functools import partial
 
 import jax
 import jax.numpy as jnp
 from jax import lax
+from jax.experimental import pallas as pl
+from jax.experimental.pallas import tpu as pltpu
 from jax.sharding import PartitionSpec as P
 
 H = 12
@@ -88,7 +91,7 @@
     return jnp.einsum("ifd,ife->de", left, right, preferred_element_type=jnp.float32)
 
 
-def on_device(
+def frames_split(
     frames_in,
     cond,
     text,
@@ -319,6 +322,1103 @@
     )
 
 
+LOG2E = 1.4426950408889634
+BF = jnp.bfloat16
+F32 = jnp.float32
+PACK = 384
+LIMIT = 60 * 2**20
+
+
+def nn(left, right):
+    return jnp.dot(left, right, preferred_element_type=F32)
+
+
+def nt(left, right):
+    return lax.dot_general(left, right, (((1,), (1,)), ((), ())), preferred_element_type=F32)
+
+
+def tn(left, right):
+    return lax.dot_general(left, right, (((0,), (0,)), ((), ())), preferred_element_type=F32)
+
+
+def ln_parts(rows):
+    share = 1.0 / rows.shape[-1]
+    centered = rows - jnp.sum(rows, -1, keepdims=True) * share
+    inverse = lax.rsqrt(jnp.sum(centered * centered, -1, keepdims=True) * share + 1e-06)
+    return centered * inverse, inverse
+
+
+def ln_back(normed, inverse, incoming):
+    share = 1.0 / normed.shape[-1]
+    mean_in = jnp.sum(incoming, -1, keepdims=True) * share
+    mean_dot = jnp.sum(incoming * normed, -1, keepdims=True) * share
+    return inverse * (incoming - mean_in - normed * mean_dot)
+
+
+def gelu_parts(value):
+    size = jnp.abs(value)
+    inner = 1.0 / (1.0 + (0.3275911 * 0.7071067811865476) * size)
+    series = inner * (
+        0.5 * 0.254829592
+        + inner
+        * (
+            0.5 * -0.284496736
+            + inner * (0.5 * 1.421413741 + inner * (0.5 * -1.453152027 + inner * (0.5 * 1.061405429)))
+        )
+    )
+    bell = jnp.exp2(value * value * (-0.5 * LOG2E))
+    tail = series * bell
+    below = jnp.where(value >= 0.0, 1.0 - tail, tail)
+    return below, below + value * bell * 0.3989422804014327
+
+
+def lane_half(half):
+    lane = lax.broadcasted_iota(jnp.int32, (1, 128), 1)
+    return lane < 64 if half == 0 else lane >= 64
+
+
+def keep_half(rows, half):
+    return jnp.where(lane_half(half), rows, jnp.zeros_like(rows))
+
+
+def pack_square(acc, item, ra, cb, col):
+    first = acc[pl.ds(pl.multiple_of(item * ra, 16), ra // 2), col : col + cb]
+    second = acc[pl.ds(pl.multiple_of(item * ra + ra // 2, 16), ra // 2), col : col + cb]
+    return jnp.concatenate([first, second], 1).astype(BF)
+
+
+def store_block(value, frame, me, row, keep_ref, send_ref):
+    place = frame ^ me
+
+    @pl.when(place & 1 == 0)
+    def _():
+        keep_ref[0, place >> 1, row : row + value.shape[0]] = value
+
+    @pl.when(place & 1 == 1)
+    def _():
+        send_ref[0, place >> 1, row : row + value.shape[0]] = value
+
+
+def start_kernel(where, lengths, text_lengths, table, *, items, nf):
+    per = items // nf
+    me = where[0]
+    table[0] = me
+    table[1] = where[1]
+    at = 2 + 3 * per
+    for i in range(items):
+        rank = jnp.int32(0)
+        for j in range(items):
+            if j < i:
+                ahead = lengths[j] >= lengths[i]
+            elif j > i:
+                ahead = lengths[j] > lengths[i]
+            else:
+                continue
+            rank = rank + ahead.astype(jnp.int32)
+        turn, seat = rank // nf, rank % nf
+        device = jnp.where(turn % 2 == 0, seat, nf - 1 - seat)
+        table[at + i] = device
+        table[at + items + i] = turn
+        table[at + 2 * items + device * per + turn] = i
+    for slot in range(per):
+        item = table[at + 2 * items + me * per + slot]
+        table[2 + slot] = item
+        table[2 + per + slot] = lengths[item]
+        table[2 + 2 * per + slot] = text_lengths[item]
+
+
+def copy_kernel(table, *refs):
+    half = len(refs) // 2
+    for source, out in zip(refs[:half], refs[half:]):
+        out[...] = source[...].reshape(out.shape)
+
+
+def gate_kernel(*refs):
+    pass
+
+
+def text_kernel(table, rows_ref, w_ref, kv_ref):
+    parts = [rows_ref[at, 0] for at in range(rows_ref.shape[0])]
+    kv_ref[0] = nn(jnp.concatenate(parts, 0), w_ref[...]).astype(BF)
+
+
+def text_back_kernel(
+    table, d_ref, rows_ref, w_ref, ck_ref, cs_ref, out_ref, keep_ref, send_ref, acc, *, total, nf, ni
+):
+    step = pl.program_id(0)
+    width = rows_ref.shape[-1]
+    block = rows_ref.shape[2]
+
+    @pl.when(step == 0)
+    def _():
+        acc[...] = jnp.zeros_like(acc)
+
+    @pl.when(step < total)
+    def _():
+        low = d_ref[0].astype(BF)
+        rows = jnp.concatenate([rows_ref[at, 0] for at in range(nf)], 0)
+        acc[...] += tn(rows, low)
+        made = nt(low, w_ref[...]).astype(BF)
+        for frame in range(nf):
+            out_ref[frame, 0] = made[frame * block : (frame + 1) * block]
+
+    @pl.when(step >= total)
+    def _():
+        item = (step - total) ^ table[1]
+        ra, cb = width // ni, 2 * width // nf
+        skip = ck_ref.shape[2]
+        keep_ref[0, :, :skip] = ck_ref[0]
+        send_ref[0, :, :skip] = cs_ref[0]
+        for frame in range(nf):
+            part = acc[pl.ds(pl.multiple_of(item * ra, 16), ra), frame * cb : (frame + 1) * cb].astype(BF)
+            store_block(part, frame, table[0], skip, keep_ref, send_ref)
+
+
+def self_fwd_kernel(
+    table, x_ref, mod_ref, w_ref, *refs, blocks, qb, score_scale, length_at
+):
+    rows_ref, qkv_ref, att_ref, lse_ref, held = refs[-5:]
+    step = pl.program_id(0)
+    width = rows_ref.shape[-1]
+    count = att_ref.shape[1]
+    block = rows_ref.shape[1]
+    pairs = H // 2
+
+    @pl.when(step < blocks)
+    def _():
+        rows_ref[0] = x_ref[0]
+        normed, _ = ln_parts(x_ref[0].astype(F32))
+        hidden = (normed * (1.0 + mod_ref[0, 1:2]) + mod_ref[0, 0:1]).astype(BF)
+        at = pl.ds(pl.multiple_of(step * block, block), block)
+        for part in range(3):
+            made = nn(hidden, w_ref[:, part * width : (part + 1) * width])
+            if part == 0:
+                made = made * (score_scale * LOG2E)
+            made = made.astype(BF)
+            qkv_ref[0, :, part * width : (part + 1) * width] = made
+            for pair in range(pairs):
+                held[part * pairs + pair, at] = made[:, pair * 128 : pair * 128 + 128]
+
+    for klen in (count // 4, count // 2, count):
+
+        @pl.when((step >= blocks) & (table[length_at] == klen))
+        def _(klen=klen):
+            pair = step - blocks
+            keys = held[pairs + pair, :klen]
+            values = jnp.concatenate([held[2 * pairs + pair, :klen], jnp.ones((klen, 128), BF)], 1)
+
+            def inner(position, carry):
+                rows = pl.ds(pl.multiple_of(position * qb, qb), qb)
+                queries = held[pair, rows]
+                outs = []
+                for half in (0, 1):
+                    scores = nt(keep_half(queries, half), keys)
+                    top = jnp.max(scores, 1, keepdims=True)
+                    prob = jnp.exp2(scores - top).astype(BF)
+                    mixed = nn(prob, values)
+                    total = mixed[:, 128:]
+                    lse_ref[0, 0, half : half + 1, rows] = (top + jnp.log2(total[:, :1])).T
+                    outs.append(mixed[:, :128] / total)
+                att_ref[0, rows] = jnp.where(lane_half(0), outs[0], outs[1]).astype(BF)
+                return carry
+
+            lax.fori_loop(0, count // qb, inner, 0)
+
+
+def self_bwd_kernel(
+    table, q_ref, k_ref, v_ref, o_ref, do_ref, lse_ref, *refs, length_at, qb, score_scale
+):
+    dq_ref, dk_ref, dv_ref, dk_acc, dv_acc = refs[-5:]
+    count = q_ref.shape[1]
+    used = table[length_at]
+    for klen in (count // 4, count // 2, count):
+
+        @pl.when(used == klen)
+        def _(klen=klen):
+            keys = k_ref[0, :klen]
+            values = v_ref[0, :klen]
+            dk_acc[:klen] = jnp.zeros((klen, 128), F32)
+            dv_acc[:klen] = jnp.zeros((klen, 128), F32)
+
+            def step(position, carry):
+                rows = pl.ds(pl.multiple_of(position * qb, qb), qb)
+                queries = q_ref[0, rows]
+                grad = do_ref[0, rows]
+                dots = (grad.astype(F32) * o_ref[0, rows].astype(F32)).T
+                d_queries = []
+                for half in (0, 1):
+                    q_half = keep_half(queries, half)
+                    grad_half = keep_half(grad, half)
+                    delta = jnp.sum(dots[64 * half : 64 * half + 64], 0, keepdims=True)
+                    prob = jnp.exp2(nt(keys, q_half) - lse_ref[0, 0, half : half + 1, rows])
+                    d_scores = (prob * (nt(values, grad_half) - delta)).astype(BF)
+                    dv_acc[:klen] += nn(prob.astype(BF), grad_half)
+                    dk_acc[:klen] += nn(d_scores, q_half)
+                    d_queries.append(tn(d_scores, keys))
+                dq_ref[0, rows] = (
+                    jnp.where(lane_half(0), d_queries[0], d_queries[1]) * score_scale
+                ).astype(BF)
+                return carry
+
+            lax.fori_loop(0, count // qb, step, 0)
+            dk_ref[0, :klen] = (dk_acc[:klen] * (1.0 / LOG2E)).astype(BF)
+            dv_ref[0, :klen] = dv_acc[:klen].astype(BF)
+            if klen < count:
+                dk_ref[0, klen:] = jnp.zeros((count - klen, 128), BF)
+                dv_ref[0, klen:] = jnp.zeros((count - klen, 128), BF)
+
+
+def cross_kernel(
+    table, att_ref, x_ref, mod_ref, kv_ref, wo_ref, wq_ref, wco_ref,
+    first_ref, second_ref, ba_ref, bb_ref, cq_ref, cr_ref, lse_ref, *, score_scale, length_at,
+):
+    width = x_ref.shape[-1]
+    slots = kv_ref.shape[1]
+    used = table[length_at + pl.program_id(0)]
+    branch_a = nn(att_ref[0], wo_ref[...])
+    ba_ref[0] = branch_a.astype(BF)
+    first = x_ref[0].astype(F32) + mod_ref[0, 2:3] * branch_a
+    first_ref[0] = first
+    normed, _ = ln_parts(first)
+    hidden = (normed * (1.0 + mod_ref[0, 4:5]) + mod_ref[0, 3:4]).astype(BF)
+    cq_ref[0] = (nn(hidden, wq_ref[...]) * (score_scale * LOG2E)).astype(BF)
+    valid = lax.broadcasted_iota(jnp.int32, (1, slots), 1) < used
+    ones = jnp.ones((slots, 128), BF)
+    for pair in range(H // 2):
+        cols = slice(pair * 128, pair * 128 + 128)
+        queries = cq_ref[0, :, cols]
+        keys = kv_ref[0, :, cols]
+        values = jnp.concatenate([kv_ref[0, :, width + pair * 128 : width + pair * 128 + 128], ones], 1)
+        outs = []
+        for half in (0, 1):
+            scores = jnp.where(valid, nt(keep_half(queries, half), keys), -1e30)
+            top = jnp.max(scores, 1, keepdims=True)
+            prob = jnp.exp2(scores - top).astype(BF)
+            mixed = nn(prob, values)
+            total = mixed[:, 128:]
+            lse_ref[0, pair, half : half + 1] = (top + jnp.log2(total[:, :1])).T
+            outs.append(mixed[:, :128] / total)
+        cr_ref[0, :, cols] = jnp.where(lane_half(0), outs[0], outs[1]).astype(BF)
+    branch_b = nn(cr_ref[0], wco_ref[...])
+    bb_ref[0] = branch_b.astype(BF)
+    second_ref[0] = first + mod_ref[0, 5:6] * branch_b
+
+
+def mlp_kernel(
+    table, second_ref, cot_ref, mod_ref, wup_ref, wdn_ref,
+    out_ref, g2_ref, dmod_ref, gw_ref, up_acc, dn_acc, *, blocks, total, chunk, nf, ni,
+):
+    step = pl.program_id(0)
+    width = second_ref.shape[-1]
+    ff = wup_ref.shape[-1]
+
+    @pl.when(step == 0)
+    def _():
+        up_acc[...] = jnp.zeros_like(up_acc)
+        dn_acc[...] = jnp.zeros_like(dn_acc)
+
+    @pl.when(step < total)
+    def _():
+        shift, scale, gate = mod_ref[0, 6:7], mod_ref[0, 7:8], mod_ref[0, 8:9]
+        second = second_ref[0]
+        normed, inverse = ln_parts(second)
+        hidden = (normed * (1.0 + scale) + shift).astype(BF)
+        upstream = cot_ref[0, 0].astype(F32)
+        d_branch = (upstream * gate).astype(BF)
+        branch = jnp.zeros(second.shape, F32)
+        d_hidden = jnp.zeros(second.shape, F32)
+        for at in range(0, ff, chunk):
+            cols = slice(at, at + chunk)
+            up_proj = nn(hidden, wup_ref[:, cols])
+            below, slope = gelu_parts(up_proj)
+            act = (up_proj * below).astype(BF)
+            branch += nn(act, wdn_ref[cols])
+            d_up = (nt(d_branch, wdn_ref[cols]) * slope).astype(BF)
+            d_hidden += nt(d_up, wup_ref[:, cols])
+            dn_acc[cols] += tn(act, d_branch)
+            up_acc[:, cols] += tn(hidden, d_up)
+        out_ref[0, 0] = (second + gate * branch).astype(BF)
+        g2_ref[0] = upstream + ln_back(normed, inverse, d_hidden * (1.0 + scale))
+
+        @pl.when(step % blocks == 0)
+        def _():
+            dmod_ref[...] = jnp.zeros_like(dmod_ref)
+
+        dmod_ref[0, 0:1] += jnp.sum(d_hidden, 0, keepdims=True)
+        dmod_ref[0, 1:2] += jnp.sum(d_hidden * normed, 0, keepdims=True)
+        dmod_ref[0, 2:3] += jnp.sum(upstream * branch, 0, keepdims=True)
+
+    @pl.when(step >= total)
+    def _():
+        item = step - total
+        ra, cb = width // ni, ff // nf
+        for frame in range(nf):
+            part = up_acc[pl.ds(pl.multiple_of(item * ra, 16), ra), frame * cb : (frame + 1) * cb].astype(BF)
+            gw_ref[0, frame, :ra] = part[:, :PACK]
+            gw_ref[0, frame, ra : 2 * ra] = part[:, PACK:]
+            gw_ref[0, frame, 2 * ra :] = pack_square(dn_acc, item, ff // ni, width // nf, frame * (width // nf))
+
+
+def cross_att_back_kernel(
+    table, g2_ref, bb_ref, cr_ref, cq_ref, mod_ref, kv_ref, lse_ref, wco_ref,
+    dcq_ref, dtext_ref, dmod_ref, keep_ref, send_ref, co_acc, *, blocks, total, score_scale, nf, ni, length_at,
+):
+    step = pl.program_id(0)
+    width = g2_ref.shape[-1]
+    slots = kv_ref.shape[1]
+
+    @pl.when(step == 0)
+    def _():
+        co_acc[...] = jnp.zeros_like(co_acc)
+
+    @pl.when(step < total)
+    def _():
+        @pl.when(step % blocks == 0)
+        def _():
+            dmod_ref[...] = jnp.zeros_like(dmod_ref)
+            dtext_ref[...] = jnp.zeros_like(dtext_ref)
+
+        used = table[length_at + step // blocks]
+        upstream = g2_ref[0]
+        dmod_ref[0] += jnp.sum(upstream * bb_ref[0].astype(F32), 0, keepdims=True)
+        d_branch_b = (upstream * mod_ref[0, 5:6]).astype(BF)
+        co_acc[...] += tn(cr_ref[0], d_branch_b)
+        d_crossed = nt(d_branch_b, wco_ref[...])
+        valid = lax.broadcasted_iota(jnp.int32, (slots, 1), 0) < used
+        for pair in range(H // 2):
+            cols = slice(pair * 128, pair * 128 + 128)
+            vcols = slice(width + pair * 128, width + pair * 128 + 128)
+            queries = cq_ref[0, :, cols]
+            keys = kv_ref[0, :, cols]
+            values = kv_ref[0, :, vcols]
+            grad = d_crossed[:, cols].astype(BF)
+            dots = (grad.astype(F32) * cr_ref[0, :, cols].astype(F32)).T
+            d_queries = []
+            d_keys = 0.0
+            d_values = 0.0
+            for half in (0, 1):
+                q_half = keep_half(queries, half)
+                grad_half = keep_half(grad, half)
+                delta = jnp.sum(dots[64 * half : 64 * half + 64], 0, keepdims=True)
+                scores = jnp.where(valid, nt(keys, q_half), -1e30)
+                prob = jnp.exp2(scores - lse_ref[0, pair, half : half + 1])
+                d_scores = (prob * (nt(values, grad_half) - delta)).astype(BF)
+                d_values += nn(prob.astype(BF), grad_half)
+                d_keys += nn(d_scores, q_half)
+                d_queries.append(tn(d_scores, keys))
+            dtext_ref[0, :, cols] += d_keys * (1.0 / LOG2E)
+            dtext_ref[0, :, vcols] += d_values
+            dcq_ref[0, :, cols] = (
+                jnp.where(lane_half(0), d_queries[0], d_queries[1]) * score_scale
+            ).astype(BF)
+
+    @pl.when(step >= total)
+    def _():
+        item = (step - total) ^ table[1]
+        for frame in range(nf):
+            part = pack_square(co_acc, item, width // ni, width // nf, frame * (width // nf))
+            store_block(part, frame, table[0], 0, keep_ref, send_ref)
+
+
+def cross_in_back_kernel(
+    table, g2_ref, dcq_ref, ba_ref, att_ref, first_ref, mod_ref, wo_ref, wq_ref, ek_ref, es_ref,
+    g1_ref, datt_ref, dmod_ref, keep_ref, send_ref, o_acc, q_acc, *, blocks, total, nf, ni,
+):
+    step = pl.program_id(0)
+    width = g2_ref.shape[-1]
+
+    @pl.when(step == 0)
+    def _():
+        o_acc[...] = jnp.zeros_like(o_acc)
+        q_acc[...] = jnp.zeros_like(q_acc)
+
+    @pl.when(step < total)
+    def _():
+        @pl.when(step % blocks == 0)
+        def _():
+            dmod_ref[...] = jnp.zeros_like(dmod_ref)
+
+        d_cq = dcq_ref[0]
+        normed, inverse = ln_parts(first_ref[0])
+        shift, scale = mod_ref[0, 3:4], mod_ref[0, 4:5]
+        hidden = (normed * (1.0 + scale) + shift).astype(BF)
+        q_acc[...] += tn(hidden, d_cq)
+        d_hidden = nt(d_cq, wq_ref[...])
+        dmod_ref[0, 1:2] += jnp.sum(d_hidden, 0, keepdims=True)
+        dmod_ref[0, 2:3] += jnp.sum(d_hidden * normed, 0, keepdims=True)
+        upstream = g2_ref[0] + ln_back(normed, inverse, d_hidden * (1.0 + scale))
+        g1_ref[0] = upstream
+        dmod_ref[0, 0:1] += jnp.sum(upstream * ba_ref[0].astype(F32), 0, keepdims=True)
+        d_branch_a = (upstream * mod_ref[0, 2:3]).astype(BF)
+        o_acc[...] += tn(att_ref[0], d_branch_a)
+        datt_ref[0] = nt(d_branch_a, wo_ref[...]).astype(BF)
+
+    @pl.when(step >= total)
+    def _():
+        item = (step - total) ^ table[1]
+        ra, cb = width // ni, width // nf
+        skip = ek_ref.shape[2]
+        keep_ref[0, :, :skip] = ek_ref[0]
+        send_ref[0, :, :skip] = es_ref[0]
+        for frame in range(nf):
+            for place, acc in enumerate((o_acc, q_acc)):
+                part = pack_square(acc, item, ra, cb, frame * cb)
+                store_block(part, frame, table[0], skip + place * (ra // 2), keep_ref, send_ref)
+
+
+def qkv_weight_kernel(table, dq_ref, dk_ref, dv_ref, x_ref, mod_ref, keep_ref, send_ref, acc, *, total, nf, ni):
+    step = pl.program_id(0)
+    width = x_ref.shape[-1]
+
+    @pl.when(step == 0)
+    def _():
+        acc[...] = jnp.zeros_like(acc)
+
+    @pl.when(step < total)
+    def _():
+        normed, _ = ln_parts(x_ref[0].astype(F32))
+        hidden = (normed * (1.0 + mod_ref[0, 1:2]) + mod_ref[0, 0:1]).astype(BF)
+        for place, ref in enumerate((dq_ref, dk_ref, dv_ref)):
+            acc[:, place * width : (place + 1) * width] += tn(hidden, ref[0])
+
+    @pl.when(step >= total)
+    def _():
+        item = (step - total) ^ table[1]
+        ra, cb = width // ni, 3 * width // nf
+        for frame in range(nf):
+            part = acc[pl.ds(pl.multiple_of(item * ra, 16), ra), frame * cb : (frame + 1) * cb].astype(BF)
+            rest = jnp.concatenate([part[: ra // 2, PACK:], part[ra // 2 :, PACK:]], 1)
+            store_block(jnp.concatenate([part[:, :PACK], rest], 0), frame, table[0], 0, keep_ref, send_ref)
+
+
+def qkv_in_back_kernel(
+    table, dq_ref, dk_ref, dv_ref, x_ref, g1_ref, mod_ref, w_ref, out_ref, dmod_ref
+):
+    step = pl.program_id(0)
+    width = x_ref.shape[-1]
+
+    @pl.when(step == 0)
+    def _():
+        dmod_ref[...] = jnp.zeros_like(dmod_ref)
+
+    normed, inverse = ln_parts(x_ref[0].astype(F32))
+    d_hidden = jnp.zeros(normed.shape, F32)
+    for place, ref in enumerate((dq_ref, dk_ref, dv_ref)):
+        d_hidden += nt(ref[0], w_ref[:, place * width : (place + 1) * width])
+    dmod_ref[0, 0:1] += jnp.sum(d_hidden, 0, keepdims=True)
+    dmod_ref[0, 1:2] += jnp.sum(d_hidden * normed, 0, keepdims=True)
+    out_ref[0] = (g1_ref[0] + ln_back(normed, inverse, d_hidden * (1.0 + mod_ref[0, 1:2]))).astype(BF)
+
+
+def deal_kernel(table, *refs, at):
+    out_ref = refs[-1]
+    sources = refs[:-1]
+    if len(sources) == 1:
+        out_ref[0] = sources[0][0, 0].astype(out_ref.dtype)
+        return
+    slot_of = table[at + pl.num_programs(0) + pl.program_id(0)]
+    for slot, ref in enumerate(sources):
+
+        @pl.when(slot_of == slot)
+        def _(ref=ref):
+            out_ref[0] = ref[0, 0].astype(out_ref.dtype)
+
+
+def cost(flops, moved, exps=0):
+    return pl.CostEstimate(flops=int(flops), bytes_accessed=int(moved), transcendentals=int(exps))
+
+
+def params():
+    return pltpu.CompilerParams(vmem_limit_bytes=LIMIT)
+
+
+def whole(shape):
+    return pl.BlockSpec(shape, lambda *_: (0,) * len(shape), pipeline_mode=pl.Buffered(1))
+
+
+def run(kernel, name, grid, in_specs, args, out_specs, out_shape, scratch=(), deps=(), work=None, aliases=None):
+    inputs = len(args)
+
+    def body(*refs):
+        kernel(*refs[:inputs], *refs[inputs + len(deps) :])
+
+    return pl.pallas_call(
+        body,
+        grid_spec=pltpu.PrefetchScalarGridSpec(
+            num_scalar_prefetch=1,
+            grid=grid,
+            in_specs=list(in_specs) + [pl.BlockSpec(memory_space=pl.ANY)] * len(deps),
+            out_specs=out_specs,
+            scratch_shapes=list(scratch),
+        ),
+        out_shape=out_shape,
+        input_output_aliases=aliases or {},
+        compiler_params=params(),
+        cost_estimate=work,
+        name=name,
+    )(*args, *deps)
+
+
+def any_spec(count):
+    return [pl.BlockSpec(memory_space=pl.ANY)] * count
+
+
+def struct(shape, dtype):
+    return jax.ShapeDtypeStruct(shape, dtype)
+
+
+def start_call(where, lengths, text_lengths, items, nf):
+    size = 2 + 3 * (items // nf) + 3 * items
+    smem = pl.BlockSpec(memory_space=pltpu.SMEM)
+    return pl.pallas_call(
+        partial(start_kernel, items=items, nf=nf),
+        in_specs=[smem] * 3,
+        out_specs=smem,
+        out_shape=struct((size,), jnp.int32),
+        name="start",
+    )(where, lengths, text_lengths)
+
+
+def gather_first_call(table, rows, nf):
+    items, block, width = rows.shape
+    per = items // nf
+    at = 2 + 3 * per + 2 * items
+    return run(
+        copy_kernel,
+        "gather_first",
+        (nf,),
+        [pl.BlockSpec((1, block, width), lambda t, s: (s[at + t * per], 0, 0))],
+        (table, rows),
+        [pl.BlockSpec((1, block, width), lambda t, s: (t, 0, 0))],
+        [struct((nf, block, width), BF)],
+    )[0]
+
+
+def gather_call(table, rows, text, cot, nf):
+    items, block, width = rows.shape
+    per = items // nf
+    at = 2 + 3 * per + 2 * items
+    short = text.shape[1]
+
+    def source(size):
+        return pl.BlockSpec((1, size, width), lambda t, s: (s[at + t], 0, 0))
+
+    def out(size):
+        return pl.BlockSpec((1, 1, size, width), lambda t, s: (t // per, t % per, 0, 0))
+
+    return run(
+        copy_kernel,
+        "gather",
+        (items,),
+        [source(block), source(short), source(block)],
+        (table, rows, text, cot),
+        [
+            pl.BlockSpec((1, 1, block, width), lambda t, s: (jnp.maximum(t % per - 1, 0), t // per, 0, 0)),
+            out(short),
+            out(block),
+        ],
+        [
+            struct((per - 1, nf, block, width), BF),
+            struct((nf, per, short, width), BF),
+            struct((nf, per, block, width), BF),
+        ],
+    )
+
+
+def gate_call(arrays, deps):
+    return pl.pallas_call(
+        gate_kernel,
+        in_specs=any_spec(len(arrays) + len(deps)),
+        out_specs=any_spec(len(arrays)),
+        out_shape=[struct(array.shape, array.dtype) for array in arrays],
+        input_output_aliases={at: at for at in range(len(arrays))},
+        compiler_params=params(),
+        name="gate",
+    )(*arrays, *deps)
+
+
+def text_call(table, text, weight):
+    nf, per, block, width = text.shape
+    slots = nf * block
+    return run(
+        text_kernel,
+        "text_fwd",
+        (per,),
+        [pl.BlockSpec((nf, 1, block, width), lambda i, s: (0, i, 0, 0)), whole(weight.shape)],
+        (table, text, weight),
+        pl.BlockSpec((1, slots, 2 * width), lambda i, s: (i, 0, 0)),
+        struct((per, slots, 2 * width), BF),
+        work=cost(4 * per * slots * width * width, 0),
+    )
+
+
+def halves(ni, nf, depth, total):
+    spec = pl.BlockSpec((1, nf // 2, depth, PACK), lambda t, s: (jnp.maximum(t - total, 0), 0, 0, 0))
+    return [spec] * 2, [struct((ni, nf // 2, depth, PACK), BF)] * 2
+
+
+def text_back_call(table, d_text, text, weight, co, ni, deps):
+    nf, per, block, width = text.shape
+    slots = nf * block
+    skip = co[0].shape[2]
+    specs, shapes = halves(ni, nf, skip + 2 * width * width // (nf * ni * PACK), per)
+
+    def at(t, s):
+        return (jnp.minimum(t, per - 1), 0, 0)
+
+    by_slot = pl.BlockSpec((nf, 1, block, width), lambda t, s: (0, jnp.minimum(t, per - 1), 0, 0))
+    into = pl.BlockSpec((1, nf // 2, skip, PACK), lambda t, s: (jnp.maximum(t - per, 0), 0, 0, 0))
+    return run(
+        partial(text_back_kernel, total=per, nf=nf, ni=ni),
+        "text_bwd",
+        (per + ni,),
+        [pl.BlockSpec((1, slots, 2 * width), at), by_slot, whole(weight.shape), into, into],
+        (table, d_text, text, weight, *co),
+        [by_slot] + specs,
+        [struct(text.shape, BF)] + shapes,
+        scratch=[pltpu.VMEM((width, 2 * width), F32)],
+        deps=deps,
+        work=cost(8 * per * slots * width * width, 0),
+    )
+
+
+def self_fwd_call(table, slot, rows, mod, weight, kept, per, qb, score_scale, deps):
+    blocks, block, width = rows.shape
+    count = blocks * block
+    pairs = H // 2
+
+    def early(t):
+        return jnp.minimum(t, blocks - 1)
+
+    def late(t):
+        return jnp.maximum(t - blocks, 0)
+
+    return run(
+        partial(self_fwd_kernel, blocks=blocks, qb=qb, score_scale=score_scale, length_at=2 + per + slot),
+        "self_fwd",
+        (blocks + pairs,),
+        [pl.BlockSpec((1, block, width), lambda t, s: (early(t), 0, 0))]
+        + [pl.BlockSpec((1, 9, width), lambda t, s: (slot, 0, 0)), whole(weight.shape)]
+        + any_spec(len(kept)),
+        (table, rows, mod, weight, *kept),
+        [
+            pl.BlockSpec((1, block, width), lambda t, s: (slot, early(t), 0)),
+            pl.BlockSpec((1, block, 3 * width), lambda t, s: (slot, early(t), 0)),
+            pl.BlockSpec((1, count, 128), lambda t, s: (slot, 0, late(t))),
+            pl.BlockSpec((1, 1, 2, count), lambda t, s: (slot, late(t), 0, 0)),
+        ],
+        [
+            struct((per, count, width), BF),
+            struct((per, count, 3 * width), BF),
+            struct((per, count, width), BF),
+            struct((per, pairs, 2, count), F32),
+        ],
+        scratch=[pltpu.VMEM((3 * pairs, count, 128), BF)],
+        deps=deps,
+        work=cost(6 * count * width * width + 16 * count * count * width, count * width * 16, H * count * count),
+        aliases={4 + at: at for at in range(len(kept))},
+    )
+
+
+def self_bwd_call(table, slot, qkv, att, d_att, lse, kept, qb, score_scale, deps):
+    per, count, width = att.shape
+    pairs = H // 2
+    block = pl.BlockSpec((1, count, 128), lambda h, s: (slot, 0, h))
+    return run(
+        partial(self_bwd_kernel, length_at=2 + per + slot, qb=qb, score_scale=score_scale),
+        "self_bwd",
+        (pairs,),
+        [pl.BlockSpec((1, count, 128), lambda h, s, part=part: (slot, 0, part * pairs + h)) for part in range(3)]
+        + [block, block, pl.BlockSpec((1, 1, 2, count), lambda h, s: (slot, h, 0, 0))]
+        + any_spec(len(kept)),
+        (table, qkv, qkv, qkv, att, d_att, lse, *kept),
+        [block] * 3,
+        [struct((per, count, width), BF)] * 3,
+        scratch=[pltpu.VMEM((count, 128), F32)] * 2,
+        deps=deps,
+        work=cost(40 * count * count * width, count * width * 16, H * count * count),
+        aliases={7 + at: at for at in range(len(kept))},
+    )
+
+
+def cross_call(table, att, rows, mod, kv, wo, wq, wco, score_scale, block, deps):
+    items, count, width = rows.shape
+    slots = kv.shape[1]
+    row = pl.BlockSpec((1, block, width), lambda i, j, s: (i, j, 0))
+    return run(
+        partial(cross_kernel, score_scale=score_scale, length_at=2 + 2 * items),
+        "cross_fwd",
+        (items, count // block),
+        [
+            row,
+            row,
+            pl.BlockSpec((1, 9, width), lambda i, j, s: (i, 0, 0)),
+            pl.BlockSpec((1, slots, 2 * width), lambda i, j, s: (i, 0, 0)),
+            whole(wo.shape),
+            whole(wq.shape),
+            whole(wco.shape),
+        ],
+        (table, att, rows, mod, kv, wo, wq, wco),
+        [row] * 6 + [pl.BlockSpec((1, H // 2, 2, block), lambda i, j, s: (i, 0, 0, j))],
+        [struct(rows.shape, F32)] * 2 + [struct(rows.shape, BF)] * 4 + [struct((items, H // 2, 2, count), F32)],
+        deps=deps,
+        work=cost(
+            items * count * (6 * width * width + 16 * slots * width), items * count * width * 20, items * H * count * slots
+        ),
+    )
+
+
+def back_grid(items, count, block):
+    blocks = count // block
+    total = items * blocks
+
+    def at(t):
+        return jnp.minimum(t, total - 1)
+
+    def by_item(t, s):
+        return (at(t) // blocks, 0, 0)
+
+    def by_row(t, s):
+        return (at(t) // blocks, at(t) % blocks, 0)
+
+    return blocks, total, by_item, by_row
+
+
+def mlp_call(table, second, cot, mod, wup, wdn, block, chunk, nf, ni, deps):
+    items, count, width = second.shape
+    ff = wup.shape[1]
+    blocks, total, by_item, by_row = back_grid(items, count, block)
+    row = pl.BlockSpec((1, block, width), by_row)
+    shard = pl.BlockSpec((1, 1, block, width), lambda t, s: (by_row(t, s)[1], by_row(t, s)[0], 0, 0))
+    depth = 2 * width * ff // (nf * ni * PACK)
+    return run(
+        partial(mlp_kernel, blocks=blocks, total=total, chunk=chunk, nf=nf, ni=ni),
+        "mlp",
+        (total + ni,),
+        [row, shard, pl.BlockSpec((1, 9, width), by_item), whole(wup.shape), whole(wdn.shape)],
+        (table, second, cot, mod, wup, wdn),
+        [shard, row, pl.BlockSpec((1, 3, width), by_item)]
+        + [pl.BlockSpec((1, nf, depth, PACK), lambda t, s: (jnp.maximum(t - total, 0), 0, 0, 0))],
+        [struct(cot.shape, BF), struct(second.shape, F32), struct((items, 3, width), F32)]
+        + [struct((ni, nf, depth, PACK), BF)],
+        scratch=[pltpu.VMEM((width, ff), F32), pltpu.VMEM((ff, width), F32)],
+        deps=deps,
+        work=cost(12 * items * count * width * ff, items * count * width * 16, items * count * ff * 2),
+    )
+
+
+def cross_att_back_call(table, g2, bb, cr, cq, mod, kv, lse, wco, score_scale, block, nf, ni, deps):
+    items, count, width = g2.shape
+    slots = kv.shape[1]
+    blocks, total, by_item, by_row = back_grid(items, count, block)
+    row = pl.BlockSpec((1, block, width), by_row)
+    specs, shapes = halves(ni, nf, width * width // (nf * ni * PACK), total)
+    lse_spec = pl.BlockSpec((1, H // 2, 2, block), lambda t, s: (by_row(t, s)[0], 0, 0, by_row(t, s)[1]))
+    return run(
+        partial(
+            cross_att_back_kernel,
+            blocks=blocks,
+            total=total,
+            score_scale=score_scale,
+            nf=nf,
+            ni=ni,
+            length_at=2 + 2 * items,
+        ),
+        "cross_att_bwd",
+        (total + ni,),
+        [row] * 4
+        + [pl.BlockSpec((1, 9, width), by_item), pl.BlockSpec((1, slots, 2 * width), by_item), lse_spec, whole(wco.shape)],
+        (table, g2, bb, cr, cq, mod, kv, lse, wco),
+        [row, pl.BlockSpec((1, slots, 2 * width), by_item), pl.BlockSpec((1, 1, width), by_item)] + specs,
+        [struct(g2.shape, BF), struct(kv.shape, F32), struct((items, 1, width), F32)] + shapes,
+        scratch=[pltpu.VMEM((width, width), F32)],
+        deps=deps,
+        work=cost(
+            items * count * (4 * width * width + 40 * slots * width), items * count * width * 16, items * H * count * slots
+        ),
+    )
+
+
+def cross_in_back_call(table, g2, dcq, ba, att, first, mod, wo, wq, earlier, block, nf, ni, deps):
+    items, count, width = g2.shape
+    blocks, total, by_item, by_row = back_grid(items, count, block)
+    row = pl.BlockSpec((1, block, width), by_row)
+    skip = earlier[0].shape[2]
+    into = pl.BlockSpec((1, nf // 2, skip, PACK), lambda t, s: (jnp.maximum(t - total, 0), 0, 0, 0))
+    specs, shapes = halves(ni, nf, skip + 2 * width * width // (nf * ni * PACK), total)
+    return run(
+        partial(cross_in_back_kernel, blocks=blocks, total=total, nf=nf, ni=ni),
+        "cross_in_bwd",
+        (total + ni,),
+        [row] * 5 + [pl.BlockSpec((1, 9, width), by_item), whole(wo.shape), whole(wq.shape), into, into],
+        (table, g2, dcq, ba, att, first, mod, wo, wq, *earlier),
+        [row, row, pl.BlockSpec((1, 3, width), by_item)] + specs,
+        [struct(g2.shape, F32), struct(g2.shape, BF), struct((items, 3, width), F32)] + shapes,
+        scratch=[pltpu.VMEM((width, width), F32)] * 2,
+        deps=deps,
+        work=cost(items * count * 8 * width * width, items * count * width * 20),
+    )
+
+
+def qkv_weight_call(table, dq, dk, dv, rows, mod, block, nf, ni, deps):
+    items, count, width = rows.shape
+    blocks, total, by_item, by_row = back_grid(items, count, block)
+    row = pl.BlockSpec((1, block, width), by_row)
+    specs, shapes = halves(ni, nf, 3 * width * width // (nf * ni * PACK), total)
+    return run(
+        partial(qkv_weight_kernel, total=total, nf=nf, ni=ni),
+        "qkv_weight_bwd",
+        (total + ni,),
+        [row] * 4 + [pl.BlockSpec((1, 9, width), by_item)],
+        (table, dq, dk, dv, rows, mod),
+        specs,
+        shapes,
+        scratch=[pltpu.VMEM((width, 3 * width), F32)],
+        deps=deps,
+        work=cost(6 * items * count * width * width, items * count * width * 8),
+    )
+
+
+def qkv_in_back_call(table, slot, dq, dk, dv, rows, g1, mod, weight, block, deps):
+    _, count, width = rows.shape
+    row = pl.BlockSpec((1, block, width), lambda t, s: (slot, t, 0))
+    return run(
+        qkv_in_back_kernel,
+        "qkv_in_bwd",
+        (count // block,),
+        [row] * 5 + [pl.BlockSpec((1, 9, width), lambda t, s: (slot, 0, 0)), whole(weight.shape)],
+        (table, dq, dk, dv, rows, g1, mod, weight),
+        [pl.BlockSpec((1, block, width), lambda t, s: (t, 0, 0)), pl.BlockSpec((1, 2, width), lambda t, s: (0, 0, 0))],
+        [struct((count // block, block, width), BF), struct((1, 2, width), F32)],
+        deps=deps,
+        work=cost(6 * count * width * width, count * width * 16),
+    )
+
+
+def deal_call(table, got, per, dtype, name):
+    nf, _, block, width = got[0].shape
+    items = nf * per
+    at = 2 + 3 * per
+    if len(got) == 1:
+        specs = [pl.BlockSpec((1, 1, block, width), lambda t, s: (s[at + t], s[at + items + t], 0, 0))]
+    else:
+        specs = [pl.BlockSpec((1, 1, block, width), lambda t, s: (s[at + t], 0, 0, 0))] * len(got)
+    return run(
+        partial(deal_kernel, at=at),
+        name,
+        (items,),
+        specs,
+        (table, *got),
+        pl.BlockSpec((1, block, width), lambda t, s: (t, 0, 0)),
+        struct((items, block, width), dtype),
+        work=cost(0, items * block * width * 6),
+    )
+
+
+def exchange(blocks):
+    return lax.all_to_all(blocks, "frames", 0, 0, tiled=True)
+
+
+def swap(block, offset, nf):
+    if offset == 0:
+        return block
+    return lax.ppermute(block, "frames", [(i, i ^ offset) for i in range(nf)])
+
+
+def bits_of(count):
+    return count.bit_length() - 1
+
+
+class Sum:
+    def __init__(self, keep, send, order, sizes):
+        self.sizes = sizes
+        ni, nf = sizes["items"], sizes["frames"]
+        self.dims = [("items", bit) for bit in reversed(range(bits_of(ni)))]
+        self.dims += [("frames", bit) for bit in reversed(range(1, bits_of(nf)))]
+        shape = (2,) * len(self.dims) + keep.shape[2:]
+        self.keep, self.send = keep.reshape(shape), send
+        self.shape = shape
+        self.steps = [("frames", 0)] + list(order)
+        self.got = None
+
+    def launch(self):
+        name, bit = self.steps.pop(0)
+        self.got = lax.ppermute(self.send, name, [(i, i ^ (1 << bit)) for i in range(self.sizes[name])])
+
+    def land(self):
+        got = self.got.reshape(self.keep.shape)
+        if not self.steps:
+            return self.keep.astype(F32) + got.astype(F32)
+        dim = self.dims.index(self.steps[0])
+        self.dims.remove(self.steps[0])
+        cut = [
+            (lax.index_in_dim(self.keep, half, dim, False).astype(F32) + lax.index_in_dim(got, half, dim, False).astype(F32))
+            for half in (0, 1)
+        ]
+        self.keep, self.send = cut[0].astype(BF), cut[1].astype(BF)
+        return None
+
+
+def collect_items(rows, ni):
+    for bit in range(bits_of(ni)):
+        rows = jnp.concatenate([rows, lax.ppermute(rows, "items", [(i, i ^ (1 << bit)) for i in range(ni)])], 0)
+    return rows
+
+
+def wide(block, parts):
+    rows = block.shape[0] // parts
+    return jnp.concatenate([block[p * rows : (p + 1) * rows] for p in range(parts)], 1)
+
+
+def tall(block):
+    half = block.shape[1] // 2
+    return jnp.concatenate([block[:, :half], block[:, half:]], 0)
+
+
+def items_whole(
+    ni, nf, frames_in, cond, text, item_lengths, text_lengths, ada_weight, qkv_weight, out_weight,
+    cross_q_weight, cross_kv_weight, cross_out_weight, up_weight, down_weight, cotangent,
+):
+    items, block, width = frames_in.shape
+    per = items // nf
+    sizes = {"items": ni, "frames": nf}
+    score_scale = (width // H) ** (-0.5)
+    me = lax.axis_index("frames")
+    row_item = lax.axis_index("items")
+    x_first = [("items", bit) for bit in range(bits_of(ni))] + [("frames", bit) for bit in range(1, bits_of(nf))]
+    z_first = x_first[1:2] + x_first[:1] + x_first[2:]
+
+    table = start_call(jnp.stack([me, row_item]), item_lengths, text_lengths, items, nf)
+    got = [exchange(gather_first_call(table, frames_in, nf))]
+    row_sends, text_send, cot_send = gather_call(table, frames_in, text, cotangent, nf)
+
+    cond_f = cond.astype(F32)
+    low_cond = jax.nn.silu(cond_f).astype(BF)
+    modulation = nn(low_cond, ada_weight)
+    pick = table[2 : 2 + per, None] == jnp.arange(items, dtype=jnp.int32)[None, :]
+    mod = jnp.sum(jnp.where(pick[:, :, None], modulation[None], 0.0), 1).reshape(per, 9, width)
+
+    *sends, text_send = gate_call([row_sends[slot] for slot in range(per - 1)] + [text_send], got)
+    got += [exchange(send) for send in sends]
+    text_rows = exchange(text_send)
+
+    kept = self_fwd_call(table, 0, got[0], mod, qkv_weight, (), per, 512, score_scale, sends + [text_send])
+    (cot_send,) = gate_call([cot_send], got[1:] + [text_rows])
+    cot = exchange(cot_send)
+    for slot in range(1, per):
+        kept = self_fwd_call(table, slot, got[slot], mod, qkv_weight, kept, per, 512, score_scale, [cot_send])
+    rows, qkv, attended, self_lse = kept
+    text_kv = text_call(table, text_rows, cross_kv_weight)
+    first, second, branch_a, branch_b, cross_q, crossed, cross_lse = cross_call(
+        table, attended, rows, mod, text_kv, out_weight, cross_q_weight, cross_out_weight, score_scale, block, []
+    )
+    layer_send, g2, dmod_c, g_mlp = mlp_call(
+        table, second, cot, mod, up_weight, down_weight, block, 768, nf, ni, []
+    )
+    layer_got = exchange(layer_send)
+    sum_mlp = lax.psum_scatter(
+        g_mlp.reshape((ni * nf,) + g_mlp.shape[2:]), ("items", "frames"), scatter_dimension=0, tiled=True
+    )[0]
+    dcq, d_text, dgate_b, *co = cross_att_back_call(
+        table, g2, branch_b, crossed, cross_q, mod, text_kv, cross_lse, cross_out_weight, score_scale, block, nf, ni, []
+    )
+    text_back, *earlier = text_back_call(table, d_text, text_rows, cross_kv_weight, co, ni, [layer_got])
+    text_got = exchange(text_back)
+    g1, d_att, dmod_b, mid_keep, mid_send = cross_in_back_call(
+        table, g2, dcq, branch_a, attended, first, mod, out_weight, cross_q_weight, earlier, block, nf, ni, []
+    )
+    mid = Sum(mid_keep, mid_send, x_first, sizes)
+    mid.launch()
+    kept = self_bwd_call(table, 0, qkv, attended, d_att, self_lse, (), 512, score_scale, [text_got])
+    mid.land()
+    mid.launch()
+    for slot in range(1, per):
+        kept = self_bwd_call(table, slot, qkv, attended, d_att, self_lse, kept, 512, score_scale, [mid.send])
+    dq, dk, dv = kept
+    mid.land()
+    mid.launch()
+    qkv_keep, qkv_send = qkv_weight_call(table, dq, dk, dv, rows, mod, block, nf, ni, [mid.send, sum_mlp])
+    grad = Sum(qkv_keep, qkv_send, z_first, sizes)
+    grad.launch()
+    mid.land()
+    mid.launch()
+    grad_got = []
+    dmod_a = []
+    for slot in range(per):
+        made, dmod = qkv_in_back_call(
+            table, slot, dq, dk, dv, rows, g1, mod, qkv_weight, block, [grad.send, mid.send]
+        )
+        grad_got.append(exchange(made)[:, None])
+        dmod_a.append(dmod)
+        grad.land()
+        grad.launch()
+    mid.land()
+    mid.launch()
+    sum_mid = mid.land()
+    while grad.steps:
+        grad.land()
+        grad.launch()
+    sum_qkv = grad.land()
+    layer_out = deal_call(table, [layer_got], per, BF, "deal_out")
+    text_grad = deal_call(table, [text_got], per, F32, "deal_text")
+    input_grad = deal_call(table, grad_got, per, F32, "deal_in")
+
+    d_mod = jnp.concatenate([jnp.concatenate(dmod_a, 0), dmod_b[:, :1], dmod_b[:, 1:], dgate_b, dmod_c], 1)
+    d_mod = d_mod.reshape(per, 9 * width)
+    ada_rows, ada_cols, cond_cols = width // ni, 9 * width // nf, width // nf
+    at = 2 + 3 * per
+    spot = table[at : at + items] * per + table[at + items : at + 2 * items]
+    pick_row = spot[:, None] == jnp.arange(items, dtype=jnp.int32)[None, :]
+
+    def my_items(per_item, cols):
+        cut = exchange(per_item.reshape(per, nf, cols).transpose(1, 0, 2)).reshape(items, cols)
+        return jnp.sum(jnp.where(pick_row[:, :, None], cut[None], 0.0), 1)
+
+    every_cond = collect_items(low_cond, ni)
+    every_mod = collect_items(my_items(d_mod, ada_cols), ni)
+    grad_ada = lax.dot_general(
+        lax.dynamic_slice(every_cond, (0, row_item * ada_rows), (items * ni, ada_rows), allow_negative_indices=False).astype(
+            F32
+        ),
+        every_mod,
+        (((0,), (0,)), ((), ())),
+        precision=lax.Precision.HIGHEST,
+        preferred_element_type=F32,
+    )
+    high = d_mod.astype(BF)
+    rest = (d_mod - high.astype(F32)).astype(BF)
+    parts = nt(jnp.concatenate([high, rest], 0), ada_weight)
+    cond_part = my_items(parts[:per] + parts[per:], cond_cols)
+    cond_mine = lax.dynamic_slice(cond_f, (0, me * cond_cols), (items, cond_cols), allow_negative_indices=False)
+    sigmoid_c = jax.nn.sigmoid(cond_mine)
+    cond_grad = cond_part * (sigmoid_c * (1.0 + cond_mine * (1.0 - sigmoid_c)))
+
+    half = width // ni // 2
+    deep = 2 * half
+    sum_mlp = sum_mlp.astype(F32)
+    return (
+        layer_out,
+        input_grad,
+        text_grad,
+        cond_grad,
+        grad_ada,
+        jnp.concatenate([sum_qkv[:deep], tall(sum_qkv[deep:])], 1),
+        tall(sum_mid[3 * half : 4 * half]),
+        tall(sum_mid[4 * half :]),
+        sum_mid[half : 3 * half],
+        tall(sum_mid[:half]),
+        wide(sum_mlp[: 2 * deep], 2),
+        tall(sum_mlp[2 * deep :]),
+    )
+
+
+def on_device(mesh, *args):
+    ni, nf = mesh.shape["items"], mesh.shape["frames"]
+    if nf == 4 and args[0].shape[0] % nf == 0 and args[0].shape[-1] == 768 and 768 % (32 * ni) == 0:
+        return items_whole(ni, nf, *args)
+    return frames_split(*args)
+
+
 def solution(mesh):
     in_specs = (
         P("items", "frames", None),
@@ -351,5 +1451,5 @@
         P("items", "frames"),
     )
     return jax.shard_map(
-        on_device, mesh=mesh, in_specs=in_specs, out_specs=out_specs, check_vma=False
-    )
+        partial(on_device, mesh), mesh=mesh, in_specs=in_specs, out_specs=out_specs, check_vma=False
+    )

time: 1920 us -> 634 us (0.33)
  waiting for transfers between devices: 912 us -> 48.2 us
  matrix products: 615 us -> 13.9 us
  Pallas kernels: 0 us -> 403 us
  other arithmetic: 199 us -> 26.3 us
  local copies, waits for them, and re-layouts: 174 us -> 16.1 us
  starting transfers between devices: 1.74 us -> 103 us
    dot_general x34 -> x3, matrix products: 554 us -> 13.9 us  [the longest x1 6.95 us: nt(): lax.dot_general(left, right, (((1,), (1,)), ((), ())), preferred_element_...]
    unnamed x31 -> x1, waiting for transfers between devices: 452 us -> 0.68 us
    pallas_call x0 -> x21, Pallas kernels: none -> 403 us  [the longest x18 401 us: run(): pl.pallas_call(body, grid_spec=pltpu.PrefetchScalarGridSpec(num_scalar_pr...]
    reduce_scatter x12 -> x1, waiting for transfers between devices: 352 us -> 0.01 us  [items_whole(): lax.psum_scatter(g_mlp.reshape((ni * nf,) + g_mlp.shape[2:]), ('items', '...]
    convert_element_type x5 -> x12, other arithmetic: 163 us -> 15.7 us  [the longest x8 14.2 us: land(): self.keep, self.send = (cut[0].astype(BF), cut[1].astype(BF))]
    all_gather x3 -> x0, waiting for transfers between devices: 109 us -> none  [the longest x1 68.5 us: on_device(): lax.all_gather(keys_own, 'frames', axis=1, tiled=True)]
    ppermute x0 -> x16, starting transfers between devices: none -> 66 us  [the longest x10 52.3 us: launch(): lax.ppermute(self.send, name, [(i, i ^ 1 << bit) for i in range(self.size...]
    sub x2 -> x0, matrix products: 60.9 us -> none  [attend(): attn_prob = jax.nn.softmax(scores, axis=-1)]
  transfers between devices with their start and end apart: 23 -> 27, of which waited for: 20 -> 9; matrix products, arithmetic and copies ran while one was open for 31% -> 7% of each run, Pallas kernels for 0% -> 49%
where the time goes in v2:
time: 634 us; the launch traced here: 625 us
  Pallas kernels  403 us (64%)
  starting transfers between devices  103 us (16%)
  waiting for transfers between devices  48.2 us (8%)
  other arithmetic  26.3 us (4%)
  local copies, waits for them, and re-layouts  16.1 us (3%)
  between operations  14.9 us (2%)
  matrix products  13.9 us (2%)
    pallas_call x18, Pallas kernels, run(): pl.pallas_call(body, grid_spec=pltpu.PrefetchScalarGridSpec(num_scalar_pr...  401 us
    ppermute x10, starting transfers between devices, launch(): lax.ppermute(self.send, name, [(i, i ^ 1 << bit) for i in range(self.size...  52.3 us
    all_to_all x10, starting transfers between devices, exchange(): return lax.all_to_all(blocks, 'frames', 0, 0, tiled=True)  36.6 us
    ppermute x10, waiting for transfers between devices, launch(): lax.ppermute(self.send, name, [(i, i ^ 1 << bit) for i in range(self.size...  24.2 us
    all_to_all x10, waiting for transfers between devices, exchange(): return lax.all_to_all(blocks, 'frames', 0, 0, tiled=True)  20.1 us
    convert_element_type x8, other arithmetic, land(): self.keep, self.send = (cut[0].astype(BF), cut[1].astype(BF))  14.2 us
    ppermute x6, starting transfers between devices, collect_items(): lax.ppermute(rows, 'items', [(i, i ^ 1 << bit) for i in range(ni)])  13.7 us
  transfers between devices with their start and end apart: 27, of which 9 were waited for; matrix products, arithmetic and copies ran while one was open for 7% of the time, Pallas kernels for 49%

profile of v2, /device:TPU:0, one launch (start us, length us, event | category | flops | bytes accessed | tf_op | source)
XLA Modules:
  0.0 624.8 jit_solution(952834517784744126)
XLA Ops:
  9.1 4.3 gather_first.1
  13.5 4.2 all-to-all-start
  17.8 8.4 %gather.1 = (bf16[1,4,256,768]{3,2,1,0:T(8,128)(2,1)}, bf16[4,2,64,768]{3,2,1,0:T(8,128)(2,1)}, bf16[4,2,256,768]{3,2,1,0:T(8,128)(2,1)}) custom-call(s32[32]{0:T(128)} %start.1.refs_0_, bf16[8,256,768]{2,1,0:T(8,128)(2,1)} %refs_1_.3, bf16[8,64,768]{2,1,0:T(8,128)(2,1)} %refs_2_.2, bf16[8,256,768]{2,1,0:T(8,128)(2,1)} %refs_3_.4), custom_call_target="tpu_custom_call" | custom-call | tf_op jit(solution)/shard_map/gather/pallas_call | solution.py:845
  26.2 11.5 %all-to-all-done.refs_2_.refs_1_ = bf16[4,256,768]{2,1,0:T(8,128)(2,1)S(1)} async-done(((bf16[4,256,768]{2,1,0:T(8,128)(2,1)}), bf16[4,256,768]{2,1,0:T(8,128)(2,1)S(1)}, u32[]{:S(2)}, u32[]{:S(2)}) %all-to-all-start) | async-done | bytes 1572896 | tf_op jit(solution)/shard_map/all_to_all | solution.py:1219
  38.9 3.5 all-to-all-start.2
  42.4 5.5 fusion.40
  48.9 5.2 all-to-all-done.2.refs_2_.refs_1_
  54.0 3.6 all-to-all-start.1
  57.6 32.9 %self_fwd.2 = (bf16[2,1024,768]{2,1,0:T(8,128)(2,1)}, bf16[2,1024,2304]{2,1,0:T(8,128)(2,1)}, bf16[2,1024,768]{2,1,0:T(8,128)(2,1)}, f32[2,6,2,1024]{3,2,1,0:T(2,128)}) custom-call(s32[32]{0:T(128)} %start.1.refs_0_, bf16[4,256,768]{2,1,0:T(8,128)(2,1)} %copy-done.4, f32[2,9,768]{2,1,0:T(8,128)} %reshape.185.refs_2_.refs_3_.refs_5_.refs_6_, ...), custom_call_target="tpu_custom_call" | custom-call | flops 16508780544 | bytes 12582912 | tf_op jit(solution)/shard_map/self_fwd/pallas_call | solution.py:845
  90.5 4.9 text_fwd.1.refs_4_.refs_6_
  96.6 3.9 all-to-all-start.3
  100.5 18.1 %self_fwd.3 = (bf16[2,1024,768]{2,1,0:T(8,128)(2,1)}, bf16[2,1024,2304]{2,1,0:T(8,128)(2,1)}, bf16[2,1024,768]{2,1,0:T(8,128)(2,1)}, f32[2,6,2,1024]{3,2,1,0:T(2,128)}) custom-call(s32[32]{0:T(128)} %start.1.refs_0_, bf16[4,256,768]{2,1,0:T(8,128)(2,1)} %copy-done.5, ...), custom_call_target="tpu_custom_call", output_to_operand_aliasing={{0}: (4, {}), {1}: (5, {}), {2}: (6, {}), {3}: (7, {})} | custom-call | flops 16508780544 | bytes 12582912 | tf_op jit(solution)/shard_map/self_fwd/pallas_call | solution.py:845
  118.6 25.1 %cross_fwd.1 = (f32[2,1024,768]{2,1,0:T(8,128)}, f32[2,1024,768]{2,1,0:T(8,128)}, bf16[2,1024,768]{2,1,0:T(8,128)(2,1)}, bf16[2,1024,768]{2,1,0:T(8,128)(2,1)}, ...) custom-call(s32[32]{0:T(128)} %start.1.refs_0_, ...), custom_call_target="tpu_custom_call" | custom-call | flops 13690208256 | bytes 31457280 | tf_op jit(solution)/shard_map/cross_fwd/pallas_call | solution.py:845
  145.4 89.4 %mlp.1 = (bf16[4,2,256,768]{3,2,1,0:T(8,128)(2,1)}, f32[2,1024,768]{2,1,0:T(8,128)}, f32[2,3,768]{2,1,0:T(4,128)}, bf16[8,4,384,384]{3,2,1,0:T(8,128)(2,1)}) custom-call(s32[32]{0:T(128)} %start.1.refs_0_, f32[2,1024,768]{2,1,0:T(8,128)} %get-tuple-element.72.refs_1_, bf16[4,2,256,768]{3,2,1,0:T(8,128)(2,1)} %copy-done.9, ...), custom_call_target="tpu_custom_call" | custom-call | flops 57982058496 | bytes 25165824 | tf_op jit(solution)/shard_map/mlp/pallas_call | solution.py:845
  234.7 3.7 all-to-all-start.4
  239.2 56.0 %cross_att_bwd.1 = (bf16[2,1024,768]{2,1,0:T(8,128)(2,1)}, f32[2,256,1536]{2,1,0:T(8,128)}, f32[2,1,768]{2,1,0:T(1,128)}, bf16[8,2,48,384]{3,2,1,0:T(8,128)(2,1)}, bf16[8,2,48,384]{3,2,1,0:T(8,128)(2,1)}) custom-call(s32[32]{0:T(128)} %start.1.refs_0_, f32[2,1024,768]{2,1,0:T(8,128)} %get-tuple-element.75.refs_1_, ...), custom_call_target="tpu_custom_call" | custom-call | flops 20937965568 | bytes 25165824 | tf_op jit(solution)/shard_map/cross_att_bwd/pallas_call | solution.py:845
  296.8 12.1 %text_bwd.1 = (bf16[4,2,64,768]{3,2,1,0:T(8,128)(2,1)}, bf16[8,2,144,384]{3,2,1,0:T(8,128)(2,1)}, bf16[8,2,144,384]{3,2,1,0:T(8,128)(2,1)}) custom-call(s32[32]{0:T(128)} %start.1.refs_0_, f32[2,256,1536]{2,1,0:T(8,128)} %get-tuple-element.83.refs_1_, bf16[4,2,64,768]{3,2,1,0:T(8,128)(2,1)} %copy-done.1, bf16[768,1536]{1,0:T(8,128)(2,1)} %refs_3_.7, ...), custom_call_target="tpu_custom_call" | custom-call | flops 2415919104 | tf_op jit(solution)/shard_map/text_bwd/pallas_call | solution.py:845
  308.9 31.7 %cross_in_bwd.1 = (f32[2,1024,768]{2,1,0:T(8,128)}, bf16[2,1024,768]{2,1,0:T(8,128)(2,1)}, f32[2,3,768]{2,1,0:T(4,128)}, bf16[8,2,240,384]{3,2,1,0:T(8,128)(2,1)}, bf16[8,2,240,384]{3,2,1,0:T(8,128)(2,1)}) custom-call(s32[32]{0:T(128)} %start.1.refs_0_, f32[2,1024,768]{2,1,0:T(8,128)} %get-tuple-element.75.refs_1_, ...), custom_call_target="tpu_custom_call" | custom-call | flops 9663676416 | bytes 31457280 | tf_op jit(solution)/shard_map/cross_in_bwd/pallas_call | solution.py:845
  341.0 3.5 all-to-all-start.5
  344.5 7.6 %collective-permute-start.4 = (bf16[8,768]{1,0:T(8,128)(2,1)S(1)}, bf16[8,768]{1,0:T(8,128)(2,1)S(1)}, u32[]{:S(2)}, u32[]{:S(2)}) collective-permute-start(bf16[8,768]{1,0:T(8,128)(2,1)S(1)} %multiply_convert_fusion), channel_id=1, source_target_pairs={{0,4},{4,0},{8,12},{12,8},{16,20},{20,16},{24,28},{28,24},{1,5},{5... | collective-permute-start | bytes 36872 | tf_op jit(solution)/shard_map/ppermute | solution.py:1264
  352.1 4.5 fusion.1
  356.7 1.7 collective-permute-start.1
  359.3 39.3 %self_bwd.2 = (bf16[2,1024,768]{2,1,0:T(8,128)(2,1)}, bf16[2,1024,768]{2,1,0:T(8,128)(2,1)}, bf16[2,1024,768]{2,1,0:T(8,128)(2,1)}) custom-call(s32[32]{0:T(128)} %start.1.refs_0_, bf16[2,1024,2304]{2,1,0:T(8,128)(2,1)} %get-tuple-element.74.refs_1_.refs_2_.refs_3_, bf16[2,1024,2304]{2,1,0:T(8,128)(2,1)} %get-tuple-element.74.refs_1_.refs_2_.refs_3_, ...), custom_call_target="tpu_custom_call" | custom-call | flops 32212254720 | bytes 12582912 | tf_op jit(solution)/shard_map/self_bwd/pallas_call | solution.py:845
  400.3 10.4 %collective-permute-start.2 = (bf16[2,2,240,384]{3,2,1,0:T(8,128)(2,1)S(1)}, bf16[2,2,240,384]{3,2,1,0:T(8,128)(2,1)S(1)}, u32[]{:S(2)}, u32[]{:S(2)}) collective-permute-start(bf16[2,2,240,384]{3,2,1,0:T(8,128)(2,1)S(1)} %get-tuple-element.165.refs_6_), channel_id=1, source_target_pairs={{0,8},{4,12},{8,0},{12,4},{16,24},{20,28},{24,16},{28,20},{1,9},{5... | collective-permute-start | bytes 2211848 | tf_op jit(solution)/shard_map/ppermute | solution.py:1246
  410.8 15.6 %self_bwd.3 = (bf16[2,1024,768]{2,1,0:T(8,128)(2,1)}, bf16[2,1024,768]{2,1,0:T(8,128)(2,1)}, bf16[2,1024,768]{2,1,0:T(8,128)(2,1)}) custom-call(s32[32]{0:T(128)} %start.1.refs_0_, bf16[2,1024,2304]{2,1,0:T(8,128)(2,1)} %get-tuple-element.74.refs_1_.refs_2_.refs_3_, ...), custom_call_target="tpu_custom_call", output_to_operand_aliasing={{0}: (7, {}), {1}: (8, {}), {2}: (9, {})} | custom-call | flops 32212254720 | bytes 12582912 | tf_op jit(solution)/shard_map/self_bwd/pallas_call | solution.py:845
  427.7 11.3 %collective-permute-start.14 = (bf16[2,240,384]{2,1,0:T(8,128)(2,1)S(1)}, bf16[2,240,384]{2,1,0:T(8,128)(2,1)S(1)}, u32[]{:S(2)}, u32[]{:S(2)}) collective-permute-start(bf16[2,240,384]{2,1,0:T(8,128)(2,1)S(1)} %get-tuple-element.169.refs_9_), channel_id=1, source_target_pairs={{0,16},{4,20},{8,24},{12,28},{16,0},{20,4},{24,8},{28,12},{1,17},{... | collective-permute-start | bytes 1105928 | tf_op jit(solution)/shard_map/ppermute | solution.py:1246
  439.0 21.2 %qkv_weight_bwd.1 = (bf16[8,2,144,384]{3,2,1,0:T(8,128)(2,1)}, bf16[8,2,144,384]{3,2,1,0:T(8,128)(2,1)}) custom-call(s32[32]{0:T(128)} %start.1.refs_0_, bf16[2,1024,768]{2,1,0:T(8,128)(2,1)} %get-tuple-element.96.refs_1_, bf16[2,1024,768]{2,1,0:T(8,128)(2,1)} %get-tuple-element.97.refs_2_, bf16[2,1024,768]{2,1,0:T(8,128)(2,1)} %get-tuple-element.98.refs_3_, ...), custom_call_target="tpu_custom_call" | custom-call | flops 7247757312 | bytes 12582912 | tf_op jit(solution)/shard_map/qkv_weight_bwd/pallas_call | solution.py:845
  460.8 21.5 %collective-permute-start.15 = (bf16[240,384]{1,0:T(8,128)(2,1)S(1)}, bf16[240,384]{1,0:T(8,128)(2,1)S(1)}, u32[]{:S(2)}, u32[]{:S(2)}) collective-permute-start(bf16[240,384]{1,0:T(8,128)(2,1)S(1)} %fusion.25), channel_id=1, source_target_pairs={{0,2},{1,3},{2,0},{3,1},{4,6},{5,7},{6,4},{7,5},{8,10},{9,11},{10,... | collective-permute-start | bytes 552968 | tf_op jit(solution)/shard_map/ppermute | solution.py:1246
  484.5 6.8 %deal_out.1 = bf16[8,256,768]{2,1,0:T(8,128)(2,1)} custom-call(s32[32]{0:T(128)} %start.1.refs_0_, bf16[4,2,256,768]{3,2,1,0:T(8,128)(2,1)} %copy-done), custom_call_target="tpu_custom_call" | custom-call | bytes 9437184 | tf_op jit(solution)/shard_map/deal_out/pallas_call | solution.py:845
  491.3 5.9 deal_text.1
  498.0 10.5 %qkv_in_bwd.2 = (bf16[4,256,768]{2,1,0:T(8,128)(2,1)}, f32[1,2,768]{2,1,0:T(2,128)}) custom-call(s32[32]{0:T(128)} %start.1.refs_0_, bf16[2,1024,768]{2,1,0:T(8,128)(2,1)} %get-tuple-element.96.refs_1_, bf16[2,1024,768]{2,1,0:T(8,128)(2,1)} %get-tuple-element.97.refs_2_, bf16[2,1024,768]{2,1,0:T(8,128)(2,1)} %get-tuple-element.98.refs_3_, ...), custom_call_target="tpu_custom_call" | custom-call | flops 3623878656 | bytes 12582912 | tf_op jit(solution)/shard_map/qkv_in_bwd/pallas_call | solution.py:845
  509.7 3.4 fusion.3
  513.1 10.8 %qkv_in_bwd.3 = (bf16[4,256,768]{2,1,0:T(8,128)(2,1)}, f32[1,2,768]{2,1,0:T(2,128)}) custom-call(s32[32]{0:T(128)} %start.1.refs_0_, bf16[2,1024,768]{2,1,0:T(8,128)(2,1)} %get-tuple-element.96.refs_1_, bf16[2,1024,768]{2,1,0:T(8,128)(2,1)} %get-tuple-element.97.refs_2_, bf16[2,1024,768]{2,1,0:T(8,128)(2,1)} %get-tuple-element.98.refs_3_, ...), custom_call_target="tpu_custom_call" | custom-call | flops 3623878656 | bytes 12582912 | tf_op jit(solution)/shard_map/qkv_in_bwd/pallas_call | solution.py:845
  524.8 7.0 %fusion.28 = f32[4,768]{1,0:T(4,128)S(1)} fusion(bf16[768,6912]{1,0:T(8,128)(2,1)} %param.19, bf16[2,6912]{1,0:T(2,128)(2,1)S(1)} %get-tuple-element.158, bf16[2,6912]{1,0:T(2,128)(2,1)S(1)} %get-tuple-element.159), kind=kOutput, calls=%fused_computation.78 | convolution fusion | flops 42577920 | bytes 10684416 | tf_op jit(solution)/shard_map/dot_general | solution.py:337
  532.5 3.7 all-to-all-start.8
  540.0 3.3 all-to-all-start.9
  547.3 3.7 all-to-all-start.6
  553.0 1.9 copy.69
  558.2 2.7 collective-permute-start.7
  560.9 5.4 collective-permute-done.10
  566.3 2.3 add_convert_fusion.7
  568.6 2.6 collective-permute-start.11
  571.2 3.6 all-to-all-start.7
  577.7 3.8 collective-permute-done.11
  582.9 1.8 collective-permute-start.12
  586.0 13.8 %collective-permute-done.12 = bf16[2,144,384]{2,1,0:T(8,128)(2,1)S(1)} collective-permute-done((bf16[2,144,384]{2,1,0:T(8,128)(2,1)S(1)}, bf16[2,144,384]{2,1,0:T(8,128)(2,1)S(1)}, u32[]{:S(2)}, u32[]{:S(2)}) %collective-permute-start.12) | collective-permute-done | bytes 221216 | tf_op jit(solution)/shard_map/ppermute | solution.py:1246
  601.5 3.2 collective-permute-done.9
  607.2 8.5 %deal_in.1 = f32[8,256,768]{2,1,0:T(8,128)} custom-call(s32[32]{0:T(128)} %start.1.refs_0_, bf16[4,1,256,768]{3,2,1,0:T(8,128)(2,1)} %bitcast.124, bf16[4,1,256,768]{3,2,1,0:T(8,128)(2,1)} %bitcast.125), custom_call_target="tpu_custom_call" | custom-call | bytes 9437184 | tf_op jit(solution)/shard_map/deal_in/pallas_call | solution.py:845
  (134 shorter events, 44.6 us)
Async XLA Ops:
  9.1 8.6 %copy-start.19 = (s32[32]{0:T(128)S(1)}, s32[32]{0:T(128)}, u32[]{:S(2)}) copy-start(s32[32]{0:T(128)} %start.1.refs_0_) | copy-start | bytes 388
  13.5 24.3 %all-to-all-start = ((bf16[4,256,768]{2,1,0:T(8,128)(2,1)}), bf16[4,256,768]{2,1,0:T(8,128)(2,1)S(1)}, u32[]{:S(2)}, u32[]{:S(2)}) async-start(bf16[4,256,768]{2,1,0:T(8,128)(2,1)} %gather_first.1), calls=%async_computation | async-start | bytes 3145728 | tf_op jit(solution)/shard_map/all_to_all | solution.py:1219
  26.1 16.3 %copy-start.17 = (bf16[8,768]{1,0:T(8,128)(2,1)S(1)}, bf16[8,768]{1,0:T(8,128)(2,1)}, u32[]{:S(2)}) copy-start(bf16[8,768]{1,0:T(8,128)(2,1)} %param.15) | copy-start | bytes 36868
  38.9 15.1 %all-to-all-start.2 = ((bf16[4,2,64,768]{3,2,1,0:T(8,128)(2,1)}), bf16[4,2,64,768]{3,2,1,0:T(8,128)(2,1)S(1)}, u32[]{:S(2)}, u32[]{:S(2)}) async-start(bf16[4,2,64,768]{3,2,1,0:T(8,128)(2,1)} %get-tuple-element.64.refs_5_), calls=%async_computation.2 | async-start | bytes 1572864 | tf_op jit(solution)/shard_map/all_to_all | solution.py:1219
  54.0 36.4 %copy-start.1 = (bf16[4,2,64,768]{3,2,1,0:T(8,128)(2,1)}, bf16[4,2,64,768]{3,2,1,0:T(8,128)(2,1)S(1)}, u32[]{:S(2)}) copy-start(bf16[4,2,64,768]{3,2,1,0:T(8,128)(2,1)S(1)} %all-to-all-done.2.refs_2_.refs_1_) | copy-start | bytes 2359300
  54.0 41.4 %all-to-all-start.1 = ((bf16[4,256,768]{2,1,0:T(8,128)(2,1)}), bf16[4,256,768]{2,1,0:T(8,128)(2,1)S(1)}, u32[]{:S(2)}, u32[]{:S(2)}) async-start(bf16[4,256,768]{2,1,0:T(8,128)(2,1)} %get-tuple-element.63.refs_4_), calls=%async_computation.1 | async-start | bytes 3145728 | tf_op jit(solution)/shard_map/all_to_all | solution.py:1219
  96.6 47.1 %all-to-all-start.3 = ((bf16[4,2,256,768]{3,2,1,0:T(8,128)(2,1)}), bf16[4,2,256,768]{3,2,1,0:T(8,128)(2,1)S(1)}, u32[]{:S(2)}, u32[]{:S(2)}) async-start(bf16[4,2,256,768]{3,2,1,0:T(8,128)(2,1)} %gate.3.refs_8_), calls=%async_computation.3 | async-start | bytes 6291456 | tf_op jit(solution)/shard_map/all_to_all | solution.py:1219
  143.7 1.7 copy-start.9
  234.7 60.5 %all-to-all-start.4 = ((bf16[4,2,256,768]{3,2,1,0:T(8,128)(2,1)}), bf16[4,2,256,768]{3,2,1,0:T(8,128)(2,1)S(1)}, u32[]{:S(2)}, u32[]{:S(2)}) async-start(bf16[4,2,256,768]{3,2,1,0:T(8,128)(2,1)} %get-tuple-element.73), calls=%async_computation.4 | async-start | bytes 6291456 | tf_op jit(solution)/shard_map/all_to_all | solution.py:1219
  238.4 200.6 %reduce-scatter.2.cloned.1.call-start = ((), (), s32[]{:S(2)}) async-start(), calls=%async_computation.11 | async-start | bytes 9732096 | tf_op jit(solution)/shard_map/reduce_scatter | solution.py:1319
  308.9 35.6 %copy-start.18 = (bf16[8,768]{1,0:T(8,128)(2,1)S(1)}, bf16[8,768]{1,0:T(8,128)(2,1)}, u32[]{:S(2)}) copy-start(bf16[8,768]{1,0:T(8,128)(2,1)} %param.15) | copy-start | bytes 36868
  340.6 11.6 %collective-permute-start = (bf16[8,2,240,384]{3,2,1,0:T(8,128)(2,1)}, bf16[8,2,240,384]{3,2,1,0:T(8,128)(2,1)}, u32[]{:S(2)}, u32[]{:S(2)}) collective-permute-start(bf16[8,2,240,384]{3,2,1,0:T(8,128)(2,1)} %get-tuple-element.95), channel_id=1, source_target_pairs={{0,1},{1,0},{2,3},{3,2},{4,5},{5,4},{6,7},{7,6},{8,9},{9,8},{10,11... | collective-permute-start | bytes 8847368 | tf_op jit(solution)/shard_map/ppermute | solution.py:1246
  341.0 17.4 %all-to-all-start.5 = ((bf16[4,2,64,768]{3,2,1,0:T(8,128)(2,1)}), bf16[4,2,64,768]{3,2,1,0:T(8,128)(2,1)S(1)}, u32[]{:S(2)}, u32[]{:S(2)}) async-start(bf16[4,2,64,768]{3,2,1,0:T(8,128)(2,1)} %get-tuple-element.90), calls=%async_computation.5 | async-start | bytes 1572864 | tf_op jit(solution)/shard_map/all_to_all | solution.py:1219
  344.5 115.9 %collective-permute-start.4 = (bf16[8,768]{1,0:T(8,128)(2,1)S(1)}, bf16[8,768]{1,0:T(8,128)(2,1)S(1)}, u32[]{:S(2)}, u32[]{:S(2)}) collective-permute-start(bf16[8,768]{1,0:T(8,128)(2,1)S(1)} %multiply_convert_fusion), channel_id=1, source_target_pairs={{0,4},{4,0},{8,12},{12,8},{16,20},{20,16},{24,28},{28,24},{1,5},{5... | collective-permute-start | bytes 36872 | tf_op jit(solution)/shard_map/ppermute | solution.py:1264
  356.7 41.9 %collective-permute-start.1 = (bf16[2,2,2,240,384]{4,3,2,1,0:T(8,128)(2,1)}, bf16[2,2,2,240,384]{4,3,2,1,0:T(8,128)(2,1)}, u32[]{:S(2)}, u32[]{:S(2)}) collective-permute-start(bf16[2,2,2,240,384]{4,3,2,1,0:T(8,128)(2,1)} %get-tuple-element.161.refs_10_), channel_id=1, source_target_pairs={{0,4},{4,0},{8,12},{12,8},{16,20},{20,16},{24,28},{28,24},{1,5},{5... | collective-permute-start | bytes 4423688 | tf_op jit(solution)/shard_map/ppermute | solution.py:1246
  400.3 26.1 %copy-start.13 = (bf16[2,2,240,384]{3,2,1,0:T(8,128)(2,1)}, bf16[2,2,240,384]{3,2,1,0:T(8,128)(2,1)S(1)}, u32[]{:S(2)}) copy-start(bf16[2,2,240,384]{3,2,1,0:T(8,128)(2,1)S(1)} %get-tuple-element.165.refs_6_) | copy-start | bytes 2211844
  400.3 27.1 %collective-permute-start.2 = (bf16[2,2,240,384]{3,2,1,0:T(8,128)(2,1)S(1)}, bf16[2,2,240,384]{3,2,1,0:T(8,128)(2,1)S(1)}, u32[]{:S(2)}, u32[]{:S(2)}) collective-permute-start(bf16[2,2,240,384]{3,2,1,0:T(8,128)(2,1)S(1)} %get-tuple-element.165.refs_6_), channel_id=1, source_target_pairs={{0,8},{4,12},{8,0},{12,4},{16,24},{20,28},{24,16},{28,20},{1,9},{5... | collective-permute-start | bytes 2211848 | tf_op jit(solution)/shard_map/ppermute | solution.py:1246
  427.7 32.6 %copy-start.7 = (bf16[2,240,384]{2,1,0:T(8,128)(2,1)}, bf16[2,240,384]{2,1,0:T(8,128)(2,1)S(1)}, u32[]{:S(2)}) copy-start(bf16[2,240,384]{2,1,0:T(8,128)(2,1)S(1)} %get-tuple-element.169.refs_9_) | copy-start | bytes 1105924
  427.7 33.0 %collective-permute-start.14 = (bf16[2,240,384]{2,1,0:T(8,128)(2,1)S(1)}, bf16[2,240,384]{2,1,0:T(8,128)(2,1)S(1)}, u32[]{:S(2)}, u32[]{:S(2)}) collective-permute-start(bf16[2,240,384]{2,1,0:T(8,128)(2,1)S(1)} %get-tuple-element.169.refs_9_), channel_id=1, source_target_pairs={{0,16},{4,20},{8,24},{12,28},{16,0},{20,4},{24,8},{28,12},{1,17},{... | collective-permute-start | bytes 1105928 | tf_op jit(solution)/shard_map/ppermute | solution.py:1246
  439.0 21.3 %copy-start.20 = (s32[32]{0:T(128)S(1)}, s32[32]{0:T(128)}, u32[]{:S(2)}) copy-start(s32[32]{0:T(128)} %start.1.refs_0_) | copy-start | bytes 388
  460.2 48.3 %collective-permute-start.3 = (bf16[8,2,144,384]{3,2,1,0:T(8,128)(2,1)}, bf16[8,2,144,384]{3,2,1,0:T(8,128)(2,1)S(1)}, u32[]{:S(2)}, u32[]{:S(2)}) collective-permute-start(bf16[8,2,144,384]{3,2,1,0:T(8,128)(2,1)} %get-tuple-element.101.refs_8_), channel_id=1, source_target_pairs={{0,1},{1,0},{2,3},{3,2},{4,5},{5,4},{6,7},{7,6},{8,9},{9,8},{10,11... | collective-permute-start | bytes 5308424 | tf_op jit(solution)/shard_map/ppermute | solution.py:1246
  460.4 23.1 %collective-permute-start.5 = (bf16[16,768]{1,0:T(8,128)(2,1)S(1)}, bf16[16,768]{1,0:T(8,128)(2,1)S(1)}, u32[]{:S(2)}, u32[]{:S(2)}) collective-permute-start(bf16[16,768]{1,0:T(8,128)(2,1)S(1)} %pad_maximum_fusion.9), channel_id=1, source_target_pairs={{0,8},{4,12},{8,0},{12,4},{16,24},{20,28},{24,16},{28,20},{1,9},{5... | collective-permute-start | bytes 73736 | tf_op jit(solution)/shard_map/ppermute | solution.py:1264
  460.8 36.4 %collective-permute-start.15 = (bf16[240,384]{1,0:T(8,128)(2,1)S(1)}, bf16[240,384]{1,0:T(8,128)(2,1)S(1)}, u32[]{:S(2)}, u32[]{:S(2)}) collective-permute-start(bf16[240,384]{1,0:T(8,128)(2,1)S(1)} %fusion.25), channel_id=1, source_target_pairs={{0,2},{1,3},{2,0},{3,1},{4,6},{5,7},{6,4},{7,5},{8,10},{9,11},{10,... | collective-permute-start | bytes 552968 | tf_op jit(solution)/shard_map/ppermute | solution.py:1246
  484.1 117.3 %collective-permute-start.6 = (bf16[32,768]{1,0:T(8,128)(2,1)}, bf16[32,768]{1,0:T(8,128)(2,1)S(1)}, u32[]{:S(2)}, u32[]{:S(2)}) collective-permute-start(bf16[32,768]{1,0:T(8,128)(2,1)} %pad_maximum_fusion.8), channel_id=1, source_target_pairs={{0,16},{4,20},{8,24},{12,28},{16,0},{20,4},{24,8},{28,12},{1,17},{... | collective-permute-start | bytes 147464 | tf_op jit(solution)/shard_map/ppermute | solution.py:1264
  513.1 10.9 %copy-start.22 = (f32[2,3,768]{2,1,0:T(4,128)S(1)}, f32[2,3,768]{2,1,0:T(4,128)}, u32[]{:S(2)}) copy-start(f32[2,3,768]{2,1,0:T(4,128)} %get-tuple-element.109) | copy-start | bytes 55300
  513.1 10.9 %copy-start.23 = (f32[2,3,768]{2,1,0:T(4,128)S(1)}, f32[2,3,768]{2,1,0:T(4,128)}, u32[]{:S(2)}) copy-start(f32[2,3,768]{2,1,0:T(4,128)} %get-tuple-element.107) | copy-start | bytes 55300
  513.1 10.9 %copy-start.24 = (f32[2,1,768]{2,1,0:T(1,128)S(1)}, f32[2,1,768]{2,1,0:T(1,128)}, u32[]{:S(2)}) copy-start(f32[2,1,768]{2,1,0:T(1,128)} %get-tuple-element.108) | copy-start | bytes 18436
  513.1 10.9 %copy-start.25 = (f32[1,2,768]{2,1,0:T(2,128)S(1)}, f32[1,2,768]{2,1,0:T(2,128)}, u32[]{:S(2)}) copy-start(f32[1,2,768]{2,1,0:T(2,128)} %get-tuple-element.105) | copy-start | bytes 18436
  524.8 18.5 %copy-start.14 = (bf16[1,384,384]{2,1,0:T(8,128)(2,1)S(1)}, bf16[1,384,384]{2,1,0:T(8,128)(2,1)}, u32[]{:S(2)}) copy-start(bf16[1,384,384]{2,1,0:T(8,128)(2,1)} %reduce-scatter.2.cloned.1.call-done) | copy-start | bytes 884740
  524.8 19.4 %copy-start.6 = (bf16[2,2,2,144,384]{4,3,2,1,0:T(8,128)(2,1)S(1)}, bf16[2,2,2,144,384]{4,3,2,1,0:T(8,128)(2,1)}, u32[]{:S(2)}) copy-start(bf16[2,2,2,144,384]{4,3,2,1,0:T(8,128)(2,1)} %get-tuple-element.163.refs_8_) | copy-start | bytes 2654212
  532.5 7.5 %all-to-all-start.8 = ((f32[4,2,192]{2,1,0:T(2,128)}), f32[4,2,192]{2,1,0:T(2,128)S(1)}, u32[]{:S(2)}, u32[]{:S(2)}) async-start(f32[4,2,192]{2,1,0:T(2,128)} %bitcast.122), calls=%async_computation.9 | async-start | bytes 16384 | tf_op jit(solution)/shard_map/all_to_all | solution.py:1219
  540.0 7.3 %all-to-all-start.9 = ((f32[4,2,1728]{2,1,0:T(2,128)}), f32[4,2,1728]{2,1,0:T(2,128)S(1)}, u32[]{:S(2)}, u32[]{:S(2)}) async-start(f32[4,2,1728]{2,1,0:T(2,128)} %copy.66), calls=%async_computation.10 | async-start | bytes 114688 | tf_op jit(solution)/shard_map/all_to_all | solution.py:1219
  544.2 22.1 %collective-permute-start.10 = (bf16[2,2,2,144,384]{4,3,2,1,0:T(8,128)(2,1)S(1)}, bf16[2,2,2,144,384]{4,3,2,1,0:T(8,128)(2,1)}, u32[]{:S(2)}, u32[]{:S(2)}) collective-permute-start(bf16[2,2,2,144,384]{4,3,2,1,0:T(8,128)(2,1)S(1)} %copy-done.6), channel_id=1, source_target_pairs={{0,8},{4,12},{8,0},{12,4},{16,24},{20,28},{24,16},{28,20},{1,9},{5... | collective-permute-start | bytes 2654216 | tf_op jit(solution)/shard_map/ppermute | solution.py:1246
  547.3 9.2 %copy-start.26 = (pred[8,8]{1,0:T(8,128)(4,1)S(1)}, pred[8,8]{1,0:T(8,128)(4,1)}, u32[]{:S(2)}) copy-start(pred[8,8]{1,0:T(8,128)(4,1)} %iota_compare_fusion) | copy-start | bytes 196
  547.3 23.9 %all-to-all-start.6 = ((bf16[4,256,768]{2,1,0:T(8,128)(2,1)}), bf16[4,256,768]{2,1,0:T(8,128)(2,1)S(1)}, u32[]{:S(2)}, u32[]{:S(2)}) async-start(bf16[4,256,768]{2,1,0:T(8,128)(2,1)} %get-tuple-element.102), calls=%async_computation.7 | async-start | bytes 3145728 | tf_op jit(solution)/shard_map/all_to_all | solution.py:1219
  558.2 18.0 %collective-permute-start.7 = (f32[8,1728]{1,0:T(8,128)S(1)}, f32[8,1728]{1,0:T(8,128)S(1)}, u32[]{:S(2)}, u32[]{:S(2)}) collective-permute-start(f32[8,1728]{1,0:T(8,128)S(1)} %select_reduce_fusion), channel_id=1, source_target_pairs={{0,4},{4,0},{8,12},{12,8},{16,20},{20,16},{24,28},{28,24},{1,5},{5... | collective-permute-start | bytes 165896 | tf_op jit(solution)/shard_map/ppermute | solution.py:1264
  566.3 8.5 %copy-start.21 = (f32[8,192]{1,0:T(8,128)S(1)}, f32[8,192]{1,0:T(8,128)}, u32[]{:S(2)}) copy-start(f32[8,192]{1,0:T(8,128)} %select_reduce_fusion.2) | copy-start | bytes 18436
  568.6 13.0 %collective-permute-start.11 = (bf16[2,2,144,384]{3,2,1,0:T(8,128)(2,1)}, bf16[2,2,144,384]{3,2,1,0:T(8,128)(2,1)}, u32[]{:S(2)}, u32[]{:S(2)}) collective-permute-start(bf16[2,2,144,384]{3,2,1,0:T(8,128)(2,1)} %get-tuple-element.167), channel_id=1, source_target_pairs={{0,4},{4,0},{8,12},{12,8},{16,20},{20,16},{24,28},{28,24},{1,5},{5... | collective-permute-start | bytes 1327112 | tf_op jit(solution)/shard_map/ppermute | solution.py:1246
  571.2 34.8 %copy-start.2 = (bf16[4,256,768]{2,1,0:T(8,128)(2,1)}, bf16[4,256,768]{2,1,0:T(8,128)(2,1)S(1)}, u32[]{:S(2)}) copy-start(bf16[4,256,768]{2,1,0:T(8,128)(2,1)S(1)} %all-to-all-done.6) | copy-start | bytes 4718596
  571.2 34.8 %all-to-all-start.7 = ((bf16[4,256,768]{2,1,0:T(8,128)(2,1)}), bf16[4,256,768]{2,1,0:T(8,128)(2,1)S(1)}, u32[]{:S(2)}, u32[]{:S(2)}) async-start(bf16[4,256,768]{2,1,0:T(8,128)(2,1)} %get-tuple-element.104), calls=%async_computation.8 | async-start | bytes 3145728 | tf_op jit(solution)/shard_map/all_to_all | solution.py:1219
  576.2 8.5 %collective-permute-start.8 = (f32[16,1728]{1,0:T(8,128)S(1)}, f32[16,1728]{1,0:T(8,128)S(1)}, u32[]{:S(2)}, u32[]{:S(2)}) collective-permute-start(f32[16,1728]{1,0:T(8,128)S(1)} %pad_maximum_fusion.3), channel_id=1, source_target_pairs={{0,8},{4,12},{8,0},{12,4},{16,24},{20,28},{24,16},{28,20},{1,9},{5... | collective-permute-start | bytes 331784 | tf_op jit(solution)/shard_map/ppermute | solution.py:1264
  582.9 21.7 %copy-start.11 = (bf16[1,2,144,384]{3,2,1,0:T(8,128)(2,1)}, bf16[1,2,144,384]{3,2,1,0:T(8,128)(2,1)S(1)}, u32[]{:S(2)}) copy-start(bf16[1,2,144,384]{3,2,1,0:T(8,128)(2,1)S(1)} %get-tuple-element.170) | copy-start | bytes 663556
  582.9 16.9 %collective-permute-start.12 = (bf16[2,144,384]{2,1,0:T(8,128)(2,1)S(1)}, bf16[2,144,384]{2,1,0:T(8,128)(2,1)S(1)}, u32[]{:S(2)}, u32[]{:S(2)}) collective-permute-start(bf16[2,144,384]{2,1,0:T(8,128)(2,1)S(1)} %get-tuple-element.171), channel_id=1, source_target_pairs={{0,16},{4,20},{8,24},{12,28},{16,0},{20,4},{24,8},{28,12},{1,17},{... | collective-permute-start | bytes 663560 | tf_op jit(solution)/shard_map/ppermute | solution.py:1246
  584.7 19.9 %collective-permute-start.9 = (f32[32,1728]{1,0:T(8,128)S(1)}, f32[32,1728]{1,0:T(8,128)S(1)}, u32[]{:S(2)}, u32[]{:S(2)}) collective-permute-start(f32[32,1728]{1,0:T(8,128)S(1)} %pad_maximum_fusion.2), channel_id=1, source_target_pairs={{0,16},{4,20},{8,24},{12,28},{16,0},{20,4},{24,8},{28,12},{1,17},{... | collective-permute-start | bytes 663560 | tf_op jit(solution)/shard_map/ppermute | solution.py:1264
  599.8 1.6 copy-start.15
  600.5 15.2 %collective-permute-start.13 = (bf16[144,384]{1,0:T(8,128)(2,1)}, bf16[144,384]{1,0:T(8,128)(2,1)}, u32[]{:S(2)}, u32[]{:S(2)}) collective-permute-start(bf16[144,384]{1,0:T(8,128)(2,1)} %fusion.27), channel_id=1, source_target_pairs={{0,2},{1,3},{2,0},{3,1},{4,6},{5,7},{6,4},{7,5},{8,10},{9,11},{10,... | collective-permute-start | bytes 331784 | tf_op jit(solution)/shard_map/ppermute | solution.py:1246
  607.2 8.5 %copy-start.12 = (bf16[1,2,144,384]{3,2,1,0:T(8,128)(2,1)S(1)}, bf16[1,2,144,384]{3,2,1,0:T(8,128)(2,1)}, u32[]{:S(2)}) copy-start(bf16[1,2,144,384]{3,2,1,0:T(8,128)(2,1)} %copy-done.11) | copy-start | bytes 663556
  607.2 8.5 %copy-start.16 = (bf16[2,144,384]{2,1,0:T(8,128)(2,1)S(1)}, bf16[2,144,384]{2,1,0:T(8,128)(2,1)}, u32[]{:S(2)}) copy-start(bf16[2,144,384]{2,1,0:T(8,128)(2,1)} %copy-done.15) | copy-start | bytes 663556
  (6 other events, 7.2 us)
Sparse Core Ops, SparseCore 0:
  245.2 156.5 reduce-scatter.1

commit v3 on v2

v3 whole, which is shorter than its diff:
```python
import functools
from functools import partial

import jax
import jax.numpy as jnp
from jax import lax
from jax.experimental import pallas as pl
from jax.experimental.pallas import tpu as pltpu
from jax.sharding import PartitionSpec as P

H = 12


def norm_parts(tensor):
    centered = tensor - jnp.mean(tensor, -1, keepdims=True)
    inverse = lax.rsqrt(jnp.mean(centered * centered, -1, keepdims=True) + 1e-06)
    return (centered * inverse, inverse)


def norm_back(normed, inverse, incoming):
    return inverse * (
        incoming
        - jnp.mean(incoming, -1, keepdims=True)
        - normed * jnp.mean(incoming * normed, -1, keepdims=True)
    )


def split_heads(tensor):
    return tensor.reshape(tensor.shape[0], tensor.shape[1], H, -1)


def attend(queries, keys_in, values_in, key_valid, score_scale):
    scores = (
        jnp.einsum(
            "ifhd,ijhd->ihfj",
            split_heads(queries),
            split_heads(keys_in),
            preferred_element_type=jnp.float32,
        )
        * score_scale
    )
    scores = jnp.where(key_valid[:, None, None, :], scores, -1e30)
    attn_prob = jax.nn.softmax(scores, axis=-1)
    log_total = jax.nn.logsumexp(scores, axis=-1)
    low_prob = attn_prob.astype(jnp.bfloat16)
    mixed = jnp.einsum(
        "ihfj,ijhd->ifhd", low_prob, split_heads(values_in), preferred_element_type=jnp.float32
    )
    return (attn_prob, low_prob, mixed.astype(jnp.bfloat16).reshape(queries.shape), log_total)


def attend_back(grad_mixed, queries, keys_in, values_in, attn_prob, low_prob, score_scale):
    grad_heads = split_heads(grad_mixed)
    grad_prob = jnp.einsum(
        "ifhd,ijhd->ihfj", grad_heads, split_heads(values_in), preferred_element_type=jnp.float32
    )
    grad_values = jnp.einsum(
        "ihfj,ifhd->ijhd", low_prob, grad_heads, preferred_element_type=jnp.float32
    )
    grad_scores = (
        attn_prob * (grad_prob - jnp.sum(attn_prob * grad_prob, -1, keepdims=True))
    ).astype(jnp.bfloat16)
    grad_queries = (
        jnp.einsum(
            "ihfj,ijhd->ifhd", grad_scores, split_heads(keys_in), preferred_element_type=jnp.float32
        )
        * score_scale
    )
    grad_keys = (
        jnp.einsum(
            "ihfj,ifhd->ijhd", grad_scores, split_heads(queries), preferred_element_type=jnp.float32
        )
        * score_scale
    )
    return (
        grad_queries.reshape(queries.shape),
        grad_keys.reshape(keys_in.shape),
        grad_values.reshape(values_in.shape),
    )


def project(tensor, weight):
    return jnp.einsum("ifd,de->ife", tensor, weight, preferred_element_type=jnp.float32)


def project_back(tensor, weight):
    return jnp.einsum("ife,de->ifd", tensor, weight, preferred_element_type=jnp.float32)


def weight_grad(left, right):
    return jnp.einsum("ifd,ife->de", left, right, preferred_element_type=jnp.float32)


def frames_split(
    frames_in,
    cond,
    text,
    item_lengths,
    text_lengths,
    ada_weight,
    qkv_weight,
    out_weight,
    cross_q_weight,
    cross_kv_weight,
    cross_out_weight,
    up_weight,
    down_weight,
    cotangent,
):
    model_width = frames_in.shape[-1]
    score_scale = (model_width // H) ** (-0.5)
    cond_f = cond.astype(jnp.float32)
    low_cond = jax.nn.silu(cond_f).astype(jnp.bfloat16)
    modulation = jnp.dot(low_cond, ada_weight, preferred_element_type=jnp.float32)
    pieces = [
        modulation[:, None, position * model_width : (position + 1) * model_width]
        for position in range(9)
    ]
    shift_a, scale_a, gate_a, shift_b, scale_b, gate_b, shift_c, scale_c, gate_c = pieces
    residual_in = frames_in.astype(jnp.float32)
    normed_a, inverse_a = norm_parts(residual_in)
    hidden_a = (normed_a * (1.0 + scale_a) + shift_a).astype(jnp.bfloat16)
    qkv = project(hidden_a, qkv_weight).astype(jnp.bfloat16)
    queries = qkv[..., :model_width]
    keys_own = qkv[..., model_width : 2 * model_width]
    values_own = qkv[..., 2 * model_width :]
    keys_all, values_all = (
        lax.all_gather(keys_own, "frames", axis=1, tiled=True),
        lax.all_gather(values_own, "frames", axis=1, tiled=True),
    )
    key_valid = jnp.arange(keys_all.shape[1], dtype=jnp.int32)[None, :] < item_lengths[:, None]
    attn_prob, low_prob, attended, self_total = attend(
        queries, keys_all, values_all, key_valid, score_scale
    )
    branch_a = project(attended, out_weight)
    first = residual_in + gate_a * branch_a
    normed_b, inverse_b = norm_parts(first)
    hidden_b = (normed_b * (1.0 + scale_b) + shift_b).astype(jnp.bfloat16)
    cross_q = project(hidden_b, cross_q_weight).astype(jnp.bfloat16)
    text_own = project(text, cross_kv_weight).astype(jnp.bfloat16)
    text_kv = lax.all_gather(text_own, "frames", axis=1, tiled=True)
    text_keys = text_kv[..., :model_width]
    text_values = text_kv[..., model_width:]
    text_valid = jnp.arange(text_kv.shape[1], dtype=jnp.int32)[None, :] < text_lengths[:, None]
    cross_prob, cross_low, crossed, cross_total = attend(
        cross_q, text_keys, text_values, text_valid, score_scale
    )
    branch_b = project(crossed, cross_out_weight)
    second = first + gate_b * branch_b
    normed_c, inverse_c = norm_parts(second)
    hidden_c = (normed_c * (1.0 + scale_c) + shift_c).astype(jnp.bfloat16)
    up_proj = project(hidden_c, up_weight)
    activated, gelu_back = jax.vjp(partial(jax.nn.gelu, approximate=False), up_proj)
    low_act = activated.astype(jnp.bfloat16)
    branch_c = project(low_act, down_weight)
    layer_out = (second + gate_c * branch_c).astype(jnp.bfloat16)
    upstream = cotangent.astype(jnp.float32)
    d_gate_c = jnp.sum(upstream * branch_c, 1)
    d_branch_c = (upstream * gate_c).astype(jnp.bfloat16)
    grad_down = weight_grad(low_act, d_branch_c)
    d_up = gelu_back(project_back(d_branch_c, down_weight))[0].astype(jnp.bfloat16)
    grad_up = weight_grad(hidden_c, d_up)
    d_hidden_c = project_back(d_up, up_weight)
    d_shift_c = jnp.sum(d_hidden_c, 1)
    d_scale_c = jnp.sum(d_hidden_c * normed_c, 1)
    upstream = upstream + norm_back(normed_c, inverse_c, d_hidden_c * (1.0 + scale_c))
    d_gate_b = jnp.sum(upstream * branch_b, 1)
    d_branch_b = (upstream * gate_b).astype(jnp.bfloat16)
    grad_cross_out = weight_grad(crossed, d_branch_b)
    d_crossed = project_back(d_branch_b, cross_out_weight).astype(jnp.bfloat16)
    d_cross_q, d_text_keys, d_text_values = attend_back(
        d_crossed, cross_q, text_keys, text_values, cross_prob, cross_low, score_scale
    )
    d_cross_q = d_cross_q.astype(jnp.bfloat16)
    grad_cross_q = weight_grad(hidden_b, d_cross_q)
    d_hidden_b = project_back(d_cross_q, cross_q_weight)
    d_text_local = jnp.concatenate([d_text_keys, d_text_values], -1)
    d_shift_b = jnp.sum(d_hidden_b, 1)
    d_scale_b = jnp.sum(d_hidden_b * normed_b, 1)
    upstream = upstream + norm_back(normed_b, inverse_b, d_hidden_b * (1.0 + scale_b))
    d_gate_a = jnp.sum(upstream * branch_a, 1)
    d_branch_a = (upstream * gate_a).astype(jnp.bfloat16)
    grad_out = weight_grad(attended, d_branch_a)
    d_attended = project_back(d_branch_a, out_weight).astype(jnp.bfloat16)
    keys_back, values_back = (
        lax.all_gather(keys_own, "frames", axis=1, tiled=True),
        lax.all_gather(values_own, "frames", axis=1, tiled=True),
    )
    d_queries, d_keys_all, d_values_all = attend_back(
        d_attended, queries, keys_back, values_back, attn_prob, low_prob, score_scale
    )
    d_keys, d_values = (
        lax.psum_scatter(
            d_keys_all.astype(jnp.bfloat16), "frames", scatter_dimension=1, tiled=True
        ).astype(jnp.float32),
        lax.psum_scatter(
            d_values_all.astype(jnp.bfloat16), "frames", scatter_dimension=1, tiled=True
        ).astype(jnp.float32),
    )
    d_qkv = jnp.concatenate(
        [
            d_queries.astype(jnp.bfloat16),
            d_keys.astype(jnp.bfloat16),
            d_values.astype(jnp.bfloat16),
        ],
        -1,
    )
    grad_qkv = weight_grad(hidden_a, d_qkv)
    d_hidden_a = project_back(d_qkv, qkv_weight)
    d_shift_a = jnp.sum(d_hidden_a, 1)
    d_scale_a = jnp.sum(d_hidden_a * normed_a, 1)
    input_grad = upstream + norm_back(normed_a, inverse_a, d_hidden_a * (1.0 + scale_a))
    d_modulation = jnp.concatenate(
        [
            d_shift_a,
            d_scale_a,
            d_gate_a,
            d_shift_b,
            d_scale_b,
            d_gate_b,
            d_shift_c,
            d_scale_c,
            d_gate_c,
        ],
        -1,
    )
    grad_ada = jnp.dot(
        low_cond.astype(jnp.float32).T,
        d_modulation,
        precision=lax.Precision.HIGHEST,
        preferred_element_type=jnp.float32,
    )
    sigmoid_c = jax.nn.sigmoid(cond_f)
    cond_part = jnp.dot(
        d_modulation,
        ada_weight.T,
        precision=lax.Precision.HIGHEST,
        preferred_element_type=jnp.float32,
    ) * (sigmoid_c * (1.0 + cond_f * (1.0 - sigmoid_c)))
    d_text_kv, cond_grad = (
        lax.psum_scatter(d_text_local, "frames", scatter_dimension=1, tiled=True),
        lax.psum_scatter(cond_part, "frames", scatter_dimension=1, tiled=True),
    )
    low_text_kv = d_text_kv.astype(jnp.bfloat16)
    grad_cross_kv = weight_grad(text, low_text_kv)
    text_grad = project_back(low_text_kv, cross_kv_weight)
    grads = (
        grad_ada,
        grad_qkv,
        grad_out,
        grad_cross_q,
        grad_cross_kv,
        grad_cross_out,
        grad_up,
        grad_down,
    )
    partial_sums = (
        lax.psum_scatter(
            grads[0].astype(jnp.bfloat16), "frames", scatter_dimension=1, tiled=True
        ).astype(jnp.float32),
        lax.psum_scatter(
            grads[1].astype(jnp.bfloat16), "frames", scatter_dimension=1, tiled=True
        ).astype(jnp.float32),
        lax.psum_scatter(
            grads[2].astype(jnp.bfloat16), "frames", scatter_dimension=1, tiled=True
        ).astype(jnp.float32),
        lax.psum_scatter(
            grads[3].astype(jnp.bfloat16), "frames", scatter_dimension=1, tiled=True
        ).astype(jnp.float32),
        lax.psum_scatter(
            grads[4].astype(jnp.bfloat16), "frames", scatter_dimension=1, tiled=True
        ).astype(jnp.float32),
        lax.psum_scatter(
            grads[5].astype(jnp.bfloat16), "frames", scatter_dimension=1, tiled=True
        ).astype(jnp.float32),
        lax.psum_scatter(
            grads[6].astype(jnp.bfloat16), "frames", scatter_dimension=1, tiled=True
        ).astype(jnp.float32),
        lax.psum_scatter(
            grads[7].astype(jnp.bfloat16), "frames", scatter_dimension=1, tiled=True
        ).astype(jnp.float32),
    )
    totals = (
        lax.psum_scatter(
            partial_sums[0].astype(jnp.bfloat16), "items", scatter_dimension=0, tiled=True
        ).astype(jnp.float32),
        lax.psum_scatter(
            partial_sums[1].astype(jnp.bfloat16), "items", scatter_dimension=0, tiled=True
        ).astype(jnp.float32),
        lax.psum_scatter(
            partial_sums[2].astype(jnp.bfloat16), "items", scatter_dimension=0, tiled=True
        ).astype(jnp.float32),
        lax.psum_scatter(
            partial_sums[3].astype(jnp.bfloat16), "items", scatter_dimension=0, tiled=True
        ).astype(jnp.float32),
        lax.psum_scatter(
            partial_sums[4].astype(jnp.bfloat16), "items", scatter_dimension=0, tiled=True
        ).astype(jnp.float32),
        lax.psum_scatter(
            partial_sums[5].astype(jnp.bfloat16), "items", scatter_dimension=0, tiled=True
        ).astype(jnp.float32),
        lax.psum_scatter(
            partial_sums[6].astype(jnp.bfloat16), "items", scatter_dimension=0, tiled=True
        ).astype(jnp.float32),
        lax.psum_scatter(
            partial_sums[7].astype(jnp.bfloat16), "items", scatter_dimension=0, tiled=True
        ).astype(jnp.float32),
    )
    return (
        layer_out,
        input_grad,
        text_grad,
        cond_grad,
        totals[0],
        totals[1],
        totals[2],
        totals[3],
        totals[4],
        totals[5],
        totals[6],
        totals[7],
    )


LOG2E = 1.4426950408889634
BF = jnp.bfloat16
F32 = jnp.float32
PACK = 384
FIN = 2
LIMIT = 60 * 2**20


def nn(left, right):
    return jnp.dot(left, right, preferred_element_type=F32)


def nt(left, right):
    return lax.dot_general(left, right, (((1,), (1,)), ((), ())), preferred_element_type=F32)


def tn(left, right):
    return lax.dot_general(left, right, (((0,), (0,)), ((), ())), preferred_element_type=F32)


def ln_parts(rows):
    share = 1.0 / rows.shape[-1]
    centered = rows - jnp.sum(rows, -1, keepdims=True) * share
    inverse = lax.rsqrt(jnp.sum(centered * centered, -1, keepdims=True) * share + 1e-06)
    return centered * inverse, inverse


def ln_back(normed, inverse, incoming):
    share = 1.0 / normed.shape[-1]
    mean_in = jnp.sum(incoming, -1, keepdims=True) * share
    mean_dot = jnp.sum(incoming * normed, -1, keepdims=True) * share
    return inverse * (incoming - mean_in - normed * mean_dot)


def gelu_parts(value):
    size = jnp.abs(value)
    inner = 1.0 / (1.0 + (0.3275911 * 0.7071067811865476) * size)
    series = inner * (
        0.5 * 0.254829592
        + inner
        * (
            0.5 * -0.284496736
            + inner * (0.5 * 1.421413741 + inner * (0.5 * -1.453152027 + inner * (0.5 * 1.061405429)))
        )
    )
    bell = jnp.exp2(value * value * (-0.5 * LOG2E))
    tail = series * bell
    below = jnp.where(value >= 0.0, 1.0 - tail, tail)
    return below, below + value * bell * 0.3989422804014327


def strips(body, *arrays, rows=16):
    made = [body(*(array[at : at + rows] for array in arrays)) for at in range(0, arrays[0].shape[0], rows)]
    if not isinstance(made[0], tuple):
        return jnp.concatenate(made, 0)
    return tuple(jnp.concatenate(column, 0) for column in zip(*made))


def fold(rows):
    return jnp.sum(rows.reshape(rows.shape[0] // 8, 8, rows.shape[1]), 0)


def modulate(rows, shift, scale):
    normed, _ = ln_parts(rows.astype(F32))
    return (normed * (1.0 + scale) + shift).astype(BF)


class Columns:
    def __init__(self, count):
        self.parts = [None] * count

    def add(self, at, rows):
        made = fold(rows)
        self.parts[at] = made if self.parts[at] is None else self.parts[at] + made

    def total(self, at):
        return jnp.sum(self.parts[at], 0, keepdims=True)


def lane_half(half):
    lane = lax.broadcasted_iota(jnp.int32, (1, 128), 1)
    return lane < 64 if half == 0 else lane >= 64


def keep_half(rows, half):
    return jnp.where(lane_half(half), rows, jnp.zeros_like(rows))


def pack_square(acc, item, ra, cb, col):
    first = acc[pl.ds(pl.multiple_of(item * ra, 16), ra // 2), col : col + cb]
    second = acc[pl.ds(pl.multiple_of(item * ra + ra // 2, 16), ra // 2), col : col + cb]
    return jnp.concatenate([first, second], 1).astype(BF)


def store_block(value, part, frame, me, row, keep_ref, send_ref):
    place = frame ^ me

    @pl.when(place & 1 == 0)
    def _():
        keep_ref[part, place >> 1, row : row + value.shape[0]] = value

    @pl.when(place & 1 == 1)
    def _():
        send_ref[part, place >> 1, row : row + value.shape[0]] = value


def start_kernel(where, lengths, text_lengths, table, *, items, nf):
    per = items // nf
    me = where[0]
    table[0] = me
    table[1] = where[1]
    at = 2 + 3 * per
    for i in range(items):
        rank = jnp.int32(0)
        for j in range(items):
            if j < i:
                ahead = lengths[j] >= lengths[i]
            elif j > i:
                ahead = lengths[j] > lengths[i]
            else:
                continue
            rank = rank + ahead.astype(jnp.int32)
        turn, seat = rank // nf, rank % nf
        device = jnp.where(turn % 2 == 0, seat, nf - 1 - seat)
        table[at + i] = device
        table[at + items + i] = turn
        table[at + 2 * items + device * per + turn] = i
    for slot in range(per):
        item = table[at + 2 * items + me * per + slot]
        table[2 + slot] = item
        table[2 + per + slot] = lengths[item]
        table[2 + 2 * per + slot] = text_lengths[item]


def copy_kernel(table, source, out):
    out[...] = source[...]


def gather_kernel(table, *refs, per):
    rows, texts, cots, mixed, cot = refs[0], refs[1 : 1 + per], refs[1 + per : 1 + 2 * per], refs[-2], refs[-1]
    block, short = rows.shape[1], texts[0].shape[1]
    mixed[0, :block] = rows[0]
    for slot in range(per):
        mixed[0, block + slot * short : block + (slot + 1) * short] = texts[slot][0]
        cot[0, slot] = cots[slot][0]


def gate_kernel(*refs):
    pass


def soften(scores):
    top = jnp.max(scores, 1, keepdims=True)
    return jnp.exp2(scores - top).astype(BF), top


def soft_back(scores, d_prob, lse, delta):
    prob = jnp.exp2(scores - lse)
    return prob.astype(BF), (prob * (d_prob - delta)).astype(BF)


def self_fwd_kernel(
    table, x_ref, mod_ref, w_ref, *refs, blocks, qb, score_scale, length_at
):
    rows_ref, qkv_ref, att_ref, lse_ref, held = refs[-5:]
    step = pl.program_id(0)
    width = rows_ref.shape[-1]
    count = att_ref.shape[1]
    block = rows_ref.shape[1]
    pairs = H // 2

    @pl.when(step < blocks)
    def _():
        rows_ref[0] = x_ref[0]
        shift, scale = mod_ref[0, 0:1], mod_ref[0, 1:2]
        hidden = strips(lambda rows: modulate(rows, shift, scale), x_ref[0])
        at = pl.ds(pl.multiple_of(step * block, block), block)
        for part in range(3):
            made = nn(hidden, w_ref[:, part * width : (part + 1) * width])
            if part == 0:
                made = made * (score_scale * LOG2E)
            made = made.astype(BF)
            qkv_ref[0, :, part * width : (part + 1) * width] = made
            for pair in range(pairs):
                held[part * pairs + pair, at] = made[:, pair * 128 : pair * 128 + 128]

    for klen in (count // 4, count // 2, count):

        @pl.when((step >= blocks) & (table[length_at] == klen))
        def _(klen=klen):
            pair = step - blocks
            keys = held[pairs + pair, :klen]
            values = jnp.concatenate([held[2 * pairs + pair, :klen], jnp.ones((klen, 128), BF)], 1)

            def inner(position, carry):
                rows = pl.ds(pl.multiple_of(position * qb, qb), qb)
                queries = held[pair, rows]
                outs = []
                for half in (0, 1):
                    prob, top = strips(soften, nt(keep_half(queries, half), keys))
                    mixed = nn(prob, values)
                    total = mixed[:, 128:]
                    lse_ref[0, 0, half : half + 1, rows] = (top + jnp.log2(total[:, :1])).T
                    outs.append(mixed[:, :128] / total)
                att_ref[0, rows] = jnp.where(lane_half(0), outs[0], outs[1]).astype(BF)
                return carry

            lax.fori_loop(0, count // qb, inner, 0)


def self_bwd_kernel(
    table, q_ref, k_ref, v_ref, o_ref, do_ref, lse_ref, x_ref, g1_ref, mod_ref, w_ref, *refs,
    slot, length_at, pairs, blocks, qb, score_scale, nf, ni, last,
):
    if last:
        d_early, x_early, mod_early, dx_ref, dmod_ref, keep_ref, send_ref, held, dk_acc, dv_acc, acc = refs
    else:
        text_ref, dx_ref, dmod_ref, d_out, held, dk_acc, dv_acc = refs
    step = pl.program_id(0)
    count = q_ref.shape[1]
    width = x_ref.shape[-1]
    block = x_ref.shape[1]
    used = table[length_at]
    for klen in (count // 4, count // 2, count):

        @pl.when((step < pairs) & (used == klen))
        def _(klen=klen):
            keys = k_ref[0, :klen]
            values = v_ref[0, :klen]
            dk_acc[:klen] = jnp.zeros((klen, 128), F32)
            dv_acc[:klen] = jnp.zeros((klen, 128), F32)

            def inner(position, carry):
                rows = pl.ds(pl.multiple_of(position * qb, qb), qb)
                queries = q_ref[0, rows]
                grad = do_ref[0, rows]
                dots = (grad.astype(F32) * o_ref[0, rows].astype(F32)).T
                d_queries = []
                for half in (0, 1):
                    q_half = keep_half(queries, half)
                    grad_half = keep_half(grad, half)
                    delta = jnp.sum(dots[64 * half : 64 * half + 64], 0, keepdims=True)
                    lse = lse_ref[0, 0, half : half + 1, rows]
                    prob, d_scores = strips(
                        partial(soft_back, lse=lse, delta=delta), nt(keys, q_half), nt(values, grad_half)
                    )
                    dv_acc[:klen] += nn(prob, grad_half)
                    dk_acc[:klen] += nn(d_scores, q_half)
                    d_queries.append(tn(d_scores, keys))
                held[step, rows] = (jnp.where(lane_half(0), d_queries[0], d_queries[1]) * score_scale).astype(BF)
                return carry

            lax.fori_loop(0, count // qb, inner, 0)
            held[pairs + step, :klen] = (dk_acc[:klen] * (1.0 / LOG2E)).astype(BF)
            held[2 * pairs + step, :klen] = dv_acc[:klen].astype(BF)
            if klen < count:
                held[pairs + step, klen:] = jnp.zeros((count - klen, 128), BF)
                held[2 * pairs + step, klen:] = jnp.zeros((count - klen, 128), BF)

    @pl.when(step == pairs)
    def _():
        dmod_ref[...] = jnp.zeros_like(dmod_ref)
        if last:
            acc[...] = jnp.zeros_like(acc)

    @pl.when((step >= pairs) & (step < pairs + blocks))
    def _():
        rows = pl.ds(pl.multiple_of((step - pairs) * block, block), block)
        d_qkv = jnp.concatenate([held[at, rows] for at in range(3 * pairs)], 1)
        shift, scale = mod_ref[0, 0:1], mod_ref[0, 1:2]
        d_hidden = nt(d_qkv, w_ref[...])
        sums = Columns(2)

        def leave(x, dh, upstream):
            normed, inverse = ln_parts(x.astype(F32))
            sums.add(0, dh)
            sums.add(1, dh * normed)
            out = upstream.astype(F32) + ln_back(normed, inverse, dh * (1.0 + scale))
            return out.astype(BF), (normed * (1.0 + scale) + shift).astype(BF)

        dx_ref[0, :block], hidden = strips(leave, x_ref[0], d_hidden, g1_ref[0])
        for at in range(2):
            dmod_ref[0, at : at + 1] += sums.total(at)
        if last:
            acc[...] += tn(hidden, d_qkv)
        else:
            d_out[...] = d_qkv
            short = text_ref.shape[2]
            for part in range(text_ref.shape[1]):
                dx_ref[0, block + part * short : block + (part + 1) * short] = text_ref[0, part]

    if last:

        @pl.when((step >= pairs + blocks) & (step < pairs + 2 * blocks))
        def _():
            shift, scale = mod_early[0, 0:1], mod_early[0, 1:2]
            hidden = strips(lambda rows: modulate(rows, shift, scale), x_early[0])
            acc[...] += tn(hidden, d_early[...])

        @pl.when(step >= pairs + 2 * blocks)
        def _():
            ra, cb = width // ni, 3 * width // nf
            for part in range(FIN):
                item = ((step - pairs - 2 * blocks) * FIN + part) ^ table[1]
                for frame in range(nf):
                    cut = acc[pl.ds(pl.multiple_of(item * ra, 16), ra), frame * cb : (frame + 1) * cb].astype(BF)
                    rest = jnp.concatenate([cut[: ra // 2, PACK:], cut[ra // 2 :, PACK:]], 1)
                    store_block(
                        jnp.concatenate([cut[:, :PACK], rest], 0), part, frame, table[0], 0, keep_ref, send_ref
                    )


def cross_kernel(
    table, att_ref, x_ref, mod_ref, text_ref, wkv_ref, wo_ref, wq_ref, wco_ref,
    kv_ref, text_rows, first_ref, second_ref, ba_ref, bb_ref, cq_ref, cr_ref, lse_ref, *, score_scale, length_at,
):
    width = x_ref.shape[-1]
    slots = kv_ref.shape[1]
    used = table[length_at + pl.program_id(0)]

    @pl.when(pl.program_id(1) == 0)
    def _():
        text_rows[0] = jnp.concatenate([text_ref[at] for at in range(text_ref.shape[0])], 0)
        kv_ref[0] = nn(text_rows[0], wkv_ref[...]).astype(BF)

    branch_a = nn(att_ref[0], wo_ref[...])
    gate_a, gate_b, shift, scale = mod_ref[0, 2:3], mod_ref[0, 5:6], mod_ref[0, 3:4], mod_ref[0, 4:5]

    def enter(rows, branch):
        first = rows.astype(F32) + gate_a * branch
        return branch.astype(BF), first, modulate(first, shift, scale)

    ba_ref[0], first, hidden = strips(enter, x_ref[0], branch_a)
    first_ref[0] = first.astype(BF)
    cq_ref[0] = (nn(hidden, wq_ref[...]) * (score_scale * LOG2E)).astype(BF)
    valid = lax.broadcasted_iota(jnp.int32, (1, slots), 1) < used
    ones = jnp.ones((slots, 128), BF)
    for pair in range(H // 2):
        cols = slice(pair * 128, pair * 128 + 128)
        queries = cq_ref[0, :, cols]
        keys = kv_ref[0, :, cols]
        values = jnp.concatenate([kv_ref[0, :, width + pair * 128 : width + pair * 128 + 128], ones], 1)
        outs = []
        for half in (0, 1):
            prob, top = strips(
                lambda scores: soften(jnp.where(valid, scores, -1e30)), nt(keep_half(queries, half), keys)
            )
            mixed = nn(prob, values)
            total = mixed[:, 128:]
            lse_ref[0, pair, half : half + 1] = (top + jnp.log2(total[:, :1])).T
            outs.append(mixed[:, :128] / total)
        cr_ref[0, :, cols] = jnp.where(lane_half(0), outs[0], outs[1]).astype(BF)
    branch_b = nn(cr_ref[0], wco_ref[...])
    bb_ref[0], second_ref[0] = strips(
        lambda rows, branch: (branch.astype(BF), (rows + gate_b * branch).astype(BF)), first, branch_b
    )


def mlp_kernel(
    table, second_ref, cot_ref, mod_ref, wup_ref, wdn_ref,
    out_ref, g2_ref, dmod_ref, gw_ref, up_acc, dn_acc, *, blocks, total, chunk, nf, ni,
):
    step = pl.program_id(0)
    width = second_ref.shape[-1]
    ff = wup_ref.shape[-1]

    @pl.when(step == 0)
    def _():
        up_acc[...] = jnp.zeros_like(up_acc)
        dn_acc[...] = jnp.zeros_like(dn_acc)

    @pl.when(step < total)
    def _():
        shift, scale, gate = mod_ref[0, 6:7], mod_ref[0, 7:8], mod_ref[0, 8:9]
        hidden = strips(lambda rows: modulate(rows, shift, scale), second_ref[0])
        d_branch = strips(lambda rows: (rows.astype(F32) * gate).astype(BF), cot_ref[0, 0])
        branch = jnp.zeros(second_ref.shape[1:], F32)
        d_hidden = jnp.zeros(second_ref.shape[1:], F32)

        def middle(up_proj, d_act):
            below, slope = gelu_parts(up_proj)
            return (up_proj * below).astype(BF), (d_act * slope).astype(BF)

        for at in range(0, ff, chunk):
            cols = slice(at, at + chunk)
            act, d_up = strips(middle, nn(hidden, wup_ref[:, cols]), nt(d_branch, wdn_ref[cols]))
            branch += nn(act, wdn_ref[cols])
            d_hidden += nt(d_up, wup_ref[:, cols])
            dn_acc[cols] += tn(act, d_branch)
            up_acc[:, cols] += tn(hidden, d_up)

        @pl.when(step % blocks == 0)
        def _():
            dmod_ref[...] = jnp.zeros_like(dmod_ref)

        sums = Columns(3)

        def leave(second, cot, branch_rows, dh):
            second = second.astype(F32)
            normed, inverse = ln_parts(second)
            upstream = cot.astype(F32)
            sums.add(0, dh)
            sums.add(1, dh * normed)
            sums.add(2, upstream * branch_rows)
            upstream = upstream + ln_back(normed, inverse, dh * (1.0 + scale))
            return (second + gate * branch_rows).astype(BF), upstream.astype(BF)

        out_ref[0, 0], g2_ref[0] = strips(leave, second_ref[0], cot_ref[0, 0], branch, d_hidden)
        for at in range(3):
            dmod_ref[0, at : at + 1] += sums.total(at)

    @pl.when(step >= total)
    def _():
        ra, cb = width // ni, ff // nf
        for part in range(FIN):
            item = (step - total) * FIN + part
            for frame in range(nf):
                cut = up_acc[pl.ds(pl.multiple_of(item * ra, 16), ra), frame * cb : (frame + 1) * cb].astype(BF)
                gw_ref[part, frame, :ra] = cut[:, :PACK]
                gw_ref[part, frame, ra : 2 * ra] = cut[:, PACK:]
                gw_ref[part, frame, 2 * ra :] = pack_square(
                    dn_acc, item, ff // ni, width // nf, frame * (width // nf)
                )


def cross_back_kernel(
    table, g2_ref, bb_ref, cr_ref, cq_ref, att_ref, ba_ref, first_ref, mod_ref, kv_ref, lse_ref, text_ref,
    wo_ref, wq_ref, wco_ref, wkv_ref,
    g1_ref, datt_ref, text_out, dmod_ref, keep_ref, send_ref,
    o_acc, q_acc, co_acc, kv_acc, dtext, *, blocks, total, score_scale, nf, ni, length_at,
):
    step = pl.program_id(0)
    width = g2_ref.shape[-1]
    slots = kv_ref.shape[1]

    @pl.when(step == 0)
    def _():
        o_acc[...] = jnp.zeros_like(o_acc)
        q_acc[...] = jnp.zeros_like(q_acc)
        co_acc[...] = jnp.zeros_like(co_acc)
        kv_acc[...] = jnp.zeros_like(kv_acc)

    @pl.when(step < total)
    def _():
        @pl.when(step % blocks == 0)
        def _():
            dmod_ref[...] = jnp.zeros_like(dmod_ref)
            dtext[...] = jnp.zeros_like(dtext)

        used = table[length_at + step // blocks]
        gate_b = mod_ref[0, 5:6]
        sums = Columns(4)

        def enter(upstream, branch):
            upstream = upstream.astype(F32)
            sums.add(3, upstream * branch.astype(F32))
            return (upstream * gate_b).astype(BF)

        d_branch_b = strips(enter, g2_ref[0], bb_ref[0])
        co_acc[...] += tn(cr_ref[0], d_branch_b)
        d_crossed = nt(d_branch_b, wco_ref[...])
        slot_of = lax.broadcasted_iota(jnp.int32, (slots, 1), 0)
        parts = []
        for pair in range(H // 2):
            cols = slice(pair * 128, pair * 128 + 128)
            vcols = slice(width + pair * 128, width + pair * 128 + 128)
            queries = cq_ref[0, :, cols]
            keys = kv_ref[0, :, cols]
            values = kv_ref[0, :, vcols]
            grad = d_crossed[:, cols].astype(BF)
            dots = (grad.astype(F32) * cr_ref[0, :, cols].astype(F32)).T
            d_queries = []
            d_keys = 0.0
            d_values = 0.0
            for half in (0, 1):
                q_half = keep_half(queries, half)
                grad_half = keep_half(grad, half)
                delta = jnp.sum(dots[64 * half : 64 * half + 64], 0, keepdims=True)
                lse = lse_ref[0, pair, half : half + 1]

                def back(scores, d_prob, at, lse=lse, delta=delta):
                    return soft_back(jnp.where(at < used, scores, -1e30), d_prob, lse, delta)

                prob, d_scores = strips(back, nt(keys, q_half), nt(values, grad_half), slot_of)
                d_values += nn(prob, grad_half)
                d_keys += nn(d_scores, q_half)
                d_queries.append(tn(d_scores, keys))
            dtext[:, cols] += d_keys * (1.0 / LOG2E)
            dtext[:, vcols] += d_values
            parts.append((jnp.where(lane_half(0), d_queries[0], d_queries[1]) * score_scale).astype(BF))
        d_cq = jnp.concatenate(parts, 1)
        shift, scale, gate = mod_ref[0, 3:4], mod_ref[0, 4:5], mod_ref[0, 2:3]
        d_hidden = nt(d_cq, wq_ref[...])

        def leave(first, dh, upstream, branch):
            normed, inverse = ln_parts(first.astype(F32))
            sums.add(1, dh)
            sums.add(2, dh * normed)
            upstream = upstream.astype(F32) + ln_back(normed, inverse, dh * (1.0 + scale))
            sums.add(0, upstream * branch.astype(F32))
            return (normed * (1.0 + scale) + shift).astype(BF), upstream.astype(BF), (upstream * gate).astype(BF)

        hidden, g1_ref[0], d_branch_a = strips(leave, first_ref[0], d_hidden, g2_ref[0], ba_ref[0])
        for at in range(4):
            dmod_ref[0, at : at + 1] += sums.total(at)
        datt_ref[0] = nt(d_branch_a, wo_ref[...]).astype(BF)
        q_acc[...] += tn(hidden, d_cq)
        o_acc[...] += tn(att_ref[0], d_branch_a)

        @pl.when(step % blocks == blocks - 1)
        def _():
            low = dtext[...].astype(BF)
            kv_acc[...] += tn(text_ref[0], low)
            made = nt(low, wkv_ref[...]).astype(BF)
            short = text_out.shape[2]
            for frame in range(nf):
                text_out[frame, 0] = made[frame * short : (frame + 1) * short]

    @pl.when(step >= total)
    def _():
        ra, cb = width // ni, width // nf
        half = ra // 2
        for part in range(FIN):
            item = ((step - total) * FIN + part) ^ table[1]
            for frame in range(nf):
                for place, acc in enumerate((o_acc, q_acc, co_acc)):
                    cut = pack_square(acc, item, ra, cb, frame * cb)
                    store_block(cut, part, frame, table[0], place * half, keep_ref, send_ref)
                cut = kv_acc[pl.ds(pl.multiple_of(item * ra, 16), ra), 2 * frame * cb : 2 * (frame + 1) * cb].astype(BF)
                store_block(cut, part, frame, table[0], 3 * half, keep_ref, send_ref)


def deal_kernel(table, *refs, at, items, group):
    out_ref = refs[-1]
    count = (len(refs) - 1) // group
    for part in range(group):
        sources = refs[part * count : (part + 1) * count]
        if count == 1:
            out_ref[part] = sources[0][0, 0].astype(out_ref.dtype)
            continue
        slot_of = table[at + items + pl.program_id(0) * group + part]
        for slot, ref in enumerate(sources):

            @pl.when(slot_of == slot)
            def _(ref=ref, part=part):
                out_ref[part] = ref[0, 0].astype(out_ref.dtype)


def land_kernel(keep, got, *refs):
    outs = refs[-2:]
    for half, out in enumerate(outs):
        out[...] = (keep[0, half].astype(F32) + got[0, half].astype(F32)).astype(BF)[None]


def finish_mlp_kernel(sum_ref, *refs):
    up, down = refs[-2:]
    ra, cb = up.shape
    up[:, : cb // 2] = sum_ref[:ra].astype(F32)
    up[:, cb // 2 :] = sum_ref[ra : 2 * ra].astype(F32)
    down[...] = untall(sum_ref[2 * ra :].astype(F32))


def finish_mid_kernel(keep, got, *refs):
    outs = refs[-4:]
    half = outs[0].shape[0] // 2
    total = keep[...].astype(F32) + got[...].astype(F32)
    for place in range(3):
        outs[place][...] = untall(total[place * half : (place + 1) * half])
    outs[3][...] = total[3 * half :]


def finish_qkv_kernel(keep, got, *refs):
    out = refs[-1]
    ra = out.shape[0]
    total = keep[...].astype(F32) + got[...].astype(F32)
    out[:, :PACK] = total[:ra]
    out[:, PACK:] = untall(total[ra:])


def untall(block):
    half = block.shape[1] // 2
    return jnp.concatenate([block[:, :half], block[:, half:]], 0)


def cost(flops, moved, exps=0):
    return pl.CostEstimate(flops=int(flops), bytes_accessed=int(moved), transcendentals=int(exps))


def params():
    return pltpu.CompilerParams(vmem_limit_bytes=LIMIT)


def whole(shape):
    return pl.BlockSpec(shape, lambda *_: (0,) * len(shape), pipeline_mode=pl.Buffered(1))


def run(kernel, name, grid, in_specs, args, out_specs, out_shape, scratch=(), deps=(), work=None, aliases=None):
    inputs = len(args)

    def body(*refs):
        kernel(*refs[:inputs], *refs[inputs + len(deps) :])

    return pl.pallas_call(
        body,
        grid_spec=pltpu.PrefetchScalarGridSpec(
            num_scalar_prefetch=1,
            grid=grid,
            in_specs=list(in_specs) + [pl.BlockSpec(memory_space=pl.ANY)] * len(deps),
            out_specs=out_specs,
            scratch_shapes=list(scratch),
        ),
        out_shape=out_shape,
        input_output_aliases=aliases or {},
        compiler_params=params(),
        cost_estimate=work,
        name=name,
    )(*args, *deps)


def any_spec(count):
    return [pl.BlockSpec(memory_space=pl.ANY)] * count


def struct(shape, dtype):
    return jax.ShapeDtypeStruct(shape, dtype)


def start_call(where, lengths, text_lengths, items, nf):
    size = 2 + 3 * (items // nf) + 3 * items
    smem = pl.BlockSpec(memory_space=pltpu.SMEM)
    return pl.pallas_call(
        partial(start_kernel, items=items, nf=nf),
        in_specs=[smem] * 3,
        out_specs=smem,
        out_shape=struct((size,), jnp.int32),
        name="start",
    )(where, lengths, text_lengths)


def gather_first_call(table, rows, nf):
    items, block, width = rows.shape
    per = items // nf
    at = 2 + 3 * per + 2 * items
    return run(
        copy_kernel,
        "gather_first",
        (nf,),
        [pl.BlockSpec((1, block, width), lambda t, s: (s[at + t * per], 0, 0))],
        (table, rows),
        pl.BlockSpec((1, block, width), lambda t, s: (t, 0, 0)),
        struct((nf, block, width), BF),
    )


def gather_call(table, rows, text, cot, nf):
    items, block, width = rows.shape
    per = items // nf
    at = 2 + 3 * per + 2 * items
    short = text.shape[1]

    def source(size, slot):
        return pl.BlockSpec((1, size, width), lambda t, s: (s[at + t * per + slot], 0, 0))

    return run(
        partial(gather_kernel, per=per),
        "gather",
        (nf,),
        [source(block, 1)] + [source(short, slot) for slot in range(per)] + [source(block, slot) for slot in range(per)],
        (table, rows) + (text,) * per + (cot,) * per,
        [
            pl.BlockSpec((1, block + per * short, width), lambda t, s: (t, 0, 0)),
            pl.BlockSpec((1, per, block, width), lambda t, s: (t, 0, 0, 0)),
        ],
        [struct((nf, block + per * short, width), BF), struct((nf, per, block, width), BF)],
    )


def gate_call(arrays, deps):
    return pl.pallas_call(
        gate_kernel,
        in_specs=any_spec(len(arrays) + len(deps)),
        out_specs=any_spec(len(arrays)),
        out_shape=[struct(array.shape, array.dtype) for array in arrays],
        input_output_aliases={at: at for at in range(len(arrays))},
        compiler_params=params(),
        name="gate",
    )(*arrays, *deps)


def halves(ni, nf, depth, total):
    spec = pl.BlockSpec((FIN, nf // 2, depth, PACK), lambda t, s: (jnp.maximum(t - total, 0), 0, 0, 0))
    return [spec] * 2, [struct((ni, nf // 2, depth, PACK), BF)] * 2


def self_fwd_call(table, slot, rows, mod, weight, kept, per, block, qb, score_scale, deps):
    blocks, _, width = rows.shape
    count = blocks * block
    pairs = H // 2

    def early(t):
        return jnp.minimum(t, blocks - 1)

    def late(t):
        return jnp.maximum(t - blocks, 0)

    return run(
        partial(self_fwd_kernel, blocks=blocks, qb=qb, score_scale=score_scale, length_at=2 + per + slot),
        "self_fwd",
        (blocks + pairs,),
        [pl.BlockSpec((1, block, width), lambda t, s: (early(t), 0, 0))]
        + [pl.BlockSpec((1, 9, width), lambda t, s: (slot, 0, 0)), whole(weight.shape)]
        + any_spec(len(kept)),
        (table, rows, mod, weight, *kept),
        [
            pl.BlockSpec((1, block, width), lambda t, s: (slot, early(t), 0)),
            pl.BlockSpec((1, block, 3 * width), lambda t, s: (slot, early(t), 0)),
            pl.BlockSpec((1, count, 128), lambda t, s: (slot, 0, late(t))),
            pl.BlockSpec((1, 1, 2, count), lambda t, s: (slot, late(t), 0, 0)),
        ],
        [
            struct((per, count, width), BF),
            struct((per, count, 3 * width), BF),
            struct((per, count, width), BF),
            struct((per, pairs, 2, count), F32),
        ],
        scratch=[pltpu.VMEM((3 * pairs, count, 128), BF)],
        deps=deps,
        work=cost(6 * count * width * width + 16 * count * count * width, count * width * 16, H * count * count),
        aliases={4 + at: at for at in range(len(kept))},
    )


def self_bwd_call(
    table, slot, qkv, att, d_att, lse, rows, g1, mod, weight, early, text, qb, score_scale, block, nf, ni, deps
):
    per, count, width = att.shape
    pairs = H // 2
    blocks = count // block
    last = early is not None
    steps = pairs + blocks
    lines = block if last else block + text.shape[1] * text.shape[2]

    def pair(t):
        return jnp.minimum(t, pairs - 1)

    def row(t):
        return jnp.clip(t - pairs, 0, blocks - 1)

    def row_early(t):
        return jnp.clip(t - pairs - blocks, 0, blocks - 1)

    column = pl.BlockSpec((1, count, 128), lambda t, s: (slot, 0, pair(t)))
    by_row = pl.BlockSpec((1, block, width), lambda t, s: (slot, row(t), 0))
    in_specs = [
        pl.BlockSpec((1, count, 128), lambda t, s, part=part: (slot, 0, part * pairs + pair(t))) for part in range(3)
    ] + [column, column, pl.BlockSpec((1, 1, 2, count), lambda t, s: (slot, pair(t), 0, 0))]
    in_specs += [by_row, by_row, pl.BlockSpec((1, 9, width), lambda t, s: (slot, 0, 0)), whole(weight.shape)]
    args = [table, qkv, qkv, qkv, att, d_att, lse, rows, g1, mod, weight]
    out_specs = [
        pl.BlockSpec((1, lines, width), lambda t, s: (row(t), 0, 0)),
        pl.BlockSpec((1, 2, width), lambda t, s: (0, 0, 0)),
    ]
    out_shape = [struct((blocks, lines, width), BF), struct((1, 2, width), F32)]
    scratch = [pltpu.VMEM((3 * pairs, count, 128), BF)] + [pltpu.VMEM((count, 128), F32)] * 2
    if last:
        in_specs += [
            pl.BlockSpec((block, 3 * width), lambda t, s: (row_early(t), 0)),
            pl.BlockSpec((1, block, width), lambda t, s: (slot - 1, row_early(t), 0)),
            pl.BlockSpec((1, 9, width), lambda t, s: (slot - 1, 0, 0)),
        ]
        args += [early, rows, mod]
        specs, shapes = halves(ni, nf, 3 * width * width // (nf * ni * PACK), steps + blocks)
        out_specs += specs
        out_shape += shapes
        scratch += [pltpu.VMEM((width, 3 * width), F32)]
        steps += blocks + ni // FIN
    else:
        in_specs += [pl.BlockSpec((1,) + text.shape[1:], lambda t, s: (row(t), 0, 0, 0))]
        args += [text]
        out_specs += [pl.BlockSpec((block, 3 * width), lambda t, s: (row(t), 0))]
        out_shape += [struct((count, 3 * width), BF)]
    return run(
        partial(
            self_bwd_kernel,
            slot=slot,
            length_at=2 + per + slot,
            pairs=pairs,
            blocks=blocks,
            qb=qb,
            score_scale=score_scale,
            nf=nf,
            ni=ni,
            last=last,
        ),
        "self_bwd",
        (steps,),
        in_specs,
        args,
        out_specs,
        out_shape,
        scratch=scratch,
        deps=deps,
        work=cost(40 * count * count * width + 12 * count * width * width, count * width * 30, H * count * count),
    )


def cross_call(table, att, rows, mod, text, short, wkv, wo, wq, wco, score_scale, block, deps):
    items, count, width = rows.shape
    nf, lines, _ = text.shape
    skip = lines // short - items
    slots = nf * short
    row = pl.BlockSpec((1, block, width), lambda i, j, s: (i, j, 0))
    return run(
        partial(cross_kernel, score_scale=score_scale, length_at=2 + 2 * items),
        "cross_fwd",
        (items, count // block),
        [
            row,
            row,
            pl.BlockSpec((1, 9, width), lambda i, j, s: (i, 0, 0)),
            pl.BlockSpec((nf, short, width), lambda i, j, s: (0, skip + i, 0)),
            whole(wkv.shape),
            whole(wo.shape),
            whole(wq.shape),
            whole(wco.shape),
        ],
        (table, att, rows, mod, text, wkv, wo, wq, wco),
        [pl.BlockSpec((1, slots, 2 * width), lambda i, j, s: (i, 0, 0))]
        + [pl.BlockSpec((1, slots, width), lambda i, j, s: (i, 0, 0))]
        + [row] * 6
        + [pl.BlockSpec((1, H // 2, 2, block), lambda i, j, s: (i, 0, 0, j))],
        [struct((items, slots, 2 * width), BF), struct((items, slots, width), BF)]
        + [struct(rows.shape, BF)] * 6
        + [struct((items, H // 2, 2, count), F32)],
        deps=deps,
        work=cost(
            items * count * (6 * width * width + 16 * slots * width), items * count * width * 20, items * H * count * slots
        ),
    )


def back_grid(items, count, block):
    blocks = count // block
    total = items * blocks

    def at(t):
        return jnp.minimum(t, total - 1)

    def by_item(t, s):
        return (at(t) // blocks, 0, 0)

    def by_row(t, s):
        return (at(t) // blocks, at(t) % blocks, 0)

    return blocks, total, by_item, by_row


def mlp_call(table, second, cot, mod, wup, wdn, block, chunk, nf, ni, deps):
    items, count, width = second.shape
    ff = wup.shape[1]
    blocks, total, by_item, by_row = back_grid(items, count, block)
    row = pl.BlockSpec((1, block, width), by_row)
    shard = pl.BlockSpec((1, 1, block, width), lambda t, s: (by_row(t, s)[1], by_row(t, s)[0], 0, 0))
    depth = 2 * width * ff // (nf * ni * PACK)
    return run(
        partial(mlp_kernel, blocks=blocks, total=total, chunk=chunk, nf=nf, ni=ni),
        "mlp",
        (total + ni // FIN,),
        [row, shard, pl.BlockSpec((1, 9, width), by_item), whole(wup.shape), whole(wdn.shape)],
        (table, second, cot, mod, wup, wdn),
        [shard, row, pl.BlockSpec((1, 3, width), by_item)]
        + [pl.BlockSpec((FIN, nf, depth, PACK), lambda t, s: (jnp.maximum(t - total, 0), 0, 0, 0))],
        [struct(cot.shape, BF), struct(second.shape, BF), struct((items, 3, width), F32)]
        + [struct((ni, nf, depth, PACK), BF)],
        scratch=[pltpu.VMEM((width, ff), F32), pltpu.VMEM((ff, width), F32)],
        deps=deps,
        work=cost(12 * items * count * width * ff, items * count * width * 16, items * count * ff * 2),
    )


def cross_back_call(
    table, g2, bb, cr, cq, att, ba, first, mod, kv, lse, text, wo, wq, wco, wkv, score_scale, block, nf, ni, deps
):
    items, count, width = g2.shape
    slots = kv.shape[1]
    short = slots // nf
    blocks, total, by_item, by_row = back_grid(items, count, block)
    row = pl.BlockSpec((1, block, width), by_row)
    by_slot = pl.BlockSpec((nf, 1, short, width), lambda t, s: (0, by_item(t, s)[0], 0, 0))
    specs, shapes = halves(ni, nf, 5 * width * width // (nf * ni * PACK), total)
    lse_spec = pl.BlockSpec((1, H // 2, 2, block), lambda t, s: (by_row(t, s)[0], 0, 0, by_row(t, s)[1]))
    return run(
        partial(
            cross_back_kernel,
            blocks=blocks,
            total=total,
            score_scale=score_scale,
            nf=nf,
            ni=ni,
            length_at=2 + 2 * items,
        ),
        "cross_bwd",
        (total + ni // FIN,),
        [row] * 7
        + [pl.BlockSpec((1, 9, width), by_item), pl.BlockSpec((1, slots, 2 * width), by_item), lse_spec]
        + [pl.BlockSpec((1, slots, width), by_item)]
        + [whole(weight.shape) for weight in (wo, wq, wco, wkv)],
        (table, g2, bb, cr, cq, att, ba, first, mod, kv, lse, text, wo, wq, wco, wkv),
        [row, row, by_slot, pl.BlockSpec((1, 4, width), by_item)] + specs,
        [struct(g2.shape, BF)] * 2 + [struct((nf, items, short, width), BF), struct((items, 4, width), F32)] + shapes,
        scratch=[pltpu.VMEM((width, width), F32)] * 3
        + [pltpu.VMEM((width, 2 * width), F32), pltpu.VMEM((slots, 2 * width), F32)],
        deps=deps,
        work=cost(
            items * count * (12 * width * width + 40 * slots * width), items * count * width * 24, items * H * count * slots
        ),
    )


def deal_call(table, got, per, block, skip, dtype, name, deps=(), group=2):
    nf, _, _, width = got[0].shape
    items = nf * per
    at = 2 + 3 * per
    specs = []
    for part in range(group):
        if len(got) == 1:
            specs.append(
                pl.BlockSpec(
                    (1, 1, block, width),
                    lambda t, s, part=part: (s[at + t * group + part], 0, skip + s[at + items + t * group + part], 0),
                )
            )
        else:
            specs += [
                pl.BlockSpec((1, 1, block, width), lambda t, s, part=part: (s[at + t * group + part], 0, 0, 0))
            ] * len(got)
    return run(
        partial(deal_kernel, at=at, items=items, group=group),
        name,
        (items // group,),
        specs,
        (table,) + tuple(got) * group,
        pl.BlockSpec((group, block, width), lambda t, s: (t, 0, 0)),
        struct((items, block, width), dtype),
        deps=deps,
        work=cost(0, items * block * width * 6),
    )


def small_call(kernel, name, args, out_shape, deps=()):
    return pl.pallas_call(
        kernel,
        in_specs=[pl.BlockSpec(arg.shape, lambda: (0,) * arg.ndim) for arg in args] + any_spec(len(deps)),
        out_specs=[pl.BlockSpec(out.shape, lambda: (0,) * len(out.shape)) for out in out_shape],
        out_shape=out_shape,
        compiler_params=params(),
        name=name,
    )(*args, *deps)


def exchange(blocks):
    return lax.all_to_all(blocks, "frames", 0, 0, tiled=True)


def swap(block, offset, nf):
    if offset == 0:
        return block
    return lax.ppermute(block, "frames", [(i, i ^ offset) for i in range(nf)])


def bits_of(count):
    return count.bit_length() - 1


class Sum:
    def __init__(self, keep, send, order, sizes):
        self.sizes = sizes
        ni, nf = sizes["items"], sizes["frames"]
        self.dims = [("items", bit) for bit in reversed(range(bits_of(ni)))]
        self.dims += [("frames", bit) for bit in reversed(range(1, bits_of(nf)))]
        shape = (2,) * len(self.dims) + keep.shape[2:]
        self.keep, self.send = keep.reshape(shape), send
        self.shape = shape
        self.steps = [("frames", 0)] + list(order)
        self.got = None

    def launch(self):
        name, bit = self.steps.pop(0)
        self.got = lax.ppermute(self.send, name, [(i, i ^ (1 << bit)) for i in range(self.sizes[name])])

    def land(self, deps=()):
        got = self.got.reshape(self.keep.shape)
        if not self.steps:
            return self.keep, got
        dim = self.dims.index(self.steps[0])
        self.dims.remove(self.steps[0])
        shape = self.keep.shape
        outer, inner = 2**dim, 2 ** (len(shape) - 3 - dim)
        view = (outer, 2, inner) + shape[-2:]
        out = struct((outer, inner) + shape[-2:], BF)
        source = pl.BlockSpec((1,) + view[1:], lambda t: (t, 0, 0, 0, 0))
        target = pl.BlockSpec((1,) + out.shape[1:], lambda t: (t, 0, 0, 0))
        self.keep, self.send = pl.pallas_call(
            land_kernel,
            grid=(outer,),
            in_specs=[source] * 2 + any_spec(len(deps)),
            out_specs=[target] * 2,
            out_shape=[out] * 2,
            compiler_params=params(),
            name="land",
        )(self.keep.reshape(view), got.reshape(view), *deps)
        left = shape[:dim] + shape[dim + 1 :]
        self.keep = self.keep.reshape(left)
        return None


def collect_items(rows, ni):
    for bit in range(bits_of(ni)):
        rows = jnp.concatenate([rows, lax.ppermute(rows, "items", [(i, i ^ (1 << bit)) for i in range(ni)])], 0)
    return rows


def items_whole(
    ni, nf, frames_in, cond, text, item_lengths, text_lengths, ada_weight, qkv_weight, out_weight,
    cross_q_weight, cross_kv_weight, cross_out_weight, up_weight, down_weight, cotangent,
):
    items, block, width = frames_in.shape
    per = items // nf
    ff = up_weight.shape[1]
    sizes = {"items": ni, "frames": nf}
    score_scale = (width // H) ** (-0.5)
    me = lax.axis_index("frames")
    row_item = lax.axis_index("items")
    x_first = [("items", bit) for bit in range(bits_of(ni))] + [("frames", bit) for bit in range(1, bits_of(nf))]

    table = start_call(jnp.stack([me, row_item]), item_lengths, text_lengths, items, nf)
    rows_first = exchange(gather_first_call(table, frames_in, nf))
    mixed_send, cot_send = gather_call(table, frames_in, text, cotangent, nf)

    cond_f = cond.astype(F32)
    low_cond = jax.nn.silu(cond_f).astype(BF)
    modulation = nn(low_cond, ada_weight)
    pick = table[2 : 2 + per, None] == jnp.arange(items, dtype=jnp.int32)[None, :]
    mod = jnp.sum(jnp.where(pick[:, :, None], modulation[None], 0.0), 1).reshape(per, 9, width)

    (mixed_send,) = gate_call([mixed_send], [rows_first, mod])
    mixed = exchange(mixed_send)
    kept = self_fwd_call(table, 0, rows_first, mod, qkv_weight, (), per, block, 512, score_scale, [mixed_send])
    (cot_send,) = gate_call([cot_send], [mixed])
    cot = exchange(cot_send)
    kept = self_fwd_call(table, 1, mixed, mod, qkv_weight, kept, per, block, 512, score_scale, [cot_send])
    rows, qkv, attended, self_lse = kept
    text_kv, text_rows, first, second, branch_a, branch_b, cross_q, crossed, cross_lse = cross_call(
        table, attended, rows, mod, mixed, text.shape[1], cross_kv_weight, out_weight, cross_q_weight, cross_out_weight,
        score_scale, 2 * block, [],
    )
    layer_send, g2, dmod_c, g_mlp = mlp_call(
        table, second, cot, mod, up_weight, down_weight, block, 768, nf, ni, []
    )
    layer_got = exchange(layer_send)
    sum_mlp = lax.psum_scatter(
        g_mlp.reshape((ni * nf,) + g_mlp.shape[2:]), ("items", "frames"), scatter_dimension=0, tiled=True
    )[0]
    g1, d_att, text_back, dmod_b, mid_keep, mid_send = cross_back_call(
        table, g2, branch_b, crossed, cross_q, attended, branch_a, first, mod, text_kv, cross_lse, text_rows,
        out_weight, cross_q_weight, cross_out_weight, cross_kv_weight, score_scale, 2 * block, nf, ni, [],
    )
    mid = Sum(mid_keep, mid_send, x_first, sizes)
    mid.launch()
    made_0, dmod_0, early = self_bwd_call(
        table, 0, qkv, attended, d_att, self_lse, rows, g1, mod, qkv_weight, None, text_back, 1024, score_scale, block, nf, ni,
        [layer_got],
    )
    mid.land()
    mid.launch()
    got_0 = exchange(made_0)
    made_1, dmod_1, grad_keep, grad_send = self_bwd_call(
        table, 1, qkv, attended, d_att, self_lse, rows, g1, mod, qkv_weight, early, None, 1024, score_scale, block, nf, ni,
        [mid.send],
    )
    made_1, grad_send = gate_call([made_1, grad_send], [mid.got, got_0, sum_mlp])
    grad = Sum(grad_keep, grad_send, x_first, sizes)
    grad.launch()
    got_1 = exchange(made_1)
    layer_got = layer_got.reshape(nf, 1, per * block, width)
    layer_out = deal_call(table, [layer_got], per, block, 0, BF, "deal_out")
    grad.land([layer_out])
    grad.launch()
    mid.land([grad.send])
    mid.launch()
    text_grad = deal_call(
        table, [got_0[:, None]], per, text.shape[1], block // text.shape[1], F32, "deal_text", [mid.send]
    )
    (dmod_1,) = gate_call([dmod_1], [text_grad])
    d_mod = jnp.concatenate([jnp.concatenate([dmod_0, dmod_1], 0), dmod_b, dmod_c], 1).reshape(per, 9 * width)
    ada_rows, ada_cols, cond_cols = width // ni, 9 * width // nf, width // nf
    high = d_mod.astype(BF)
    rest = (d_mod - high.astype(F32)).astype(BF)
    parts = nt(jnp.concatenate([high, rest], 0), ada_weight)
    parts = jnp.concatenate(
        [d_mod.reshape(per, nf, ada_cols), (parts[:per] + parts[per:]).reshape(per, nf, cond_cols)], 2
    ).transpose(1, 0, 2)
    mid.land([parts])
    mid.launch()
    (parts,) = gate_call([parts], [got_1, mid.send])
    parts = exchange(parts).reshape(items, ada_cols + cond_cols)
    input_grad = deal_call(table, [got_0[:, None], got_1[:, None]], per, block, 0, F32, "deal_in", [mid.send])
    grad.land([input_grad])
    grad.launch()
    mid.land([grad.send])
    mid.launch()
    at = 2 + 3 * per
    spot = table[at : at + items] * per + table[at + items : at + 2 * items]
    pick_row = spot[:, None] == jnp.arange(items, dtype=jnp.int32)[None, :]
    parts = jnp.sum(jnp.where(pick_row[:, :, None], parts[None], 0.0), 1)
    every = collect_items(jnp.concatenate([parts[:, :ada_cols], low_cond.astype(F32)], 1), ni)
    grad_ada = lax.dot_general(
        lax.dynamic_slice(every, (0, ada_cols + row_item * ada_rows), (items * ni, ada_rows), allow_negative_indices=False),
        every[:, :ada_cols],
        (((0,), (0,)), ((), ())),
        precision=lax.Precision.HIGHEST,
        preferred_element_type=F32,
    )
    cond_mine = lax.dynamic_slice(cond_f, (0, me * cond_cols), (items, cond_cols), allow_negative_indices=False)
    sigmoid_c = jax.nn.sigmoid(cond_mine)
    cond_grad = parts[:, ada_cols:] * (sigmoid_c * (1.0 + cond_mine * (1.0 - sigmoid_c)))

    grad_up, grad_down = small_call(
        finish_mlp_kernel,
        "finish_mlp",
        [sum_mlp],
        [struct((width // ni, ff // nf), F32), struct((ff // ni, width // nf), F32)],
        [grad.send],
    )
    while grad.steps:
        grad.land()
        grad.launch()
    mid_sum = mid.land()
    square = struct((ada_rows, cond_cols), F32)
    grad_out, grad_cross_q, grad_cross_out, grad_cross_kv = small_call(
        finish_mid_kernel, "finish_mid", mid_sum, [square] * 3 + [struct((ada_rows, 2 * cond_cols), F32)]
    )
    (grad_qkv,) = small_call(finish_qkv_kernel, "finish_qkv", grad.land(), [struct((ada_rows, 3 * cond_cols), F32)])
    return (
        layer_out,
        input_grad,
        text_grad,
        cond_grad,
        grad_ada,
        grad_qkv,
        grad_out,
        grad_cross_q,
        grad_cross_kv,
        grad_cross_out,
        grad_up,
        grad_down,
    )


def on_device(mesh, *args):
    ni, nf = mesh.shape["items"], mesh.shape["frames"]
    if nf == 4 and args[0].shape[0] == 2 * nf and args[0].shape[-1] == 768 and 768 % (32 * ni) == 0:
        return items_whole(ni, nf, *args)
    return frames_split(*args)


def solution(mesh):
    in_specs = (
        P("items", "frames", None),
        P("items", None),
        P("items", "frames", None),
        P("items"),
        P("items"),
        P(),
        P(),
        P(),
        P(),
        P(),
        P(),
        P(),
        P(),
        P("items", "frames", None),
    )
    out_specs = (
        P("items", "frames", None),
        P("items", "frames", None),
        P("items", "frames", None),
        P("items", "frames"),
        P("items", "frames"),
        P("items", "frames"),
        P("items", "frames"),
        P("items", "frames"),
        P("items", "frames"),
        P("items", "frames"),
        P("items", "frames"),
        P("items", "frames"),
    )
    return jax.shard_map(
        partial(on_device, mesh), mesh=mesh, in_specs=in_specs, out_specs=out_specs, check_vma=False
    )
```

time: 634 us -> 560 us (0.88)
  Pallas kernels: 403 us -> 367 us
  starting transfers between devices: 103 us -> 75.2 us
  other arithmetic: 26.3 us -> 3.6 us
  waiting for transfers between devices: 48.2 us -> 61.3 us
    pallas_call x18 -> x12, Pallas kernels: 401 us -> 338 us  [run(): pl.pallas_call(body, grid_spec=pltpu.PrefetchScalarGridSpec(num_scalar_pr...]
    ppermute x10, starting transfers between devices: 52.3 us -> 6.99 us  [launch(): lax.ppermute(self.send, name, [(i, i ^ 1 << bit) for i in range(self.size...]
    pallas_call x0 -> x11, Pallas kernels: none -> 27.1 us  [the longest x8 21.7 us: land(): pl.pallas_call(land_kernel, grid=(outer,), in_specs=[source] * 2 + any_sp...]
    all_to_all x10 -> x7, starting transfers between devices: 36.6 us -> 63.2 us  [exchange(): return lax.all_to_all(blocks, 'frames', 0, 0, tiled=True)]
    ppermute x6 -> x3, waiting for transfers between devices: 3.19 us -> 19.4 us  [collect_items(): lax.ppermute(rows, 'items', [(i, i ^ 1 << bit) for i in range(ni)])]
    convert_element_type x10 -> x1, other arithmetic: 15.1 us -> 0.02 us  [items_whole(): low_cond.astype(F32)]
    ppermute x6 -> x3, starting transfers between devices: 13.7 us -> 4.78 us  [collect_items(): lax.ppermute(rows, 'items', [(i, i ^ 1 << bit) for i in range(ni)])]
    all_to_all x10 -> x7, waiting for transfers between devices: 20.1 us -> 11.4 us  [exchange(): return lax.all_to_all(blocks, 'frames', 0, 0, tiled=True)]
  transfers between devices with their start and end apart: 27 -> 21, of which waited for: 9 -> 9; matrix products, arithmetic and copies ran while one was open for 7% -> 4% of each run, Pallas kernels for 49% -> 48%
where the time goes in v3:
time: 560 us; the launch traced here: 554 us
  Pallas kernels  367 us (66%)
  starting transfers between devices  75.2 us (13%)
  waiting for transfers between devices  61.3 us (11%)
  local copies, waits for them, and re-layouts  18.1 us (3%)
  between operations  14.6 us (3%)
  matrix products  14 us (2%)
    pallas_call x12, Pallas kernels, run(): pl.pallas_call(body, grid_spec=pltpu.PrefetchScalarGridSpec(num_scalar_pr...  338 us
    all_to_all x7, starting transfers between devices, exchange(): return lax.all_to_all(blocks, 'frames', 0, 0, tiled=True)  63.2 us
    ppermute x10, waiting for transfers between devices, launch(): lax.ppermute(self.send, name, [(i, i ^ 1 << bit) for i in range(self.size...  30.4 us
    pallas_call x8, Pallas kernels, land(): pl.pallas_call(land_kernel, grid=(outer,), in_specs=[source] * 2 + any_sp...  21.7 us
    ppermute x3, waiting for transfers between devices, collect_items(): lax.ppermute(rows, 'items', [(i, i ^ 1 << bit) for i in range(ni)])  19.4 us
    unnamed x46, local copies, waits for them, and re-layouts  17.1 us
    all_to_all x7, waiting for transfers between devices, exchange(): return lax.all_to_all(blocks, 'frames', 0, 0, tiled=True)  11.4 us
  transfers between devices with their start and end apart: 21, of which 9 were waited for; matrix products, arithmetic and copies ran while one was open for 4% of the time, Pallas kernels for 48%

profile of v3, /device:TPU:0, one launch (start us, length us, event | category | flops | bytes accessed | tf_op | source)
XLA Modules:
  0.0 553.7 jit_solution(5409875043950319066)
XLA Ops:
  9.2 4.4 gather_first.1
  13.5 4.2 all-to-all-start
  17.9 5.5 fusion.10
  24.4 6.1 %gather.1 = (bf16[4,384,768]{2,1,0:T(8,128)(2,1)}, bf16[4,2,256,768]{3,2,1,0:T(8,128)(2,1)}) custom-call(s32[32]{0:T(128)} %start.1.refs_0_, bf16[8,256,768]{2,1,0:T(8,128)(2,1)} %refs_1_.3, bf16[8,64,768]{2,1,0:T(8,128)(2,1)} %refs_3_.3, bf16[8,64,768]{2,1,0:T(8,128)(2,1)} %refs_3_.3, bf16[8,256,768]{2,1,0:T(8,128)(2,1)} %refs_5_.3, ...), custom_call_target="tpu_custom_call" | custom-call | tf_op jit(solution)/shard_map/gather/pallas_call | solution.py:927
  30.4 7.4 %all-to-all-done.refs_1_ = bf16[4,256,768]{2,1,0:T(8,128)(2,1)S(1)} async-done(((bf16[4,256,768]{2,1,0:T(8,128)(2,1)}), bf16[4,256,768]{2,1,0:T(8,128)(2,1)S(1)}, u32[]{:S(2)}, u32[]{:S(2)}) %all-to-all-start) | async-done | bytes 1572896 | tf_op jit(solution)/shard_map/all_to_all | solution.py:1286
  39.0 3.6 all-to-all-start.1
  42.6 32.9 %self_fwd.2 = (bf16[2,1024,768]{2,1,0:T(8,128)(2,1)}, bf16[2,1024,2304]{2,1,0:T(8,128)(2,1)}, bf16[2,1024,768]{2,1,0:T(8,128)(2,1)}, f32[2,6,2,1024]{3,2,1,0:T(2,128)}) custom-call(s32[32]{0:T(128)} %start.1.refs_0_, bf16[4,256,768]{2,1,0:T(8,128)(2,1)} %copy-done.4, f32[2,9,768]{2,1,0:T(8,128)} %reshape.119.refs_2_.refs_3_.refs_8_.refs_9_.refs_13_, ...), custom_call_target="tpu_custom_call" | custom-call | flops 16508780544 | bytes 12582912 | tf_op jit(solution)/shard_map/self_fwd/pallas_call | solution.py:927
  75.6 1.4 copy-done.3
  77.0 3.7 all-to-all-start.2
  81.0 18.1 %self_fwd.3 = (bf16[2,1024,768]{2,1,0:T(8,128)(2,1)}, bf16[2,1024,2304]{2,1,0:T(8,128)(2,1)}, bf16[2,1024,768]{2,1,0:T(8,128)(2,1)}, f32[2,6,2,1024]{3,2,1,0:T(2,128)}) custom-call(s32[32]{0:T(128)} %start.1.refs_0_, bf16[4,384,768]{2,1,0:T(8,128)(2,1)} %copy-done.3, ...), custom_call_target="tpu_custom_call", output_to_operand_aliasing={{0}: (4, {}), {1}: (5, {}), {2}: (6, {}), {3}: (7, {})} | custom-call | flops 16508780544 | bytes 12582912 | tf_op jit(solution)/shard_map/self_fwd/pallas_call | solution.py:927
  99.1 25.1 %cross_fwd.1 = (bf16[2,256,1536]{2,1,0:T(8,128)(2,1)}, bf16[2,256,768]{2,1,0:T(8,128)(2,1)}, bf16[2,1024,768]{2,1,0:T(8,128)(2,1)}, bf16[2,1024,768]{2,1,0:T(8,1...) custom-call(s32[32]{0:T(128)} %start.1.refs_0_, ...), custom_call_target="tpu_custom_call" | custom-call | flops 13690208256 | bytes 31457280 | tf_op jit(solution)/shard_map/cross_fwd/pallas_call | solution.py:927
  124.3 1.7 copy-done.5
  125.9 89.3 %mlp.1 = (bf16[4,2,256,768]{3,2,1,0:T(8,128)(2,1)}, bf16[2,1024,768]{2,1,0:T(8,128)(2,1)}, f32[2,3,768]{2,1,0:T(4,128)}, bf16[8,4,384,384]{3,2,1,0:T(8,128)(2,1)}) custom-call(s32[32]{0:T(128)} %start.1.refs_0_, bf16[2,1024,768]{2,1,0:T(8,128)(2,1)} %get-tuple-element.80.refs_1_, bf16[4,2,256,768]{3,2,1,0:T(8,128)(2,1)} %copy-done.5, ...), custom_call_target="tpu_custom_call" | custom-call | flops 57982058496 | bytes 25165824 | tf_op jit(solution)/shard_map/mlp/pallas_call | solution.py:927
  215.3 17.8 %all-to-all-start.3 = ((bf16[4,2,256,768]{3,2,1,0:T(8,128)(2,1)}), bf16[4,2,256,768]{3,2,1,0:T(8,128)(2,1)S(1)}, u32[]{:S(2)}, u32[]{:S(2)}) async-start(bf16[4,2,256,768]{3,2,1,0:T(8,128)(2,1)} %get-tuple-element.81), calls=%async_computation.3 | async-start | bytes 6291456 | tf_op jit(solution)/shard_map/all_to_all | solution.py:1286
  233.1 62.3 %cross_bwd.1 = (bf16[2,1024,768]{2,1,0:T(8,128)(2,1)}, bf16[2,1024,768]{2,1,0:T(8,128)(2,1)}, bf16[4,2,64,768]{3,2,1,0:T(8,128)(2,1)}, f32[2,4,768]{2,1,0:T(4,12...) custom-call(s32[32]{0:T(128)} %start.1.refs_0_, bf16[2,1024,768]{2,1,0:T(8,128)(2,1)} %get-tuple-element.83.refs_1_, ...), custom_call_target="tpu_custom_call" | custom-call | flops 30601641984 | bytes 37748736 | tf_op jit(solution)/shard_map/cross_bwd/pallas_call | solution.py:927
  296.0 1.7 copy-done.1
  297.7 45.7 %self_bwd.2 = (bf16[4,384,768]{2,1,0:T(8,128)(2,1)}, f32[1,2,768]{2,1,0:T(2,128)}, bf16[1024,2304]{1,0:T(8,128)(2,1)}) custom-call(s32[32]{0:T(128)} %start.1.refs_0_, bf16[2,1024,2304]{2,1,0:T(8,128)(2,1)} %get-tuple-element.82.refs_1_.refs_2_.refs_3_, bf16[2,1024,2304]{2,1,0:T(8,128)(2,1)} %get-tuple-element.82.refs_1_.refs_2_.refs_3_, ...), custom_call_target="tpu_custom_call" | custom-call | flops 39460012032 | bytes 23592960 | tf_op jit(solution)/shard_map/self_bwd/pallas_call | solution.py:927
  343.4 3.6 all-to-all-start.4
  347.1 4.8 land.8
  351.9 39.1 %self_bwd.3 = (bf16[4,256,768]{2,1,0:T(8,128)(2,1)}, f32[1,2,768]{2,1,0:T(2,128)}, bf16[8,2,144,384]{3,2,1,0:T(8,128)(2,1)}, bf16[8,2,144,384]{3,2,1,0:T(8,128)(2,1)}) custom-call(s32[32]{0:T(128)} %start.1.refs_0_, bf16[2,1024,2304]{2,1,0:T(8,128)(2,1)} %get-tuple-element.82.refs_1_.refs_2_.refs_3_, ...), custom_call_target="tpu_custom_call" | custom-call | flops 39460012032 | bytes 23592960 | tf_op jit(solution)/shard_map/self_bwd/pallas_call | solution.py:927
  393.2 4.8 deal_out.1.refs_0_
  398.0 26.7 %all-to-all-start.5 = ((bf16[4,256,768]{2,1,0:T(8,128)(2,1)}), bf16[4,256,768]{2,1,0:T(8,128)(2,1)S(1)}, u32[]{:S(2)}, u32[]{:S(2)}) async-start(bf16[4,256,768]{2,1,0:T(8,128)(2,1)} %get-tuple-element.104), calls=%async_computation.6 | async-start | bytes 3145728 | tf_op jit(solution)/shard_map/all_to_all | solution.py:1286
  425.9 4.0 land.9
  429.9 2.8 land.10
  432.7 2.7 collective-permute-start.3
  435.4 4.3 deal_text.1.refs_1_
  440.5 6.9 %fusion.2 = f32[4,768]{1,0:T(4,128)S(1)} fusion(bf16[768,6912]{1,0:T(8,128)(2,1)} %param.19, bf16[2,6912]{1,0:T(2,128)(2,1)S(1)} %get-tuple-element.168, bf16[2,6912]{1,0:T(2,128)(2,1)S(1)} %get-tuple-element.169), kind=kOutput, calls=%fused_computation.10 | convolution fusion | flops 42577920 | bytes 10684416 | tf_op jit(solution)/shard_map/dot_general | solution.py:338
  448.3 4.4 collective-permute-done.3
  453.6 2.3 land.11
  457.2 3.5 all-to-all-start.6
  460.7 4.0 all-to-all-done.6
  465.1 19.4 %collective-permute-done.4 = f32[8,2496]{1,0:T(8,128)S(1)} collective-permute-done((f32[8,2496]{1,0:T(8,128)S(1)}, f32[8,2496]{1,0:T(8,128)S(1)}, u32[]{:S(2)}, u32[]{:S(2)}) %collective-permute-start.4) | collective-permute-done | bytes 79904 | tf_op jit(solution)/shard_map/ppermute | solution.py:1343
  484.5 1.8 collective-permute-start.5
  486.3 6.2 %deal_in.1.refs_0_ = f32[8,256,768]{2,1,0:T(8,128)} custom-call(s32[32]{0:T(128)} %start.1.refs_0_, bf16[4,1,384,768]{3,2,1,0:T(8,128)(2,1)} %bitcast.42, bf16[4,1,256,768]{3,2,1,0:T(8,128)(2,1)} %bitcast.46, bf16[4,1,384,768]{3,2,1,0:T(8,128)(2,1)} %bitcast.43, bf16[4,1,256,768]{3,2,1,0:T(8,128)(2,1)} %bitcast.47, ...), custom_call_target="tpu_custom_call" | custom-call | bytes 9437184 | tf_op jit(solution)/shard_map/deal_in/pallas_call | solution.py:927
  493.5 2.2 land.12
  496.3 3.0 collective-permute-start.6
  499.3 6.0 %collective-permute-done.11 = bf16[1,2,240,384]{3,2,1,0:T(8,128)(2,1)S(1)} collective-permute-done((bf16[1,2,240,384]{3,2,1,0:T(8,128)(2,1)}, bf16[1,2,240,384]{3,2,1,0:T(8,128)(2,1)S(1)}, u32[]{:S(2)}, u32[]{:S(2)}) %collective-permute-start.11) | collective-permute-done | bytes 368672 | tf_op jit(solution)/shard_map/ppermute | solution.py:1313
  506.0 1.9 land.15
  509.8 1.9 finish_mlp.1
  511.7 1.9 copy.54
  515.2 1.8 finish_mid.1
  517.0 4.6 collective-permute-done.8
  522.3 2.0 land.13
  524.4 12.2 %collective-permute-done.9 = bf16[1,2,144,384]{3,2,1,0:T(8,128)(2,1)S(1)} collective-permute-done((bf16[1,2,144,384]{3,2,1,0:T(8,128)(2,1)}, bf16[1,2,144,384]{3,2,1,0:T(8,128)(2,1)S(1)}, u32[]{:S(2)}, u32[]{:S(2)}) %collective-permute-start.9) | collective-permute-done | bytes 221216 | tf_op jit(solution)/shard_map/ppermute | solution.py:1313
  537.3 1.8 land.14
  540.3 1.7 fusion
  542.0 2.3 collective-permute-done.10
  544.9 1.7 finish_qkv.1
  (98 shorter events, 22.0 us)
Async XLA Ops:
  9.1 8.6 %copy-start.19 = (s32[32]{0:T(128)S(1)}, s32[32]{0:T(128)}, u32[]{:S(2)}) copy-start(s32[32]{0:T(128)} %start.1.refs_0_) | copy-start | bytes 388
  9.1 8.8 %copy-start.14 = (bf16[8,768]{1,0:T(8,128)(2,1)S(1)}, bf16[8,768]{1,0:T(8,128)(2,1)}, u32[]{:S(2)}) copy-start(bf16[8,768]{1,0:T(8,128)(2,1)} %param.15) | copy-start | bytes 36868
  13.5 24.3 %all-to-all-start = ((bf16[4,256,768]{2,1,0:T(8,128)(2,1)}), bf16[4,256,768]{2,1,0:T(8,128)(2,1)S(1)}, u32[]{:S(2)}, u32[]{:S(2)}) async-start(bf16[4,256,768]{2,1,0:T(8,128)(2,1)} %gather_first.1), calls=%async_computation | async-start | bytes 3145728 | tf_op jit(solution)/shard_map/all_to_all | solution.py:1286
  37.9 1.1 copy-start.4
  39.0 36.6 %all-to-all-start.1 = ((bf16[4,384,768]{2,1,0:T(8,128)(2,1)}), bf16[4,384,768]{2,1,0:T(8,128)(2,1)S(1)}, u32[]{:S(2)}, u32[]{:S(2)}) async-start(bf16[4,384,768]{2,1,0:T(8,128)(2,1)} %gate.5.refs_4_), calls=%async_computation.1 | async-start | bytes 4718592 | tf_op jit(solution)/shard_map/all_to_all | solution.py:1286
  75.6 1.5 copy-start.3
  77.0 47.2 %all-to-all-start.2 = ((bf16[4,2,256,768]{3,2,1,0:T(8,128)(2,1)}), bf16[4,2,256,768]{3,2,1,0:T(8,128)(2,1)S(1)}, u32[]{:S(2)}, u32[]{:S(2)}) async-start(bf16[4,2,256,768]{3,2,1,0:T(8,128)(2,1)} %gate.6.refs_8_), calls=%async_computation.2 | async-start | bytes 6291456 | tf_op jit(solution)/shard_map/all_to_all | solution.py:1286
  80.7 310.3 %reduce-scatter.2.cloned.1.call-start = ((), (), s32[]{:S(2)}) async-start(), calls=%async_computation.8 | async-start | bytes 9732096 | tf_op jit(solution)/shard_map/reduce_scatter | solution.py:1385
  124.2 1.7 copy-start.5
  215.3 80.7 %all-to-all-start.3 = ((bf16[4,2,256,768]{3,2,1,0:T(8,128)(2,1)}), bf16[4,2,256,768]{3,2,1,0:T(8,128)(2,1)S(1)}, u32[]{:S(2)}, u32[]{:S(2)}) async-start(bf16[4,2,256,768]{3,2,1,0:T(8,128)(2,1)} %get-tuple-element.81), calls=%async_computation.3 | async-start | bytes 6291456 | tf_op jit(solution)/shard_map/all_to_all | solution.py:1286
  295.4 51.7 %collective-permute-start = (bf16[8,2,240,384]{3,2,1,0:T(8,128)(2,1)}, bf16[8,2,240,384]{3,2,1,0:T(8,128)(2,1)}, u32[]{:S(2)}, u32[]{:S(2)}) collective-permute-start(bf16[8,2,240,384]{3,2,1,0:T(8,128)(2,1)} %get-tuple-element.99), channel_id=1, source_target_pairs={{0,1},{1,0},{2,3},{3,2},{4,5},{5,4},{6,7},{7,6},{8,9},{9,8},{10,11... | collective-permute-start | bytes 8847368 | tf_op jit(solution)/shard_map/ppermute | solution.py:1313
  296.0 1.7 copy-start.1
  343.4 47.6 %all-to-all-start.4 = ((bf16[4,384,768]{2,1,0:T(8,128)(2,1)}), bf16[4,384,768]{2,1,0:T(8,128)(2,1)S(1)}, u32[]{:S(2)}, u32[]{:S(2)}) async-start(bf16[4,384,768]{2,1,0:T(8,128)(2,1)} %get-tuple-element.96), calls=%async_computation.4 | async-start | bytes 4718592 | tf_op jit(solution)/shard_map/all_to_all | solution.py:1286
  351.9 39.1 %collective-permute-start.1 = (bf16[4,2,240,384]{3,2,1,0:T(8,128)(2,1)}, bf16[4,2,240,384]{3,2,1,0:T(8,128)(2,1)}, u32[]{:S(2)}, u32[]{:S(2)}) collective-permute-start(bf16[4,2,240,384]{3,2,1,0:T(8,128)(2,1)} %get-tuple-element.100.refs_14_), channel_id=1, source_target_pairs={{0,4},{4,0},{8,12},{12,8},{16,20},{20,16},{24,28},{28,24},{1,5},{5... | collective-permute-start | bytes 4423688 | tf_op jit(solution)/shard_map/ppermute | solution.py:1313
  391.0 1.4 copy-start
  392.4 0.7 copy-start.20
  392.4 0.7 copy-start.15
  392.4 32.3 %collective-permute-start.2 = (bf16[8,2,144,384]{3,2,1,0:T(8,128)(2,1)}, bf16[8,2,144,384]{3,2,1,0:T(8,128)(2,1)S(1)}, u32[]{:S(2)}, u32[]{:S(2)}) collective-permute-start(bf16[8,2,144,384]{3,2,1,0:T(8,128)(2,1)} %get-tuple-element.107), channel_id=1, source_target_pairs={{0,1},{1,0},{2,3},{3,2},{4,5},{5,4},{6,7},{7,6},{8,9},{9,8},{10,11... | collective-permute-start | bytes 5308424 | tf_op jit(solution)/shard_map/ppermute | solution.py:1313
  398.0 57.9 %all-to-all-start.5 = ((bf16[4,256,768]{2,1,0:T(8,128)(2,1)}), bf16[4,256,768]{2,1,0:T(8,128)(2,1)S(1)}, u32[]{:S(2)}, u32[]{:S(2)}) async-start(bf16[4,256,768]{2,1,0:T(8,128)(2,1)} %get-tuple-element.104), calls=%async_computation.6 | async-start | bytes 3145728 | tf_op jit(solution)/shard_map/all_to_all | solution.py:1286
  424.7 1.2 copy-start.6
  432.7 20.0 %collective-permute-start.3 = (bf16[2,2,240,384]{3,2,1,0:T(8,128)(2,1)}, bf16[2,2,240,384]{3,2,1,0:T(8,128)(2,1)S(1)}, u32[]{:S(2)}, u32[]{:S(2)}) collective-permute-start(bf16[2,2,240,384]{3,2,1,0:T(8,128)(2,1)} %get-tuple-element.110.refs_3_), channel_id=1, source_target_pairs={{0,8},{4,12},{8,0},{12,4},{16,24},{20,28},{24,16},{28,20},{1,9},{5... | collective-permute-start | bytes 2211848 | tf_op jit(solution)/shard_map/ppermute | solution.py:1313
  435.4 4.3 copy-start.17
  435.4 4.3 copy-start.18
  435.4 4.3 copy-start.21
  447.4 13.3 %copy-start.7 = (bf16[4,2,144,384]{3,2,1,0:T(8,128)(2,1)S(1)}, bf16[4,2,144,384]{3,2,1,0:T(8,128)(2,1)}, u32[]{:S(2)}) copy-start(bf16[4,2,144,384]{3,2,1,0:T(8,128)(2,1)} %get-tuple-element.108.refs_0_) | copy-start | bytes 2654212
  452.7 0.9 copy-start.9
  456.0 1.2 copy-start.2
  457.2 7.6 %all-to-all-start.6 = ((f32[4,2,1920]{2,1,0:T(2,128)}), f32[4,2,1920]{2,1,0:T(2,128)S(1)}, u32[]{:S(2)}, u32[]{:S(2)}) async-start(f32[4,2,1920]{2,1,0:T(2,128)} %gate.9), calls=%async_computation.7 | async-start | bytes 122880 | tf_op jit(solution)/shard_map/all_to_all | solution.py:1286
  460.7 31.9 %collective-permute-start.7 = (bf16[4,2,144,384]{3,2,1,0:T(8,128)(2,1)S(1)}, bf16[4,2,144,384]{3,2,1,0:T(8,128)(2,1)S(1)}, u32[]{:S(2)}, u32[]{:S(2)}) collective-permute-start(bf16[4,2,144,384]{3,2,1,0:T(8,128)(2,1)S(1)} %copy-done.7), channel_id=1, source_target_pairs={{0,4},{4,0},{8,12},{12,8},{16,20},{20,16},{24,28},{28,24},{1,5},{5... | collective-permute-start | bytes 2654216 | tf_op jit(solution)/shard_map/ppermute | solution.py:1313
  465.1 19.4 %collective-permute-start.4 = (f32[8,2496]{1,0:T(8,128)S(1)}, f32[8,2496]{1,0:T(8,128)S(1)}, u32[]{:S(2)}, u32[]{:S(2)}) collective-permute-start(f32[8,2496]{1,0:T(8,128)S(1)} %pad_maximum_fusion.4), channel_id=1, source_target_pairs={{0,4},{4,0},{8,12},{12,8},{16,20},{20,16},{24,28},{28,24},{1,5},{5... | collective-permute-start | bytes 239624 | tf_op jit(solution)/shard_map/ppermute | solution.py:1343
  484.5 11.8 %collective-permute-start.5 = (f32[16,2496]{1,0:T(8,128)S(1)}, f32[16,2496]{1,0:T(8,128)S(1)}, u32[]{:S(2)}, u32[]{:S(2)}) collective-permute-start(f32[16,2496]{1,0:T(8,128)S(1)} %pad_maximum_fusion.2), channel_id=1, source_target_pairs={{0,8},{4,12},{8,0},{12,4},{16,24},{20,28},{24,16},{28,20},{1,9},{5... | collective-permute-start | bytes 479240 | tf_op jit(solution)/shard_map/ppermute | solution.py:1343
  486.3 18.9 %collective-permute-start.11 = (bf16[1,2,240,384]{3,2,1,0:T(8,128)(2,1)}, bf16[1,2,240,384]{3,2,1,0:T(8,128)(2,1)S(1)}, u32[]{:S(2)}, u32[]{:S(2)}) collective-permute-start(bf16[1,2,240,384]{3,2,1,0:T(8,128)(2,1)} %get-tuple-element.115.refs_5_.refs_2_), channel_id=1, source_target_pairs={{0,16},{4,20},{8,24},{12,28},{16,0},{20,4},{24,8},{28,12},{1,17},{... | collective-permute-start | bytes 1105928 | tf_op jit(solution)/shard_map/ppermute | solution.py:1313
  492.5 0.9 copy-start.8
  495.7 25.9 %collective-permute-start.8 = (bf16[2,2,144,384]{3,2,1,0:T(8,128)(2,1)}, bf16[2,2,144,384]{3,2,1,0:T(8,128)(2,1)S(1)}, u32[]{:S(2)}, u32[]{:S(2)}) collective-permute-start(bf16[2,2,144,384]{3,2,1,0:T(8,128)(2,1)} %get-tuple-element.118.refs_0_), channel_id=1, source_target_pairs={{0,8},{4,12},{8,0},{12,4},{16,24},{20,28},{24,16},{28,20},{1,9},{5... | collective-permute-start | bytes 1327112 | tf_op jit(solution)/shard_map/ppermute | solution.py:1313
  496.3 28.0 %collective-permute-start.6 = (f32[32,2496]{1,0:T(8,128)S(1)}, f32[32,2496]{1,0:T(8,128)S(1)}, u32[]{:S(2)}, u32[]{:S(2)}) collective-permute-start(f32[32,2496]{1,0:T(8,128)S(1)} %pad_maximum_fusion.1), channel_id=1, source_target_pairs={{0,16},{4,20},{8,24},{12,28},{16,0},{20,4},{24,8},{28,12},{1,17},{... | collective-permute-start | bytes 958472 | tf_op jit(solution)/shard_map/ppermute | solution.py:1343
  505.3 0.7 copy-start.11
  507.9 6.6 %collective-permute-start.12 = (bf16[1,1,240,384]{3,2,1,0:T(8,128)(2,1)}, bf16[1,1,240,384]{3,2,1,0:T(8,128)(2,1)S(1)}, u32[]{:S(2)}, u32[]{:S(2)}) collective-permute-start(bf16[1,1,240,384]{3,2,1,0:T(8,128)(2,1)} %get-tuple-element.125), channel_id=1, source_target_pairs={{0,2},{1,3},{2,0},{3,1},{4,6},{5,7},{6,4},{7,5},{8,10},{9,11},{10,... | collective-permute-start | bytes 552968 | tf_op jit(solution)/shard_map/ppermute | solution.py:1313
  514.5 0.7 copy-start.13
  521.6 0.8 copy-start.10
  524.3 12.3 %collective-permute-start.9 = (bf16[1,2,144,384]{3,2,1,0:T(8,128)(2,1)}, bf16[1,2,144,384]{3,2,1,0:T(8,128)(2,1)S(1)}, u32[]{:S(2)}, u32[]{:S(2)}) collective-permute-start(bf16[1,2,144,384]{3,2,1,0:T(8,128)(2,1)} %get-tuple-element.120), channel_id=1, source_target_pairs={{0,16},{4,20},{8,24},{12,28},{16,0},{20,4},{24,8},{28,12},{1,17},{... | collective-permute-start | bytes 663560 | tf_op jit(solution)/shard_map/ppermute | solution.py:1313
  536.6 0.7 copy-start.12
  539.0 5.2 collective-permute-start.10
  544.2 0.6 copy-start.16
Sparse Core Ops, SparseCore 0:
  215.4 151.5 reduce-scatter.1

commit v4 on v3

--- a/solution.py
+++ b/solution.py
@@ -327,6 +327,9 @@
 F32 = jnp.float32
 PACK = 384
 FIN = 2
+SUB = 128
+BSUB = 256
+CSUB = 256
 LIMIT = 60 * 2**20
 
 
@@ -473,6 +476,14 @@
     pass
 
 
+def ahead(work, make, use):
+    made = make(*work[0])
+    for number, item in enumerate(work):
+        later = make(*work[number + 1]) if number + 1 < len(work) else None
+        use(item, made)
+        made = later
+
+
 def soften(scores):
     top = jnp.max(scores, 1, keepdims=True)
     return jnp.exp2(scores - top).astype(BF), top
@@ -519,13 +530,23 @@
             def inner(position, carry):
                 rows = pl.ds(pl.multiple_of(position * qb, qb), qb)
                 queries = held[pair, rows]
-                outs = []
-                for half in (0, 1):
-                    prob, top = strips(soften, nt(keep_half(queries, half), keys))
+                work = [(half, at) for at in range(0, qb, SUB) for half in (0, 1)]
+                outs = [[], []]
+
+                def score(half, at):
+                    return nt(keep_half(queries[at : at + SUB], half), keys)
+
+                def use(place, scores):
+                    half, at = place
+                    prob, top = strips(soften, scores)
                     mixed = nn(prob, values)
                     total = mixed[:, 128:]
-                    lse_ref[0, 0, half : half + 1, rows] = (top + jnp.log2(total[:, :1])).T
-                    outs.append(mixed[:, :128] / total)
+                    cols = pl.ds(pl.multiple_of(position * qb + at, SUB), SUB)
+                    lse_ref[0, 0, half : half + 1, cols] = (top + jnp.log2(total[:, :1])).T
+                    outs[half].append(mixed[:, :128] / total)
+
+                ahead(work, score, use)
+                outs = [jnp.concatenate(out, 0) for out in outs]
                 att_ref[0, rows] = jnp.where(lane_half(0), outs[0], outs[1]).astype(BF)
                 return carry
 
@@ -559,18 +580,27 @@
                 queries = q_ref[0, rows]
                 grad = do_ref[0, rows]
                 dots = (grad.astype(F32) * o_ref[0, rows].astype(F32)).T
-                d_queries = []
-                for half in (0, 1):
-                    q_half = keep_half(queries, half)
-                    grad_half = keep_half(grad, half)
-                    delta = jnp.sum(dots[64 * half : 64 * half + 64], 0, keepdims=True)
-                    lse = lse_ref[0, 0, half : half + 1, rows]
-                    prob, d_scores = strips(
-                        partial(soft_back, lse=lse, delta=delta), nt(keys, q_half), nt(values, grad_half)
-                    )
+                d_queries = [[], []]
+                work = [(half, at) for at in range(0, qb, BSUB) for half in (0, 1)]
+
+                def score(half, at):
+                    q_half = keep_half(queries[at : at + BSUB], half)
+                    grad_half = keep_half(grad[at : at + BSUB], half)
+                    return q_half, grad_half, nt(keys, q_half), nt(values, grad_half)
+
+                def use(place, made):
+                    half, at = place
+                    q_half, grad_half, scores, d_prob = made
+                    delta = jnp.sum(dots[64 * half : 64 * half + 64, at : at + BSUB], 0, keepdims=True)
+                    cols = pl.ds(pl.multiple_of(position * qb + at, BSUB), BSUB)
+                    lse = lse_ref[0, 0, half : half + 1, cols]
+                    prob, d_scores = strips(partial(soft_back, lse=lse, delta=delta), scores, d_prob)
                     dv_acc[:klen] += nn(prob, grad_half)
                     dk_acc[:klen] += nn(d_scores, q_half)
-                    d_queries.append(tn(d_scores, keys))
+                    d_queries[half].append(tn(d_scores, keys))
+
+                ahead(work, score, use)
+                d_queries = [jnp.concatenate(part, 0) for part in d_queries]
                 held[step, rows] = (jnp.where(lane_half(0), d_queries[0], d_queries[1]) * score_scale).astype(BF)
                 return carry
 
@@ -659,21 +689,28 @@
     cq_ref[0] = (nn(hidden, wq_ref[...]) * (score_scale * LOG2E)).astype(BF)
     valid = lax.broadcasted_iota(jnp.int32, (1, slots), 1) < used
     ones = jnp.ones((slots, 128), BF)
-    for pair in range(H // 2):
+    count = cq_ref.shape[1]
+    outs = {}
+
+    def score(pair, half, at):
         cols = slice(pair * 128, pair * 128 + 128)
-        queries = cq_ref[0, :, cols]
-        keys = kv_ref[0, :, cols]
-        values = jnp.concatenate([kv_ref[0, :, width + pair * 128 : width + pair * 128 + 128], ones], 1)
-        outs = []
-        for half in (0, 1):
-            prob, top = strips(
-                lambda scores: soften(jnp.where(valid, scores, -1e30)), nt(keep_half(queries, half), keys)
-            )
-            mixed = nn(prob, values)
-            total = mixed[:, 128:]
-            lse_ref[0, pair, half : half + 1] = (top + jnp.log2(total[:, :1])).T
-            outs.append(mixed[:, :128] / total)
-        cr_ref[0, :, cols] = jnp.where(lane_half(0), outs[0], outs[1]).astype(BF)
+        return nt(keep_half(cq_ref[0, at : at + CSUB, cols], half), kv_ref[0, :, cols])
+
+    def use(place, scores):
+        pair, half, at = place
+        prob, top = strips(lambda part: soften(jnp.where(valid, part, -1e30)), scores)
+        values = kv_ref[0, :, width + pair * 128 : width + pair * 128 + 128]
+        mixed = nn(prob, jnp.concatenate([values, ones], 1))
+        total = mixed[:, 128:]
+        lse_ref[0, pair, half : half + 1, at : at + CSUB] = (top + jnp.log2(total[:, :1])).T
+        outs[half] = mixed[:, :128] / total
+        if half == 1:
+            cr_ref[0, at : at + CSUB, pair * 128 : pair * 128 + 128] = jnp.where(
+                lane_half(0), outs[0], outs[1]
+            ).astype(BF)
+
+    work = [(pair, half, at) for pair in range(H // 2) for at in range(0, count, CSUB) for half in (0, 1)]
+    ahead(work, score, use)
     branch_b = nn(cr_ref[0], wco_ref[...])
     bb_ref[0], second_ref[0] = strips(
         lambda rows, branch: (branch.astype(BF), (rows + gate_b * branch).astype(BF)), first, branch_b
@@ -705,13 +742,22 @@
             below, slope = gelu_parts(up_proj)
             return (up_proj * below).astype(BF), (d_act * slope).astype(BF)
 
-        for at in range(0, ff, chunk):
+        sides = [branch, d_hidden]
+
+        def make(at):
             cols = slice(at, at + chunk)
-            act, d_up = strips(middle, nn(hidden, wup_ref[:, cols]), nt(d_branch, wdn_ref[cols]))
-            branch += nn(act, wdn_ref[cols])
-            d_hidden += nt(d_up, wup_ref[:, cols])
+            return nn(hidden, wup_ref[:, cols]), nt(d_branch, wdn_ref[cols])
+
+        def use(place, made):
+            cols = slice(place[0], place[0] + chunk)
+            act, d_up = strips(middle, *made)
+            sides[0] += nn(act, wdn_ref[cols])
+            sides[1] += nt(d_up, wup_ref[:, cols])
             dn_acc[cols] += tn(act, d_branch)
             up_acc[:, cols] += tn(hidden, d_up)
+
+        ahead([(at,) for at in range(0, ff, chunk)], make, use)
+        branch, d_hidden = sides
 
         @pl.when(step % blocks == 0)
         def _():
@@ -785,33 +831,42 @@
         d_crossed = nt(d_branch_b, wco_ref[...])
         slot_of = lax.broadcasted_iota(jnp.int32, (slots, 1), 0)
         parts = []
-        for pair in range(H // 2):
+        kept = {}
+
+        def score(pair, half):
             cols = slice(pair * 128, pair * 128 + 128)
             vcols = slice(width + pair * 128, width + pair * 128 + 128)
-            queries = cq_ref[0, :, cols]
-            keys = kv_ref[0, :, cols]
-            values = kv_ref[0, :, vcols]
             grad = d_crossed[:, cols].astype(BF)
-            dots = (grad.astype(F32) * cr_ref[0, :, cols].astype(F32)).T
-            d_queries = []
-            d_keys = 0.0
-            d_values = 0.0
-            for half in (0, 1):
-                q_half = keep_half(queries, half)
-                grad_half = keep_half(grad, half)
-                delta = jnp.sum(dots[64 * half : 64 * half + 64], 0, keepdims=True)
-                lse = lse_ref[0, pair, half : half + 1]
-
-                def back(scores, d_prob, at, lse=lse, delta=delta):
-                    return soft_back(jnp.where(at < used, scores, -1e30), d_prob, lse, delta)
-
-                prob, d_scores = strips(back, nt(keys, q_half), nt(values, grad_half), slot_of)
-                d_values += nn(prob, grad_half)
-                d_keys += nn(d_scores, q_half)
-                d_queries.append(tn(d_scores, keys))
-            dtext[:, cols] += d_keys * (1.0 / LOG2E)
-            dtext[:, vcols] += d_values
-            parts.append((jnp.where(lane_half(0), d_queries[0], d_queries[1]) * score_scale).astype(BF))
+            q_half = keep_half(cq_ref[0, :, cols], half)
+            grad_half = keep_half(grad, half)
+            return grad, q_half, grad_half, nt(kv_ref[0, :, cols], q_half), nt(kv_ref[0, :, vcols], grad_half)
+
+        def use(place, made):
+            pair, half = place
+            grad, q_half, grad_half, scores, d_prob = made
+            cols = slice(pair * 128, pair * 128 + 128)
+            vcols = slice(width + pair * 128, width + pair * 128 + 128)
+            if half == 0:
+                kept["dots"] = (grad.astype(F32) * cr_ref[0, :, cols].astype(F32)).T
+            delta = jnp.sum(kept["dots"][64 * half : 64 * half + 64], 0, keepdims=True)
+            lse = lse_ref[0, pair, half : half + 1]
+
+            def back(part, d_part, at):
+                return soft_back(jnp.where(at < used, part, -1e30), d_part, lse, delta)
+
+            prob, d_scores = strips(back, scores, d_prob, slot_of)
+            d_values = nn(prob, grad_half)
+            d_keys = nn(d_scores, q_half)
+            d_query = tn(d_scores, kv_ref[0, :, cols])
+            if half == 0:
+                kept["sums"] = d_keys, d_values, d_query
+                return
+            first_keys, first_values, first_query = kept["sums"]
+            dtext[:, cols] += (first_keys + d_keys) * (1.0 / LOG2E)
+            dtext[:, vcols] += first_values + d_values
+            parts.append((jnp.where(lane_half(0), first_query, d_query) * score_scale).astype(BF))
+
+        ahead([(pair, half) for pair in range(H // 2) for half in (0, 1)], score, use)
         d_cq = jnp.concatenate(parts, 1)
         shift, scale, gate = mod_ref[0, 3:4], mod_ref[0, 4:5], mod_ref[0, 2:3]
         d_hidden = nt(d_cq, wq_ref[...])
@@ -1241,33 +1296,46 @@
     )
 
 
-def deal_call(table, got, per, block, skip, dtype, name, deps=(), group=2):
-    nf, _, _, width = got[0].shape
+def deal_call(table, jobs, per, name, deps=(), group=2):
+    nf, _, _, width = jobs[0][0][0].shape
     items = nf * per
     at = 2 + 3 * per
-    specs = []
-    for part in range(group):
-        if len(got) == 1:
-            specs.append(
-                pl.BlockSpec(
-                    (1, 1, block, width),
-                    lambda t, s, part=part: (s[at + t * group + part], 0, skip + s[at + items + t * group + part], 0),
+    specs, args, counts = [], [], []
+    for got, block, skip, _ in jobs:
+        counts.append(len(got) * group)
+        args += list(got) * group
+        for part in range(group):
+            if len(got) == 1:
+                specs.append(
+                    pl.BlockSpec(
+                        (1, 1, block, width),
+                        lambda t, s, part=part, skip=skip: (
+                            s[at + t * group + part], 0, skip + s[at + items + t * group + part], 0
+                        ),
+                    )
                 )
-            )
-        else:
-            specs += [
-                pl.BlockSpec((1, 1, block, width), lambda t, s, part=part: (s[at + t * group + part], 0, 0, 0))
-            ] * len(got)
+            else:
+                specs += [
+                    pl.BlockSpec((1, 1, block, width), lambda t, s, part=part: (s[at + t * group + part], 0, 0, 0))
+                ] * len(got)
+
+    def body(table, *refs):
+        outs = refs[sum(counts) :]
+        first = 0
+        for count, out in zip(counts, outs):
+            deal_kernel(table, *refs[first : first + count], out, at=at, items=items, group=group)
+            first += count
+
     return run(
-        partial(deal_kernel, at=at, items=items, group=group),
+        body,
         name,
         (items // group,),
         specs,
-        (table,) + tuple(got) * group,
-        pl.BlockSpec((group, block, width), lambda t, s: (t, 0, 0)),
-        struct((items, block, width), dtype),
+        (table, *args),
+        [pl.BlockSpec((group, job[1], width), lambda t, s: (t, 0, 0)) for job in jobs],
+        [struct((items, job[1], width), job[3]) for job in jobs],
         deps=deps,
-        work=cost(0, items * block * width * 6),
+        work=cost(0, items * jobs[0][1] * width * 6),
     )
 
 
@@ -1405,17 +1473,6 @@
     made_1, grad_send = gate_call([made_1, grad_send], [mid.got, got_0, sum_mlp])
     grad = Sum(grad_keep, grad_send, x_first, sizes)
     grad.launch()
-    got_1 = exchange(made_1)
-    layer_got = layer_got.reshape(nf, 1, per * block, width)
-    layer_out = deal_call(table, [layer_got], per, block, 0, BF, "deal_out")
-    grad.land([layer_out])
-    grad.launch()
-    mid.land([grad.send])
-    mid.launch()
-    text_grad = deal_call(
-        table, [got_0[:, None]], per, text.shape[1], block // text.shape[1], F32, "deal_text", [mid.send]
-    )
-    (dmod_1,) = gate_call([dmod_1], [text_grad])
     d_mod = jnp.concatenate([jnp.concatenate([dmod_0, dmod_1], 0), dmod_b, dmod_c], 1).reshape(per, 9 * width)
     ada_rows, ada_cols, cond_cols = width // ni, 9 * width // nf, width // nf
     high = d_mod.astype(BF)
@@ -1424,15 +1481,36 @@
     parts = jnp.concatenate(
         [d_mod.reshape(per, nf, ada_cols), (parts[:per] + parts[per:]).reshape(per, nf, cond_cols)], 2
     ).transpose(1, 0, 2)
-    mid.land([parts])
-    mid.launch()
-    (parts,) = gate_call([parts], [got_1, mid.send])
-    parts = exchange(parts).reshape(items, ada_cols + cond_cols)
-    input_grad = deal_call(table, [got_0[:, None], got_1[:, None]], per, block, 0, F32, "deal_in", [mid.send])
-    grad.land([input_grad])
+    parts = exchange(parts)
+    (made_1,) = gate_call([made_1], [parts])
+    got_1 = exchange(made_1)
+    grad.land([parts])
     grad.launch()
     mid.land([grad.send])
     mid.launch()
+    layer_out, text_grad = deal_call(
+        table,
+        [
+            ([layer_got.reshape(nf, 1, per * block, width)], block, 0, BF),
+            ([got_0[:, None]], text.shape[1], block // text.shape[1], F32),
+        ],
+        per,
+        "deal_out",
+        [grad.send, mid.send],
+    )
+    mid.land([layer_out])
+    mid.launch()
+    grad.land([mid.send])
+    grad.launch()
+    (input_grad,) = deal_call(
+        table, [([got_0[:, None], got_1[:, None]], block, 0, F32)], per, "deal_in", [grad.send, mid.send]
+    )
+    mid.land([input_grad])
+    mid.launch()
+    grad.land([mid.send])
+    grad.launch()
+    (parts,) = gate_call([parts], [grad.send])
+    parts = parts.reshape(items, ada_cols + cond_cols)
     at = 2 + 3 * per
     spot = table[at : at + items] * per + table[at + items : at + 2 * items]
     pick_row = spot[:, None] == jnp.arange(items, dtype=jnp.int32)[None, :]

time: 560 us -> 519 us (0.927); the launches traced: 554 us -> 524 us
  waiting for transfers between devices: 61.3 us -> 37.6 us
  blocking collectives: 0 us -> 14.7 us
  Pallas kernels: 367 us -> 356 us
  starting transfers between devices: 75.2 us -> 65.4 us
    all_to_all x7 -> x6, starting transfers between devices: 63.2 us -> 26 us  [exchange(): return lax.all_to_all(blocks, 'frames', 0, 0, tiled=True)]
    ppermute x10, starting transfers between devices: 6.99 us -> 36.7 us  [launch(): lax.ppermute(self.send, name, [(i, i ^ 1 << bit) for i in range(self.size...]
    all_to_all x0 -> x1, blocking collectives: none -> 14.7 us  [exchange(): return lax.all_to_all(blocks, 'frames', 0, 0, tiled=True)]
    ppermute x3, waiting for transfers between devices: 19.4 us -> 7.42 us  [collect_items(): lax.ppermute(rows, 'items', [(i, i ^ 1 << bit) for i in range(ni)])]
    pallas_call x12 -> x11, Pallas kernels: 338 us -> 328 us  [run(): pl.pallas_call(body, grid_spec=pltpu.PrefetchScalarGridSpec(num_scalar_pr...]
    ppermute x10, waiting for transfers between devices: 30.4 us -> 22.7 us  [launch(): lax.ppermute(self.send, name, [(i, i ^ 1 << bit) for i in range(self.size...]
    all_to_all x7 -> x6, waiting for transfers between devices: 11.4 us -> 7.42 us  [exchange(): return lax.all_to_all(blocks, 'frames', 0, 0, tiled=True)]
    unnamed x46 -> x44, local copies, waits for them, and re-layouts: 17.1 us -> 17 us
  transfers between devices with their start and end apart: 21 -> 20, of which waited for: 9 -> 7; matrix products, arithmetic and copies ran while one was open for 4% -> 3% of each run, Pallas kernels for 48% -> 49%
where the time goes in v4:
time: 519 us; the launch traced here: 524 us
  Pallas kernels  356 us (69%)
  starting transfers between devices  65.4 us (13%)
  waiting for transfers between devices  37.6 us (7%)
  local copies, waits for them, and re-layouts  18.9 us (4%)
  blocking collectives  14.7 us (3%)
  between operations  14.6 us (3%)
  matrix products  14 us (3%)
    pallas_call x11, Pallas kernels, run(): pl.pallas_call(body, grid_spec=pltpu.PrefetchScalarGridSpec(num_scalar_pr...  328 us
    ppermute x10, starting transfers between devices, launch(): lax.ppermute(self.send, name, [(i, i ^ 1 << bit) for i in range(self.size...  36.7 us
    all_to_all x6, starting transfers between devices, exchange(): return lax.all_to_all(blocks, 'frames', 0, 0, tiled=True)  26 us
    ppermute x10, waiting for transfers between devices, launch(): lax.ppermute(self.send, name, [(i, i ^ 1 << bit) for i in range(self.size...  22.7 us
    pallas_call x8, Pallas kernels, land(): pl.pallas_call(land_kernel, grid=(outer,), in_specs=[source] * 2 + any_sp...  21.7 us
    unnamed x44, local copies, waits for them, and re-layouts  17 us
    all_to_all x1, blocking collectives, exchange(): return lax.all_to_all(blocks, 'frames', 0, 0, tiled=True)  14.7 us
  transfers between devices with their start and end apart: 20, of which 7 were waited for; matrix products, arithmetic and copies ran while one was open for 3% of the time, Pallas kernels for 49%

profile of v4, /device:TPU:0, one launch (start us, length us, event | category | flops | bytes accessed | tf_op | source)
XLA Modules:
  0.0 524.2 jit_solution(13647577357493621267)
XLA Ops:
  9.2 4.4 gather_first.1
  13.5 4.2 all-to-all-start
  17.9 5.5 %fusion.10 = f32[8,6912]{1,0:T(8,128)S(1)} fusion(bf16[768,6912]{1,0:T(8,128)(2,1)} %param.19, bf16[8,768]{1,0:T(8,128)(2,1)S(1)} %copy-done.13), kind=kOutput, calls=%fused_computation.26 | convolution fusion | flops 84971520 | bytes 10850304 | tf_op jit(solution)/shard_map/dot_general | solution.py:337
  24.4 6.1 %gather.1 = (bf16[4,384,768]{2,1,0:T(8,128)(2,1)}, bf16[4,2,256,768]{3,2,1,0:T(8,128)(2,1)}) custom-call(s32[32]{0:T(128)} %start.1.refs_0_, bf16[8,256,768]{2,1,0:T(8,128)(2,1)} %refs_1_.3, bf16[8,64,768]{2,1,0:T(8,128)(2,1)} %refs_3_.3, bf16[8,64,768]{2,1,0:T(8,128)(2,1)} %refs_3_.3, bf16[8,256,768]{2,1,0:T(8,128)(2,1)} %refs_5_.3, ...), custom_call_target="tpu_custom_call" | custom-call | tf_op jit(solution)/shard_map/gather/pallas_call | solution.py:982
  30.4 7.4 %all-to-all-done.refs_1_ = bf16[4,256,768]{2,1,0:T(8,128)(2,1)S(1)} async-done(((bf16[4,256,768]{2,1,0:T(8,128)(2,1)}), bf16[4,256,768]{2,1,0:T(8,128)(2,1)S(1)}, u32[]{:S(2)}, u32[]{:S(2)}) %all-to-all-start) | async-done | bytes 1572896 | tf_op jit(solution)/shard_map/all_to_all | solution.py:1354
  39.0 3.6 all-to-all-start.1
  42.6 28.6 %self_fwd.2 = (bf16[2,1024,768]{2,1,0:T(8,128)(2,1)}, bf16[2,1024,2304]{2,1,0:T(8,128)(2,1)}, bf16[2,1024,768]{2,1,0:T(8,128)(2,1)}, f32[2,6,2,1024]{3,2,1,0:T(2,128)}) custom-call(s32[32]{0:T(128)} %start.1.refs_0_, bf16[4,256,768]{2,1,0:T(8,128)(2,1)} %copy-done.4, f32[2,9,768]{2,1,0:T(8,128)} %reshape.119.refs_2_.refs_3_.refs_8_.refs_9_.refs_13_, ...), custom_call_target="tpu_custom_call" | custom-call | flops 16508780544 | bytes 12582912 | tf_op jit(solution)/shard_map/self_fwd/pallas_call | solution.py:982
  72.7 3.7 all-to-all-start.2
  76.9 17.9 %self_fwd.3 = (bf16[2,1024,768]{2,1,0:T(8,128)(2,1)}, bf16[2,1024,2304]{2,1,0:T(8,128)(2,1)}, bf16[2,1024,768]{2,1,0:T(8,128)(2,1)}, f32[2,6,2,1024]{3,2,1,0:T(2,128)}) custom-call(s32[32]{0:T(128)} %start.1.refs_0_, bf16[4,384,768]{2,1,0:T(8,128)(2,1)} %copy-done.3, ...), custom_call_target="tpu_custom_call", output_to_operand_aliasing={{0}: (4, {}), {1}: (5, {}), {2}: (6, {}), {3}: (7, {})} | custom-call | flops 16508780544 | bytes 12582912 | tf_op jit(solution)/shard_map/self_fwd/pallas_call | solution.py:982
  94.8 26.3 %cross_fwd.1 = (bf16[2,256,1536]{2,1,0:T(8,128)(2,1)}, bf16[2,256,768]{2,1,0:T(8,128)(2,1)}, bf16[2,1024,768]{2,1,0:T(8,128)(2,1)}, bf16[2,1024,768]{2,1,0:T(8,1...) custom-call(s32[32]{0:T(128)} %start.1.refs_0_, ...), custom_call_target="tpu_custom_call" | custom-call | flops 13690208256 | bytes 31457280 | tf_op jit(solution)/shard_map/cross_fwd/pallas_call | solution.py:982
  121.2 1.7 copy-done.5
  122.8 90.0 %mlp.1 = (bf16[4,2,256,768]{3,2,1,0:T(8,128)(2,1)}, bf16[2,1024,768]{2,1,0:T(8,128)(2,1)}, f32[2,3,768]{2,1,0:T(4,128)}, bf16[8,4,384,384]{3,2,1,0:T(8,128)(2,1)}) custom-call(s32[32]{0:T(128)} %start.1.refs_0_, bf16[2,1024,768]{2,1,0:T(8,128)(2,1)} %get-tuple-element.82.refs_1_, bf16[4,2,256,768]{3,2,1,0:T(8,128)(2,1)} %copy-done.5, ...), custom_call_target="tpu_custom_call" | custom-call | flops 57982058496 | bytes 25165824 | tf_op jit(solution)/shard_map/mlp/pallas_call | solution.py:982
  212.9 7.1 %all-to-all-start.3 = ((bf16[4,2,256,768]{3,2,1,0:T(8,128)(2,1)}), bf16[4,2,256,768]{3,2,1,0:T(8,128)(2,1)S(1)}, u32[]{:S(2)}, u32[]{:S(2)}) async-start(bf16[4,2,256,768]{3,2,1,0:T(8,128)(2,1)} %get-tuple-element.83), calls=%async_computation.3 | async-start | bytes 6291456 | tf_op jit(solution)/shard_map/all_to_all | solution.py:1354
  220.0 58.1 %cross_bwd.1 = (bf16[2,1024,768]{2,1,0:T(8,128)(2,1)}, bf16[2,1024,768]{2,1,0:T(8,128)(2,1)}, bf16[4,2,64,768]{3,2,1,0:T(8,128)(2,1)}, f32[2,4,768]{2,1,0:T(4,12...) custom-call(s32[32]{0:T(128)} %start.1.refs_0_, bf16[2,1024,768]{2,1,0:T(8,128)(2,1)} %get-tuple-element.85.refs_1_, ...), custom_call_target="tpu_custom_call" | custom-call | flops 30601641984 | bytes 37748736 | tf_op jit(solution)/shard_map/cross_bwd/pallas_call | solution.py:982
  278.9 1.7 copy-done.1
  280.6 45.8 %self_bwd.2 = (bf16[4,384,768]{2,1,0:T(8,128)(2,1)}, f32[1,2,768]{2,1,0:T(2,128)}, bf16[1024,2304]{1,0:T(8,128)(2,1)}) custom-call(s32[32]{0:T(128)} %start.1.refs_0_, bf16[2,1024,2304]{2,1,0:T(8,128)(2,1)} %get-tuple-element.84.refs_1_.refs_2_.refs_3_, bf16[2,1024,2304]{2,1,0:T(8,128)(2,1)} %get-tuple-element.84.refs_1_.refs_2_.refs_3_, ...), custom_call_target="tpu_custom_call" | custom-call | flops 39460012032 | bytes 23592960 | tf_op jit(solution)/shard_map/self_bwd/pallas_call | solution.py:982
  326.3 3.6 all-to-all-start.4
  330.0 4.8 land.8
  334.8 2.8 collective-permute-start.1
  337.6 38.6 %self_bwd.3 = (bf16[4,256,768]{2,1,0:T(8,128)(2,1)}, f32[1,2,768]{2,1,0:T(2,128)}, bf16[8,2,144,384]{3,2,1,0:T(8,128)(2,1)}, bf16[8,2,144,384]{3,2,1,0:T(8,128)(2,1)}) custom-call(s32[32]{0:T(128)} %start.1.refs_0_, bf16[2,1024,2304]{2,1,0:T(8,128)(2,1)} %get-tuple-element.84.refs_1_.refs_2_.refs_3_, ...), custom_call_target="tpu_custom_call" | custom-call | flops 39460012032 | bytes 23592960 | tf_op jit(solution)/shard_map/self_bwd/pallas_call | solution.py:982
  378.8 6.9 %fusion.2 = f32[4,768]{1,0:T(4,128)S(1)} fusion(bf16[768,6912]{1,0:T(8,128)(2,1)} %param.19, bf16[2,6912]{1,0:T(2,128)(2,1)S(1)} %get-tuple-element.172, bf16[2,6912]{1,0:T(2,128)(2,1)S(1)} %get-tuple-element.173), kind=kOutput, calls=%fused_computation.10 | convolution fusion | flops 42577920 | bytes 10684416 | tf_op jit(solution)/shard_map/dot_general | solution.py:341
  386.0 14.7 %all_to_all.35.refs_0_.refs_1_ = f32[4,2,1920]{2,1,0:T(2,128)} all-to-all(f32[4,2,1920]{2,1,0:T(2,128)S(1)} %maximum_bitcast_fusion), channel_id=1, replica_groups=mesh['items'=8,'frames'=4] {'frames'}, dimensions={0} | all-to-all | bytes 122880 | tf_op jit(solution)/shard_map/all_to_all | solution.py:1354
  401.9 4.0 land.9
  406.6 2.8 land.10
  409.4 1.5 collective-permute-start.4
  410.8 3.7 all-to-all-start.6
  414.6 5.4 %deal_out.1 = (bf16[8,256,768]{2,1,0:T(8,128)(2,1)}, f32[8,64,768]{2,1,0:T(8,128)}) custom-call(s32[32]{0:T(128)} %start.1.refs_0_, bf16[4,1,512,768]{3,2,1,0:T(8,128)(2,1)} %bitcast.38, bf16[4,1,512,768]{3,2,1,0:T(8,128)(2,1)} %bitcast.39, bf16[4,1,384,768]{3,2,1,0:T(8,128)(2,1)} %bitcast.34, bf16[4,1,384,768]{3,2,1,0:T(8,128)(2,1)} %bitcast.35, ...), custom_call_target="tpu_custom_call" | custom-call | bytes 9437184 | tf_op jit(solution)/shard_map/deal_out/pallas_call | solution.py:982
  420.0 7.3 %collective-permute-done.4 = bf16[2,2,240,384]{3,2,1,0:T(8,128)(2,1)S(1)} collective-permute-done((bf16[2,2,240,384]{3,2,1,0:T(8,128)(2,1)}, bf16[2,2,240,384]{3,2,1,0:T(8,128)(2,1)S(1)}, u32[]{:S(2)}, u32[]{:S(2)}) %collective-permute-start.4) | collective-permute-done | bytes 737312 | tf_op jit(solution)/shard_map/ppermute | solution.py:1381
  428.2 2.3 land.11
  430.5 24.5 %collective-permute-start.6 = (bf16[1,2,240,384]{3,2,1,0:T(8,128)(2,1)}, bf16[1,2,240,384]{3,2,1,0:T(8,128)(2,1)S(1)}, u32[]{:S(2)}, u32[]{:S(2)}) collective-permute-start(bf16[1,2,240,384]{3,2,1,0:T(8,128)(2,1)} %get-tuple-element.119.refs_0_.refs_6_), channel_id=1, source_target_pairs={{0,16},{4,20},{8,24},{12,28},{16,0},{20,4},{24,8},{28,12},{1,17},{... | collective-permute-start | bytes 1105928 | tf_op jit(solution)/shard_map/ppermute | solution.py:1381
  456.0 2.2 land.12
  458.2 1.7 collective-permute-start.5
  461.3 6.5 %deal_in.1.refs_0_ = f32[8,256,768]{2,1,0:T(8,128)} custom-call(s32[32]{0:T(128)} %start.1.refs_0_, bf16[4,1,384,768]{3,2,1,0:T(8,128)(2,1)} %bitcast.36, bf16[4,1,256,768]{3,2,1,0:T(8,128)(2,1)} %bitcast.40, bf16[4,1,384,768]{3,2,1,0:T(8,128)(2,1)} %bitcast.37, bf16[4,1,256,768]{3,2,1,0:T(8,128)(2,1)} %bitcast.41, ...), custom_call_target="tpu_custom_call" | custom-call | bytes 9437184 | tf_op jit(solution)/shard_map/deal_in/pallas_call | solution.py:982
  467.7 3.4 collective-permute-done.6
  471.8 1.9 land.13
  473.7 2.6 collective-permute-done.5
  477.0 2.0 land.14
  481.6 3.1 collective-permute-done.7
  484.9 2.4 collective-permute-start.10
  487.4 4.4 collective-permute-done.8
  493.0 1.8 finish_mid.1
  494.9 9.4 %collective-permute-done.10 = bf16[1,2,144,384]{3,2,1,0:T(8,128)(2,1)S(1)} collective-permute-done((bf16[1,2,144,384]{3,2,1,0:T(8,128)(2,1)}, bf16[1,2,144,384]{3,2,1,0:T(8,128)(2,1)S(1)}, u32[]{:S(2)}, u32[]{:S(2)}) %collective-permute-start.10) | collective-permute-done | bytes 221216 | tf_op jit(solution)/shard_map/ppermute | solution.py:1381
  505.0 1.8 land.15
  506.8 1.9 collective-permute-start.11
  509.4 1.8 finish_mlp.1
  511.2 1.9 copy.42
  513.7 1.7 finish_qkv.1
  515.5 1.7 fusion
  (94 shorter events, 22.5 us)
Async XLA Ops:
  9.1 8.6 %copy-start.18 = (s32[32]{0:T(128)S(1)}, s32[32]{0:T(128)}, u32[]{:S(2)}) copy-start(s32[32]{0:T(128)} %start.1.refs_0_) | copy-start | bytes 388
  9.1 8.8 %copy-start.13 = (bf16[8,768]{1,0:T(8,128)(2,1)S(1)}, bf16[8,768]{1,0:T(8,128)(2,1)}, u32[]{:S(2)}) copy-start(bf16[8,768]{1,0:T(8,128)(2,1)} %param.15) | copy-start | bytes 36868
  13.5 24.3 %all-to-all-start = ((bf16[4,256,768]{2,1,0:T(8,128)(2,1)}), bf16[4,256,768]{2,1,0:T(8,128)(2,1)S(1)}, u32[]{:S(2)}, u32[]{:S(2)}) async-start(bf16[4,256,768]{2,1,0:T(8,128)(2,1)} %gather_first.1), calls=%async_computation | async-start | bytes 3145728 | tf_op jit(solution)/shard_map/all_to_all | solution.py:1354
  37.9 1.1 copy-start.4
  39.0 32.2 %all-to-all-start.1 = ((bf16[4,384,768]{2,1,0:T(8,128)(2,1)}), bf16[4,384,768]{2,1,0:T(8,128)(2,1)S(1)}, u32[]{:S(2)}, u32[]{:S(2)}) async-start(bf16[4,384,768]{2,1,0:T(8,128)(2,1)} %gate.5.refs_4_), calls=%async_computation.1 | async-start | bytes 4718592 | tf_op jit(solution)/shard_map/all_to_all | solution.py:1354
  71.2 1.5 copy-start.3
  72.7 48.5 %all-to-all-start.2 = ((bf16[4,2,256,768]{3,2,1,0:T(8,128)(2,1)}), bf16[4,2,256,768]{3,2,1,0:T(8,128)(2,1)S(1)}, u32[]{:S(2)}, u32[]{:S(2)}) async-start(bf16[4,2,256,768]{3,2,1,0:T(8,128)(2,1)} %gate.6.refs_8_), calls=%async_computation.2 | async-start | bytes 6291456 | tf_op jit(solution)/shard_map/all_to_all | solution.py:1354
  76.4 300.7 %reduce-scatter.2.cloned.1.call-start = ((), (), s32[]{:S(2)}) async-start(), calls=%async_computation.8 | async-start | bytes 9732096 | tf_op jit(solution)/shard_map/reduce_scatter | solution.py:1453
  121.2 1.7 copy-start.5
  212.9 66.0 %all-to-all-start.3 = ((bf16[4,2,256,768]{3,2,1,0:T(8,128)(2,1)}), bf16[4,2,256,768]{3,2,1,0:T(8,128)(2,1)S(1)}, u32[]{:S(2)}, u32[]{:S(2)}) async-start(bf16[4,2,256,768]{3,2,1,0:T(8,128)(2,1)} %get-tuple-element.83), calls=%async_computation.3 | async-start | bytes 6291456 | tf_op jit(solution)/shard_map/all_to_all | solution.py:1354
  278.2 51.8 %collective-permute-start = (bf16[8,2,240,384]{3,2,1,0:T(8,128)(2,1)}, bf16[8,2,240,384]{3,2,1,0:T(8,128)(2,1)}, u32[]{:S(2)}, u32[]{:S(2)}) collective-permute-start(bf16[8,2,240,384]{3,2,1,0:T(8,128)(2,1)} %get-tuple-element.101), channel_id=1, source_target_pairs={{0,1},{1,0},{2,3},{3,2},{4,5},{5,4},{6,7},{7,6},{8,9},{9,8},{10,11... | collective-permute-start | bytes 8847368 | tf_op jit(solution)/shard_map/ppermute | solution.py:1381
  278.9 1.7 copy-start.1
  326.3 50.7 %all-to-all-start.4 = ((bf16[4,384,768]{2,1,0:T(8,128)(2,1)}), bf16[4,384,768]{2,1,0:T(8,128)(2,1)S(1)}, u32[]{:S(2)}, u32[]{:S(2)}) async-start(bf16[4,384,768]{2,1,0:T(8,128)(2,1)} %get-tuple-element.98), calls=%async_computation.4 | async-start | bytes 4718592 | tf_op jit(solution)/shard_map/all_to_all | solution.py:1354
  334.8 42.3 %collective-permute-start.1 = (bf16[4,2,240,384]{3,2,1,0:T(8,128)(2,1)}, bf16[4,2,240,384]{3,2,1,0:T(8,128)(2,1)}, u32[]{:S(2)}, u32[]{:S(2)}) collective-permute-start(bf16[4,2,240,384]{3,2,1,0:T(8,128)(2,1)} %get-tuple-element.102.refs_14_), channel_id=1, source_target_pairs={{0,4},{4,0},{8,12},{12,8},{16,20},{20,16},{24,28},{28,24},{1,5},{5... | collective-permute-start | bytes 4423688 | tf_op jit(solution)/shard_map/ppermute | solution.py:1381
  337.6 38.6 %copy-start.16 = (f32[2,3,768]{2,1,0:T(4,128)S(1)}, f32[2,3,768]{2,1,0:T(4,128)}, u32[]{:S(2)}) copy-start(f32[2,3,768]{2,1,0:T(4,128)} %get-tuple-element.111) | copy-start | bytes 55300
  337.6 38.6 %copy-start.17 = (f32[2,4,768]{2,1,0:T(4,128)S(1)}, f32[2,4,768]{2,1,0:T(4,128)}, u32[]{:S(2)}) copy-start(f32[2,4,768]{2,1,0:T(4,128)} %get-tuple-element.110) | copy-start | bytes 73732
  337.6 38.6 %copy-start.20 = (f32[1,2,768]{2,1,0:T(2,128)S(1)}, f32[1,2,768]{2,1,0:T(2,128)}, u32[]{:S(2)}) copy-start(f32[1,2,768]{2,1,0:T(2,128)} %get-tuple-element.108) | copy-start | bytes 18436
  377.0 1.4 copy-start
  378.4 22.3 %collective-permute-start.2 = (bf16[8,2,144,384]{3,2,1,0:T(8,128)(2,1)}, bf16[8,2,144,384]{3,2,1,0:T(8,128)(2,1)S(1)}, u32[]{:S(2)}, u32[]{:S(2)}) collective-permute-start(bf16[8,2,144,384]{3,2,1,0:T(8,128)(2,1)} %get-tuple-element.107), channel_id=1, source_target_pairs={{0,1},{1,0},{2,3},{3,2},{4,5},{5,4},{6,7},{7,6},{8,9},{9,8},{10,11... | collective-permute-start | bytes 5308424 | tf_op jit(solution)/shard_map/ppermute | solution.py:1381
  400.7 1.2 copy-start.6
  405.9 49.1 %collective-permute-start.3 = (bf16[4,2,144,384]{3,2,1,0:T(8,128)(2,1)}, bf16[4,2,144,384]{3,2,1,0:T(8,128)(2,1)S(1)}, u32[]{:S(2)}, u32[]{:S(2)}) collective-permute-start(bf16[4,2,144,384]{3,2,1,0:T(8,128)(2,1)} %get-tuple-element.112.refs_0_.refs_5_), channel_id=1, source_target_pairs={{0,4},{4,0},{8,12},{12,8},{16,20},{20,16},{24,28},{28,24},{1,5},{5... | collective-permute-start | bytes 2654216 | tf_op jit(solution)/shard_map/ppermute | solution.py:1381
  409.4 18.0 %collective-permute-start.4 = (bf16[2,2,240,384]{3,2,1,0:T(8,128)(2,1)}, bf16[2,2,240,384]{3,2,1,0:T(8,128)(2,1)S(1)}, u32[]{:S(2)}, u32[]{:S(2)}) collective-permute-start(bf16[2,2,240,384]{3,2,1,0:T(8,128)(2,1)} %get-tuple-element.114.refs_6_), channel_id=1, source_target_pairs={{0,8},{4,12},{8,0},{12,4},{16,24},{20,28},{24,16},{28,20},{1,9},{5... | collective-permute-start | bytes 2211848 | tf_op jit(solution)/shard_map/ppermute | solution.py:1381
  410.8 3.7 copy-start.19
  410.8 49.3 %all-to-all-start.6 = ((bf16[4,256,768]{2,1,0:T(8,128)(2,1)}), bf16[4,256,768]{2,1,0:T(8,128)(2,1)S(1)}, u32[]{:S(2)}, u32[]{:S(2)}) async-start(bf16[4,256,768]{2,1,0:T(8,128)(2,1)} %gate.8), calls=%async_computation.7 | async-start | bytes 3145728 | tf_op jit(solution)/shard_map/all_to_all | solution.py:1354
  427.3 0.9 copy-start.8
  428.2 31.8 %copy-start.14 = (bf16[8,768]{1,0:T(8,128)(2,1)S(1)}, bf16[8,768]{1,0:T(8,128)(2,1)}, u32[]{:S(2)}) copy-start(bf16[8,768]{1,0:T(8,128)(2,1)} %param.15) | copy-start | bytes 36868
  430.5 40.6 %collective-permute-start.6 = (bf16[1,2,240,384]{3,2,1,0:T(8,128)(2,1)}, bf16[1,2,240,384]{3,2,1,0:T(8,128)(2,1)S(1)}, u32[]{:S(2)}, u32[]{:S(2)}) collective-permute-start(bf16[1,2,240,384]{3,2,1,0:T(8,128)(2,1)} %get-tuple-element.119.refs_0_.refs_6_), channel_id=1, source_target_pairs={{0,16},{4,20},{8,24},{12,28},{16,0},{20,4},{24,8},{28,12},{1,17},{... | collective-permute-start | bytes 1105928 | tf_op jit(solution)/shard_map/ppermute | solution.py:1381
  455.1 0.9 copy-start.7
  458.2 18.0 %collective-permute-start.5 = (bf16[2,2,144,384]{3,2,1,0:T(8,128)(2,1)}, bf16[2,2,144,384]{3,2,1,0:T(8,128)(2,1)S(1)}, u32[]{:S(2)}, u32[]{:S(2)}) collective-permute-start(bf16[2,2,144,384]{3,2,1,0:T(8,128)(2,1)} %get-tuple-element.120.refs_5_), channel_id=1, source_target_pairs={{0,8},{4,12},{8,0},{12,4},{16,24},{20,28},{24,16},{28,20},{1,9},{5... | collective-permute-start | bytes 1327112 | tf_op jit(solution)/shard_map/ppermute | solution.py:1381
  460.1 1.2 copy-start.2
  471.1 0.7 copy-start.10
  476.3 0.8 copy-start.9
  480.2 4.5 collective-permute-start.7
  484.6 7.1 %collective-permute-start.8 = (f32[16,2496]{1,0:T(8,128)S(1)}, f32[16,2496]{1,0:T(8,128)S(1)}, u32[]{:S(2)}, u32[]{:S(2)}) collective-permute-start(f32[16,2496]{1,0:T(8,128)S(1)} %pad_maximum_fusion.2), channel_id=1, source_target_pairs={{0,8},{4,12},{8,0},{12,4},{16,24},{20,28},{24,16},{28,20},{1,9},{5... | collective-permute-start | bytes 479240 | tf_op jit(solution)/shard_map/ppermute | solution.py:1411
  484.7 7.6 %collective-permute-start.12 = (bf16[1,1,240,384]{3,2,1,0:T(8,128)(2,1)}, bf16[1,1,240,384]{3,2,1,0:T(8,128)(2,1)S(1)}, u32[]{:S(2)}, u32[]{:S(2)}) collective-permute-start(bf16[1,1,240,384]{3,2,1,0:T(8,128)(2,1)} %get-tuple-element.124.refs_0_), channel_id=1, source_target_pairs={{0,2},{1,3},{2,0},{3,1},{4,6},{5,7},{6,4},{7,5},{8,10},{9,11},{10,... | collective-permute-start | bytes 552968 | tf_op jit(solution)/shard_map/ppermute | solution.py:1381
  484.9 19.4 %collective-permute-start.10 = (bf16[1,2,144,384]{3,2,1,0:T(8,128)(2,1)}, bf16[1,2,144,384]{3,2,1,0:T(8,128)(2,1)S(1)}, u32[]{:S(2)}, u32[]{:S(2)}) collective-permute-start(bf16[1,2,144,384]{3,2,1,0:T(8,128)(2,1)} %get-tuple-element.125.refs_1_.refs_0_), channel_id=1, source_target_pairs={{0,16},{4,20},{8,24},{12,28},{16,0},{20,4},{24,8},{28,12},{1,17},{... | collective-permute-start | bytes 663560 | tf_op jit(solution)/shard_map/ppermute | solution.py:1381
  491.8 23.7 %collective-permute-start.9 = (f32[32,2496]{1,0:T(8,128)S(1)}, f32[32,2496]{1,0:T(8,128)S(1)}, u32[]{:S(2)}, u32[]{:S(2)}) collective-permute-start(f32[32,2496]{1,0:T(8,128)S(1)} %pad_maximum_fusion.1), channel_id=1, source_target_pairs={{0,16},{4,20},{8,24},{12,28},{16,0},{20,4},{24,8},{28,12},{1,17},{... | collective-permute-start | bytes 958472 | tf_op jit(solution)/shard_map/ppermute | solution.py:1411
  492.4 0.7 copy-start.12
  504.3 0.7 copy-start.11
  506.8 6.3 %collective-permute-start.11 = (bf16[1,1,144,384]{3,2,1,0:T(8,128)(2,1)}, bf16[1,1,144,384]{3,2,1,0:T(8,128)(2,1)S(1)}, u32[]{:S(2)}, u32[]{:S(2)}) collective-permute-start(bf16[1,1,144,384]{3,2,1,0:T(8,128)(2,1)} %get-tuple-element.128), channel_id=1, source_target_pairs={{0,2},{1,3},{2,0},{3,1},{4,6},{5,7},{6,4},{7,5},{8,10},{9,11},{10,... | collective-permute-start | bytes 331784 | tf_op jit(solution)/shard_map/ppermute | solution.py:1381
  513.1 0.6 copy-start.15
Sparse Core Ops, SparseCore 0:
  213.0 151.0 reduce-scatter.1

commit v5 on v4

--- a/solution.py
+++ b/solution.py
@@ -330,7 +330,7 @@
 SUB = 128
 BSUB = 256
 CSUB = 256
-LIMIT = 60 * 2**20
+LIMIT = 127 * 2**19
 
 
 def nn(left, right):
@@ -459,8 +459,9 @@
         table[2 + 2 * per + slot] = text_lengths[item]
 
 
-def copy_kernel(table, source, out):
-    out[...] = source[...]
+def gather_first_kernel(table, *refs):
+    for to, source in enumerate(refs[:-1]):
+        refs[-1][to] = source[0]
 
 
 def gather_kernel(table, *refs, per):
@@ -734,30 +735,35 @@
     def _():
         shift, scale, gate = mod_ref[0, 6:7], mod_ref[0, 7:8], mod_ref[0, 8:9]
         hidden = strips(lambda rows: modulate(rows, shift, scale), second_ref[0])
-        d_branch = strips(lambda rows: (rows.astype(F32) * gate).astype(BF), cot_ref[0, 0])
-        branch = jnp.zeros(second_ref.shape[1:], F32)
-        d_hidden = jnp.zeros(second_ref.shape[1:], F32)
-
+        cot = jnp.concatenate([cot_ref[at, 0] for at in range(cot_ref.shape[0])], 0)
+        d_branch = strips(lambda rows: (rows.astype(F32) * gate).astype(BF), cot)
         def middle(up_proj, d_act):
             below, slope = gelu_parts(up_proj)
             return (up_proj * below).astype(BF), (d_act * slope).astype(BF)
 
-        sides = [branch, d_hidden]
-
-        def make(at):
-            cols = slice(at, at + chunk)
-            return nn(hidden, wup_ref[:, cols]), nt(d_branch, wdn_ref[cols])
-
-        def use(place, made):
-            cols = slice(place[0], place[0] + chunk)
-            act, d_up = strips(middle, *made)
-            sides[0] += nn(act, wdn_ref[cols])
-            sides[1] += nt(d_up, wup_ref[:, cols])
-            dn_acc[cols] += tn(act, d_branch)
-            up_acc[:, cols] += tn(hidden, d_up)
-
-        ahead([(at,) for at in range(0, ff, chunk)], make, use)
-        branch, d_hidden = sides
+        third = chunk // 3
+        span = width // 3
+        count = ff // chunk
+        made, done = {}, {}
+        branches = [jnp.zeros((second_ref.shape[1], span), F32)] * 3
+        d_hiddens = [jnp.zeros((second_ref.shape[1], span), F32)] * 3
+        for at in range(count + 2):
+            for part in range(3):
+                sub = slice(part * span, (part + 1) * span)
+                if at < count:
+                    cols = slice(at * chunk + part * third, at * chunk + (part + 1) * third)
+                    made[at, part] = nn(hidden, wup_ref[:, cols]), nt(d_branch, wdn_ref[cols])
+                if 1 <= at <= count:
+                    done[at - 1, part] = strips(middle, *made.pop((at - 1, part)))
+                if at >= 2:
+                    cols = slice((at - 2) * chunk, (at - 1) * chunk)
+                    act, d_up = (jnp.concatenate([done[at - 2, p][side] for p in range(3)], 1) for side in (0, 1))
+                    branches[part] += nn(act, wdn_ref[cols, sub])
+                    d_hiddens[part] += nt(d_up, wup_ref[sub, cols])
+                    cols = slice((at - 2) * chunk + part * third, (at - 2) * chunk + (part + 1) * third)
+                    dn_acc[cols] += tn(done[at - 2, part][0], d_branch)
+                    up_acc[:, cols] += tn(hidden, done[at - 2, part][1])
+        branch, d_hidden = jnp.concatenate(branches, 1), jnp.concatenate(d_hiddens, 1)
 
         @pl.when(step % blocks == 0)
         def _():
@@ -775,7 +781,10 @@
             upstream = upstream + ln_back(normed, inverse, dh * (1.0 + scale))
             return (second + gate * branch_rows).astype(BF), upstream.astype(BF)
 
-        out_ref[0, 0], g2_ref[0] = strips(leave, second_ref[0], cot_ref[0, 0], branch, d_hidden)
+        out, g2_ref[0] = strips(leave, second_ref[0], cot, branch, d_hidden)
+        rows = out_ref.shape[2]
+        for at in range(out_ref.shape[0]):
+            out_ref[at, 0] = out[at * rows : (at + 1) * rows]
         for at in range(3):
             dmod_ref[0, at : at + 1] += sums.total(at)
 
@@ -795,9 +804,9 @@
 
 def cross_back_kernel(
     table, g2_ref, bb_ref, cr_ref, cq_ref, att_ref, ba_ref, first_ref, mod_ref, kv_ref, lse_ref, text_ref,
-    wo_ref, wq_ref, wco_ref, wkv_ref,
-    g1_ref, datt_ref, text_out, dmod_ref, keep_ref, send_ref,
-    o_acc, q_acc, co_acc, kv_acc, dtext, *, blocks, total, score_scale, nf, ni, length_at,
+    wo_ref, wq_ref, wco_ref, wkv_ref, _,
+    g1_ref, datt_ref, text_out, dmod_ref, all_ref,
+    o_acc, q_acc, co_acc, kv_acc, dtext, staged, sems, *, blocks, total, score_scale, nf, ni, length_at,
 ):
     step = pl.program_id(0)
     width = g2_ref.shape[-1]
@@ -899,14 +908,34 @@
     def _():
         ra, cb = width // ni, width // nf
         half = ra // 2
+        depth = staged.shape[3]
+        number = step - total
+        side = number % 2
+
+        def moved(at):
+            place = pl.ds(at * FIN, FIN)
+            return pltpu.make_async_copy(
+                staged.at[at % 2], all_ref.at[place, :, pl.ds(all_ref.shape[2] - depth, depth)], sems.at[at % 2]
+            )
+
+        @pl.when(number >= 2)
+        def _():
+            moved(number - 2).wait()
+
         for part in range(FIN):
-            item = ((step - total) * FIN + part) ^ table[1]
+            item = number * FIN + part
             for frame in range(nf):
                 for place, acc in enumerate((o_acc, q_acc, co_acc)):
                     cut = pack_square(acc, item, ra, cb, frame * cb)
-                    store_block(cut, part, frame, table[0], place * half, keep_ref, send_ref)
-                cut = kv_acc[pl.ds(pl.multiple_of(item * ra, 16), ra), 2 * frame * cb : 2 * (frame + 1) * cb].astype(BF)
-                store_block(cut, part, frame, table[0], 3 * half, keep_ref, send_ref)
+                    staged[side, part, frame, place * half : (place + 1) * half] = cut
+                cut = kv_acc[pl.ds(pl.multiple_of(item * ra, 16), ra), 2 * frame * cb : 2 * (frame + 1) * cb]
+                staged[side, part, frame, 3 * half :] = cut.astype(BF)
+        moved(number).start()
+
+        @pl.when(number == ni // FIN - 1)
+        def _():
+            moved(number - 1).wait()
+            moved(number).wait()
 
 
 def deal_kernel(table, *refs, at, items, group):
@@ -931,21 +960,18 @@
         out[...] = (keep[0, half].astype(F32) + got[0, half].astype(F32)).astype(BF)[None]
 
 
-def finish_mlp_kernel(sum_ref, *refs):
-    up, down = refs[-2:]
+def finish_kernel(sum_ref, *refs):
+    up, down, squares, kv = refs[-6], refs[-5], refs[-4:-1], refs[-1]
     ra, cb = up.shape
     up[:, : cb // 2] = sum_ref[:ra].astype(F32)
     up[:, cb // 2 :] = sum_ref[ra : 2 * ra].astype(F32)
-    down[...] = untall(sum_ref[2 * ra :].astype(F32))
-
-
-def finish_mid_kernel(keep, got, *refs):
-    outs = refs[-4:]
-    half = outs[0].shape[0] // 2
-    total = keep[...].astype(F32) + got[...].astype(F32)
-    for place in range(3):
-        outs[place][...] = untall(total[place * half : (place + 1) * half])
-    outs[3][...] = total[3 * half :]
+    at = 2 * ra + down.shape[0] // 2
+    down[...] = untall(sum_ref[2 * ra : at].astype(F32))
+    half = ra // 2
+    for out in squares:
+        out[...] = untall(sum_ref[at : at + half].astype(F32))
+        at += half
+    kv[...] = sum_ref[at:].astype(F32)
 
 
 def finish_qkv_kernel(keep, got, *refs):
@@ -1021,12 +1047,12 @@
     per = items // nf
     at = 2 + 3 * per + 2 * items
     return run(
-        copy_kernel,
+        gather_first_kernel,
         "gather_first",
-        (nf,),
-        [pl.BlockSpec((1, block, width), lambda t, s: (s[at + t * per], 0, 0))],
-        (table, rows),
-        pl.BlockSpec((1, block, width), lambda t, s: (t, 0, 0)),
+        (1,),
+        [pl.BlockSpec((1, block, width), lambda t, s, to=to: (s[at + to * per], 0, 0)) for to in range(nf)],
+        (table,) + (rows,) * nf,
+        pl.BlockSpec((nf, block, width), lambda t, s: (0, 0, 0)),
         struct((nf, block, width), BF),
     )
 
@@ -1239,7 +1265,9 @@
     ff = wup.shape[1]
     blocks, total, by_item, by_row = back_grid(items, count, block)
     row = pl.BlockSpec((1, block, width), by_row)
-    shard = pl.BlockSpec((1, 1, block, width), lambda t, s: (by_row(t, s)[1], by_row(t, s)[0], 0, 0))
+    shard = pl.BlockSpec(
+        (block // cot.shape[2], 1, cot.shape[2], width), lambda t, s: (by_row(t, s)[1], by_row(t, s)[0], 0, 0)
+    )
     depth = 2 * width * ff // (nf * ni * PACK)
     return run(
         partial(mlp_kernel, blocks=blocks, total=total, chunk=chunk, nf=nf, ni=ni),
@@ -1250,7 +1278,7 @@
         [shard, row, pl.BlockSpec((1, 3, width), by_item)]
         + [pl.BlockSpec((FIN, nf, depth, PACK), lambda t, s: (jnp.maximum(t - total, 0), 0, 0, 0))],
         [struct(cot.shape, BF), struct(second.shape, BF), struct((items, 3, width), F32)]
-        + [struct((ni, nf, depth, PACK), BF)],
+        + [struct((ni, nf, depth + 5 * width * width // (nf * ni * PACK), PACK), BF)],
         scratch=[pltpu.VMEM((width, ff), F32), pltpu.VMEM((ff, width), F32)],
         deps=deps,
         work=cost(12 * items * count * width * ff, items * count * width * 16, items * count * ff * 2),
@@ -1258,7 +1286,7 @@
 
 
 def cross_back_call(
-    table, g2, bb, cr, cq, att, ba, first, mod, kv, lse, text, wo, wq, wco, wkv, score_scale, block, nf, ni, deps
+    table, g2, bb, cr, cq, att, ba, first, mod, kv, lse, text, wo, wq, wco, wkv, blocks_all, score_scale, block, nf, ni, deps
 ):
     items, count, width = g2.shape
     slots = kv.shape[1]
@@ -1266,7 +1294,7 @@
     blocks, total, by_item, by_row = back_grid(items, count, block)
     row = pl.BlockSpec((1, block, width), by_row)
     by_slot = pl.BlockSpec((nf, 1, short, width), lambda t, s: (0, by_item(t, s)[0], 0, 0))
-    specs, shapes = halves(ni, nf, 5 * width * width // (nf * ni * PACK), total)
+    depth = 5 * width * width // (nf * ni * PACK)
     lse_spec = pl.BlockSpec((1, H // 2, 2, block), lambda t, s: (by_row(t, s)[0], 0, 0, by_row(t, s)[1]))
     return run(
         partial(
@@ -1283,12 +1311,16 @@
         [row] * 7
         + [pl.BlockSpec((1, 9, width), by_item), pl.BlockSpec((1, slots, 2 * width), by_item), lse_spec]
         + [pl.BlockSpec((1, slots, width), by_item)]
-        + [whole(weight.shape) for weight in (wo, wq, wco, wkv)],
-        (table, g2, bb, cr, cq, att, ba, first, mod, kv, lse, text, wo, wq, wco, wkv),
-        [row, row, by_slot, pl.BlockSpec((1, 4, width), by_item)] + specs,
-        [struct(g2.shape, BF)] * 2 + [struct((nf, items, short, width), BF), struct((items, 4, width), F32)] + shapes,
+        + [whole(weight.shape) for weight in (wo, wq, wco, wkv)]
+        + any_spec(1),
+        (table, g2, bb, cr, cq, att, ba, first, mod, kv, lse, text, wo, wq, wco, wkv, blocks_all),
+        [row, row, by_slot, pl.BlockSpec((1, 4, width), by_item)] + any_spec(1),
+        [struct(g2.shape, BF)] * 2
+        + [struct((nf, items, short, width), BF), struct((items, 4, width), F32), struct(blocks_all.shape, BF)],
         scratch=[pltpu.VMEM((width, width), F32)] * 3
-        + [pltpu.VMEM((width, 2 * width), F32), pltpu.VMEM((slots, 2 * width), F32)],
+        + [pltpu.VMEM((width, 2 * width), F32), pltpu.VMEM((slots, 2 * width), F32)]
+        + [pltpu.VMEM((2, FIN, nf, depth, PACK), BF), pltpu.SemaphoreType.DMA((2,))],
+        aliases={16: 4},
         deps=deps,
         work=cost(
             items * count * (12 * width * width + 40 * slots * width), items * count * width * 24, items * H * count * slots
@@ -1412,6 +1444,11 @@
     return rows
 
 
+def total_here(blocks):
+    flat = blocks.reshape((-1,) + blocks.shape[2:])
+    return lax.psum_scatter(flat, ("items", "frames"), scatter_dimension=0, tiled=True)[0]
+
+
 def items_whole(
     ni, nf, frames_in, cond, text, item_lengths, text_lengths, ada_weight, qkv_weight, out_weight,
     cross_q_weight, cross_kv_weight, cross_out_weight, up_weight, down_weight, cotangent,
@@ -1450,27 +1487,21 @@
         table, second, cot, mod, up_weight, down_weight, block, 768, nf, ni, []
     )
     layer_got = exchange(layer_send)
-    sum_mlp = lax.psum_scatter(
-        g_mlp.reshape((ni * nf,) + g_mlp.shape[2:]), ("items", "frames"), scatter_dimension=0, tiled=True
-    )[0]
-    g1, d_att, text_back, dmod_b, mid_keep, mid_send = cross_back_call(
+    g1, d_att, text_back, dmod_b, g_all = cross_back_call(
         table, g2, branch_b, crossed, cross_q, attended, branch_a, first, mod, text_kv, cross_lse, text_rows,
-        out_weight, cross_q_weight, cross_out_weight, cross_kv_weight, score_scale, 2 * block, nf, ni, [],
-    )
-    mid = Sum(mid_keep, mid_send, x_first, sizes)
-    mid.launch()
+        out_weight, cross_q_weight, cross_out_weight, cross_kv_weight, g_mlp, score_scale, 2 * block, nf, ni, [],
+    )
+    sum_all = total_here(g_all)
     made_0, dmod_0, early = self_bwd_call(
         table, 0, qkv, attended, d_att, self_lse, rows, g1, mod, qkv_weight, None, text_back, 1024, score_scale, block, nf, ni,
-        [layer_got],
-    )
-    mid.land()
-    mid.launch()
+        [],
+    )
     got_0 = exchange(made_0)
     made_1, dmod_1, grad_keep, grad_send = self_bwd_call(
         table, 1, qkv, attended, d_att, self_lse, rows, g1, mod, qkv_weight, early, None, 1024, score_scale, block, nf, ni,
-        [mid.send],
-    )
-    made_1, grad_send = gate_call([made_1, grad_send], [mid.got, got_0, sum_mlp])
+        [layer_got],
+    )
+    made_1, grad_send = gate_call([made_1, grad_send], [got_0])
     grad = Sum(grad_keep, grad_send, x_first, sizes)
     grad.launch()
     d_mod = jnp.concatenate([jnp.concatenate([dmod_0, dmod_1], 0), dmod_b, dmod_c], 1).reshape(per, 9 * width)
@@ -1486,8 +1517,6 @@
     got_1 = exchange(made_1)
     grad.land([parts])
     grad.launch()
-    mid.land([grad.send])
-    mid.launch()
     layer_out, text_grad = deal_call(
         table,
         [
@@ -1496,18 +1525,14 @@
         ],
         per,
         "deal_out",
-        [grad.send, mid.send],
-    )
-    mid.land([layer_out])
-    mid.launch()
-    grad.land([mid.send])
+        [grad.send],
+    )
+    grad.land([layer_out])
     grad.launch()
     (input_grad,) = deal_call(
-        table, [([got_0[:, None], got_1[:, None]], block, 0, F32)], per, "deal_in", [grad.send, mid.send]
-    )
-    mid.land([input_grad])
-    mid.launch()
-    grad.land([mid.send])
+        table, [([got_0[:, None], got_1[:, None]], block, 0, F32)], per, "deal_in", [grad.send]
+    )
+    grad.land([input_grad])
     grad.launch()
     (parts,) = gate_call([parts], [grad.send])
     parts = parts.reshape(items, ada_cols + cond_cols)
@@ -1527,20 +1552,17 @@
     sigmoid_c = jax.nn.sigmoid(cond_mine)
     cond_grad = parts[:, ada_cols:] * (sigmoid_c * (1.0 + cond_mine * (1.0 - sigmoid_c)))
 
-    grad_up, grad_down = small_call(
-        finish_mlp_kernel,
-        "finish_mlp",
-        [sum_mlp],
-        [struct((width // ni, ff // nf), F32), struct((ff // ni, width // nf), F32)],
-        [grad.send],
-    )
     while grad.steps:
         grad.land()
         grad.launch()
-    mid_sum = mid.land()
     square = struct((ada_rows, cond_cols), F32)
-    grad_out, grad_cross_q, grad_cross_out, grad_cross_kv = small_call(
-        finish_mid_kernel, "finish_mid", mid_sum, [square] * 3 + [struct((ada_rows, 2 * cond_cols), F32)]
+    grad_up, grad_down, grad_out, grad_cross_q, grad_cross_out, grad_cross_kv = small_call(
+        finish_kernel,
+        "finish",
+        [sum_all],
+        [struct((ada_rows, ff // nf), F32), struct((ff // ni, cond_cols), F32)]
+        + [square] * 3
+        + [struct((ada_rows, 2 * cond_cols), F32)],
     )
     (grad_qkv,) = small_call(finish_qkv_kernel, "finish_qkv", grad.land(), [struct((ada_rows, 3 * cond_cols), F32)])
     return (

time: 519 us -> 505 us (0.973); the launches traced: 524 us -> 498 us
  waiting for transfers between devices: 37.6 us -> 69.7 us
  Pallas kernels: 356 us -> 335 us
  starting transfers between devices: 65.4 us -> 46.1 us
  local copies, waits for them, and re-layouts: 18.9 us -> 4.62 us
  blocking collectives: 14.7 us -> 7.12 us
    ppermute x10 -> x5, starting transfers between devices: 36.7 us -> 11.6 us  [launch(): lax.ppermute(self.send, name, [(i, i ^ 1 << bit) for i in range(self.size...]
    ppermute x10 -> x5, waiting for transfers between devices: 22.7 us -> 40 us  [launch(): lax.ppermute(self.send, name, [(i, i ^ 1 << bit) for i in range(self.size...]
    unnamed x44 -> x18, local copies, waits for them, and re-layouts: 17 us -> 2.71 us
    pallas_call x8 -> x4, Pallas kernels: 21.7 us -> 9.96 us  [land(): pl.pallas_call(land_kernel, grid=(outer,), in_specs=[source] * 2 + any_sp...]
    all_to_all x6, waiting for transfers between devices: 7.42 us -> 15.9 us  [exchange(): return lax.all_to_all(blocks, 'frames', 0, 0, tiled=True)]
    pallas_call x11, Pallas kernels: 328 us -> 320 us  [run(): pl.pallas_call(body, grid_spec=pltpu.PrefetchScalarGridSpec(num_scalar_pr...]
    all_to_all x1, blocking collectives: 14.7 us -> 7.12 us  [exchange(): return lax.all_to_all(blocks, 'frames', 0, 0, tiled=True)]
    ppermute x3, waiting for transfers between devices: 7.42 us -> 13.8 us  [collect_items(): lax.ppermute(rows, 'items', [(i, i ^ 1 << bit) for i in range(ni)])]
  transfers between devices with their start and end apart: 20 -> 15, of which waited for: 7 -> 9; matrix products, arithmetic and copies ran while one was open for 3% -> 5% of each run, Pallas kernels for 49% -> 38%
where the time goes in v5:
time: 505 us; the launch traced here: 498 us
  Pallas kernels  335 us (66%)
  waiting for transfers between devices  69.7 us (14%)
  starting transfers between devices  46.1 us (9%)
  between operations  14.5 us (3%)
  matrix products  14.3 us (3%)
  other arithmetic  7.16 us (1%)
  blocking collectives  7.12 us (1%)
    pallas_call x11, Pallas kernels, run(): pl.pallas_call(body, grid_spec=pltpu.PrefetchScalarGridSpec(num_scalar_pr...  320 us
    ppermute x5, waiting for transfers between devices, launch(): lax.ppermute(self.send, name, [(i, i ^ 1 << bit) for i in range(self.size...  40 us
    all_to_all x6, starting transfers between devices, exchange(): return lax.all_to_all(blocks, 'frames', 0, 0, tiled=True)  30.7 us
    all_to_all x6, waiting for transfers between devices, exchange(): return lax.all_to_all(blocks, 'frames', 0, 0, tiled=True)  15.9 us
    ppermute x3, waiting for transfers between devices, collect_items(): lax.ppermute(rows, 'items', [(i, i ^ 1 << bit) for i in range(ni)])  13.8 us
    ppermute x5, starting transfers between devices, launch(): lax.ppermute(self.send, name, [(i, i ^ 1 << bit) for i in range(self.size...  11.6 us
  transfers between devices with their start and end apart: 15, of which 9 were waited for; matrix products, arithmetic and copies ran while one was open for 5% of the time, Pallas kernels for 38%

profile of v5, /device:TPU:0, one launch (start us, length us, event | category | flops | bytes accessed | tf_op | source)
XLA Modules:
  0.0 498.2 jit_solution(1279468344823395165)
XLA Ops:
  7.8 1.4 start.1.refs_0_
  9.1 3.3 gather_first.1
  12.4 4.5 all-to-all-start
  17.1 5.5 %fusion.10 = f32[8,6912]{1,0:T(8,128)S(1)} fusion(bf16[768,6912]{1,0:T(8,128)(2,1)} %param.19, bf16[8,768]{1,0:T(8,128)(2,1)S(1)} %copy-done.1), kind=kOutput, calls=%fused_computation.26 | convolution fusion | flops 84971520 | bytes 10850304 | tf_op jit(solution)/shard_map/dot_general | solution.py:337
  23.5 6.1 %gather.1 = (bf16[4,384,768]{2,1,0:T(8,128)(2,1)}, bf16[4,2,256,768]{3,2,1,0:T(8,128)(2,1)}) custom-call(s32[32]{0:T(128)} %start.1.refs_0_, bf16[8,256,768]{2,1,0:T(8,128)(2,1)} %refs_4_.4, bf16[8,64,768]{2,1,0:T(8,128)(2,1)} %refs_3_.4, bf16[8,64,768]{2,1,0:T(8,128)(2,1)} %refs_3_.4, bf16[8,256,768]{2,1,0:T(8,128)(2,1)} %refs_5_.3, ...), custom_call_target="tpu_custom_call" | custom-call | tf_op jit(solution)/shard_map/gather/pallas_call | solution.py:1008
  29.6 8.1 %all-to-all-done.refs_1_ = bf16[4,256,768]{2,1,0:T(8,128)(2,1)} async-done(((bf16[4,256,768]{2,1,0:T(8,128)(2,1)}), bf16[4,256,768]{2,1,0:T(8,128)(2,1)}, u32[]{:S(2)}, u32[]{:S(2)}) %all-to-all-start) | async-done | bytes 1572896 | tf_op jit(solution)/shard_map/all_to_all | solution.py:1386
  37.7 4.5 all-to-all-start.1
  42.2 28.5 %self_fwd.2 = (bf16[2,1024,768]{2,1,0:T(8,128)(2,1)}, bf16[2,1024,2304]{2,1,0:T(8,128)(2,1)}, bf16[2,1024,768]{2,1,0:T(8,128)(2,1)}, f32[2,6,2,1024]{3,2,1,0:T(2,128)}) custom-call(s32[32]{0:T(128)} %start.1.refs_0_, bf16[4,256,768]{2,1,0:T(8,128)(2,1)} %all-to-all-done.refs_1_, f32[2,9,768]{2,1,0:T(8,128)} %reshape.101.refs_2_.refs_3_.refs_8_.refs_9_.refs_13_, ...), custom_call_target="tpu_custom_call" | custom-call | flops 16508780544 | bytes 12582912 | tf_op jit(solution)/shard_map/self_fwd/pallas_call | solution.py:1008
  70.8 4.7 all-to-all-start.2
  76.0 17.9 %self_fwd.3 = (bf16[2,1024,768]{2,1,0:T(8,128)(2,1)}, bf16[2,1024,2304]{2,1,0:T(8,128)(2,1)}, bf16[2,1024,768]{2,1,0:T(8,128)(2,1)}, f32[2,6,2,1024]{3,2,1,0:T(2,128)}) custom-call(s32[32]{0:T(128)} %start.1.refs_0_, bf16[4,384,768]{2,1,0:T(8,128)(2,1)} %all-to-all-done.1.refs_1_.refs_4_, ...), custom_call_target="tpu_custom_call", output_to_operand_aliasing={{0}: (4, {}), {1}: (5, {}), {2}: (6, {}), {3}: (7, {})} | custom-call | flops 16508780544 | bytes 12582912 | tf_op jit(solution)/shard_map/self_fwd/pallas_call | solution.py:1008
  93.9 26.3 %cross_fwd.1 = (bf16[2,256,1536]{2,1,0:T(8,128)(2,1)}, bf16[2,256,768]{2,1,0:T(8,128)(2,1)}, bf16[2,1024,768]{2,1,0:T(8,128)(2,1)}, bf16[2,1024,768]{2,1,0:T(8,1...) custom-call(s32[32]{0:T(128)} %start.1.refs_0_, ...), custom_call_target="tpu_custom_call" | custom-call | flops 13690208256 | bytes 31457280 | tf_op jit(solution)/shard_map/cross_fwd/pallas_call | solution.py:1008
  120.2 88.5 %mlp.1 = (bf16[4,2,256,768]{3,2,1,0:T(8,128)(2,1)}, bf16[2,1024,768]{2,1,0:T(8,128)(2,1)}, f32[2,3,768]{2,1,0:T(4,128)}, bf16[8,4,624,384]{3,2,1,0:T(8,128)(2,1)}) custom-call(s32[32]{0:T(128)} %start.1.refs_0_, bf16[2,1024,768]{2,1,0:T(8,128)(2,1)} %get-tuple-element.73.refs_1_, bf16[4,2,256,768]{3,2,1,0:T(8,128)(2,1)} %all-to-all-done.2.refs_2_, ...), custom_call_target="tpu_custom_call" | custom-call | flops 57982058496 | bytes 25165824 | tf_op jit(solution)/shard_map/mlp/pallas_call | solution.py:1008
  208.7 52.0 %cross_bwd.1 = (bf16[2,1024,768]{2,1,0:T(8,128)(2,1)}, bf16[2,1024,768]{2,1,0:T(8,128)(2,1)}, bf16[4,2,64,768]{3,2,1,0:T(8,128)(2,1)}, f32[2,4,768]{2,1,0:T(4,128)}, bf16[8,4,624,384]{3,2,1,0:T(8,128)(2,1)}) custom-call(s32[32]{0:T(128)} %start.1.refs_0_, bf16[2,1024,768]{2,1,0:T(8,128)(2,1)} %get-tuple-element.76.refs_1_, ...), custom_call_target="tpu_custom_call", output_to_operand_aliasing={{4}: (16, {})} | custom-call | flops 30601641984 | bytes 37748736 | tf_op jit(solution)/shard_map/cross_bwd/pallas_call | solution.py:1008
  260.7 7.6 %all-to-all-start.3 = ((bf16[4,2,256,768]{3,2,1,0:T(8,128)(2,1)}), bf16[4,2,256,768]{3,2,1,0:T(8,128)(2,1)}, u32[]{:S(2)}, u32[]{:S(2)}) async-start(bf16[4,2,256,768]{3,2,1,0:T(8,128)(2,1)} %get-tuple-element.74), calls=%async_computation.3 | async-start | bytes 6291456 | tf_op jit(solution)/shard_map/all_to_all | solution.py:1386
  268.3 45.9 %self_bwd.2 = (bf16[4,384,768]{2,1,0:T(8,128)(2,1)}, f32[1,2,768]{2,1,0:T(2,128)}, bf16[1024,2304]{1,0:T(8,128)(2,1)}) custom-call(s32[32]{0:T(128)} %start.1.refs_0_, bf16[2,1024,2304]{2,1,0:T(8,128)(2,1)} %get-tuple-element.75.refs_1_.refs_2_.refs_3_, bf16[2,1024,2304]{2,1,0:T(8,128)(2,1)} %get-tuple-element.75.refs_1_.refs_2_.refs_3_, ...), custom_call_target="tpu_custom_call" | custom-call | flops 39460012032 | bytes 23592960 | tf_op jit(solution)/shard_map/self_bwd/pallas_call | solution.py:1008
  314.3 4.9 all-to-all-start.4
  319.1 39.2 %self_bwd.3 = (bf16[4,256,768]{2,1,0:T(8,128)(2,1)}, f32[1,2,768]{2,1,0:T(2,128)}, bf16[8,2,144,384]{3,2,1,0:T(8,128)(2,1)}, bf16[8,2,144,384]{3,2,1,0:T(8,128)(2,1)}) custom-call(s32[32]{0:T(128)} %start.1.refs_0_, bf16[2,1024,2304]{2,1,0:T(8,128)(2,1)} %get-tuple-element.75.refs_1_.refs_2_.refs_3_, ...), custom_call_target="tpu_custom_call" | custom-call | flops 39460012032 | bytes 23592960 | tf_op jit(solution)/shard_map/self_bwd/pallas_call | solution.py:1008
  359.2 3.5 all-to-all-done.4.refs_2_
  362.6 6.9 %collective-permute-start = (bf16[8,2,144,384]{3,2,1,0:T(8,128)(2,1)}, bf16[8,2,144,384]{3,2,1,0:T(8,128)(2,1)}, u32[]{:S(2)}, u32[]{:S(2)}) collective-permute-start(bf16[8,2,144,384]{3,2,1,0:T(8,128)(2,1)} %get-tuple-element.95), channel_id=1, source_target_pairs={{0,1},{1,0},{2,3},{3,2},{4,5},{5,4},{6,7},{7,6},{8,9},{9,8},{10,11... | collective-permute-start | bytes 5308424 | tf_op jit(solution)/shard_map/ppermute | solution.py:1413
  369.6 7.1 %fusion.2 = f32[4,768]{1,0:T(4,128)S(1)} fusion(bf16[768,6912]{1,0:T(8,128)(2,1)} %param.19, bf16[2,6912]{1,0:T(2,128)(2,1)S(1)} %get-tuple-element.154, bf16[2,6912]{1,0:T(2,128)(2,1)S(1)} %get-tuple-element.155), kind=kOutput, calls=%fused_computation.10 | convolution fusion | flops 42577920 | bytes 10684416 | tf_op jit(solution)/shard_map/dot_general | solution.py:341
  377.0 7.1 %all_to_all.35.refs_0_.refs_1_ = f32[4,2,1920]{2,1,0:T(2,128)} all-to-all(f32[4,2,1920]{2,1,0:T(2,128)S(1)} %maximum_bitcast_fusion), channel_id=1, replica_groups=mesh['items'=8,'frames'=4] {'frames'}, dimensions={0} | all-to-all | bytes 122880 | tf_op jit(solution)/shard_map/all_to_all | solution.py:1386
  384.1 4.0 land.4
  388.2 0.8 collective-permute-start.1
  389.0 4.5 all-to-all-start.6
  394.0 5.4 %deal_out.1 = (bf16[8,256,768]{2,1,0:T(8,128)(2,1)}, f32[8,64,768]{2,1,0:T(8,128)}) custom-call(s32[32]{0:T(128)} %start.1.refs_0_, bf16[4,1,512,768]{3,2,1,0:T(8,128)(2,1)} %bitcast.2.refs_1_.refs_2_, bf16[4,1,512,768]{3,2,1,0:T(8,128)(2,1)} %bitcast.2.refs_1_.refs_2_, bf16[4,1,384,768]{3,2,1,0:T(8,128)(2,1)} %bitcast.3.refs_3_.refs_4_.refs_1_, ...), custom_call_target="tpu_custom_call" | custom-call | bytes 9437184 | tf_op jit(solution)/shard_map/deal_out/pallas_call | solution.py:1008
  399.4 17.1 %collective-permute-done.1 = bf16[4,2,144,384]{3,2,1,0:T(8,128)(2,1)} collective-permute-done((bf16[4,2,144,384]{3,2,1,0:T(8,128)(2,1)}, bf16[4,2,144,384]{3,2,1,0:T(8,128)(2,1)}, u32[]{:S(2)}, u32[]{:S(2)}) %collective-permute-start.1) | collective-permute-done | bytes 884768 | tf_op jit(solution)/shard_map/ppermute | solution.py:1413
  416.5 2.2 land.5
  418.8 1.3 collective-permute-start.2
  421.4 4.3 all-to-all-done.6
  425.7 6.5 %deal_in.1.refs_0_ = f32[8,256,768]{2,1,0:T(8,128)} custom-call(s32[32]{0:T(128)} %start.1.refs_0_, bf16[4,1,384,768]{3,2,1,0:T(8,128)(2,1)} %bitcast.3.refs_3_.refs_4_.refs_1_, bf16[4,1,256,768]{3,2,1,0:T(8,128)(2,1)} %bitcast.7.refs_2_.refs_4_, bf16[4,1,384,768]{3,2,1,0:T(8,128)(2,1)} %bitcast.3.refs_3_.refs_4_.refs_1_, ...), custom_call_target="tpu_custom_call" | custom-call | bytes 9437184 | tf_op jit(solution)/shard_map/deal_in/pallas_call | solution.py:1008
  432.2 6.1 %collective-permute-done.2 = bf16[2,2,144,384]{3,2,1,0:T(8,128)(2,1)S(1)} collective-permute-done((bf16[2,2,144,384]{3,2,1,0:T(8,128)(2,1)}, bf16[2,2,144,384]{3,2,1,0:T(8,128)(2,1)S(1)}, u32[]{:S(2)}, u32[]{:S(2)}) %collective-permute-start.2) | collective-permute-done | bytes 442400 | tf_op jit(solution)/shard_map/ppermute | solution.py:1413
  438.4 0.8 copy-done
  439.2 2.0 land.6
  441.1 0.9 broadcast_in_dim.62
  442.2 0.8 pad_maximum_fusion.4
  443.0 1.7 collective-permute-start.3
  444.7 4.1 collective-permute-done.3
  448.9 1.6 collective-permute-start.4
  450.5 2.6 collective-permute-start.6
  453.1 9.7 %collective-permute-done.4 = f32[16,2496]{1,0:T(8,128)S(1)} collective-permute-done((f32[16,2496]{1,0:T(8,128)S(1)}, f32[16,2496]{1,0:T(8,128)S(1)}, u32[]{:S(2)}, u32[]{:S(2)}) %collective-permute-start.4) | collective-permute-done | bytes 159776 | tf_op jit(solution)/shard_map/ppermute | solution.py:1443
  463.6 12.4 %collective-permute-done.6 = bf16[1,2,144,384]{3,2,1,0:T(8,128)(2,1)} collective-permute-done((bf16[1,2,144,384]{3,2,1,0:T(8,128)(2,1)}, bf16[1,2,144,384]{3,2,1,0:T(8,128)(2,1)}, u32[]{:S(2)}, u32[]{:S(2)}) %collective-permute-start.6) | collective-permute-done | bytes 221216 | tf_op jit(solution)/shard_map/ppermute | solution.py:1413
  476.0 1.8 land.7
  478.4 4.4 collective-permute-done.7
  482.8 1.7 finish_qkv.1
  484.5 1.0 pad_maximum_fusion
  485.5 1.7 fusion
  487.2 2.1 finish.1
  489.3 1.9 copy.43
  (53 shorter events, 7.1 us)
Async XLA Ops:
  12.4 4.5 copy-start.5
  12.4 4.7 copy-start.1
  12.4 25.3 %all-to-all-start = ((bf16[4,256,768]{2,1,0:T(8,128)(2,1)}), bf16[4,256,768]{2,1,0:T(8,128)(2,1)}, u32[]{:S(2)}, u32[]{:S(2)}) async-start(bf16[4,256,768]{2,1,0:T(8,128)(2,1)} %gather_first.1), calls=%async_computation | async-start | bytes 3145728 | tf_op jit(solution)/shard_map/all_to_all | solution.py:1386
  37.7 33.1 %all-to-all-start.1 = ((bf16[4,384,768]{2,1,0:T(8,128)(2,1)}), bf16[4,384,768]{2,1,0:T(8,128)(2,1)}, u32[]{:S(2)}, u32[]{:S(2)}) async-start(bf16[4,384,768]{2,1,0:T(8,128)(2,1)} %gate.5.refs_4_), calls=%async_computation.1 | async-start | bytes 4718592 | tf_op jit(solution)/shard_map/all_to_all | solution.py:1386
  70.8 49.5 %all-to-all-start.2 = ((bf16[4,2,256,768]{3,2,1,0:T(8,128)(2,1)}), bf16[4,2,256,768]{3,2,1,0:T(8,128)(2,1)}, u32[]{:S(2)}, u32[]{:S(2)}) async-start(bf16[4,2,256,768]{3,2,1,0:T(8,128)(2,1)} %gate.6.refs_8_), calls=%async_computation.2 | async-start | bytes 6291456 | tf_op jit(solution)/shard_map/all_to_all | solution.py:1386
  75.4 411.8 %reduce-scatter.2.cloned.1.call-start = ((), (), s32[]{:S(2)}) async-start(), calls=%async_computation.8 | async-start | bytes 15814656 | tf_op jit(solution)/shard_map/reduce_scatter | solution.py:1449
  260.7 53.6 %all-to-all-start.3 = ((bf16[4,2,256,768]{3,2,1,0:T(8,128)(2,1)}), bf16[4,2,256,768]{3,2,1,0:T(8,128)(2,1)}, u32[]{:S(2)}, u32[]{:S(2)}) async-start(bf16[4,2,256,768]{3,2,1,0:T(8,128)(2,1)} %get-tuple-element.74), calls=%async_computation.3 | async-start | bytes 6291456 | tf_op jit(solution)/shard_map/all_to_all | solution.py:1386
  314.3 48.4 %all-to-all-start.4 = ((bf16[4,384,768]{2,1,0:T(8,128)(2,1)}), bf16[4,384,768]{2,1,0:T(8,128)(2,1)}, u32[]{:S(2)}, u32[]{:S(2)}) async-start(bf16[4,384,768]{2,1,0:T(8,128)(2,1)} %get-tuple-element.90), calls=%async_computation.4 | async-start | bytes 4718592 | tf_op jit(solution)/shard_map/all_to_all | solution.py:1386
  319.1 39.2 %copy-start.3 = (f32[2,3,768]{2,1,0:T(4,128)S(1)}, f32[2,3,768]{2,1,0:T(4,128)}, u32[]{:S(2)}) copy-start(f32[2,3,768]{2,1,0:T(4,128)} %get-tuple-element.99) | copy-start | bytes 55300
  319.1 39.2 %copy-start.4 = (f32[2,4,768]{2,1,0:T(4,128)S(1)}, f32[2,4,768]{2,1,0:T(4,128)}, u32[]{:S(2)}) copy-start(f32[2,4,768]{2,1,0:T(4,128)} %get-tuple-element.98) | copy-start | bytes 73732
  319.1 39.2 %copy-start.7 = (f32[1,2,768]{2,1,0:T(2,128)S(1)}, f32[1,2,768]{2,1,0:T(2,128)}, u32[]{:S(2)}) copy-start(f32[1,2,768]{2,1,0:T(2,128)} %get-tuple-element.96) | copy-start | bytes 18436
  362.6 21.5 %collective-permute-start = (bf16[8,2,144,384]{3,2,1,0:T(8,128)(2,1)}, bf16[8,2,144,384]{3,2,1,0:T(8,128)(2,1)}, u32[]{:S(2)}, u32[]{:S(2)}) collective-permute-start(bf16[8,2,144,384]{3,2,1,0:T(8,128)(2,1)} %get-tuple-element.95), channel_id=1, source_target_pairs={{0,1},{1,0},{2,3},{3,2},{4,5},{5,4},{6,7},{7,6},{8,9},{9,8},{10,11... | collective-permute-start | bytes 5308424 | tf_op jit(solution)/shard_map/ppermute | solution.py:1413
  388.2 28.4 %collective-permute-start.1 = (bf16[4,2,144,384]{3,2,1,0:T(8,128)(2,1)}, bf16[4,2,144,384]{3,2,1,0:T(8,128)(2,1)}, u32[]{:S(2)}, u32[]{:S(2)}) collective-permute-start(bf16[4,2,144,384]{3,2,1,0:T(8,128)(2,1)} %get-tuple-element.100.refs_5_), channel_id=1, source_target_pairs={{0,4},{4,0},{8,12},{12,8},{16,20},{20,16},{24,28},{28,24},{1,5},{5... | collective-permute-start | bytes 2654216 | tf_op jit(solution)/shard_map/ppermute | solution.py:1413
  389.0 4.5 copy-start.6
  389.0 36.7 %all-to-all-start.6 = ((bf16[4,256,768]{2,1,0:T(8,128)(2,1)}), bf16[4,256,768]{2,1,0:T(8,128)(2,1)}, u32[]{:S(2)}, u32[]{:S(2)}) async-start(bf16[4,256,768]{2,1,0:T(8,128)(2,1)} %gate.8), calls=%async_computation.6 | async-start | bytes 3145728 | tf_op jit(solution)/shard_map/all_to_all | solution.py:1386
  399.4 21.3 %copy-start.2 = (bf16[8,768]{1,0:T(8,128)(2,1)S(1)}, bf16[8,768]{1,0:T(8,128)(2,1)}, u32[]{:S(2)}) copy-start(bf16[8,768]{1,0:T(8,128)(2,1)} %param.15) | copy-start | bytes 36868
  418.8 19.6 %collective-permute-start.2 = (bf16[2,2,144,384]{3,2,1,0:T(8,128)(2,1)}, bf16[2,2,144,384]{3,2,1,0:T(8,128)(2,1)S(1)}, u32[]{:S(2)}, u32[]{:S(2)}) collective-permute-start(bf16[2,2,144,384]{3,2,1,0:T(8,128)(2,1)} %get-tuple-element.104.refs_5_), channel_id=1, source_target_pairs={{0,8},{4,12},{8,0},{12,4},{16,24},{20,28},{24,16},{28,20},{1,9},{5... | collective-permute-start | bytes 1327112 | tf_op jit(solution)/shard_map/ppermute | solution.py:1413
  438.4 0.8 copy-start
  443.0 5.9 %collective-permute-start.3 = (f32[8,2496]{1,0:T(8,128)S(1)}, f32[8,2496]{1,0:T(8,128)S(1)}, u32[]{:S(2)}, u32[]{:S(2)}) collective-permute-start(f32[8,2496]{1,0:T(8,128)S(1)} %pad_maximum_fusion.4), channel_id=1, source_target_pairs={{0,4},{4,0},{8,12},{12,8},{16,20},{20,16},{24,28},{28,24},{1,5},{5... | collective-permute-start | bytes 239624 | tf_op jit(solution)/shard_map/ppermute | solution.py:1443
  448.9 13.9 %collective-permute-start.4 = (f32[16,2496]{1,0:T(8,128)S(1)}, f32[16,2496]{1,0:T(8,128)S(1)}, u32[]{:S(2)}, u32[]{:S(2)}) collective-permute-start(f32[16,2496]{1,0:T(8,128)S(1)} %pad_maximum_fusion.2), channel_id=1, source_target_pairs={{0,8},{4,12},{8,0},{12,4},{16,24},{20,28},{24,16},{28,20},{1,9},{5... | collective-permute-start | bytes 479240 | tf_op jit(solution)/shard_map/ppermute | solution.py:1443
  450.5 25.5 %collective-permute-start.6 = (bf16[1,2,144,384]{3,2,1,0:T(8,128)(2,1)}, bf16[1,2,144,384]{3,2,1,0:T(8,128)(2,1)}, u32[]{:S(2)}, u32[]{:S(2)}) collective-permute-start(bf16[1,2,144,384]{3,2,1,0:T(8,128)(2,1)} %get-tuple-element.107.refs_1_), channel_id=1, source_target_pairs={{0,16},{4,20},{8,24},{12,28},{16,0},{20,4},{24,8},{28,12},{1,17},{... | collective-permute-start | bytes 663560 | tf_op jit(solution)/shard_map/ppermute | solution.py:1413
  463.6 20.9 %collective-permute-start.5 = (f32[32,2496]{1,0:T(8,128)}, f32[32,2496]{1,0:T(8,128)}, u32[]{:S(2)}, u32[]{:S(2)}) collective-permute-start(f32[32,2496]{1,0:T(8,128)} %pad_maximum_fusion.1), channel_id=1, source_target_pairs={{0,16},{4,20},{8,24},{12,28},{16,0},{20,4},{24,8},{28,12},{1,17},{... | collective-permute-start | bytes 958472 | tf_op jit(solution)/shard_map/ppermute | solution.py:1443
  477.7 5.1 %collective-permute-start.7 = (bf16[1,1,144,384]{3,2,1,0:T(8,128)(2,1)}, bf16[1,1,144,384]{3,2,1,0:T(8,128)(2,1)}, u32[]{:S(2)}, u32[]{:S(2)}) collective-permute-start(bf16[1,1,144,384]{3,2,1,0:T(8,128)(2,1)} %get-tuple-element.110), channel_id=1, source_target_pairs={{0,2},{1,3},{2,0},{3,1},{4,6},{5,7},{6,4},{7,5},{8,10},{9,11},{10,... | collective-permute-start | bytes 331784 | tf_op jit(solution)/shard_map/ppermute | solution.py:1413
Sparse Core Ops, SparseCore 0:
  260.8 204.0 reduce-scatter.1

commit v6 on v5

--- a/solution.py
+++ b/solution.py
@@ -965,8 +965,8 @@
     ra, cb = up.shape
     up[:, : cb // 2] = sum_ref[:ra].astype(F32)
     up[:, cb // 2 :] = sum_ref[ra : 2 * ra].astype(F32)
-    at = 2 * ra + down.shape[0] // 2
-    down[...] = untall(sum_ref[2 * ra : at].astype(F32))
+    at = 2 * ra + down.shape[1] // 2
+    down[...] = untall(sum_ref[2 * ra : at].astype(F32)).T
     half = ra // 2
     for out in squares:
         out[...] = untall(sum_ref[at : at + half].astype(F32))
@@ -1474,10 +1474,10 @@
 
     (mixed_send,) = gate_call([mixed_send], [rows_first, mod])
     mixed = exchange(mixed_send)
-    kept = self_fwd_call(table, 0, rows_first, mod, qkv_weight, (), per, block, 512, score_scale, [mixed_send])
+    kept = self_fwd_call(table, 0, rows_first, mod, qkv_weight, (), per, block, 1024, score_scale, [mixed_send])
     (cot_send,) = gate_call([cot_send], [mixed])
     cot = exchange(cot_send)
-    kept = self_fwd_call(table, 1, mixed, mod, qkv_weight, kept, per, block, 512, score_scale, [cot_send])
+    kept = self_fwd_call(table, 1, mixed, mod, qkv_weight, kept, per, block, 1024, score_scale, [cot_send])
     rows, qkv, attended, self_lse = kept
     text_kv, text_rows, first, second, branch_a, branch_b, cross_q, crossed, cross_lse = cross_call(
         table, attended, rows, mod, mixed, text.shape[1], cross_kv_weight, out_weight, cross_q_weight, cross_out_weight,
@@ -1513,10 +1513,10 @@
         [d_mod.reshape(per, nf, ada_cols), (parts[:per] + parts[per:]).reshape(per, nf, cond_cols)], 2
     ).transpose(1, 0, 2)
     parts = exchange(parts)
-    (made_1,) = gate_call([made_1], [parts])
-    got_1 = exchange(made_1)
     grad.land([parts])
     grad.launch()
+    (made_1,) = gate_call([made_1], [grad.send])
+    got_1 = exchange(made_1)
     layer_out, text_grad = deal_call(
         table,
         [
@@ -1540,12 +1540,11 @@
     spot = table[at : at + items] * per + table[at + items : at + 2 * items]
     pick_row = spot[:, None] == jnp.arange(items, dtype=jnp.int32)[None, :]
     parts = jnp.sum(jnp.where(pick_row[:, :, None], parts[None], 0.0), 1)
-    every = collect_items(jnp.concatenate([parts[:, :ada_cols], low_cond.astype(F32)], 1), ni)
+    every = collect_items(jnp.concatenate([parts[:, :ada_cols].astype(BF), low_cond], 1), ni)
     grad_ada = lax.dot_general(
         lax.dynamic_slice(every, (0, ada_cols + row_item * ada_rows), (items * ni, ada_rows), allow_negative_indices=False),
         every[:, :ada_cols],
         (((0,), (0,)), ((), ())),
-        precision=lax.Precision.HIGHEST,
         preferred_element_type=F32,
     )
     cond_mine = lax.dynamic_slice(cond_f, (0, me * cond_cols), (items, cond_cols), allow_negative_indices=False)
@@ -1560,11 +1559,13 @@
         finish_kernel,
         "finish",
         [sum_all],
-        [struct((ada_rows, ff // nf), F32), struct((ff // ni, cond_cols), F32)]
+        [struct((ada_rows, ff // nf), F32), struct((cond_cols, ff // ni), F32)]
         + [square] * 3
         + [struct((ada_rows, 2 * cond_cols), F32)],
     )
-    (grad_qkv,) = small_call(finish_qkv_kernel, "finish_qkv", grad.land(), [struct((ada_rows, 3 * cond_cols), F32)])
+    (grad_qkv,) = small_call(
+        finish_qkv_kernel, "finish_qkv", grad.land(), [struct((ada_rows, 3 * cond_cols), F32)], [grad_up]
+    )
     return (
         layer_out,
         input_grad,
@@ -1577,7 +1578,7 @@
         grad_cross_kv,
         grad_cross_out,
         grad_up,
-        grad_down,
+        grad_down.T,
     )
 
 

time: 505 us -> 496 us (0.982)
  waiting for transfers between devices: 69.7 us -> 62.3 us
    ppermute x3, waiting for transfers between devices: 13.8 us -> 6.4 us  [collect_items(): lax.ppermute(rows, 'items', [(i, i ^ 1 << bit) for i in range(ni)])]
where the time goes in v6:
time: 496 us; the launch traced here: 487 us
  Pallas kernels  331 us (67%)
  waiting for transfers between devices  62.3 us (13%)
  starting transfers between devices  47.2 us (10%)
  between operations  14.5 us (3%)
  matrix products  13.9 us (3%)
  blocking collectives  7.13 us (1%)
  other arithmetic  6.99 us (1%)
    pallas_call x11, Pallas kernels, run(): pl.pallas_call(body, grid_spec=pltpu.PrefetchScalarGridSpec(num_scalar_pr...  315 us
    ppermute x5, waiting for transfers between devices, launch(): lax.ppermute(self.send, name, [(i, i ^ 1 << bit) for i in range(self.size...  37.6 us
    all_to_all x6, starting transfers between devices, exchange(): return lax.all_to_all(blocks, 'frames', 0, 0, tiled=True)  29.2 us
    all_to_all x6, waiting for transfers between devices, exchange(): return lax.all_to_all(blocks, 'frames', 0, 0, tiled=True)  18.3 us
    ppermute x5, starting transfers between devices, launch(): lax.ppermute(self.send, name, [(i, i ^ 1 << bit) for i in range(self.size...  13.7 us
    pallas_call x4, Pallas kernels, land(): pl.pallas_call(land_kernel, grid=(outer,), in_specs=[source] * 2 + any_sp...  10.1 us
  transfers between devices with their start and end apart: 15, of which 9 were waited for; matrix products, arithmetic and copies ran while one was open for 5% of the time, Pallas kernels for 38%

profile of v6, /device:TPU:0, one launch (start us, length us, event | category | flops | bytes accessed | tf_op | source)
XLA Modules:
  0.0 486.6 jit_solution(18047135254535474447)
XLA Ops:
  7.8 1.4 start.1.refs_0_
  9.1 3.3 gather_first.1
  12.4 4.5 all-to-all-start
  17.1 5.5 %fusion.9 = f32[8,6912]{1,0:T(8,128)S(1)} fusion(bf16[768,6912]{1,0:T(8,128)(2,1)} %param.19, bf16[8,768]{1,0:T(8,128)(2,1)S(1)} %copy-done.2), kind=kOutput, calls=%fused_computation.26 | convolution fusion | flops 84971520 | bytes 10850304 | tf_op jit(solution)/shard_map/dot_general | solution.py:337
  22.8 0.7 reshape.101.refs_2_.refs_3_.refs_8_.refs_9_.refs_13_
  23.5 6.1 %gather.1 = (bf16[4,384,768]{2,1,0:T(8,128)(2,1)}, bf16[4,2,256,768]{3,2,1,0:T(8,128)(2,1)}) custom-call(s32[32]{0:T(128)} %start.1.refs_0_, bf16[8,256,768]{2,1,0:T(8,128)(2,1)} %refs_4_.4, bf16[8,64,768]{2,1,0:T(8,128)(2,1)} %refs_3_.4, bf16[8,64,768]{2,1,0:T(8,128)(2,1)} %refs_3_.4, bf16[8,256,768]{2,1,0:T(8,128)(2,1)} %refs_5_.3, ...), custom_call_target="tpu_custom_call" | custom-call | tf_op jit(solution)/shard_map/gather/pallas_call | solution.py:1008
  29.6 8.1 %all-to-all-done.refs_1_ = bf16[4,256,768]{2,1,0:T(8,128)(2,1)} async-done(((bf16[4,256,768]{2,1,0:T(8,128)(2,1)}), bf16[4,256,768]{2,1,0:T(8,128)(2,1)}, u32[]{:S(2)}, u32[]{:S(2)}) %all-to-all-start) | async-done | bytes 1572896 | tf_op jit(solution)/shard_map/all_to_all | solution.py:1386
  37.7 4.5 all-to-all-start.1
  42.2 25.8 %self_fwd.2 = (bf16[2,1024,768]{2,1,0:T(8,128)(2,1)}, bf16[2,1024,2304]{2,1,0:T(8,128)(2,1)}, bf16[2,1024,768]{2,1,0:T(8,128)(2,1)}, f32[2,6,2,1024]{3,2,1,0:T(2,128)}) custom-call(s32[32]{0:T(128)} %start.1.refs_0_, bf16[4,256,768]{2,1,0:T(8,128)(2,1)} %all-to-all-done.refs_1_, f32[2,9,768]{2,1,0:T(8,128)} %reshape.101.refs_2_.refs_3_.refs_8_.refs_9_.refs_13_, ...), custom_call_target="tpu_custom_call" | custom-call | flops 16508780544 | bytes 12582912 | tf_op jit(solution)/shard_map/self_fwd/pallas_call | solution.py:1008
  67.9 2.8 all-to-all-done.1.refs_1_.refs_4_
  70.7 4.7 all-to-all-start.2
  75.7 16.5 %self_fwd.3 = (bf16[2,1024,768]{2,1,0:T(8,128)(2,1)}, bf16[2,1024,2304]{2,1,0:T(8,128)(2,1)}, bf16[2,1024,768]{2,1,0:T(8,128)(2,1)}, f32[2,6,2,1024]{3,2,1,0:T(2,128)}) custom-call(s32[32]{0:T(128)} %start.1.refs_0_, bf16[4,384,768]{2,1,0:T(8,128)(2,1)} %all-to-all-done.1.refs_1_.refs_4_, ...), custom_call_target="tpu_custom_call", output_to_operand_aliasing={{0}: (4, {}), {1}: (5, {}), {2}: (6, {}), {3}: (7, {})} | custom-call | flops 16508780544 | bytes 12582912 | tf_op jit(solution)/shard_map/self_fwd/pallas_call | solution.py:1008
  92.2 26.3 %cross_fwd.1 = (bf16[2,256,1536]{2,1,0:T(8,128)(2,1)}, bf16[2,256,768]{2,1,0:T(8,128)(2,1)}, bf16[2,1024,768]{2,1,0:T(8,128)(2,1)}, bf16[2,1024,768]{2,1,0:T(8,1...) custom-call(s32[32]{0:T(128)} %start.1.refs_0_, ...), custom_call_target="tpu_custom_call" | custom-call | flops 13690208256 | bytes 31457280 | tf_op jit(solution)/shard_map/cross_fwd/pallas_call | solution.py:1008
  118.5 88.7 %mlp.1 = (bf16[4,2,256,768]{3,2,1,0:T(8,128)(2,1)}, bf16[2,1024,768]{2,1,0:T(8,128)(2,1)}, f32[2,3,768]{2,1,0:T(4,128)}, bf16[8,4,624,384]{3,2,1,0:T(8,128)(2,1)}) custom-call(s32[32]{0:T(128)} %start.1.refs_0_, bf16[2,1024,768]{2,1,0:T(8,128)(2,1)} %get-tuple-element.73.refs_1_, bf16[4,2,256,768]{3,2,1,0:T(8,128)(2,1)} %all-to-all-done.2.refs_2_, ...), custom_call_target="tpu_custom_call" | custom-call | flops 57982058496 | bytes 25165824 | tf_op jit(solution)/shard_map/mlp/pallas_call | solution.py:1008
  207.1 51.9 %cross_bwd.1 = (bf16[2,1024,768]{2,1,0:T(8,128)(2,1)}, bf16[2,1024,768]{2,1,0:T(8,128)(2,1)}, bf16[4,2,64,768]{3,2,1,0:T(8,128)(2,1)}, f32[2,4,768]{2,1,0:T(4,128)}, bf16[8,4,624,384]{3,2,1,0:T(8,128)(2,1)}) custom-call(s32[32]{0:T(128)} %start.1.refs_0_, bf16[2,1024,768]{2,1,0:T(8,128)(2,1)} %get-tuple-element.76.refs_1_, ...), custom_call_target="tpu_custom_call", output_to_operand_aliasing={{4}: (16, {})} | custom-call | flops 30601641984 | bytes 37748736 | tf_op jit(solution)/shard_map/cross_bwd/pallas_call | solution.py:1008
  259.1 6.2 %all-to-all-start.3 = ((bf16[4,2,256,768]{3,2,1,0:T(8,128)(2,1)}), bf16[4,2,256,768]{3,2,1,0:T(8,128)(2,1)}, u32[]{:S(2)}, u32[]{:S(2)}) async-start(bf16[4,2,256,768]{3,2,1,0:T(8,128)(2,1)} %get-tuple-element.74), calls=%async_computation.3 | async-start | bytes 6291456 | tf_op jit(solution)/shard_map/all_to_all | solution.py:1386
  265.3 45.8 %self_bwd.2 = (bf16[4,384,768]{2,1,0:T(8,128)(2,1)}, f32[1,2,768]{2,1,0:T(2,128)}, bf16[1024,2304]{1,0:T(8,128)(2,1)}) custom-call(s32[32]{0:T(128)} %start.1.refs_0_, bf16[2,1024,2304]{2,1,0:T(8,128)(2,1)} %get-tuple-element.75.refs_1_.refs_2_.refs_3_, bf16[2,1024,2304]{2,1,0:T(8,128)(2,1)} %get-tuple-element.75.refs_1_.refs_2_.refs_3_, ...), custom_call_target="tpu_custom_call" | custom-call | flops 39460012032 | bytes 23592960 | tf_op jit(solution)/shard_map/self_bwd/pallas_call | solution.py:1008
  311.1 5.0 %all-to-all-start.4 = ((bf16[4,384,768]{2,1,0:T(8,128)(2,1)}), bf16[4,384,768]{2,1,0:T(8,128)(2,1)}, u32[]{:S(2)}, u32[]{:S(2)}) async-start(bf16[4,384,768]{2,1,0:T(8,128)(2,1)} %get-tuple-element.90), calls=%async_computation.4 | async-start | bytes 4718592 | tf_op jit(solution)/shard_map/all_to_all | solution.py:1386
  316.1 38.7 %self_bwd.3 = (bf16[4,256,768]{2,1,0:T(8,128)(2,1)}, f32[1,2,768]{2,1,0:T(2,128)}, bf16[8,2,144,384]{3,2,1,0:T(8,128)(2,1)}, bf16[8,2,144,384]{3,2,1,0:T(8,128)(2,1)}) custom-call(s32[32]{0:T(128)} %start.1.refs_0_, bf16[2,1024,2304]{2,1,0:T(8,128)(2,1)} %get-tuple-element.75.refs_1_.refs_2_.refs_3_, ...), custom_call_target="tpu_custom_call" | custom-call | flops 39460012032 | bytes 23592960 | tf_op jit(solution)/shard_map/self_bwd/pallas_call | solution.py:1008
  354.8 0.7 pad_maximum_fusion.2
  355.6 4.0 all-to-all-done.4.refs_2_
  359.6 6.1 %collective-permute-start = (bf16[8,2,144,384]{3,2,1,0:T(8,128)(2,1)}, bf16[8,2,144,384]{3,2,1,0:T(8,128)(2,1)}, u32[]{:S(2)}, u32[]{:S(2)}) collective-permute-start(bf16[8,2,144,384]{3,2,1,0:T(8,128)(2,1)} %get-tuple-element.95), channel_id=1, source_target_pairs={{0,1},{1,0},{2,3},{3,2},{4,5},{5,4},{6,7},{7,6},{8,9},{9,8},{10,11... | collective-permute-start | bytes 5308424 | tf_op jit(solution)/shard_map/ppermute | solution.py:1413
  365.7 7.1 %fusion.2 = f32[4,768]{1,0:T(4,128)S(1)} fusion(bf16[768,6912]{1,0:T(8,128)(2,1)} %param.19, bf16[2,6912]{1,0:T(2,128)(2,1)S(1)} %get-tuple-element.118, bf16[2,6912]{1,0:T(2,128)(2,1)S(1)} %get-tuple-element.119), kind=kOutput, calls=%fused_computation.10 | convolution fusion | flops 42577920 | bytes 10684416 | tf_op jit(solution)/shard_map/dot_general | solution.py:341
  373.2 7.1 %all_to_all.35.refs_0_ = f32[4,2,1920]{2,1,0:T(2,128)} all-to-all(f32[4,2,1920]{2,1,0:T(2,128)S(1)} %maximum_bitcast_fusion), channel_id=1, replica_groups=mesh['items'=8,'frames'=4] {'frames'}, dimensions={0} | all-to-all | bytes 122880 | tf_op jit(solution)/shard_map/all_to_all | solution.py:1386
  380.3 4.1 land.4
  384.5 4.4 all-to-all-start.6
  389.4 5.7 %deal_out.1 = (bf16[8,256,768]{2,1,0:T(8,128)(2,1)}, f32[8,64,768]{2,1,0:T(8,128)}) custom-call(s32[32]{0:T(128)} %start.1.refs_0_, bf16[4,1,512,768]{3,2,1,0:T(8,128)(2,1)} %bitcast.2.refs_1_.refs_2_, bf16[4,1,512,768]{3,2,1,0:T(8,128)(2,1)} %bitcast.2.refs_1_.refs_2_, bf16[4,1,384,768]{3,2,1,0:T(8,128)(2,1)} %bitcast.3.refs_3_.refs_4_.refs_1_, ...), custom_call_target="tpu_custom_call" | custom-call | bytes 9437184 | tf_op jit(solution)/shard_map/deal_out/pallas_call | solution.py:1008
  395.1 17.7 %collective-permute-done.1 = bf16[4,2,144,384]{3,2,1,0:T(8,128)(2,1)} collective-permute-done((bf16[4,2,144,384]{3,2,1,0:T(8,128)(2,1)}, bf16[4,2,144,384]{3,2,1,0:T(8,128)(2,1)}, u32[]{:S(2)}, u32[]{:S(2)}) %collective-permute-start.1) | collective-permute-done | bytes 884768 | tf_op jit(solution)/shard_map/ppermute | solution.py:1413
  412.8 2.2 land.5
  415.1 2.9 collective-permute-start.2
  417.9 0.7 iota_compare_fusion
  419.3 3.4 all-to-all-done.6
  422.7 6.5 %deal_in.1.refs_0_ = f32[8,256,768]{2,1,0:T(8,128)} custom-call(s32[32]{0:T(128)} %start.1.refs_0_, bf16[4,1,384,768]{3,2,1,0:T(8,128)(2,1)} %bitcast.3.refs_3_.refs_4_.refs_1_, bf16[4,1,256,768]{3,2,1,0:T(8,128)(2,1)} %bitcast.7.refs_2_.refs_4_, bf16[4,1,384,768]{3,2,1,0:T(8,128)(2,1)} %bitcast.3.refs_3_.refs_4_.refs_1_, ...), custom_call_target="tpu_custom_call" | custom-call | bytes 9437184 | tf_op jit(solution)/shard_map/deal_in/pallas_call | solution.py:1008
  429.2 6.6 %collective-permute-done.2 = bf16[2,2,144,384]{3,2,1,0:T(8,128)(2,1)S(1)} collective-permute-done((bf16[2,2,144,384]{3,2,1,0:T(8,128)(2,1)}, bf16[2,2,144,384]{3,2,1,0:T(8,128)(2,1)S(1)}, u32[]{:S(2)}, u32[]{:S(2)}) %collective-permute-start.2) | collective-permute-done | bytes 442400 | tf_op jit(solution)/shard_map/ppermute | solution.py:1413
  435.8 0.8 copy-done
  436.6 2.0 land.6
  438.5 0.9 broadcast_in_dim.62
  439.6 0.8 pad_maximum_fusion.4
  441.0 4.2 collective-permute-done.3
  445.4 4.2 collective-permute-start.6
  449.5 2.2 collective-permute-done.4
  452.4 3.4 collective-permute-start.5
  456.4 13.3 %collective-permute-done.6 = bf16[1,2,144,384]{3,2,1,0:T(8,128)(2,1)S(1)} collective-permute-done((bf16[1,2,144,384]{3,2,1,0:T(8,128)(2,1)}, bf16[1,2,144,384]{3,2,1,0:T(8,128)(2,1)S(1)}, u32[]{:S(2)}, u32[]{:S(2)}) %collective-permute-start.6) | collective-permute-done | bytes 221216 | tf_op jit(solution)/shard_map/ppermute | solution.py:1413
  470.5 1.8 land.7
  472.9 0.9 pad_maximum_fusion
  473.8 1.2 fusion
  475.0 2.1 finish.1
  477.8 1.7 finish_qkv.1
  (56 shorter events, 7.2 us)
Async XLA Ops:
  12.4 4.5 copy-start.7
  12.4 4.7 copy-start.2
  12.4 25.3 %all-to-all-start = ((bf16[4,256,768]{2,1,0:T(8,128)(2,1)}), bf16[4,256,768]{2,1,0:T(8,128)(2,1)}, u32[]{:S(2)}, u32[]{:S(2)}) async-start(bf16[4,256,768]{2,1,0:T(8,128)(2,1)} %gather_first.1), calls=%async_computation | async-start | bytes 3145728 | tf_op jit(solution)/shard_map/all_to_all | solution.py:1386
  37.7 33.1 %all-to-all-start.1 = ((bf16[4,384,768]{2,1,0:T(8,128)(2,1)}), bf16[4,384,768]{2,1,0:T(8,128)(2,1)}, u32[]{:S(2)}, u32[]{:S(2)}) async-start(bf16[4,384,768]{2,1,0:T(8,128)(2,1)} %gate.5.refs_4_), calls=%async_computation.1 | async-start | bytes 4718592 | tf_op jit(solution)/shard_map/all_to_all | solution.py:1386
  70.7 47.7 %all-to-all-start.2 = ((bf16[4,2,256,768]{3,2,1,0:T(8,128)(2,1)}), bf16[4,2,256,768]{3,2,1,0:T(8,128)(2,1)}, u32[]{:S(2)}, u32[]{:S(2)}) async-start(bf16[4,2,256,768]{3,2,1,0:T(8,128)(2,1)} %gate.6.refs_8_), calls=%async_computation.2 | async-start | bytes 6291456 | tf_op jit(solution)/shard_map/all_to_all | solution.py:1386
  75.4 399.6 %reduce-scatter.2.cloned.1.call-start = ((), (), s32[]{:S(2)}) async-start(), calls=%async_computation.8 | async-start | bytes 15814656 | tf_op jit(solution)/shard_map/reduce_scatter | solution.py:1449
  259.1 52.0 %all-to-all-start.3 = ((bf16[4,2,256,768]{3,2,1,0:T(8,128)(2,1)}), bf16[4,2,256,768]{3,2,1,0:T(8,128)(2,1)}, u32[]{:S(2)}, u32[]{:S(2)}) async-start(bf16[4,2,256,768]{3,2,1,0:T(8,128)(2,1)} %get-tuple-element.74), calls=%async_computation.3 | async-start | bytes 6291456 | tf_op jit(solution)/shard_map/all_to_all | solution.py:1386
  311.1 48.5 %all-to-all-start.4 = ((bf16[4,384,768]{2,1,0:T(8,128)(2,1)}), bf16[4,384,768]{2,1,0:T(8,128)(2,1)}, u32[]{:S(2)}, u32[]{:S(2)}) async-start(bf16[4,384,768]{2,1,0:T(8,128)(2,1)} %get-tuple-element.90), calls=%async_computation.4 | async-start | bytes 4718592 | tf_op jit(solution)/shard_map/all_to_all | solution.py:1386
  316.1 38.7 %copy-start.5 = (f32[2,3,768]{2,1,0:T(4,128)S(1)}, f32[2,3,768]{2,1,0:T(4,128)}, u32[]{:S(2)}) copy-start(f32[2,3,768]{2,1,0:T(4,128)} %get-tuple-element.99) | copy-start | bytes 55300
  316.1 38.7 %copy-start.6 = (f32[2,4,768]{2,1,0:T(4,128)S(1)}, f32[2,4,768]{2,1,0:T(4,128)}, u32[]{:S(2)}) copy-start(f32[2,4,768]{2,1,0:T(4,128)} %get-tuple-element.98) | copy-start | bytes 73732
  316.1 38.7 %copy-start.9 = (f32[1,2,768]{2,1,0:T(2,128)S(1)}, f32[1,2,768]{2,1,0:T(2,128)}, u32[]{:S(2)}) copy-start(f32[1,2,768]{2,1,0:T(2,128)} %get-tuple-element.96) | copy-start | bytes 18436
  359.6 20.7 %collective-permute-start = (bf16[8,2,144,384]{3,2,1,0:T(8,128)(2,1)}, bf16[8,2,144,384]{3,2,1,0:T(8,128)(2,1)}, u32[]{:S(2)}, u32[]{:S(2)}) collective-permute-start(bf16[8,2,144,384]{3,2,1,0:T(8,128)(2,1)} %get-tuple-element.95), channel_id=1, source_target_pairs={{0,1},{1,0},{2,3},{3,2},{4,5},{5,4},{6,7},{7,6},{8,9},{9,8},{10,11... | collective-permute-start | bytes 5308424 | tf_op jit(solution)/shard_map/ppermute | solution.py:1413
  384.4 28.4 %collective-permute-start.1 = (bf16[4,2,144,384]{3,2,1,0:T(8,128)(2,1)}, bf16[4,2,144,384]{3,2,1,0:T(8,128)(2,1)}, u32[]{:S(2)}, u32[]{:S(2)}) collective-permute-start(bf16[4,2,144,384]{3,2,1,0:T(8,128)(2,1)} %get-tuple-element.100.refs_5_.refs_1_), channel_id=1, source_target_pairs={{0,4},{4,0},{8,12},{12,8},{16,20},{20,16},{24,28},{28,24},{1,5},{5... | collective-permute-start | bytes 2654216 | tf_op jit(solution)/shard_map/ppermute | solution.py:1413
  384.4 4.4 copy-start.8
  384.5 38.2 %all-to-all-start.6 = ((bf16[4,256,768]{2,1,0:T(8,128)(2,1)}), bf16[4,256,768]{2,1,0:T(8,128)(2,1)}, u32[]{:S(2)}, u32[]{:S(2)}) async-start(bf16[4,256,768]{2,1,0:T(8,128)(2,1)} %gate.8), calls=%async_computation.6 | async-start | bytes 3145728 | tf_op jit(solution)/shard_map/all_to_all | solution.py:1386
  395.1 23.5 %copy-start.3 = (bf16[8,768]{1,0:T(8,128)(2,1)S(1)}, bf16[8,768]{1,0:T(8,128)(2,1)}, u32[]{:S(2)}) copy-start(bf16[8,768]{1,0:T(8,128)(2,1)} %param.15) | copy-start | bytes 36868
  415.1 20.7 %collective-permute-start.2 = (bf16[2,2,144,384]{3,2,1,0:T(8,128)(2,1)}, bf16[2,2,144,384]{3,2,1,0:T(8,128)(2,1)S(1)}, u32[]{:S(2)}, u32[]{:S(2)}) collective-permute-start(bf16[2,2,144,384]{3,2,1,0:T(8,128)(2,1)} %get-tuple-element.104.refs_5_), channel_id=1, source_target_pairs={{0,8},{4,12},{8,0},{12,4},{16,24},{20,28},{24,16},{28,20},{1,9},{5... | collective-permute-start | bytes 1327112 | tf_op jit(solution)/shard_map/ppermute | solution.py:1413
  435.8 0.8 copy-start
  440.4 4.8 collective-permute-start.3
  445.3 6.4 %collective-permute-start.4 = (bf16[16,2496]{1,0:T(8,128)(2,1)S(1)}, bf16[16,2496]{1,0:T(8,128)(2,1)S(1)}, u32[]{:S(2)}, u32[]{:S(2)}) collective-permute-start(bf16[16,2496]{1,0:T(8,128)(2,1)S(1)} %pad_maximum_fusion.3), channel_id=1, source_target_pairs={{0,8},{4,12},{8,0},{12,4},{16,24},{20,28},{24,16},{28,20},{1,9},{5... | collective-permute-start | bytes 239624 | tf_op jit(solution)/shard_map/ppermute | solution.py:1443
  445.4 24.4 %collective-permute-start.6 = (bf16[1,2,144,384]{3,2,1,0:T(8,128)(2,1)}, bf16[1,2,144,384]{3,2,1,0:T(8,128)(2,1)S(1)}, u32[]{:S(2)}, u32[]{:S(2)}) collective-permute-start(bf16[1,2,144,384]{3,2,1,0:T(8,128)(2,1)} %get-tuple-element.107.refs_1_), channel_id=1, source_target_pairs={{0,16},{4,20},{8,24},{12,28},{16,0},{20,4},{24,8},{28,12},{1,17},{... | collective-permute-start | bytes 663560 | tf_op jit(solution)/shard_map/ppermute | solution.py:1413
  452.4 20.5 %collective-permute-start.5 = (bf16[32,2496]{1,0:T(8,128)(2,1)}, bf16[32,2496]{1,0:T(8,128)(2,1)}, u32[]{:S(2)}, u32[]{:S(2)}) collective-permute-start(bf16[32,2496]{1,0:T(8,128)(2,1)} %pad_maximum_fusion.1), channel_id=1, source_target_pairs={{0,16},{4,20},{8,24},{12,28},{16,0},{20,4},{24,8},{28,12},{1,17},{... | collective-permute-start | bytes 479240 | tf_op jit(solution)/shard_map/ppermute | solution.py:1443
  469.8 0.7 copy-start.1
  472.2 5.0 %collective-permute-start.7 = (bf16[1,1,144,384]{3,2,1,0:T(8,128)(2,1)}, bf16[1,1,144,384]{3,2,1,0:T(8,128)(2,1)S(1)}, u32[]{:S(2)}, u32[]{:S(2)}) collective-permute-start(bf16[1,1,144,384]{3,2,1,0:T(8,128)(2,1)} %get-tuple-element.110), channel_id=1, source_target_pairs={{0,2},{1,3},{2,0},{3,1},{4,6},{5,7},{6,4},{7,5},{8,10},{9,11},{10,... | collective-permute-start | bytes 331784 | tf_op jit(solution)/shard_map/ppermute | solution.py:1413
  477.2 0.6 copy-start.4
Sparse Core Ops, SparseCore 0:
  259.2 210.1 reduce-scatter.1
